TPU v7x, 256 devices: a whole 4x4x8 slice. The times are simulated.
256 devices in a mesh: roll: 64 (over z, y, core), head: 4 (over x).
Axes of the slice: x: 4, y: 4, z: 8, core: 2. Of those that a mesh axis runs over, the one named last changes fastest.
Arguments:
- query: bfloat16 [64, 384, 3584], P('roll', None, 'head'), may hold values from -6 to 6
- key_suffix: bfloat16 [64, 384, 512], P('roll', None, 'head'), may hold values from -6 to 6
- value_suffix: bfloat16 [64, 384, 512], P('roll', None, 'head'), may hold values from -6 to 6
- key_prompt: bfloat16 [2, 2048, 512], P(None, 'roll', 'head'), may hold values from -6 to 6
- value_prompt: bfloat16 [2, 2048, 512], P(None, 'roll', 'head'), may hold values from -6 to 6
- attn_out: bfloat16 [64, 384, 3584], P('roll', None, 'head'), may hold values from -6 to 6
- grad_out: bfloat16 [64, 384, 3584], P('roll', 'head'), may hold values from -24 to 24
- log_norm: float32 [64, 28, 384], P('roll', 'head'), as said below
- prompt_id: int32 [64], P('roll'), may hold values from 0 to 1
- lengths: int32 [64], P('roll'), may hold values from 48 to 384, as said below
Outputs:
- grad_query: bfloat16 [64, 384, 3584], P('roll', None, 'head')
- grad_key_suffix: bfloat16 [64, 384, 512], P('roll', None, 'head')
- grad_value_suffix: bfloat16 [64, 384, 512], P('roll', None, 'head')
- grad_key_prompt: bfloat16 [2, 2048, 512], P(None, 'roll', 'head')
- grad_value_prompt: bfloat16 [2, 2048, 512], P(None, 'roll', 'head')
Inputs may be any that keep to these rules, and one draw needn't show every extreme that they name: Valid lengths of the rollouts; some rollout has 384 valid tokens and some has 48. `log_norm`: one value a query row and head.
All inputs are finite; a program needn't handle non-finite values.
Results may differ from a plain program's by a relative error of at most 0.005.
Values may be sent and summed in bfloat16 or wider, within the bound.
No kernel may reach another device: no remote copies, remote signals or barrier semaphores. Data moves between devices by JAX's collectives and lax.ppermute only.
A program may use at most 64 MiB of HBM per device.

v0:
```python
import jax
import jax.numpy as jnp
from jax import lax
from jax.sharding import PartitionSpec as P


def attend_grads(rows_query, rows_grad, norm_rows, row_delta, key_rows, value_rows, visible):
    score_scale = key_rows.shape[-1] ** (-0.5)
    scores = (
        lax.dot_general(
            rows_query, key_rows, (((1,), (1,)), ((), ())), preferred_element_type=jnp.float32
        )
        * score_scale
    )
    weights = jnp.exp(scores - norm_rows[:, None])
    weights = jnp.where(visible, weights, jnp.zeros_like(weights))
    weight_grad = lax.dot_general(
        rows_grad, value_rows, (((1,), (1,)), ((), ())), preferred_element_type=jnp.float32
    )
    score_grad = (weights * (weight_grad - row_delta[:, None]) * score_scale).astype(jnp.bfloat16)
    weights_rounded = weights.astype(jnp.bfloat16)
    query_grad = jnp.dot(score_grad, key_rows, preferred_element_type=jnp.float32)
    key_grad = lax.dot_general(
        score_grad, rows_query, (((0,), (0,)), ((), ())), preferred_element_type=jnp.float32
    )
    value_grad = lax.dot_general(
        weights_rounded, rows_grad, (((0,), (0,)), ((), ())), preferred_element_type=jnp.float32
    )
    return (query_grad, key_grad, value_grad)


def prompt_tile(rows_query, rows_grad, norm_rows, row_delta, key_rows, value_rows):
    score_scale = key_rows.shape[-1] ** (-0.5)
    scores_t = (
        lax.dot_general(
            key_rows, rows_query, (((1,), (1,)), ((), ())), preferred_element_type=jnp.float32
        )
        * score_scale
    )
    weights_t = jnp.exp(scores_t - norm_rows[None, :])
    weight_grad_t = lax.dot_general(
        value_rows, rows_grad, (((1,), (1,)), ((), ())), preferred_element_type=jnp.float32
    )
    score_grad_t = (weights_t * (weight_grad_t - row_delta[None, :]) * score_scale).astype(
        jnp.bfloat16
    )
    weights_rounded_t = weights_t.astype(jnp.bfloat16)
    query_grad = lax.dot_general(
        score_grad_t, key_rows, (((0,), (0,)), ((), ())), preferred_element_type=jnp.float32
    )
    key_grad = jnp.dot(score_grad_t, rows_query, preferred_element_type=jnp.float32)
    value_grad = jnp.dot(weights_rounded_t, rows_grad, preferred_element_type=jnp.float32)
    return (query_grad, key_grad, value_grad)


def prompt_part(rows_query, rows_grad, norm_rows, row_delta, key_rows, value_rows):
    key_count = key_rows.shape[0]
    tile_rows = 256
    width = key_rows.shape[1]

    def visit_tile(query_acc, pair_tiles):
        part_query, part_key, part_value = prompt_tile(
            rows_query, rows_grad, norm_rows, row_delta, pair_tiles[0], pair_tiles[1]
        )
        return (query_acc + part_query, (part_key, part_value))

    start_acc = jnp.zeros(rows_query.shape, jnp.float32)
    query_acc, (key_tiles, value_tiles) = lax.scan(
        visit_tile,
        start_acc,
        (
            key_rows.reshape(key_count // tile_rows, tile_rows, width),
            value_rows.reshape(key_count // tile_rows, tile_rows, width),
        ),
    )
    return (query_acc, key_tiles.reshape(key_count, width), value_tiles.reshape(key_count, width))


def per_device(
    query,
    key_suffix,
    value_suffix,
    key_prompt,
    value_prompt,
    attn_out,
    grad_out,
    log_norm,
    prompt_id,
    lengths,
):
    width = key_suffix.shape[2]
    group_size = query.shape[2] // width
    seq_len = query.shape[1]
    row_count = seq_len * group_size
    grad_local = lax.all_to_all(grad_out, "head", split_axis=2, concat_axis=1, tiled=True)
    rows_query = query[0].reshape(row_count, width)
    rows_out = attn_out[0].reshape(row_count, width)
    position = jnp.arange(row_count) // group_size
    live_row = position < lengths[0]
    rows_grad = grad_local[0].reshape(row_count, width)
    rows_grad = jnp.where(live_row[:, None], rows_grad, jnp.zeros_like(rows_grad))
    norm_rows = log_norm[0].T.reshape(row_count)
    row_delta = jnp.sum(rows_grad.astype(jnp.float32) * rows_out.astype(jnp.float32), axis=1)
    causal = jnp.arange(seq_len)[None, :] <= position[:, None]
    suffix_query, suffix_key, suffix_value = attend_grads(
        rows_query, rows_grad, norm_rows, row_delta, key_suffix[0], value_suffix[0], causal
    )
    chosen = prompt_id[0]
    prompt_count = key_prompt.shape[0]
    whole_keys, whole_values = (
        lax.all_gather(key_prompt, "roll", axis=1, tiled=True),
        lax.all_gather(value_prompt, "roll", axis=1, tiled=True),
    )
    key_rows = lax.dynamic_index_in_dim(whole_keys, chosen, 0, keepdims=False)
    value_rows = lax.dynamic_index_in_dim(whole_values, chosen, 0, keepdims=False)
    prompt_query, prompt_key, prompt_value = prompt_part(
        rows_query, rows_grad, norm_rows, row_delta, key_rows, value_rows
    )
    grad_query = (
        (prompt_query + suffix_query)
        .reshape(seq_len, group_size * width)
        .astype(jnp.bfloat16)[None]
    )
    prompt_mask = (jnp.arange(prompt_count) == chosen).astype(jnp.float32)[:, None, None]
    key_terms = prompt_mask * prompt_key[None]
    value_terms = prompt_mask * prompt_value[None]
    key_share, value_share = (
        lax.psum_scatter(key_terms, "roll", scatter_dimension=1, tiled=True),
        lax.psum_scatter(value_terms, "roll", scatter_dimension=1, tiled=True),
    )
    return (
        grad_query,
        suffix_key.astype(jnp.bfloat16)[None],
        suffix_value.astype(jnp.bfloat16)[None],
        key_share.astype(jnp.bfloat16),
        value_share.astype(jnp.bfloat16),
    )


def solution(mesh):
    in_specs = (
        P("roll", None, "head"),
        P("roll", None, "head"),
        P("roll", None, "head"),
        P(None, "roll", "head"),
        P(None, "roll", "head"),
        P("roll", None, "head"),
        P("roll", "head", None),
        P("roll", "head", None),
        P("roll"),
        P("roll"),
    )
    out_specs = (
        P("roll", None, "head"),
        P("roll", None, "head"),
        P("roll", None, "head"),
        P(None, "roll", "head"),
        P(None, "roll", "head"),
    )
    return jax.shard_map(
        per_device, mesh=mesh, in_specs=in_specs, out_specs=out_specs, check_vma=False
    )
```

profile of v0, /device:TPU:6, one launch (start us, length us, event | category | flops | bytes accessed | tf_op | source)
XLA Modules:
  0.0 509.2 jit_solution(10414499697248437702)
XLA Ops:
  8.7 4.3 copy.30
  13.4 19.7 %reduce = bf16[3584,96]{1,0:T(8,128)(2,1)S(1)} reduce(bf16[3584,1,96]{2,1,0:T(2,128)(2,1)S(1)} %bitcast.97, bf16[]{:T(256)} %broadcast.96), dimensions={1}, to_apply=%bitcast.43.reduce_sub_computation | reduce | bytes 1376258
  33.2 2.2 reshape.87
  35.3 5.7 %all-to-all-start = ((bf16[4,2,43008]{2,1,0:T(2,128)(2,1)}), bf16[4,2,43008]{2,1,0:T(2,128)(2,1)S(1)}, u32[]{:S(2)}, u32[]{:S(2)}) async-start(bf16[4,2,43008]{2,1,0:T(2,128)(2,1)} %reshape.87), calls=%async_computation | async-start | bytes 1376256 | tf_op jit(solution)/shard_map/all_to_all | solution.py:95
  44.6 2.6 reshape.86
  47.9 1.4 all-to-all-done
  49.3 2.5 reshape.88
  51.8 3.7 copy.31
  55.8 1.5 reshape_squeeze.8
  57.3 2.3 multiply_reduce_fusion
  59.6 24.3 %all-gather.3.cloned.1.call-done = bf16[2,2048,128]{2,1,0:T(8,128)(2,1)} async-done(((bf16[2,32,128]{2,1,0:T(8,128)(2,1)}), bf16[2,2048,128]{2,1,0:T(8,128)(2,1)}) %all-gather.3.cloned.1.call-update) | async-done | bytes 1048592 | tf_op jit(solution)/shard_map/all_gather | solution.py:111
  84.0 1.9 constant_dynamic-slice_fusion.1
  85.8 70.3 %all-gather.5.cloned.1.call-done = bf16[2,2048,128]{2,1,0:T(8,128)(2,1)} async-done(((bf16[2,32,128]{2,1,0:T(8,128)(2,1)}), bf16[2,2048,128]{2,1,0:T(8,128)(2,1)}) %all-gather.5.cloned.1.call-update) | async-done | bytes 1048592 | tf_op jit(solution)/shard_map/all_gather | solution.py:112
  156.1 1.9 constant_dynamic-slice_fusion
  158.0 55.9 %while.16 = (s32[]{:T(128)}, f32[2688,128]{1,0:T(8,128)S(1)}, f32[8,256,128]{2,1,0:T(8,128)}, f32[8,256,128]{2,1,0:T(8,128)}, bf16[8,256,128]{2,1,0:T(8,128)(2,1...) while((s32[]{:T(128)}, f32[2688,128]{1,0:T(8,128)S(1)}, ...), condition=%wide.wide.region_2.3_spmd.clone, body=%wide.wide.region_1.2_spmd.clone.sunk | while | flops 886308864 | bytes 18373284 | solution.py:68
  158.0 1.4 fusion.97
  159.4 1.2 fusion.100
  160.6 1.4 fusion.98
  162.0 1.2 fusion.99
  163.2 1.8 convolution_add_fusion.4
  165.0 1.4 fusion.97
  166.4 1.2 fusion.100
  167.6 1.4 fusion.98
  170.1 1.8 convolution_add_fusion.4
  172.0 1.4 fusion.97
  173.3 1.2 fusion.100
  174.6 1.4 fusion.98
  175.9 1.2 fusion.99
  177.1 1.8 convolution_add_fusion.4
  179.0 1.4 fusion.97
  180.3 1.2 fusion.100
  181.5 1.4 fusion.98
  184.1 1.8 convolution_add_fusion.4
  185.9 1.4 fusion.97
  188.5 1.4 fusion.98
  191.1 1.8 convolution_add_fusion.4
  192.9 1.4 fusion.97
  194.3 1.2 fusion.100
  195.5 1.4 fusion.98
  196.9 1.2 fusion.99
  198.1 1.8 convolution_add_fusion.4
  199.9 1.4 fusion.97
  201.3 1.2 fusion.100
  202.5 1.4 fusion.98
  203.9 1.2 fusion.99
  205.1 1.8 convolution_add_fusion.4
  206.9 1.4 fusion.97
  208.3 1.2 fusion.100
  209.5 1.4 fusion.98
  212.1 1.8 convolution_add_fusion.4
  213.9 3.9 broadcast_multiply_fusion
  218.3 1.7 sub.47
  220.9 2.0 broadcast_in_dim.47
  222.9 2.4 broadcast_in_dim.48
  225.3 4.6 fusion.27
  231.4 1.8 select_n.45
  233.2 3.3 fusion.28
  236.5 1.4 fusion.35
  237.9 1.4 fusion.36
  240.1 1.5 convert_element_type.66
  241.6 116.1 %reduce-scatter.5.cloned.1.call-done = f32[2,32,128]{2,1,0:T(8,128)} async-done(((f32[2,2048,128]{2,1,0:T(8,128)}), f32[2,32,128]{2,1,0:T(8,128)}) %reduce-scatter.5.cloned.1.call-update) | async-done | bytes 32784 | tf_op jit(solution)/shard_map/reduce_scatter | solution.py:129
  357.8 1.4 convert_element_type.72
  359.1 142.1 %reduce-scatter.3.cloned.1.call-done = f32[2,32,128]{2,1,0:T(8,128)} async-done(((f32[2,2048,128]{2,1,0:T(8,128)}), f32[2,32,128]{2,1,0:T(8,128)}) %reduce-scatter.3.cloned.1.call-update) | async-done | bytes 32784 | tf_op jit(solution)/shard_map/reduce_scatter | solution.py:128
  501.3 1.4 convert_element_type.71
  (44 shorter events, 14.7 us)
Async XLA Ops:
  7.2 218.2 %copy-start = (bf16[1,384,128]{2,1,0:T(8,128)(2,1)S(1)}, bf16[1,384,128]{2,1,0:T(8,128)(2,1)}, u32[]{:S(2)}) copy-start(bf16[1,384,128]{2,1,0:T(8,128)(2,1)} %param.13) | copy-start | bytes 294916
  7.2 76.8 %all-gather.3.cloned.1.call-start = ((), (), s32[]{:S(2)}) async-start(), calls=%async_computation.3 | async-start | bytes 1064960 | tf_op jit(solution)/shard_map/all_gather | solution.py:111
  7.9 148.2 %all-gather.5.cloned.1.call-start = ((), (), s32[]{:S(2)}) async-start(), calls=%async_computation.4 | async-start | bytes 1064960 | tf_op jit(solution)/shard_map/all_gather | solution.py:112
  33.1 9.2 %copy-start.5 = (f32[1,7,384]{2,0,1:T(1,128)S(1)}, f32[1,7,384]{2,0,1:T(1,128)}, u32[]{:S(2)}) copy-start(f32[1,7,384]{2,0,1:T(1,128)} %param.19) | copy-start | bytes 32260
  33.1 10.8 %copy-start.4 = (bf16[1,384,896]{2,1,0:T(8,128)(2,1)S(1)}, bf16[1,384,896]{2,1,0:T(8,128)(2,1)}, u32[]{:S(2)}) copy-start(bf16[1,384,896]{2,1,0:T(8,128)(2,1)} %param.12) | copy-start | bytes 2064388
  35.3 13.9 %all-to-all-start = ((bf16[4,2,43008]{2,1,0:T(2,128)(2,1)}), bf16[4,2,43008]{2,1,0:T(2,128)(2,1)S(1)}, u32[]{:S(2)}, u32[]{:S(2)}) async-start(bf16[4,2,43008]{2,1,0:T(2,128)(2,1)} %reshape.87), calls=%async_computation | async-start | bytes 1376256 | tf_op jit(solution)/shard_map/all_to_all | solution.py:95
  41.0 316.8 %reduce-scatter.5.cloned.1.call-start = ((), (), s32[]{:S(2)}) async-start(), calls=%async_computation.6 | async-start | bytes 2129920 | tf_op jit(solution)/shard_map/reduce_scatter | solution.py:129
  42.5 0.7 copy-start.2
  158.0 55.9 %copy-start.6 = (f32[2]{0:T(128)S(1)}, f32[2]{0:T(128)}, u32[]{:S(2)}) copy-start(f32[2]{0:T(128)} %compare_convert_fusion) | copy-start | bytes 28
  217.8 283.5 %reduce-scatter.3.cloned.1.call-start = ((), (), s32[]{:S(2)}) async-start(), calls=%async_computation.5 | async-start | bytes 2129920 | tf_op jit(solution)/shard_map/reduce_scatter | solution.py:128
  225.3 4.6 copy-start.3
  233.2 4.7 copy-start.1
Sparse Core Ops, SparseCore 0:
  10.7 73.2 all-gather.2
  86.6 69.4 all-gather.4
  217.9 139.8 reduce-scatter.4
  362.2 139.0 reduce-scatter.2
where the time goes:
time: 511 us; the launch traced here: 509 us
  waiting for transfers between devices  356 us (70%)
  matrix products  67 us (13%)
  local copies, waits for them, and re-layouts  34.8 us (7%)
  other arithmetic  29.8 us (6%)
  between operations  15.2 us (3%)
  starting transfers between devices  6.01 us (1%)
    reduce_scatter x1, waiting for transfers between devices, per_device(): lax.psum_scatter(key_terms, 'roll', scatter_dimension=1, tiled=True)  142 us
    reduce_scatter x1, waiting for transfers between devices, per_device(): lax.psum_scatter(value_terms, 'roll', scatter_dimension=1, tiled=True)  116 us
    all_gather x1, waiting for transfers between devices, per_device(): lax.all_gather(value_prompt, 'roll', axis=1, tiled=True)  70.3 us
    all_gather x1, waiting for transfers between devices, per_device(): lax.all_gather(key_prompt, 'roll', axis=1, tiled=True)  24.3 us
    unnamed x2, other arithmetic  19.7 us
    dot_general x8, matrix products, prompt_tile(): lax.dot_general(score_grad_t, key_rows, (((0,), (0,)), ((), ())), preferr...  14.3 us
    dot_general x8, matrix products, prompt_tile(): lax.dot_general(key_rows, rows_query, (((1,), (1,)), ((), ())), preferred...  11.1 us
    dot_general x8, matrix products, prompt_tile(): lax.dot_general(value_rows, rows_grad, (((1,), (1,)), ((), ())), preferre...  10.9 us
  transfers between devices with their start and end apart: 5, of which 5 were waited for; matrix products, arithmetic and copies ran while one was open for 13% of the time, Pallas kernels for 0%

commit v1 on v0

v1 whole, which is shorter than its diff:
```python
import functools

import jax
import jax.numpy as jnp
from jax import lax
from jax.experimental import pallas as pl
from jax.experimental.pallas import tpu as pltpu
from jax.sharding import Mesh
from jax.sharding import PartitionSpec as P

BF16 = jnp.bfloat16
F32 = jnp.float32
GROUP = ("y", "c")


def score_blocks(key_rows, value_rows, query_t, grad_t, norm_row, delta_row, scale, visible=None):
    scores_t = jnp.dot(key_rows, query_t, preferred_element_type=F32) * scale
    weights_t = jnp.exp(scores_t - norm_row)
    if visible is not None:
        weights_t = jnp.where(visible, weights_t, jnp.zeros_like(weights_t))
    weight_grad_t = jnp.dot(value_rows, grad_t, preferred_element_type=F32)
    score_grad_t = (weights_t * (weight_grad_t - delta_row) * scale).astype(BF16)
    return weights_t.astype(BF16), score_grad_t


def suffix_kernel(
    length_ref, query_ref, out_ref, grad_ref, norm_ref, key_ref, value_ref,
    query_rows_ref, grad_rows_ref, query_t_ref, grad_t_ref, norm_row_ref, delta_row_ref,
    query_acc_ref, key_grad_ref, value_grad_ref,
):
    seq_len, width = key_ref.shape
    group_size = query_ref.shape[1] // width
    scale = width ** (-0.5)
    live_down = lax.broadcasted_iota(jnp.int32, (seq_len, width), 0) < length_ref[0]
    key_at = lax.broadcasted_iota(jnp.int32, (seq_len, seq_len), 0)
    query_at = lax.broadcasted_iota(jnp.int32, (seq_len, seq_len), 1)
    causal = key_at <= query_at
    key_rows, value_rows = key_ref[...], value_ref[...]
    key_t = key_rows.T
    key_acc = jnp.zeros((seq_len, width), F32)
    value_acc = jnp.zeros((seq_len, width), F32)
    for head in range(group_size):
        cols = slice(head * width, (head + 1) * width)
        rows = slice(head * seq_len, (head + 1) * seq_len)
        query_rows = query_ref[:, cols]
        grad_rows = grad_ref[:, cols]
        grad_rows = jnp.where(live_down, grad_rows, jnp.zeros_like(grad_rows))
        query_t, grad_t = query_rows.T, grad_rows.T
        out_t = out_ref[:, cols].T
        delta_row = jnp.sum(grad_t.astype(F32) * out_t.astype(F32), axis=0, keepdims=True)
        norm_row = norm_ref[head : head + 1, :]
        query_rows_ref[rows, :] = query_rows
        grad_rows_ref[rows, :] = grad_rows
        query_t_ref[:, rows] = query_t
        grad_t_ref[:, rows] = grad_t
        norm_row_ref[:, rows] = norm_row
        delta_row_ref[:, rows] = delta_row
        weights_t, score_grad_t = score_blocks(
            key_rows, value_rows, query_t, grad_t, norm_row, delta_row, scale, causal
        )
        query_acc_ref[:, rows] = jnp.dot(key_t, score_grad_t, preferred_element_type=F32)
        key_acc += jnp.dot(score_grad_t, query_rows, preferred_element_type=F32)
        value_acc += jnp.dot(weights_t, grad_rows, preferred_element_type=F32)
    key_grad_ref[...] = key_acc.astype(BF16)
    value_grad_ref[...] = value_acc.astype(BF16)


def suffix_part(length, query, attn_out, grad, log_norm, key_suffix, value_suffix):
    seq_len, width = key_suffix.shape
    row_count = query.shape[0] * query.shape[1] // width
    shape = jax.ShapeDtypeStruct
    vmem = pl.BlockSpec(memory_space=pltpu.VMEM)
    return pl.pallas_call(
        suffix_kernel,
        in_specs=[pl.BlockSpec(memory_space=pltpu.SMEM)] + [vmem] * 6,
        out_specs=[vmem] * 9,
        out_shape=[
            shape((row_count, width), BF16),
            shape((row_count, width), BF16),
            shape((width, row_count), BF16),
            shape((width, row_count), BF16),
            shape((1, row_count), F32),
            shape((1, row_count), F32),
            shape((width, row_count), F32),
            shape((seq_len, width), BF16),
            shape((seq_len, width), BF16),
        ],
        compiler_params=pltpu.CompilerParams(vmem_limit_bytes=48 * 1024 * 1024),
        name="suffix_part",
    )(length, query, attn_out, grad, log_norm, key_suffix, value_suffix)


def prompt_kernel(
    query_rows_ref, grad_rows_ref, query_t_ref, grad_t_ref, norm_row_ref, delta_row_ref,
    query_acc_ref, pair_ref, query_grad_ref, pair_grad_ref, acc_ref, *, blocks,
):
    width = query_rows_ref.shape[1]
    scale = width ** (-0.5)
    step = pl.program_id(0)

    @pl.when(step == 0)
    def _():
        acc_ref[...] = query_acc_ref[...]

    key_rows, value_rows = pair_ref[0, 0], pair_ref[0, 1]
    key_t = key_rows.T
    key_acc = jnp.zeros(key_rows.shape, F32)
    value_acc = jnp.zeros(key_rows.shape, F32)
    for rows in blocks:
        weights_t, score_grad_t = score_blocks(
            key_rows, value_rows, query_t_ref[:, rows], grad_t_ref[:, rows],
            norm_row_ref[:, rows], delta_row_ref[:, rows], scale,
        )
        acc_ref[:, rows] += jnp.dot(key_t, score_grad_t, preferred_element_type=F32)
        key_acc += jnp.dot(score_grad_t, query_rows_ref[rows, :], preferred_element_type=F32)
        value_acc += jnp.dot(weights_t, grad_rows_ref[rows, :], preferred_element_type=F32)
    pair_grad_ref[0, 0] = key_acc.astype(BF16)
    pair_grad_ref[0, 1] = value_acc.astype(BF16)

    @pl.when(step == pl.num_programs(0) - 1)
    def _():
        seq_len = query_grad_ref.shape[0]
        for head in range(query_grad_ref.shape[1] // width):
            part = acc_ref[:, head * seq_len : (head + 1) * seq_len]
            query_grad_ref[:, head * width : (head + 1) * width] = part.T.astype(BF16)


def prompt_part(rows, query_acc, pair, seq_len):
    row_count, width = rows[0].shape
    wide = 2 * seq_len
    blocks = [slice(at, min(at + wide, row_count)) for at in range(0, row_count, wide)]
    whole = pl.BlockSpec(memory_space=pltpu.VMEM)
    tile = pl.BlockSpec((1,) + pair.shape[1:], lambda i: (i, 0, 0, 0))
    out_shape = (seq_len, row_count * width // seq_len)
    return pl.pallas_call(
        functools.partial(prompt_kernel, blocks=blocks),
        grid=(pair.shape[0],),
        in_specs=[whole] * 7 + [tile],
        out_specs=[pl.BlockSpec(out_shape, lambda i: (0, 0)), tile],
        out_shape=[jax.ShapeDtypeStruct(out_shape, BF16), jax.ShapeDtypeStruct(pair.shape, BF16)],
        scratch_shapes=[pltpu.VMEM((width, row_count), F32)],
        compiler_params=pltpu.CompilerParams(vmem_limit_bytes=48 * 1024 * 1024),
        name="prompt_part",
    )(*rows, query_acc, pair)


def exchange(blocks, axes):
    return lax.all_to_all(blocks, axes, split_axis=0, concat_axis=0, tiled=True)


def per_device(
    query, key_suffix, value_suffix, key_prompt, value_prompt, attn_out, grad_out, log_norm,
    prompt_id, lengths,
):
    seq_len, columns = query.shape[1:]
    width = key_suffix.shape[2]
    prompt_count, owned = key_prompt.shape[:2]
    heads, stacks, group = lax.axis_size("head"), lax.axis_size("z"), lax.axis_size(GROUP)

    grad_parts = [grad_out[0][:, columns * i : columns * (i + 1)] for i in range(heads)]
    grad_local = exchange(jnp.concatenate(grad_parts, 0), "head")

    own_pair = jnp.stack([key_prompt, value_prompt], 1).reshape(1, -1, width)
    stacked = exchange(jnp.broadcast_to(own_pair, (stacks,) + own_pair.shape[1:]), "z")
    ids = exchange(jnp.broadcast_to(prompt_id[:, None], (group, 128)), GROUP)[:, 0]
    stacked = stacked.reshape(stacks, prompt_count, 2, owned, width)
    stacked = stacked.transpose(1, 2, 0, 3, 4).reshape(prompt_count, 2, stacks * owned, width)
    wanted = (ids == 0)[:, None, None, None]
    pair = exchange(jnp.where(wanted, stacked[:1], stacked[1:]), GROUP)

    *rows, query_acc, key_grad, value_grad = suffix_part(
        lengths, query[0], attn_out[0], grad_local, log_norm[0], key_suffix[0], value_suffix[0]
    )
    query_grad, pair_grad = prompt_part(rows, query_acc, pair, seq_len)

    shares = exchange(pair_grad, GROUP).astype(F32)
    totals = jnp.stack(
        [
            jnp.sum(jnp.where((ids == i)[:, None, None, None], shares, 0.0), 0)
            for i in range(prompt_count)
        ],
        0,
    )
    totals = totals.reshape(prompt_count, 2, stacks, owned, width).transpose(2, 0, 1, 3, 4)
    totals = totals.astype(BF16).reshape(stacks, -1, width)
    final = jnp.sum(exchange(totals, "z").astype(F32), 0).astype(BF16)
    final = final.reshape(prompt_count, 2, owned, width)
    return (query_grad[None], key_grad[None], value_grad[None], final[:, 0], final[:, 1])


def solution(mesh):
    roll, head = mesh.devices.shape
    fine = Mesh(mesh.devices.reshape(roll // 8, 4, 2, head), ("z", "y", "c", "head"))
    rolls = ("z", "y", "c")
    by_rollout = P(rolls, None, "head")
    by_key = P(None, rolls, "head")
    by_row = P(rolls, "head", None)
    in_specs = (
        by_rollout, by_rollout, by_rollout, by_key, by_key, by_rollout, by_row, by_row,
        P(rolls), P(rolls),
    )
    out_specs = (by_rollout, by_rollout, by_rollout, by_key, by_key)
    return jax.shard_map(
        per_device, mesh=fine, in_specs=in_specs, out_specs=out_specs, check_vma=False
    )
```

time: 511 us -> 122 us (0.24)
  waiting for transfers between devices: 356 us -> 28 us
  matrix products: 67 us -> 0 us
  blocking collectives: 0 us -> 32.9 us
  local copies, waits for them, and re-layouts: 34.8 us -> 8.18 us
  other arithmetic: 29.8 us -> 3.41 us
  Pallas kernels: 0 us -> 25.3 us
  starting transfers between devices: 6.01 us -> 21.3 us
  between operations: 15.2 us -> 2.12 us
    reduce_scatter x2 -> x0, waiting for transfers between devices: 258 us -> none  [the longest x1 142 us: per_device(): lax.psum_scatter(key_terms, 'roll', scatter_dimension=1, tiled=True)]
    all_gather x2 -> x0, waiting for transfers between devices: 94.6 us -> none  [the longest x1 70.3 us: per_device(): lax.all_gather(value_prompt, 'roll', axis=1, tiled=True)]
    dot_general x45 -> x0, matrix products: 67 us -> none  [the longest x8 14.3 us: prompt_tile(): lax.dot_general(score_grad_t, key_rows, (((0,), (0,)), ((), ())), preferr...]
    all_to_all x0 -> x2, blocking collectives: none -> 32.9 us  [exchange(): return lax.all_to_all(blocks, axes, split_axis=0, concat_axis=0, tiled=True)]
    all_to_all x1 -> x4, waiting for transfers between devices: 1.41 us -> 28 us  [exchange(): return lax.all_to_all(blocks, axes, split_axis=0, concat_axis=0, tiled=True)]
    pallas_call x0 -> x2, Pallas kernels: none -> 25.3 us  [the longest x1 20.6 us: prompt_part(): pl.pallas_call(functools.partial(prompt_kernel, blocks=blocks), grid=(pai...]
    unnamed x2 -> x0, other arithmetic: 19.7 us -> none
    all_to_all x1 -> x4, starting transfers between devices: 5.67 us -> 21.3 us  [exchange(): return lax.all_to_all(blocks, axes, split_axis=0, concat_axis=0, tiled=True)]
  transfers between devices with their start and end apart: 5 -> 4, of which waited for: 5 -> 4; matrix products, arithmetic and copies ran while one was open for 13% -> 2% of each run, Pallas kernels for 0% -> 4%
where the time goes in v1:
time: 122 us; the launch traced here: 121 us
  blocking collectives  32.9 us (27%)
  waiting for transfers between devices  28 us (23%)
  Pallas kernels  25.3 us (21%)
  starting transfers between devices  21.3 us (17%)
  local copies, waits for them, and re-layouts  8.18 us (7%)
  other arithmetic  3.41 us (3%)
  between operations  2.12 us (2%)
    all_to_all x2, blocking collectives, exchange(): return lax.all_to_all(blocks, axes, split_axis=0, concat_axis=0, tiled=True)  32.9 us
    all_to_all x4, waiting for transfers between devices, exchange(): return lax.all_to_all(blocks, axes, split_axis=0, concat_axis=0, tiled=True)  28 us
    all_to_all x4, starting transfers between devices, exchange(): return lax.all_to_all(blocks, axes, split_axis=0, concat_axis=0, tiled=True)  21.3 us
    pallas_call x1, Pallas kernels, prompt_part(): pl.pallas_call(functools.partial(prompt_kernel, blocks=blocks), grid=(pai...  20.6 us
    unnamed x21, local copies, waits for them, and re-layouts  6.1 us
    pallas_call x1, Pallas kernels, suffix_part(): pl.pallas_call(suffix_kernel, in_specs=[pl.BlockSpec(memory_space=pltpu.S...  4.67 us
  transfers between devices with their start and end apart: 4, of which 4 were waited for; matrix products, arithmetic and copies ran while one was open for 2% of the time, Pallas kernels for 4%

profile of v1, /device:TPU:6, one launch (start us, length us, event | category | flops | bytes accessed | tf_op | source)
XLA Modules:
  0.0 121.1 jit_solution(15067676786245816851)
XLA Ops:
  0.6 0.0 copy-start.8
  1.4 0.6 broadcast_in_dim.72
  2.0 4.5 %all-to-all-start.1 = ((s32[8,1,128]{2,1,0:T(1,128)}), s32[8,1,128]{2,1,0:T(1,128)S(1)}, u32[]{:S(2)}, u32[]{:S(2)}) async-start(s32[8,1,128]{2,1,0:T(1,128)} %broadcast_in_dim.72), calls=%async_computation.1 | async-start | bytes 8192 | tf_op jit(solution)/shard_map/all_to_all | solution.py:148
  6.4 0.7 pad_maximum_fusion.1
  7.2 4.4 %all-to-all-done.1 = s32[8,1,128]{2,1,0:T(1,128)S(1)} async-done(((s32[8,1,128]{2,1,0:T(1,128)}), s32[8,1,128]{2,1,0:T(1,128)S(1)}, u32[]{:S(2)}, u32[]{:S(2)}) %all-to-all-start.1) | async-done | bytes 4128 | tf_op jit(solution)/shard_map/all_to_all | solution.py:148
  11.6 0.7 broadcast_in_dim.75
  12.4 8.5 %all-to-all-start.2 = ((bf16[8,128,128]{2,1,0:T(8,128)(2,1)}), bf16[8,128,128]{2,1,0:T(8,128)(2,1)S(1)}, u32[]{:S(2)}, u32[]{:S(2)}) async-start(bf16[8,128,128]{2,1,0:T(8,128)(2,1)} %broadcast_in_dim.75), calls=%async_computation.2 | async-start | bytes 524288 | tf_op jit(solution)/shard_map/all_to_all | solution.py:148
  20.8 0.0 copy-done.8
  20.8 0.1 fusion.2
  20.9 0.9 pad_maximum_fusion
  21.8 10.9 %all-to-all-done.2 = bf16[8,128,128]{2,1,0:T(8,128)(2,1)S(1)} async-done(((bf16[8,128,128]{2,1,0:T(8,128)(2,1)}), bf16[8,128,128]{2,1,0:T(8,128)(2,1)S(1)}, u32[]{:S(2)}, u32[]{:S(2)}) %all-to-all-start.2) | async-done | bytes 262176 | tf_op jit(solution)/shard_map/all_to_all | solution.py:148
  32.7 4.8 %all-to-all-start = ((bf16[4,96,896]{2,1,0:T(8,128)(2,1)}), bf16[4,96,896]{2,1,0:T(8,128)(2,1)S(1)}, u32[]{:S(2)}, u32[]{:S(2)}) async-start(bf16[4,96,896]{2,1,0:T(8,128)(2,1)} %bitcast.3), calls=%async_computation | async-start | bytes 1376256 | tf_op jit(solution)/shard_map/all_to_all | solution.py:148
  37.5 0.1 compare_reduce_fusion
  37.7 1.1 broadcast_select_fusion
  38.8 0.0 copy-start.9
  38.8 0.0 copy-start.6
  38.8 0.0 copy-start.7
  38.8 6.0 %all-to-all-done = bf16[4,96,896]{2,1,0:T(8,128)(2,1)S(1)} async-done(((bf16[4,96,896]{2,1,0:T(8,128)(2,1)}), bf16[4,96,896]{2,1,0:T(8,128)(2,1)S(1)}, u32[]{:S(2)}, u32[]{:S(2)}) %all-to-all-start) | async-done | bytes 688160 | tf_op jit(solution)/shard_map/all_to_all | solution.py:148
  44.8 3.6 %all-to-all-start.3 = ((bf16[8,2,256,128]{3,2,1,0:T(8,128)(2,1)}), bf16[8,2,256,128]{3,2,1,0:T(8,128)(2,1)S(1)}, u32[]{:S(2)}, u32[]{:S(2)}) async-start(bf16[8,2,256,128]{3,2,1,0:T(8,128)(2,1)} %broadcast_select_fusion), calls=%async_computation.3 | async-start | bytes 2097152 | tf_op jit(solution)/shard_map/all_to_all | solution.py:148
  49.0 0.0 copy-done.9
  49.0 0.0 copy-done.6
  49.0 0.0 copy-done.7
  49.0 0.0 copy-start.4
  49.0 1.1 copy-done.4
  50.1 0.0 copy-start.5
  50.1 1.1 copy-done.5
  51.2 4.7 %suffix_part.1 = (bf16[2688,128]{1,0:T(8,128)(2,1)S(1)}, bf16[2688,128]{1,0:T(8,128)(2,1)S(1)}, bf16[128,2688]{1,0:T(8,128)(2,1)S(1)}, bf16[128,2688]{1,0:T(8,12...) custom-call(s32[1]{0:T(128)S(6)} %copy.28.length_ref, ...), custom_call_target="tpu_custom_call" | custom-call | tf_op jit(solution)/shard_map/suffix_part/pallas_call | solution.py:73
  55.9 0.0 copy-start
  55.9 0.8 copy-done
  56.7 0.0 copy-start.2
  56.8 0.8 copy-done.2
  57.6 6.6 %all-to-all-done.3.pair_ref = bf16[8,2,256,128]{3,2,1,0:T(8,128)(2,1)S(1)} async-done(((bf16[8,2,256,128]{3,2,1,0:T(8,128)(2,1)}), bf16[8,2,256,128]{3,2,1,0:T(8,128)(2,1)S(1)}, u32[]{:S(2)}, u32[]{:S(2)}) %all-to-all-start.3) | async-done | bytes 1048608 | tf_op jit(solution)/shard_map/all_to_all | solution.py:148
  64.2 0.0 copy-start.1
  64.2 1.1 copy-done.1
  65.3 0.0 copy-start.3
  65.3 1.1 copy-done.3
  66.4 20.6 %prompt_part.1 = (bf16[384,896]{1,0:T(8,128)(2,1)}, bf16[8,2,256,128]{3,2,1,0:T(8,128)(2,1)S(1)}) custom-call(bf16[2688,128]{1,0:T(8,128)(2,1)S(1)} %get-tuple-element.16.query_rows_ref, bf16[2688,128]{1,0:T(8,128)(2,1)S(1)} %get-tuple-element.17.grad_rows_ref, bf16[128,2688]{1,0:T(8,128)(2,1)S(1)} %copy-done.1, bf16[128,2688]{1,0:T(8,128)(2,1)S(1)} %copy-done.3, ...), custom_call_target="tpu_custom_call" | custom-call | tf_op jit(solution)/shard_map/prompt_part/pallas_call | solution.py:135
  87.1 18.5 %all_to_all.40 = bf16[8,2,256,128]{3,2,1,0:T(8,128)(2,1)S(1)} all-to-all(bf16[8,2,256,128]{3,2,1,0:T(8,128)(2,1)S(1)} %get-tuple-element.26), channel_id=1, replica_groups=mesh['z'=8,'y'=4,'c'=2,'head'=4] {'y','c'}, dimensions={0} | all-to-all | bytes 2097152 | tf_op jit(solution)/shard_map/all_to_all | solution.py:148
  105.6 0.4 fusion
  106.1 14.4 %all_to_all.41 = bf16[8,128,128]{2,1,0:T(8,128)(2,1)S(1)} all-to-all(bf16[8,128,128]{2,1,0:T(8,128)(2,1)S(1)} %bitcast.41), channel_id=1, replica_groups=mesh['z'=8,'y'=4,'c'=2,'head'=4] {'z'}, dimensions={0} | all-to-all | bytes 524288 | tf_op jit(solution)/shard_map/all_to_all | solution.py:148
  120.5 0.6 slice_bitcast_fusion
  (7 shorter events, 0.1 us)
Async XLA Ops:
  0.6 20.2 %copy-start.8 = (bf16[1,96,3584]{2,1,0:T(8,128)(2,1)S(1)}, bf16[1,96,3584]{2,1,0:T(8,128)(2,1)}, u32[]{:S(2)}) copy-start(bf16[1,96,3584]{2,1,0:T(8,128)(2,1)} %param.16) | copy-start | bytes 2064388
  2.0 9.7 %all-to-all-start.1 = ((s32[8,1,128]{2,1,0:T(1,128)}), s32[8,1,128]{2,1,0:T(1,128)S(1)}, u32[]{:S(2)}, u32[]{:S(2)}) async-start(s32[8,1,128]{2,1,0:T(1,128)} %broadcast_in_dim.72), calls=%async_computation.1 | async-start | bytes 8192 | tf_op jit(solution)/shard_map/all_to_all | solution.py:148
  12.4 20.3 %all-to-all-start.2 = ((bf16[8,128,128]{2,1,0:T(8,128)(2,1)}), bf16[8,128,128]{2,1,0:T(8,128)(2,1)S(1)}, u32[]{:S(2)}, u32[]{:S(2)}) async-start(bf16[8,128,128]{2,1,0:T(8,128)(2,1)} %broadcast_in_dim.75), calls=%async_computation.2 | async-start | bytes 524288 | tf_op jit(solution)/shard_map/all_to_all | solution.py:148
  32.7 12.1 %all-to-all-start = ((bf16[4,96,896]{2,1,0:T(8,128)(2,1)}), bf16[4,96,896]{2,1,0:T(8,128)(2,1)S(1)}, u32[]{:S(2)}, u32[]{:S(2)}) async-start(bf16[4,96,896]{2,1,0:T(8,128)(2,1)} %bitcast.3), calls=%async_computation | async-start | bytes 1376256 | tf_op jit(solution)/shard_map/all_to_all | solution.py:148
  38.8 10.2 %copy-start.9 = (f32[1,7,384]{2,0,1:T(1,128)S(1)}, f32[1,7,384]{2,0,1:T(1,128)}, u32[]{:S(2)}) copy-start(f32[1,7,384]{2,0,1:T(1,128)} %param.17) | copy-start | bytes 32260
  38.8 10.2 %copy-start.6 = (bf16[1,384,128]{2,1,0:T(8,128)(2,1)S(1)}, bf16[1,384,128]{2,1,0:T(8,128)(2,1)}, u32[]{:S(2)}) copy-start(bf16[1,384,128]{2,1,0:T(8,128)(2,1)} %param.11) | copy-start | bytes 294916
  38.8 10.2 %copy-start.7 = (bf16[1,384,128]{2,1,0:T(8,128)(2,1)S(1)}, bf16[1,384,128]{2,1,0:T(8,128)(2,1)}, u32[]{:S(2)}) copy-start(bf16[1,384,128]{2,1,0:T(8,128)(2,1)} %param.12) | copy-start | bytes 294916
  44.8 19.4 %all-to-all-start.3 = ((bf16[8,2,256,128]{3,2,1,0:T(8,128)(2,1)}), bf16[8,2,256,128]{3,2,1,0:T(8,128)(2,1)S(1)}, u32[]{:S(2)}, u32[]{:S(2)}) async-start(bf16[8,2,256,128]{3,2,1,0:T(8,128)(2,1)} %broadcast_select_fusion), calls=%async_computation.3 | async-start | bytes 2097152 | tf_op jit(solution)/shard_map/all_to_all | solution.py:148
  49.0 1.1 copy-start.4
  50.1 1.1 copy-start.5
  55.9 0.8 copy-start
  56.7 0.8 copy-start.2
  64.2 1.1 copy-start.1
  65.3 1.1 copy-start.3

commit v2 on v1

v2 whole, which is shorter than its diff:
```python
import functools

import jax
import jax.numpy as jnp
from jax import lax
from jax.experimental import pallas as pl
from jax.experimental.pallas import tpu as pltpu
from jax.sharding import Mesh
from jax.sharding import PartitionSpec as P

BF16 = jnp.bfloat16
F32 = jnp.float32
GROUP = ("y", "c")
LOG2E = 1.4426950408889634
VMEM = pl.BlockSpec(memory_space=pltpu.VMEM)
SMEM = pl.BlockSpec(memory_space=pltpu.SMEM)
PARAMS = pltpu.CompilerParams(vmem_limit_bytes=28 * 1024 * 1024)
MARK = 16


def cost(row_count, key_count, width):
    pairs = row_count * key_count
    return pl.CostEstimate(
        flops=10 * pairs * width, bytes_accessed=16 * row_count * width, transcendentals=pairs
    )


def score_blocks(key_rows, value_rows, query_t, grad_t, norm_row, delta_row, visible=None):
    scale = key_rows.shape[1] ** (-0.5)
    scores_t = jnp.dot(key_rows, query_t, preferred_element_type=F32)
    weights_t = jnp.exp2(scores_t * (scale * LOG2E) - norm_row)
    if visible is not None:
        weights_t = jnp.where(visible, weights_t, jnp.zeros_like(weights_t))
    weight_grad_t = jnp.dot(value_rows, grad_t, preferred_element_type=F32)
    score_grad_t = (weights_t * (weight_grad_t - delta_row) * scale).astype(BF16)
    return weights_t.astype(BF16), score_grad_t


def suffix_kernel(
    length_ref, place_ref, query_ref, out_ref, norm_ref, key_ref, value_ref, *refs
):
    grad_refs, refs = refs[:-10], refs[-10:]
    (
        query_rows_ref, grad_rows_ref, query_t_ref, grad_t_ref, norm_row_ref, delta_row_ref,
        query_acc_ref, key_grad_ref, value_grad_ref, grad_ref,
    ) = refs
    seq_len, width = key_ref.shape
    group_size = query_ref.shape[1] // width
    part = grad_refs[0].shape[0]
    for i, piece in enumerate(grad_refs):
        start = pl.multiple_of((place_ref[0] ^ i) * part, part)
        grad_ref[pl.ds(start, part), :] = piece[...]
    live_down = lax.broadcasted_iota(jnp.int32, (seq_len, width), 0) < length_ref[0]
    key_at = lax.broadcasted_iota(jnp.int32, (seq_len, seq_len), 0)
    query_at = lax.broadcasted_iota(jnp.int32, (seq_len, seq_len), 1)
    causal = key_at <= query_at
    key_rows, value_rows = key_ref[...], value_ref[...]
    key_t = key_rows.T
    key_acc = jnp.zeros((seq_len, width), F32)
    value_acc = jnp.zeros((seq_len, width), F32)
    for head in range(group_size):
        cols = slice(head * width, (head + 1) * width)
        rows = slice(head * seq_len, (head + 1) * seq_len)
        query_rows = query_ref[:, cols]
        grad_rows = grad_ref[:, cols]
        grad_rows = jnp.where(live_down, grad_rows, jnp.zeros_like(grad_rows))
        query_t, grad_t = query_rows.T, grad_rows.T
        out_t = out_ref[:, cols].T
        delta_row = jnp.sum(grad_t.astype(F32) * out_t.astype(F32), axis=0, keepdims=True)
        norm_row = norm_ref[head : head + 1, :] * LOG2E
        query_rows_ref[rows, :] = query_rows
        grad_rows_ref[rows, :] = grad_rows
        query_t_ref[:, rows] = query_t
        grad_t_ref[:, rows] = grad_t
        norm_row_ref[:, rows] = norm_row
        delta_row_ref[:, rows] = delta_row
        weights_t, score_grad_t = score_blocks(
            key_rows, value_rows, query_t, grad_t, norm_row, delta_row, causal
        )
        query_acc_ref[:, rows] = jnp.dot(key_t, score_grad_t, preferred_element_type=F32)
        key_acc += jnp.dot(score_grad_t, query_rows, preferred_element_type=F32)
        value_acc += jnp.dot(weights_t, grad_rows, preferred_element_type=F32)
    key_grad_ref[...] = key_acc.astype(BF16)
    value_grad_ref[...] = value_acc.astype(BF16)


def suffix_part(length, place, query, attn_out, log_norm, key_suffix, value_suffix, grads):
    seq_len, width = key_suffix.shape
    row_count = query.shape[0] * query.shape[1] // width
    shape = jax.ShapeDtypeStruct
    return pl.pallas_call(
        suffix_kernel,
        in_specs=[SMEM, SMEM] + [VMEM] * (5 + len(grads)),
        out_specs=[VMEM] * 9,
        out_shape=[
            shape((row_count, width), BF16),
            shape((row_count, width), BF16),
            shape((width, row_count), BF16),
            shape((width, row_count), BF16),
            shape((1, row_count), F32),
            shape((1, row_count), F32),
            shape((width, row_count), F32),
            shape((seq_len, width), BF16),
            shape((seq_len, width), BF16),
        ],
        scratch_shapes=[pltpu.VMEM(query.shape, BF16)],
        compiler_params=PARAMS,
        cost_estimate=cost(row_count, seq_len, width),
        name="suffix_part",
    )(length, place, query, attn_out, log_norm, key_suffix, value_suffix, *grads)


def prompt_kernel(
    chosen_ref, core_ref, query_rows_ref, grad_rows_ref, query_t_ref, grad_t_ref, norm_row_ref,
    delta_row_ref, query_acc_ref, pair_ref, *refs, blocks, last,
):
    query_grad_ref, pair_grad_ref = refs[-2:]
    places, _, _, count, width = pair_ref.shape
    chosen = chosen_ref[0]
    key_rows = pair_ref[:, chosen, 0].reshape(places * count, width)
    value_rows = pair_ref[:, chosen, 1].reshape(places * count, width)
    key_t = key_rows.T
    key_acc = jnp.zeros(key_rows.shape, F32)
    value_acc = jnp.zeros(key_rows.shape, F32)
    for head, rows in enumerate(blocks):
        weights_t, score_grad_t = score_blocks(
            key_rows, value_rows, query_t_ref[:, rows], grad_t_ref[:, rows],
            norm_row_ref[:, rows], delta_row_ref[:, rows],
        )
        query_part = jnp.dot(key_t, score_grad_t, preferred_element_type=F32)
        query_part += query_acc_ref[:, rows]
        if last:
            query_grad_ref[:, head * width : (head + 1) * width] = query_part.T.astype(BF16)
        else:
            query_grad_ref[:, rows] = query_part
        key_acc += jnp.dot(score_grad_t, query_rows_ref[rows, :], preferred_element_type=F32)
        value_acc += jnp.dot(weights_t, grad_rows_ref[rows, :], preferred_element_type=F32)
    key_grad = key_acc.astype(BF16).reshape(places, count, width)
    value_grad = value_acc.astype(BF16).reshape(places, count, width)
    if not last:
        pair_grad_ref[:, :count] = key_grad
        pair_grad_ref[:, count:] = value_grad
        return
    core = core_ref[0]
    mark = jnp.full((MARK, width), chosen.astype(F32), F32).astype(BF16)
    for i in range(places):
        mine, other = 2 * i + core, 2 * i + 1 - core
        pair_grad_ref[mine, : 2 * count] = refs[0][i]
        pair_grad_ref[other, :count] = key_grad[i]
        pair_grad_ref[other, count : 2 * count] = value_grad[i]
        pair_grad_ref[mine, 2 * count :] = mark
        pair_grad_ref[other, 2 * count :] = mark


def prompt_part(chosen, core, rows, query_acc, pair, seq_len, earlier=None):
    last = earlier is not None
    row_count, width = rows[0].shape
    blocks = [slice(at, at + seq_len) for at in range(0, row_count, seq_len)]
    out = jax.ShapeDtypeStruct((width, row_count), F32)
    places, _, _, count, _ = pair.shape
    pair_out = jax.ShapeDtypeStruct((places, 2 * count, width), BF16)
    more = []
    if last:
        out = jax.ShapeDtypeStruct((seq_len, row_count * width // seq_len), BF16)
        pair_out = jax.ShapeDtypeStruct((2 * places, 2 * count + MARK, width), BF16)
        more = [earlier]
    return pl.pallas_call(
        functools.partial(prompt_kernel, blocks=blocks, last=last),
        in_specs=[SMEM, SMEM] + [VMEM] * (8 + len(more)),
        out_specs=[VMEM] * 2,
        out_shape=[out, pair_out],
        compiler_params=PARAMS,
        cost_estimate=cost(row_count, places * count, width),
        name="prompt_last" if last else "prompt_first",
    )(chosen, core, *rows, query_acc, pair, *more)


def exchange(blocks, axes):
    return lax.all_to_all(blocks, axes, split_axis=0, concat_axis=0, tiled=True)


def swap(block, axis, flip):
    return lax.ppermute(block, axis, [(i, i ^ flip) for i in range(lax.axis_size(axis))])


def copies(block, count):
    return jnp.broadcast_to(block[None], (count,) + block.shape)


def per_device(
    query, key_suffix, value_suffix, key_prompt, value_prompt, attn_out, grad_out, log_norm,
    prompt_id, lengths,
):
    seq_len, columns = query.shape[1:]
    width = key_suffix.shape[2]
    prompt_count, owned = key_prompt.shape[:2]
    heads, stacks, lines = lax.axis_size("head"), lax.axis_size("z"), lax.axis_size("y")
    place, core = lax.axis_index("head"), lax.axis_index("c")[None]

    grads = []
    for i in range(heads):
        at = (place ^ i) * columns
        piece = lax.dynamic_slice_in_dim(grad_out[0], at, columns, axis=1)
        grads.append(swap(piece, "head", i) if i else piece)

    own_pair = jnp.stack([key_prompt, value_prompt], 1).reshape(-1, width)
    stacked = exchange(copies(own_pair, stacks).reshape(-1, width), "z")
    stacked, *grads = lax.optimization_barrier((stacked, *grads))
    stacked = stacked.reshape(stacks, prompt_count, 2, owned, width)
    stacked = stacked.transpose(1, 2, 0, 3, 4).reshape(-1, width)
    pair = exchange(copies(stacked, lines).reshape(-1, width), "y")
    pair = pair.reshape(lines, prompt_count, 2, stacks * owned, width)

    *rows, query_acc, key_grad, value_grad = suffix_part(
        lengths, place[None], query[0], attn_out[0], log_norm[0], key_suffix[0], value_suffix[0],
        grads,
    )
    pair, key_grad = lax.optimization_barrier((pair, key_grad))
    other_pair = swap(pair, "c", 1)
    query_acc, earlier = prompt_part(prompt_id, core, rows, query_acc, pair, seq_len)
    query_grad, pair_grad = prompt_part(
        prompt_id, core, rows, query_acc, other_pair, seq_len, earlier
    )

    shares = exchange(pair_grad, GROUP)
    ids = shares[:, -MARK : 1 - MARK, :1]
    shares = shares[:, :-MARK].astype(F32)
    totals = jnp.stack(
        [jnp.sum(jnp.where(ids == i, shares, 0.0), 0) for i in range(prompt_count)], 0
    )
    totals = totals.reshape(prompt_count, 2, stacks, owned, width).transpose(2, 0, 1, 3, 4)
    totals = totals.astype(BF16).reshape(stacks, -1, width)
    final = jnp.sum(exchange(totals, "z").astype(F32), 0).astype(BF16)
    final = final.reshape(prompt_count, 2, owned, width)
    return (query_grad[None], key_grad[None], value_grad[None], final[:, 0], final[:, 1])


def solution(mesh):
    roll, head = mesh.devices.shape
    fine = Mesh(mesh.devices.reshape(roll // 8, 4, 2, head), ("z", "y", "c", "head"))
    rolls = ("z", "y", "c")
    by_rollout = P(rolls, None, "head")
    by_key = P(None, rolls, "head")
    by_row = P(rolls, "head", None)
    in_specs = (
        by_rollout, by_rollout, by_rollout, by_key, by_key, by_rollout, by_row, by_row,
        P(rolls), P(rolls),
    )
    out_specs = (by_rollout, by_rollout, by_rollout, by_key, by_key)
    return jax.shard_map(
        per_device, mesh=fine, in_specs=in_specs, out_specs=out_specs, check_vma=False
    )
```

time: 122 us -> 103 us (0.84)
  waiting for transfers between devices: 28 us -> 11.2 us
  Pallas kernels: 25.3 us -> 19.7 us
  local copies, waits for them, and re-layouts: 8.18 us -> 12.8 us
  blocking collectives: 32.9 us -> 36.9 us
  starting transfers between devices: 21.3 us -> 17.9 us
  other arithmetic: 3.41 us -> 1.71 us
    all_to_all x4 -> x2, waiting for transfers between devices: 28 us -> 3.97 us  [exchange(): return lax.all_to_all(blocks, axes, split_axis=0, concat_axis=0, tiled=True)]
    all_to_all x4 -> x2, starting transfers between devices: 21.3 us -> 13.1 us  [exchange(): return lax.all_to_all(blocks, axes, split_axis=0, concat_axis=0, tiled=True)]
    ppermute x0 -> x4, waiting for transfers between devices: none -> 7.22 us  [swap(): lax.ppermute(block, axis, [(i, i ^ flip) for i in range(lax.axis_size(axi...]
    pallas_call x2 -> x3, Pallas kernels: 25.3 us -> 19.7 us  [the longest x2 15.3 us: prompt_part(): pl.pallas_call(functools.partial(prompt_kernel, blocks=blocks, last=last)...]
    ppermute x0 -> x4, starting transfers between devices: none -> 4.79 us  [swap(): lax.ppermute(block, axis, [(i, i ^ flip) for i in range(lax.axis_size(axi...]
    unnamed x21 -> x33, local copies, waits for them, and re-layouts: 6.1 us -> 10.3 us
    all_to_all x2, blocking collectives: 32.9 us -> 36.9 us  [exchange(): return lax.all_to_all(blocks, axes, split_axis=0, concat_axis=0, tiled=True)]
  transfers between devices with their start and end apart: 4 -> 6, of which waited for: 4 -> 4; matrix products, arithmetic and copies ran while one was open for 2% -> 0% of each run, Pallas kernels for 4% -> 11%
where the time goes in v2:
time: 103 us; the launch traced here: 102 us
  blocking collectives  36.9 us (36%)
  Pallas kernels  19.7 us (19%)
  starting transfers between devices  17.9 us (17%)
  local copies, waits for them, and re-layouts  12.8 us (12%)
  waiting for transfers between devices  11.2 us (11%)
  between operations  2.09 us (2%)
  other arithmetic  1.71 us (2%)
    all_to_all x2, blocking collectives, exchange(): return lax.all_to_all(blocks, axes, split_axis=0, concat_axis=0, tiled=True)  36.9 us
    pallas_call x2, Pallas kernels, prompt_part(): pl.pallas_call(functools.partial(prompt_kernel, blocks=blocks, last=last)...  15.3 us
    all_to_all x2, starting transfers between devices, exchange(): return lax.all_to_all(blocks, axes, split_axis=0, concat_axis=0, tiled=True)  13.1 us
    unnamed x33, local copies, waits for them, and re-layouts  10.3 us
    ppermute x4, waiting for transfers between devices, swap(): lax.ppermute(block, axis, [(i, i ^ flip) for i in range(lax.axis_size(axi...  7.22 us
    ppermute x4, starting transfers between devices, swap(): lax.ppermute(block, axis, [(i, i ^ flip) for i in range(lax.axis_size(axi...  4.79 us
    pallas_call x1, Pallas kernels, suffix_part(): pl.pallas_call(suffix_kernel, in_specs=[SMEM, SMEM] + [VMEM] * (5 + len(g...  4.4 us
    all_to_all x2, waiting for transfers between devices, exchange(): return lax.all_to_all(blocks, axes, split_axis=0, concat_axis=0, tiled=True)  3.97 us
  transfers between devices with their start and end apart: 6, of which 4 were waited for; matrix products, arithmetic and copies ran while one was open for 0% of the time, Pallas kernels for 11%

profile of v2, /device:TPU:6, one launch (start us, length us, event | category | flops | bytes accessed | tf_op | source)
XLA Modules:
  0.0 102.3 jit_solution(15258928667730880505)
XLA Ops:
  0.6 0.0 copy-start.14
  0.6 0.8 pad_maximum_fusion
  1.5 0.7 broadcast_in_dim.54
  2.2 8.5 %all-to-all-start = ((bf16[8,128,128]{2,1,0:T(8,128)(2,1)}), bf16[8,128,128]{2,1,0:T(8,128)(2,1)S(1)}, u32[]{:S(2)}, u32[]{:S(2)}) async-start(bf16[8,128,128]{2,1,0:T(8,128)(2,1)} %broadcast_in_dim.54), calls=%async_computation | async-start | bytes 524288 | tf_op jit(solution)/shard_map/all_to_all | solution.py:179
  10.7 0.0 copy-done.14
  10.7 0.1 dynamic-slice_bitcast_fusion
  10.7 0.6 collective-permute-start.2
  11.3 0.9 collective-permute-start
  12.2 3.3 %collective-permute-start.1 = (bf16[96,896]{1,0:T(8,128)(2,1)S(1)}, bf16[96,896]{1,0:T(8,128)(2,1)S(1)}, u32[]{:S(2)}, u32[]{:S(2)}) collective-permute-start(bf16[96,896]{1,0:T(8,128)(2,1)S(1)} %get-tuple-element.52), channel_id=1, source_target_pairs={{0,2},{1,3},{2,0},{3,1},{4,6},{5,7},{6,4},{7,5},{8,10},{9,11},{10,... | collective-permute-start | bytes 516104 | tf_op jit(solution)/shard_map/ppermute | solution.py:183
  15.5 2.9 %collective-permute-done.2.refs_3_ = bf16[96,896]{1,0:T(8,128)(2,1)S(1)} collective-permute-done((bf16[96,896]{1,0:T(8,128)(2,1)S(1)}, bf16[96,896]{1,0:T(8,128)(2,1)S(1)}, u32[]{:S(2)}, u32[]{:S(2)}) %collective-permute-start.2) | collective-permute-done | bytes 172064 | tf_op jit(solution)/shard_map/ppermute | solution.py:183
  18.4 0.2 collective-permute-done.refs_1_
  18.6 4.1 %collective-permute-done.1.refs_2_ = bf16[96,896]{1,0:T(8,128)(2,1)S(1)} collective-permute-done((bf16[96,896]{1,0:T(8,128)(2,1)S(1)}, bf16[96,896]{1,0:T(8,128)(2,1)S(1)}, u32[]{:S(2)}, u32[]{:S(2)}) %collective-permute-start.1) | collective-permute-done | bytes 172064 | tf_op jit(solution)/shard_map/ppermute | solution.py:183
  22.7 0.0 all-to-all-done
  22.8 1.1 %broadcast_in_dim.56 = bf16[4,1024,128]{2,1,0:T(8,128)(2,1)} broadcast(bf16[1024,128]{1,0:T(8,128)(2,1)S(1)} %bitcast.46), dimensions={1,2} | broadcast | bytes 1310720 | tf_op jit(solution)/shard_map/broadcast_in_dim | solution.py:187
  23.9 0.0 copy-start.15
  23.9 0.0 copy-start
  23.9 0.0 copy-start.1
  23.9 0.0 copy-start.2
  23.9 0.0 copy-start.3
  23.9 4.6 %all-to-all-start.1 = ((bf16[4,1024,128]{2,1,0:T(8,128)(2,1)}), bf16[4,1024,128]{2,1,0:T(8,128)(2,1)S(1)}, u32[]{:S(2)}, u32[]{:S(2)}) async-start(bf16[4,1024,128]{2,1,0:T(8,128)(2,1)} %broadcast_in_dim.56), calls=%async_computation.1 | async-start | bytes 2097152 | tf_op jit(solution)/shard_map/all_to_all | solution.py:179
  29.1 0.0 copy-done.15
  29.2 0.0 copy-done
  29.2 0.0 copy-done.1
  29.2 0.0 copy-done.2
  29.2 0.0 copy-done.3
  29.2 4.4 %suffix_part.1 = (bf16[2688,128]{1,0:T(8,128)(2,1)S(1)}, bf16[2688,128]{1,0:T(8,128)(2,1)S(1)}, bf16[128,2688]{1,0:T(8,128)(2,1)S(1)}, bf16[128,2688]{1,0:T(8,12...) custom-call(s32[1]{0:T(128)S(6)} %copy.21.length_ref, ...), custom_call_target="tpu_custom_call" | custom-call | flops 1321205760 | bytes 5505024 | tf_op jit(solution)/shard_map/suffix_part/pallas_call | solution.py:91
  33.6 0.0 copy-start.4
  33.6 1.1 %copy-done.4 = f32[128,2688]{1,0:T(8,128)} copy-done((f32[128,2688]{1,0:T(8,128)}, f32[128,2688]{1,0:T(8,128)S(1)}, u32[]{:S(2)}) %copy-start.4) | copy-done | bytes 1376280
  34.7 0.0 copy-start.6
  34.7 0.8 copy-done.6
  35.5 0.0 copy-start.8
  35.6 0.9 copy-done.8
  36.4 0.0 copy-start.10
  36.4 0.9 copy-done.10
  37.3 0.0 copy-start.12
  37.3 0.9 copy-done.12
  38.1 4.0 %all-to-all-done.1 = bf16[4,1024,128]{2,1,0:T(8,128)(2,1)S(1)} async-done(((bf16[4,1024,128]{2,1,0:T(8,128)(2,1)}), bf16[4,1024,128]{2,1,0:T(8,128)(2,1)S(1)}, u32[]{:S(2)}, u32[]{:S(2)}) %all-to-all-start.1) | async-done | bytes 1048608 | tf_op jit(solution)/shard_map/all_to_all | solution.py:179
  42.1 0.0 collective-permute-start.3
  42.7 0.0 copy-start.5
  42.8 1.3 %copy-done.5 = f32[128,2688]{1,0:T(8,128)S(1)} copy-done((f32[128,2688]{1,0:T(8,128)S(1)}, f32[128,2688]{1,0:T(8,128)}, u32[]{:S(2)}) %copy-start.5) | copy-done | bytes 1376280
  44.1 0.0 copy-start.7
  44.1 1.1 %copy-done.7 = bf16[2688,128]{1,0:T(8,128)(2,1)S(1)} copy-done((bf16[2688,128]{1,0:T(8,128)(2,1)S(1)}, bf16[2688,128]{1,0:T(8,128)(2,1)}, u32[]{:S(2)}) %copy-start.7) | copy-done | bytes 688152
  45.2 0.0 copy-start.9
  45.2 1.1 %copy-done.9 = bf16[2688,128]{1,0:T(8,128)(2,1)S(1)} copy-done((bf16[2688,128]{1,0:T(8,128)(2,1)S(1)}, bf16[2688,128]{1,0:T(8,128)(2,1)}, u32[]{:S(2)}) %copy-start.9) | copy-done | bytes 688152
  46.3 0.0 copy-start.11
  46.3 1.1 %copy-done.11 = bf16[128,2688]{1,0:T(8,128)(2,1)S(1)} copy-done((bf16[128,2688]{1,0:T(8,128)(2,1)S(1)}, bf16[128,2688]{1,0:T(8,128)(2,1)}, u32[]{:S(2)}) %copy-start.11) | copy-done | bytes 688152
  47.4 0.0 copy-start.13
  47.4 1.1 %copy-done.13 = bf16[128,2688]{1,0:T(8,128)(2,1)S(1)} copy-done((bf16[128,2688]{1,0:T(8,128)(2,1)S(1)}, bf16[128,2688]{1,0:T(8,128)(2,1)}, u32[]{:S(2)}) %copy-start.13) | copy-done | bytes 688152
  48.5 7.1 %prompt_first.1 = (f32[128,2688]{1,0:T(8,128)S(1)}, bf16[4,512,128]{2,1,0:T(8,128)(2,1)S(1)}) custom-call(s32[1]{0:T(128)S(6)} %copy.20.chosen_ref, s32[1]{0:T(128)} %bitcast.core_ref, bf16[2688,128]{1,0:T(8,128)(2,1)S(1)} %copy-done.7, bf16[2688,128]{1,0:T(8,128)(2,1)S(1)} %copy-done.9, bf16[128,2688]{1,0:T(8,128)(2,1)S(1)} %copy-done.11, ...), custom_call_target="tpu_custom_call" | custom-call | flops 3523215360 | bytes 5505024 | tf_op jit(solution)/shard_map/prompt_first/pallas_call | solution.py:167
  55.6 0.0 collective-permute-done.3.pair_ref
  55.6 8.2 %prompt_last.1 = (bf16[384,896]{1,0:T(8,128)(2,1)}, bf16[8,528,128]{2,1,0:T(8,128)(2,1)S(1)}) custom-call(s32[1]{0:T(128)S(6)} %copy.20.chosen_ref, s32[1]{0:T(128)} %bitcast.core_ref, bf16[2688,128]{1,0:T(8,128)(2,1)S(1)} %copy-done.7, bf16[2688,128]{1,0:T(8,128)(2,1)S(1)} %copy-done.9, bf16[128,2688]{1,0:T(8,128)(2,1)S(1)} %copy-done.11, ...), custom_call_target="tpu_custom_call" | custom-call | flops 3523215360 | bytes 5505024 | tf_op jit(solution)/shard_map/prompt_last/pallas_call | solution.py:167
  63.8 18.8 %all_to_all.25 = bf16[8,528,128]{2,1,0:T(8,128)(2,1)S(1)} all-to-all(bf16[8,528,128]{2,1,0:T(8,128)(2,1)S(1)} %get-tuple-element.44), channel_id=1, replica_groups=mesh['z'=8,'y'=4,'c'=2,'head'=4] {'y','c'}, dimensions={0} | all-to-all | bytes 2162688 | tf_op jit(solution)/shard_map/all_to_all | solution.py:179
  82.7 0.4 compare_reduce_fusion.1
  83.0 0.5 fusion
  83.6 18.1 %all_to_all.26 = bf16[8,128,128]{2,1,0:T(8,128)(2,1)S(1)} all-to-all(bf16[8,128,128]{2,1,0:T(8,128)(2,1)S(1)} %bitcast.48), channel_id=1, replica_groups=mesh['z'=8,'y'=4,'c'=2,'head'=4] {'z'}, dimensions={0} | all-to-all | bytes 524288 | tf_op jit(solution)/shard_map/all_to_all | solution.py:179
  101.7 0.6 slice_bitcast_fusion
  (5 shorter events, 0.1 us)
Async XLA Ops:
  0.6 10.0 %copy-start.14 = (bf16[1,96,3584]{2,1,0:T(8,128)(2,1)S(1)}, bf16[1,96,3584]{2,1,0:T(8,128)(2,1)}, u32[]{:S(2)}) copy-start(bf16[1,96,3584]{2,1,0:T(8,128)(2,1)} %param.16) | copy-start | bytes 2064388
  2.2 20.6 %all-to-all-start = ((bf16[8,128,128]{2,1,0:T(8,128)(2,1)}), bf16[8,128,128]{2,1,0:T(8,128)(2,1)S(1)}, u32[]{:S(2)}, u32[]{:S(2)}) async-start(bf16[8,128,128]{2,1,0:T(8,128)(2,1)} %broadcast_in_dim.54), calls=%async_computation | async-start | bytes 524288 | tf_op jit(solution)/shard_map/all_to_all | solution.py:179
  10.7 7.7 %collective-permute-start.2 = (bf16[96,896]{1,0:T(8,128)(2,1)S(1)}, bf16[96,896]{1,0:T(8,128)(2,1)S(1)}, u32[]{:S(2)}, u32[]{:S(2)}) collective-permute-start(bf16[96,896]{1,0:T(8,128)(2,1)S(1)} %get-tuple-element.49), channel_id=1, source_target_pairs={{0,3},{1,2},{2,1},{3,0},{4,7},{5,6},{6,5},{7,4},{8,11},{9,10},{10,... | collective-permute-start | bytes 516104 | tf_op jit(solution)/shard_map/ppermute | solution.py:183
  11.3 7.3 %collective-permute-start = (bf16[96,896]{1,0:T(8,128)(2,1)S(1)}, bf16[96,896]{1,0:T(8,128)(2,1)S(1)}, u32[]{:S(2)}, u32[]{:S(2)}) collective-permute-start(bf16[96,896]{1,0:T(8,128)(2,1)S(1)} %get-tuple-element.50), channel_id=1, source_target_pairs={{0,1},{1,0},{2,3},{3,2},{4,5},{5,4},{6,7},{7,6},{8,9},{9,8},{10,11... | collective-permute-start | bytes 516104 | tf_op jit(solution)/shard_map/ppermute | solution.py:183
  12.2 10.6 %collective-permute-start.1 = (bf16[96,896]{1,0:T(8,128)(2,1)S(1)}, bf16[96,896]{1,0:T(8,128)(2,1)S(1)}, u32[]{:S(2)}, u32[]{:S(2)}) collective-permute-start(bf16[96,896]{1,0:T(8,128)(2,1)S(1)} %get-tuple-element.52), channel_id=1, source_target_pairs={{0,2},{1,3},{2,0},{3,1},{4,6},{5,7},{6,4},{7,5},{8,10},{9,11},{10,... | collective-permute-start | bytes 516104 | tf_op jit(solution)/shard_map/ppermute | solution.py:183
  23.9 5.3 %copy-start.15 = (f32[1,7,384]{2,0,1:T(1,128)S(1)}, f32[1,7,384]{2,0,1:T(1,128)}, u32[]{:S(2)}) copy-start(f32[1,7,384]{2,0,1:T(1,128)} %param.17) | copy-start | bytes 32260
  23.9 5.3 %copy-start = (bf16[1,384,896]{2,1,0:T(8,128)(2,1)S(1)}, bf16[1,384,896]{2,1,0:T(8,128)(2,1)}, u32[]{:S(2)}) copy-start(bf16[1,384,896]{2,1,0:T(8,128)(2,1)} %param.10) | copy-start | bytes 2064388
  23.9 5.3 %copy-start.1 = (bf16[1,384,896]{2,1,0:T(8,128)(2,1)S(1)}, bf16[1,384,896]{2,1,0:T(8,128)(2,1)}, u32[]{:S(2)}) copy-start(bf16[1,384,896]{2,1,0:T(8,128)(2,1)} %param.15) | copy-start | bytes 2064388
  23.9 5.3 %copy-start.2 = (bf16[1,384,128]{2,1,0:T(8,128)(2,1)S(1)}, bf16[1,384,128]{2,1,0:T(8,128)(2,1)}, u32[]{:S(2)}) copy-start(bf16[1,384,128]{2,1,0:T(8,128)(2,1)} %param.11) | copy-start | bytes 294916
  23.9 5.3 %copy-start.3 = (bf16[1,384,128]{2,1,0:T(8,128)(2,1)S(1)}, bf16[1,384,128]{2,1,0:T(8,128)(2,1)}, u32[]{:S(2)}) copy-start(bf16[1,384,128]{2,1,0:T(8,128)(2,1)} %param.12) | copy-start | bytes 294916
  23.9 18.2 %all-to-all-start.1 = ((bf16[4,1024,128]{2,1,0:T(8,128)(2,1)}), bf16[4,1024,128]{2,1,0:T(8,128)(2,1)S(1)}, u32[]{:S(2)}, u32[]{:S(2)}) async-start(bf16[4,1024,128]{2,1,0:T(8,128)(2,1)} %broadcast_in_dim.56), calls=%async_computation.1 | async-start | bytes 2097152 | tf_op jit(solution)/shard_map/all_to_all | solution.py:179
  33.6 1.1 %copy-start.4 = (f32[128,2688]{1,0:T(8,128)}, f32[128,2688]{1,0:T(8,128)S(1)}, u32[]{:S(2)}) copy-start(f32[128,2688]{1,0:T(8,128)S(1)} %get-tuple-element.35.query_acc_ref) | copy-start | bytes 4128772
  34.7 0.8 copy-start.6
  35.5 0.9 copy-start.8
  36.4 0.9 copy-start.10
  37.3 0.9 copy-start.12
  42.1 13.5 %collective-permute-start.3 = (bf16[4,2,2,256,128]{4,3,2,1,0:T(8,128)(2,1)S(1)}, bf16[4,2,2,256,128]{4,3,2,1,0:T(8,128)(2,1)S(1)}, u32[]{:S(2)}, u32[]{:S(2)}) collective-permute-start(bf16[4,2,2,256,128]{4,3,2,1,0:T(8,128)(2,1)S(1)} %bitcast.39), channel_id=1, source_target_pairs={{0,4},{4,0},{1,5},{5,1},{2,6},{6,2},{3,7},{7,3},{8,12},{12,8},{9,1... | collective-permute-start | bytes 3145736 | tf_op jit(solution)/shard_map/ppermute | solution.py:183
  42.7 1.3 %copy-start.5 = (f32[128,2688]{1,0:T(8,128)S(1)}, f32[128,2688]{1,0:T(8,128)}, u32[]{:S(2)}) copy-start(f32[128,2688]{1,0:T(8,128)} %copy-done.4) | copy-start | bytes 4128772
  44.1 1.1 %copy-start.7 = (bf16[2688,128]{1,0:T(8,128)(2,1)S(1)}, bf16[2688,128]{1,0:T(8,128)(2,1)}, u32[]{:S(2)}) copy-start(bf16[2688,128]{1,0:T(8,128)(2,1)} %copy-done.6) | copy-start | bytes 2064388
  45.2 1.1 %copy-start.9 = (bf16[2688,128]{1,0:T(8,128)(2,1)S(1)}, bf16[2688,128]{1,0:T(8,128)(2,1)}, u32[]{:S(2)}) copy-start(bf16[2688,128]{1,0:T(8,128)(2,1)} %copy-done.8) | copy-start | bytes 2064388
  46.3 1.1 %copy-start.11 = (bf16[128,2688]{1,0:T(8,128)(2,1)S(1)}, bf16[128,2688]{1,0:T(8,128)(2,1)}, u32[]{:S(2)}) copy-start(bf16[128,2688]{1,0:T(8,128)(2,1)} %copy-done.10) | copy-start | bytes 2064388
  47.4 1.1 %copy-start.13 = (bf16[128,2688]{1,0:T(8,128)(2,1)S(1)}, bf16[128,2688]{1,0:T(8,128)(2,1)}, u32[]{:S(2)}) copy-start(bf16[128,2688]{1,0:T(8,128)(2,1)} %copy-done.12) | copy-start | bytes 2064388

commit v3 on v2

--- a/solution.py
+++ b/solution.py
@@ -37,7 +37,7 @@
 
 
 def suffix_kernel(
-    length_ref, place_ref, query_ref, out_ref, norm_ref, key_ref, value_ref, *refs
+    info_ref, query_ref, out_ref, norm_ref, key_ref, value_ref, *refs
 ):
     grad_refs, refs = refs[:-10], refs[-10:]
     (
@@ -48,9 +48,9 @@
     group_size = query_ref.shape[1] // width
     part = grad_refs[0].shape[0]
     for i, piece in enumerate(grad_refs):
-        start = pl.multiple_of((place_ref[0] ^ i) * part, part)
+        start = pl.multiple_of((info_ref[3] ^ i) * part, part)
         grad_ref[pl.ds(start, part), :] = piece[...]
-    live_down = lax.broadcasted_iota(jnp.int32, (seq_len, width), 0) < length_ref[0]
+    live_down = lax.broadcasted_iota(jnp.int32, (seq_len, width), 0) < info_ref[4]
     key_at = lax.broadcasted_iota(jnp.int32, (seq_len, seq_len), 0)
     query_at = lax.broadcasted_iota(jnp.int32, (seq_len, seq_len), 1)
     causal = key_at <= query_at
@@ -84,13 +84,13 @@
     value_grad_ref[...] = value_acc.astype(BF16)
 
 
-def suffix_part(length, place, query, attn_out, log_norm, key_suffix, value_suffix, grads):
+def suffix_part(info, query, attn_out, log_norm, key_suffix, value_suffix, grads):
     seq_len, width = key_suffix.shape
     row_count = query.shape[0] * query.shape[1] // width
     shape = jax.ShapeDtypeStruct
     return pl.pallas_call(
         suffix_kernel,
-        in_specs=[SMEM, SMEM] + [VMEM] * (5 + len(grads)),
+        in_specs=[SMEM] + [VMEM] * (5 + len(grads)),
         out_specs=[VMEM] * 9,
         out_shape=[
             shape((row_count, width), BF16),
@@ -107,18 +107,24 @@
         compiler_params=PARAMS,
         cost_estimate=cost(row_count, seq_len, width),
         name="suffix_part",
-    )(length, place, query, attn_out, log_norm, key_suffix, value_suffix, *grads)
-
-
-def prompt_kernel(
-    chosen_ref, core_ref, query_rows_ref, grad_rows_ref, query_t_ref, grad_t_ref, norm_row_ref,
-    delta_row_ref, query_acc_ref, pair_ref, *refs, blocks, last,
-):
-    query_grad_ref, pair_grad_ref = refs[-2:]
-    places, _, _, count, width = pair_ref.shape
-    chosen = chosen_ref[0]
-    key_rows = pair_ref[:, chosen, 0].reshape(places * count, width)
-    value_rows = pair_ref[:, chosen, 1].reshape(places * count, width)
+    )(info, query, attn_out, log_norm, key_suffix, value_suffix, *grads)
+
+
+def prompt_kernel(info_ref, *refs, blocks, count, earlier):
+    pair_refs, refs = refs[:count], refs[count:]
+    (
+        query_rows_ref, grad_rows_ref, query_t_ref, grad_t_ref, norm_row_ref, delta_row_ref,
+        query_acc_ref,
+    ) = refs[:7]
+    earlier_refs, (query_grad_ref, pair_grad_ref) = refs[7:-2], refs[-2:]
+    chosen = info_ref[0]
+    width = query_rows_ref.shape[1]
+
+    def rows_of(which):
+        parts = [ref[:, chosen, which] for ref in pair_refs]
+        return jnp.concatenate([part.reshape(-1, width) for part in parts], 0)
+
+    key_rows, value_rows = rows_of(0), rows_of(1)
     key_t = key_rows.T
     key_acc = jnp.zeros(key_rows.shape, F32)
     value_acc = jnp.zeros(key_rows.shape, F32)
@@ -129,58 +135,61 @@
         )
         query_part = jnp.dot(key_t, score_grad_t, preferred_element_type=F32)
         query_part += query_acc_ref[:, rows]
-        if last:
+        if earlier:
             query_grad_ref[:, head * width : (head + 1) * width] = query_part.T.astype(BF16)
         else:
             query_grad_ref[:, rows] = query_part
         key_acc += jnp.dot(score_grad_t, query_rows_ref[rows, :], preferred_element_type=F32)
         value_acc += jnp.dot(weights_t, grad_rows_ref[rows, :], preferred_element_type=F32)
-    key_grad = key_acc.astype(BF16).reshape(places, count, width)
-    value_grad = value_acc.astype(BF16).reshape(places, count, width)
-    if not last:
-        pair_grad_ref[:, :count] = key_grad
-        pair_grad_ref[:, count:] = value_grad
+    size = key_rows.shape[0] // count
+    key_grad, value_grad = key_acc.astype(BF16), value_acc.astype(BF16)
+    own = [
+        (key_grad[i * size : (i + 1) * size], value_grad[i * size : (i + 1) * size])
+        for i in range(count)
+    ]
+    if not earlier:
+        for i in range(count):
+            pair_grad_ref[i, 0], pair_grad_ref[i, 1] = own[i]
         return
-    core = core_ref[0]
+    core, line = info_ref[1], info_ref[2]
+    lines = pair_grad_ref.shape[0] // 2
     mark = jnp.full((MARK, width), chosen.astype(F32), F32).astype(BF16)
-    for i in range(places):
-        mine, other = 2 * i + core, 2 * i + 1 - core
-        pair_grad_ref[mine, : 2 * count] = refs[0][i]
-        pair_grad_ref[other, :count] = key_grad[i]
-        pair_grad_ref[other, count : 2 * count] = value_grad[i]
-        pair_grad_ref[mine, 2 * count :] = mark
-        pair_grad_ref[other, 2 * count :] = mark
-
-
-def prompt_part(chosen, core, rows, query_acc, pair, seq_len, earlier=None):
-    last = earlier is not None
+    found = [(ref, i) for ref in earlier_refs for i in range(ref.shape[0])]
+    found = [(ref[i, 0], ref[i, 1]) for ref, i in found] + own
+    for (steps, other), (keys, values) in zip(earlier, found, strict=True):
+        owner = 2 * lax.rem(line - steps + lines, lines) + (1 - core if other else core)
+        pair_grad_ref[owner, :size] = keys
+        pair_grad_ref[owner, size : 2 * size] = values
+        pair_grad_ref[owner, 2 * size :] = mark
+
+
+def prompt_part(info, pairs, rows, query_acc, seq_len, earlier=(), order=()):
     row_count, width = rows[0].shape
     blocks = [slice(at, at + seq_len) for at in range(0, row_count, seq_len)]
+    stacks, _, _, owned, _ = pairs[0].shape
+    size = stacks * owned
     out = jax.ShapeDtypeStruct((width, row_count), F32)
-    places, _, _, count, _ = pair.shape
-    pair_out = jax.ShapeDtypeStruct((places, 2 * count, width), BF16)
-    more = []
-    if last:
+    pair_out = jax.ShapeDtypeStruct((len(pairs), 2, size, width), BF16)
+    if order:
         out = jax.ShapeDtypeStruct((seq_len, row_count * width // seq_len), BF16)
-        pair_out = jax.ShapeDtypeStruct((2 * places, 2 * count + MARK, width), BF16)
-        more = [earlier]
+        pair_out = jax.ShapeDtypeStruct((len(order), 2 * size + MARK, width), BF16)
     return pl.pallas_call(
-        functools.partial(prompt_kernel, blocks=blocks, last=last),
-        in_specs=[SMEM, SMEM] + [VMEM] * (8 + len(more)),
+        functools.partial(prompt_kernel, blocks=blocks, count=len(pairs), earlier=order),
+        in_specs=[SMEM] + [VMEM] * (len(pairs) + 7 + len(earlier)),
         out_specs=[VMEM] * 2,
         out_shape=[out, pair_out],
         compiler_params=PARAMS,
-        cost_estimate=cost(row_count, places * count, width),
-        name="prompt_last" if last else "prompt_first",
-    )(chosen, core, *rows, query_acc, pair, *more)
+        cost_estimate=cost(row_count, len(pairs) * size, width),
+        name="prompt_part",
+    )(info, *pairs, *rows, query_acc, *earlier)
 
 
 def exchange(blocks, axes):
     return lax.all_to_all(blocks, axes, split_axis=0, concat_axis=0, tiled=True)
 
 
-def swap(block, axis, flip):
-    return lax.ppermute(block, axis, [(i, i ^ flip) for i in range(lax.axis_size(axis))])
+def trade(block, axis, target):
+    return lax.ppermute(block, axis, [(i, target(i)) for i in range(lax.axis_size(axis))])
 
 
 def copies(block, count):
@@ -195,31 +204,38 @@
     width = key_suffix.shape[2]
     prompt_count, owned = key_prompt.shape[:2]
     heads, stacks, lines = lax.axis_size("head"), lax.axis_size("z"), lax.axis_size("y")
-    place, core = lax.axis_index("head"), lax.axis_index("c")[None]
-
+    place = lax.axis_index("head")
+    info = jnp.stack(
+        [prompt_id[0], lax.axis_index("c"), lax.axis_index("y"), place, lengths[0]]
+    ).astype(jnp.int32)
+
+    own_pair = jnp.stack([key_prompt, value_prompt], 1).reshape(-1, width)
+    stacked = exchange(copies(own_pair, stacks).reshape(-1, width), "z")
     grads = []
     for i in range(heads):
         at = (place ^ i) * columns
         piece = lax.dynamic_slice_in_dim(grad_out[0], at, columns, axis=1)
-        grads.append(swap(piece, "head", i) if i else piece)
-
-    own_pair = jnp.stack([key_prompt, value_prompt], 1).reshape(-1, width)
-    stacked = exchange(copies(own_pair, stacks).reshape(-1, width), "z")
-    stacked, *grads = lax.optimization_barrier((stacked, *grads))
+        grads.append(trade(piece, "head", lambda j, i=i: j ^ i) if i else piece)
+    stacked, info, *grads = lax.optimization_barrier((stacked, info, *grads))
     stacked = stacked.reshape(stacks, prompt_count, 2, owned, width)
-    stacked = stacked.transpose(1, 2, 0, 3, 4).reshape(-1, width)
-    pair = exchange(copies(stacked, lines).reshape(-1, width), "y")
-    pair = pair.reshape(lines, prompt_count, 2, stacks * owned, width)
-
+
+    moved = {
+        steps: trade(stacked, "y", lambda j, steps=steps: (j + steps) % lines)
+        for steps in (1, lines - 1, 2)
+    }
     *rows, query_acc, key_grad, value_grad = suffix_part(
-        lengths, place[None], query[0], attn_out[0], log_norm[0], key_suffix[0], value_suffix[0],
-        grads,
-    )
-    pair, key_grad = lax.optimization_barrier((pair, key_grad))
-    other_pair = swap(pair, "c", 1)
-    query_acc, earlier = prompt_part(prompt_id, core, rows, query_acc, pair, seq_len)
+        info, query[0], attn_out[0], log_norm[0], key_suffix[0], value_suffix[0], grads
+    )
+    near, key_grad = lax.optimization_barrier(([stacked, moved[1], moved[lines - 1]], key_grad))
+    near_other = [trade(block, "c", lambda j: j ^ 1) for block in near]
+    query_acc, first = prompt_part(info, near, rows, query_acc, seq_len)
+    far, query_acc = lax.optimization_barrier((moved[2], query_acc))
+    far_other = trade(far, "c", lambda j: j ^ 1)
+    query_acc, second = prompt_part(info, near_other, rows, query_acc, seq_len)
+    order = [(steps, other) for other in (False, True) for steps in (0, 1, lines - 1)]
+    order += [(2, False), (2, True)]
     query_grad, pair_grad = prompt_part(
-        prompt_id, core, rows, query_acc, other_pair, seq_len, earlier
+        info, [far, far_other], rows, query_acc, seq_len, (first, second), order
     )
 
     shares = exchange(pair_grad, GROUP)

time: 103 us -> 99.5 us (0.966); the launches traced: 102 us -> 97.8 us
  local copies, waits for them, and re-layouts: 12.8 us -> 2.27 us
  blocking collectives: 36.9 us -> 42.3 us
  waiting for transfers between devices: 11.2 us -> 6.55 us
  Pallas kernels: 19.7 us -> 23.1 us
  starting transfers between devices: 17.9 us -> 19.7 us
    unnamed x33 -> x13, local copies, waits for them, and re-layouts: 10.3 us -> 0.03 us
    ppermute x4 -> x10, starting transfers between devices: 4.79 us -> 11.2 us  [trade(): lax.ppermute(block, axis, [(i, target(i)) for i in range(lax.axis_size(ax...]
    all_to_all x2, blocking collectives: 36.9 us -> 42.3 us  [exchange(): return lax.all_to_all(blocks, axes, split_axis=0, concat_axis=0, tiled=True)]
    all_to_all x2 -> x1, starting transfers between devices: 13.1 us -> 8.47 us  [exchange(): return lax.all_to_all(blocks, axes, split_axis=0, concat_axis=0, tiled=True)]
    all_to_all x2 -> x1, waiting for transfers between devices: 3.97 us -> 0.01 us  [exchange(): return lax.all_to_all(blocks, axes, split_axis=0, concat_axis=0, tiled=True)]
    pallas_call x3 -> x4, Pallas kernels: 19.7 us -> 23.1 us  [the longest x3 18.1 us: prompt_part(): pl.pallas_call(functools.partial(prompt_kernel, blocks=blocks, count=len(...]
    broadcast_in_dim x2 -> x1, local copies, waits for them, and re-layouts: 1.83 us -> 0.74 us  [copies(): return jnp.broadcast_to(block[None], (count,) + block.shape)]
    ppermute x4 -> x10, waiting for transfers between devices: 7.22 us -> 6.55 us  [trade(): lax.ppermute(block, axis, [(i, target(i)) for i in range(lax.axis_size(ax...]
  transfers between devices with their start and end apart: 6 -> 11, of which waited for: 4 -> 4; matrix products, arithmetic and copies ran while one was open for 0% -> 1% of each run, Pallas kernels for 11% -> 18%
where the time goes in v3:
time: 99.5 us; the launch traced here: 97.8 us
  blocking collectives  42.3 us (43%)
  Pallas kernels  23.1 us (23%)
  starting transfers between devices  19.7 us (20%)
  waiting for transfers between devices  6.55 us (7%)
  local copies, waits for them, and re-layouts  2.27 us (2%)
  between operations  2.06 us (2%)
  other arithmetic  1.79 us (2%)
    all_to_all x2, blocking collectives, exchange(): return lax.all_to_all(blocks, axes, split_axis=0, concat_axis=0, tiled=True)  42.3 us
    pallas_call x3, Pallas kernels, prompt_part(): pl.pallas_call(functools.partial(prompt_kernel, blocks=blocks, count=len(...  18.1 us
    ppermute x10, starting transfers between devices, trade(): lax.ppermute(block, axis, [(i, target(i)) for i in range(lax.axis_size(ax...  11.2 us
    all_to_all x1, starting transfers between devices, exchange(): return lax.all_to_all(blocks, axes, split_axis=0, concat_axis=0, tiled=True)  8.47 us
    ppermute x10, waiting for transfers between devices, trade(): lax.ppermute(block, axis, [(i, target(i)) for i in range(lax.axis_size(ax...  6.55 us
    pallas_call x1, Pallas kernels, suffix_part(): pl.pallas_call(suffix_kernel, in_specs=[SMEM] + [VMEM] * (5 + len(grads))...  4.95 us
  transfers between devices with their start and end apart: 11, of which 4 were waited for; matrix products, arithmetic and copies ran while one was open for 1% of the time, Pallas kernels for 18%

profile of v3, /device:TPU:6, one launch (start us, length us, event | category | flops | bytes accessed | tf_op | source)
XLA Modules:
  0.0 97.8 jit_solution(7879284981490175614)
XLA Ops:
  0.6 0.0 copy-start.4
  0.6 0.0 copy-start.5
  0.7 0.0 copy-start
  0.7 0.0 copy-start.1
  0.7 0.0 copy-start.2
  0.7 0.0 copy-start.3
  0.7 0.9 pad_maximum_fusion
  1.6 0.7 broadcast_in_dim.39
  2.3 8.5 %all-to-all-start = ((bf16[8,128,128]{2,1,0:T(8,128)(2,1)}), bf16[8,128,128]{2,1,0:T(8,128)(2,1)S(1)}, u32[]{:S(2)}, u32[]{:S(2)}) async-start(bf16[8,128,128]{2,1,0:T(8,128)(2,1)} %broadcast_in_dim.39), calls=%async_computation | async-start | bytes 524288 | tf_op jit(solution)/shard_map/all_to_all | solution.py:188
  10.8 0.0 copy-done.4
  10.8 0.8 dynamic-slice_bitcast_fusion
  11.6 0.8 collective-permute-start
  12.4 1.1 %collective-permute-start.1 = (bf16[96,896]{1,0:T(8,128)(2,1)}, bf16[96,896]{1,0:T(8,128)(2,1)S(1)}, u32[]{:S(2)}, u32[]{:S(2)}) collective-permute-start(bf16[96,896]{1,0:T(8,128)(2,1)} %get-tuple-element.66), channel_id=1, source_target_pairs={{0,2},{1,3},{2,0},{3,1},{4,6},{5,7},{6,4},{7,5},{8,10},{9,11},{10,... | collective-permute-start | bytes 516104 | tf_op jit(solution)/shard_map/ppermute | solution.py:192
  13.5 2.8 %collective-permute-start.2 = (bf16[96,896]{1,0:T(8,128)(2,1)S(1)}, bf16[96,896]{1,0:T(8,128)(2,1)S(1)}, u32[]{:S(2)}, u32[]{:S(2)}) collective-permute-start(bf16[96,896]{1,0:T(8,128)(2,1)S(1)} %get-tuple-element.63), channel_id=1, source_target_pairs={{0,3},{1,2},{2,1},{3,0},{4,7},{5,6},{6,5},{7,4},{8,11},{9,10},{10,... | collective-permute-start | bytes 516104 | tf_op jit(solution)/shard_map/ppermute | solution.py:192
  17.6 0.1 stack.36.info_ref
  17.7 1.4 %collective-permute-done.refs_1_ = bf16[96,896]{1,0:T(8,128)(2,1)S(1)} collective-permute-done((bf16[96,896]{1,0:T(8,128)(2,1)}, bf16[96,896]{1,0:T(8,128)(2,1)S(1)}, u32[]{:S(2)}, u32[]{:S(2)}) %collective-permute-start) | collective-permute-done | bytes 172064 | tf_op jit(solution)/shard_map/ppermute | solution.py:192
  19.1 2.2 %collective-permute-done.1.refs_2_ = bf16[96,896]{1,0:T(8,128)(2,1)S(1)} collective-permute-done((bf16[96,896]{1,0:T(8,128)(2,1)}, bf16[96,896]{1,0:T(8,128)(2,1)S(1)}, u32[]{:S(2)}, u32[]{:S(2)}) %collective-permute-start.1) | collective-permute-done | bytes 172064 | tf_op jit(solution)/shard_map/ppermute | solution.py:192
  21.3 2.2 %collective-permute-done.2.refs_3_ = bf16[96,896]{1,0:T(8,128)(2,1)S(1)} collective-permute-done((bf16[96,896]{1,0:T(8,128)(2,1)S(1)}, bf16[96,896]{1,0:T(8,128)(2,1)S(1)}, u32[]{:S(2)}, u32[]{:S(2)}) %collective-permute-start.2) | collective-permute-done | bytes 172064 | tf_op jit(solution)/shard_map/ppermute | solution.py:192
  23.6 0.0 all-to-all-done
  23.6 1.6 %collective-permute-start.4 = (bf16[8,2,2,32,128]{4,3,2,1,0:T(8,128)(2,1)S(1)}, bf16[8,2,2,32,128]{4,3,2,1,0:T(8,128)(2,1)S(1)}, u32[]{:S(2)}, u32[]{:S(2)}) collective-permute-start(bf16[8,2,2,32,128]{4,3,2,1,0:T(8,128)(2,1)S(1)} %bitcast.36), channel_id=1, source_target_pairs={{0,8},{8,16},{16,24},{24,0},{1,9},{9,17},{17,25},{25,1},{2,10},{10... | collective-permute-start | bytes 786440 | tf_op jit(solution)/shard_map/ppermute | solution.py:192
  25.1 1.7 %collective-permute-start.5 = (bf16[8,2,2,32,128]{4,3,2,1,0:T(8,128)(2,1)S(1)}, bf16[8,2,2,32,128]{4,3,2,1,0:T(8,128)(2,1)S(1)}, u32[]{:S(2)}, u32[]{:S(2)}) collective-permute-start(bf16[8,2,2,32,128]{4,3,2,1,0:T(8,128)(2,1)S(1)} %bitcast.37), channel_id=1, source_target_pairs={{0,24},{8,0},{16,8},{24,16},{1,25},{9,1},{17,9},{25,17},{2,26},{10... | collective-permute-start | bytes 786440 | tf_op jit(solution)/shard_map/ppermute | solution.py:192
  26.8 0.0 copy-done.5
  26.8 2.0 %collective-permute-start.3 = (bf16[8,2,2,32,128]{4,3,2,1,0:T(8,128)(2,1)S(1)}, bf16[8,2,2,32,128]{4,3,2,1,0:T(8,128)(2,1)S(1)}, u32[]{:S(2)}, u32[]{:S(2)}) collective-permute-start(bf16[8,2,2,32,128]{4,3,2,1,0:T(8,128)(2,1)S(1)} %bitcast.38), channel_id=1, source_target_pairs={{0,16},{8,24},{16,0},{24,8},{1,17},{9,25},{17,1},{25,9},{2,18},{10... | collective-permute-start | bytes 786440 | tf_op jit(solution)/shard_map/ppermute | solution.py:192
  28.8 0.0 copy-done
  28.8 0.0 copy-done.1
  28.8 0.0 copy-done.2
  28.8 0.0 copy-done.3
  28.8 4.9 %suffix_part.1 = (bf16[2688,128]{1,0:T(8,128)(2,1)S(1)}, bf16[2688,128]{1,0:T(8,128)(2,1)S(1)}, bf16[128,2688]{1,0:T(8,128)(2,1)S(1)}, bf16[128,2688]{1,0:T(8,12...) custom-call(s32[5]{0:T(128)S(1)} %stack.36.info_ref, ...), custom_call_target="tpu_custom_call" | custom-call | flops 1321205760 | bytes 5505024 | tf_op jit(solution)/shard_map/suffix_part/pallas_call | solution.py:91
  33.8 0.0 collective-permute-done.4.refs_1_
  33.8 0.6 collective-permute-done.5.refs_2_
  34.4 0.0 collective-permute-start.7
  34.4 0.5 collective-permute-start.8
  34.9 0.0 collective-permute-start.9
  34.9 6.3 %prompt_part.3 = (f32[128,2688]{1,0:T(8,128)S(1)}, bf16[3,2,256,128]{3,2,1,0:T(8,128)(2,1)S(1)}) custom-call(s32[5]{0:T(128)S(1)} %stack.36.info_ref, bf16[8,2,2,32,128]{4,3,2,1,0:T(8,128)(2,1)S(1)} %bitcast.40, bf16[8,2,2,32,128]{4,3,2,1,0:T(8,128)(2,1)S(1)} %collective-permute-done.4.refs_1_, ...), custom_call_target="tpu_custom_call" | custom-call | flops 2642411520 | bytes 5505024 | tf_op jit(solution)/shard_map/prompt_part/pallas_call | solution.py:176
  41.2 0.0 collective-permute-done.3.refs_0_
  41.2 0.8 collective-permute-start.6
  42.0 0.0 collective-permute-done.7.refs_0_
  42.0 0.0 collective-permute-done.8.refs_1_
  42.0 0.0 collective-permute-done.9.refs_2_
  42.0 6.3 %prompt_part.4 = (f32[128,2688]{1,0:T(8,128)S(1)}, bf16[3,2,256,128]{3,2,1,0:T(8,128)(2,1)S(1)}) custom-call(s32[5]{0:T(128)S(1)} %stack.36.info_ref, bf16[8,2,2,32,128]{4,3,2,1,0:T(8,128)(2,1)S(1)} %collective-permute-done.7.refs_0_, bf16[8,2,2,32,128]{4,3,2,1,0:T(8,128)(2,1)S(1)} %collective-permute-done.8.refs_1_, ...), custom_call_target="tpu_custom_call" | custom-call | flops 2642411520 | bytes 5505024 | tf_op jit(solution)/shard_map/prompt_part/pallas_call | solution.py:176
  48.3 0.0 collective-permute-done.6.refs_1_
  48.3 5.6 %prompt_part.5 = (bf16[384,896]{1,0:T(8,128)(2,1)}, bf16[8,528,128]{2,1,0:T(8,128)(2,1)S(1)}) custom-call(s32[5]{0:T(128)S(1)} %stack.36.info_ref, bf16[8,2,2,32,128]{4,3,2,1,0:T(8,128)(2,1)S(1)} %collective-permute-done.3.refs_0_, bf16[8,2,2,32,128]{4,3,2,1,0:T(8,128)(2,1)S(1)} %collective-permute-done.6.refs_1_, ...), custom_call_target="tpu_custom_call" | custom-call | flops 1761607680 | bytes 5505024 | tf_op jit(solution)/shard_map/prompt_part/pallas_call | solution.py:176
  53.9 23.8 %all_to_all.19 = bf16[8,528,128]{2,1,0:T(8,128)(2,1)S(1)} all-to-all(bf16[8,528,128]{2,1,0:T(8,128)(2,1)S(1)} %get-tuple-element.58), channel_id=1, replica_groups=mesh['z'=8,'y'=4,'c'=2,'head'=4] {'y','c'}, dimensions={0} | all-to-all | bytes 2162688 | tf_op jit(solution)/shard_map/all_to_all | solution.py:188
  77.7 0.4 compare_reduce_fusion.1
  78.1 0.5 fusion
  78.6 18.5 %all_to_all.20 = bf16[8,128,128]{2,1,0:T(8,128)(2,1)S(1)} all-to-all(bf16[8,128,128]{2,1,0:T(8,128)(2,1)S(1)} %bitcast.46), channel_id=1, replica_groups=mesh['z'=8,'y'=4,'c'=2,'head'=4] {'z'}, dimensions={0} | all-to-all | bytes 524288 | tf_op jit(solution)/shard_map/all_to_all | solution.py:188
  97.1 0.6 slice_bitcast_fusion
  (4 shorter events, 0.1 us)
Async XLA Ops:
  0.6 10.2 %copy-start.4 = (bf16[1,96,3584]{2,1,0:T(8,128)(2,1)S(1)}, bf16[1,96,3584]{2,1,0:T(8,128)(2,1)}, u32[]{:S(2)}) copy-start(bf16[1,96,3584]{2,1,0:T(8,128)(2,1)} %param.16) | copy-start | bytes 2064388
  0.6 26.2 %copy-start.5 = (f32[1,7,384]{2,0,1:T(1,128)S(1)}, f32[1,7,384]{2,0,1:T(1,128)}, u32[]{:S(2)}) copy-start(f32[1,7,384]{2,0,1:T(1,128)} %param.17) | copy-start | bytes 32260
  0.7 28.1 %copy-start = (bf16[1,384,896]{2,1,0:T(8,128)(2,1)S(1)}, bf16[1,384,896]{2,1,0:T(8,128)(2,1)}, u32[]{:S(2)}) copy-start(bf16[1,384,896]{2,1,0:T(8,128)(2,1)} %param.10) | copy-start | bytes 2064388
  0.7 28.1 %copy-start.1 = (bf16[1,384,896]{2,1,0:T(8,128)(2,1)S(1)}, bf16[1,384,896]{2,1,0:T(8,128)(2,1)}, u32[]{:S(2)}) copy-start(bf16[1,384,896]{2,1,0:T(8,128)(2,1)} %param.15) | copy-start | bytes 2064388
  0.7 28.1 %copy-start.2 = (bf16[1,384,128]{2,1,0:T(8,128)(2,1)S(1)}, bf16[1,384,128]{2,1,0:T(8,128)(2,1)}, u32[]{:S(2)}) copy-start(bf16[1,384,128]{2,1,0:T(8,128)(2,1)} %param.11) | copy-start | bytes 294916
  0.7 28.1 %copy-start.3 = (bf16[1,384,128]{2,1,0:T(8,128)(2,1)S(1)}, bf16[1,384,128]{2,1,0:T(8,128)(2,1)}, u32[]{:S(2)}) copy-start(bf16[1,384,128]{2,1,0:T(8,128)(2,1)} %param.12) | copy-start | bytes 294916
  2.3 21.2 %all-to-all-start = ((bf16[8,128,128]{2,1,0:T(8,128)(2,1)}), bf16[8,128,128]{2,1,0:T(8,128)(2,1)S(1)}, u32[]{:S(2)}, u32[]{:S(2)}) async-start(bf16[8,128,128]{2,1,0:T(8,128)(2,1)} %broadcast_in_dim.39), calls=%async_computation | async-start | bytes 524288 | tf_op jit(solution)/shard_map/all_to_all | solution.py:188
  11.6 7.5 %collective-permute-start = (bf16[96,896]{1,0:T(8,128)(2,1)}, bf16[96,896]{1,0:T(8,128)(2,1)S(1)}, u32[]{:S(2)}, u32[]{:S(2)}) collective-permute-start(bf16[96,896]{1,0:T(8,128)(2,1)} %get-tuple-element.64), channel_id=1, source_target_pairs={{0,1},{1,0},{2,3},{3,2},{4,5},{5,4},{6,7},{7,6},{8,9},{9,8},{10,11... | collective-permute-start | bytes 516104 | tf_op jit(solution)/shard_map/ppermute | solution.py:192
  12.4 8.9 %collective-permute-start.1 = (bf16[96,896]{1,0:T(8,128)(2,1)}, bf16[96,896]{1,0:T(8,128)(2,1)S(1)}, u32[]{:S(2)}, u32[]{:S(2)}) collective-permute-start(bf16[96,896]{1,0:T(8,128)(2,1)} %get-tuple-element.66), channel_id=1, source_target_pairs={{0,2},{1,3},{2,0},{3,1},{4,6},{5,7},{6,4},{7,5},{8,10},{9,11},{10,... | collective-permute-start | bytes 516104 | tf_op jit(solution)/shard_map/ppermute | solution.py:192
  13.5 10.0 %collective-permute-start.2 = (bf16[96,896]{1,0:T(8,128)(2,1)S(1)}, bf16[96,896]{1,0:T(8,128)(2,1)S(1)}, u32[]{:S(2)}, u32[]{:S(2)}) collective-permute-start(bf16[96,896]{1,0:T(8,128)(2,1)S(1)} %get-tuple-element.63), channel_id=1, source_target_pairs={{0,3},{1,2},{2,1},{3,0},{4,7},{5,6},{6,5},{7,4},{8,11},{9,10},{10,... | collective-permute-start | bytes 516104 | tf_op jit(solution)/shard_map/ppermute | solution.py:192
  23.6 10.2 %collective-permute-start.4 = (bf16[8,2,2,32,128]{4,3,2,1,0:T(8,128)(2,1)S(1)}, bf16[8,2,2,32,128]{4,3,2,1,0:T(8,128)(2,1)S(1)}, u32[]{:S(2)}, u32[]{:S(2)}) collective-permute-start(bf16[8,2,2,32,128]{4,3,2,1,0:T(8,128)(2,1)S(1)} %bitcast.36), channel_id=1, source_target_pairs={{0,8},{8,16},{16,24},{24,0},{1,9},{9,17},{17,25},{25,1},{2,10},{10... | collective-permute-start | bytes 786440 | tf_op jit(solution)/shard_map/ppermute | solution.py:192
  25.1 9.2 %collective-permute-start.5 = (bf16[8,2,2,32,128]{4,3,2,1,0:T(8,128)(2,1)S(1)}, bf16[8,2,2,32,128]{4,3,2,1,0:T(8,128)(2,1)S(1)}, u32[]{:S(2)}, u32[]{:S(2)}) collective-permute-start(bf16[8,2,2,32,128]{4,3,2,1,0:T(8,128)(2,1)S(1)} %bitcast.37), channel_id=1, source_target_pairs={{0,24},{8,0},{16,8},{24,16},{1,25},{9,1},{17,9},{25,17},{2,26},{10... | collective-permute-start | bytes 786440 | tf_op jit(solution)/shard_map/ppermute | solution.py:192
  26.8 14.4 %collective-permute-start.3 = (bf16[8,2,2,32,128]{4,3,2,1,0:T(8,128)(2,1)S(1)}, bf16[8,2,2,32,128]{4,3,2,1,0:T(8,128)(2,1)S(1)}, u32[]{:S(2)}, u32[]{:S(2)}) collective-permute-start(bf16[8,2,2,32,128]{4,3,2,1,0:T(8,128)(2,1)S(1)} %bitcast.38), channel_id=1, source_target_pairs={{0,16},{8,24},{16,0},{24,8},{1,17},{9,25},{17,1},{25,9},{2,18},{10... | collective-permute-start | bytes 786440 | tf_op jit(solution)/shard_map/ppermute | solution.py:192
  34.4 7.6 %collective-permute-start.7 = (bf16[8,2,2,32,128]{4,3,2,1,0:T(8,128)(2,1)S(1)}, bf16[8,2,2,32,128]{4,3,2,1,0:T(8,128)(2,1)S(1)}, u32[]{:S(2)}, u32[]{:S(2)}) collective-permute-start(bf16[8,2,2,32,128]{4,3,2,1,0:T(8,128)(2,1)S(1)} %bitcast.39), channel_id=1, source_target_pairs={{0,4},{4,0},{1,5},{5,1},{2,6},{6,2},{3,7},{7,3},{8,12},{12,8},{9,1... | collective-permute-start | bytes 786440 | tf_op jit(solution)/shard_map/ppermute | solution.py:192
  34.4 7.6 %collective-permute-start.8 = (bf16[8,2,2,32,128]{4,3,2,1,0:T(8,128)(2,1)S(1)}, bf16[8,2,2,32,128]{4,3,2,1,0:T(8,128)(2,1)S(1)}, u32[]{:S(2)}, u32[]{:S(2)}) collective-permute-start(bf16[8,2,2,32,128]{4,3,2,1,0:T(8,128)(2,1)S(1)} %collective-permute-done.4.refs_1_), channel_id=1, source_target_pairs={{0,4},{4,0},{1,5},{5,1},{2,6},{6,2},{3,7},{7,3},{8,12},{12,8},{9,1... | collective-permute-start | bytes 786440 | tf_op jit(solution)/shard_map/ppermute | solution.py:192
  34.9 7.1 %collective-permute-start.9 = (bf16[8,2,2,32,128]{4,3,2,1,0:T(8,128)(2,1)S(1)}, bf16[8,2,2,32,128]{4,3,2,1,0:T(8,128)(2,1)S(1)}, u32[]{:S(2)}, u32[]{:S(2)}) collective-permute-start(bf16[8,2,2,32,128]{4,3,2,1,0:T(8,128)(2,1)S(1)} %collective-permute-done.5.refs_2_), channel_id=1, source_target_pairs={{0,4},{4,0},{1,5},{5,1},{2,6},{6,2},{3,7},{7,3},{8,12},{12,8},{9,1... | collective-permute-start | bytes 786440 | tf_op jit(solution)/shard_map/ppermute | solution.py:192
  41.2 7.1 %collective-permute-start.6 = (bf16[8,2,2,32,128]{4,3,2,1,0:T(8,128)(2,1)S(1)}, bf16[8,2,2,32,128]{4,3,2,1,0:T(8,128)(2,1)S(1)}, u32[]{:S(2)}, u32[]{:S(2)}) collective-permute-start(bf16[8,2,2,32,128]{4,3,2,1,0:T(8,128)(2,1)S(1)} %collective-permute-done.3.refs_0_), channel_id=1, source_target_pairs={{0,4},{4,0},{1,5},{5,1},{2,6},{6,2},{3,7},{7,3},{8,12},{12,8},{9,1... | collective-permute-start | bytes 786440 | tf_op jit(solution)/shard_map/ppermute | solution.py:192

commit v4 on v3

--- a/solution.py
+++ b/solution.py
@@ -48,9 +48,9 @@
     group_size = query_ref.shape[1] // width
     part = grad_refs[0].shape[0]
     for i, piece in enumerate(grad_refs):
-        start = pl.multiple_of((info_ref[3] ^ i) * part, part)
+        start = pl.multiple_of((info_ref[1] ^ i) * part, part)
         grad_ref[pl.ds(start, part), :] = piece[...]
-    live_down = lax.broadcasted_iota(jnp.int32, (seq_len, width), 0) < info_ref[4]
+    live_down = lax.broadcasted_iota(jnp.int32, (seq_len, width), 0) < info_ref[2]
     key_at = lax.broadcasted_iota(jnp.int32, (seq_len, seq_len), 0)
     query_at = lax.broadcasted_iota(jnp.int32, (seq_len, seq_len), 1)
     causal = key_at <= query_at
@@ -110,13 +110,13 @@
     )(info, query, attn_out, log_norm, key_suffix, value_suffix, *grads)
 
 
-def prompt_kernel(info_ref, *refs, blocks, count, earlier):
+def prompt_kernel(info_ref, *refs, blocks, count, last):
     pair_refs, refs = refs[:count], refs[count:]
     (
         query_rows_ref, grad_rows_ref, query_t_ref, grad_t_ref, norm_row_ref, delta_row_ref,
-        query_acc_ref,
-    ) = refs[:7]
-    earlier_refs, (query_grad_ref, pair_grad_ref) = refs[7:-2], refs[-2:]
+        query_acc_ref, query_grad_ref,
+    ) = refs[:8]
+    pair_grad_refs = refs[8:]
     chosen = info_ref[0]
     width = query_rows_ref.shape[1]
 
@@ -135,7 +135,7 @@
         )
         query_part = jnp.dot(key_t, score_grad_t, preferred_element_type=F32)
         query_part += query_acc_ref[:, rows]
-        if earlier:
+        if last:
             query_grad_ref[:, head * width : (head + 1) * width] = query_part.T.astype(BF16)
         else:
             query_grad_ref[:, rows] = query_part
@@ -143,45 +143,58 @@
         value_acc += jnp.dot(weights_t, grad_rows_ref[rows, :], preferred_element_type=F32)
     size = key_rows.shape[0] // count
     key_grad, value_grad = key_acc.astype(BF16), value_acc.astype(BF16)
-    own = [
-        (key_grad[i * size : (i + 1) * size], value_grad[i * size : (i + 1) * size])
-        for i in range(count)
-    ]
-    if not earlier:
-        for i in range(count):
-            pair_grad_ref[i, 0], pair_grad_ref[i, 1] = own[i]
-        return
-    core, line = info_ref[1], info_ref[2]
-    lines = pair_grad_ref.shape[0] // 2
     mark = jnp.full((MARK, width), chosen.astype(F32), F32).astype(BF16)
-    found = [(ref, i) for ref in earlier_refs for i in range(ref.shape[0])]
-    found = [(ref[i, 0], ref[i, 1]) for ref, i in found] + own
-    for (steps, other), (keys, values) in zip(earlier, found, strict=True):
-        owner = 2 * lax.rem(line - steps + lines, lines) + (1 - core if other else core)
-        pair_grad_ref[owner, :size] = keys
-        pair_grad_ref[owner, size : 2 * size] = values
-        pair_grad_ref[owner, 2 * size :] = mark
-
-
-def prompt_part(info, pairs, rows, query_acc, seq_len, earlier=(), order=()):
+    for i, ref in enumerate(pair_grad_refs):
+        ref[:size] = key_grad[i * size : (i + 1) * size]
+        ref[size : 2 * size] = value_grad[i * size : (i + 1) * size]
+        ref[2 * size :] = mark
+
+
+def prompt_part(info, pairs, rows, query_acc, seq_len, last=False):
     row_count, width = rows[0].shape
     blocks = [slice(at, at + seq_len) for at in range(0, row_count, seq_len)]
     stacks, _, _, owned, _ = pairs[0].shape
     size = stacks * owned
     out = jax.ShapeDtypeStruct((width, row_count), F32)
-    pair_out = jax.ShapeDtypeStruct((len(pairs), 2, size, width), BF16)
-    if order:
+    if last:
         out = jax.ShapeDtypeStruct((seq_len, row_count * width // seq_len), BF16)
-        pair_out = jax.ShapeDtypeStruct((len(order), 2 * size + MARK, width), BF16)
+    pair_out = jax.ShapeDtypeStruct((2 * size + MARK, width), BF16)
     return pl.pallas_call(
-        functools.partial(prompt_kernel, blocks=blocks, count=len(pairs), earlier=order),
-        in_specs=[SMEM] + [VMEM] * (len(pairs) + 7 + len(earlier)),
-        out_specs=[VMEM] * 2,
-        out_shape=[out, pair_out],
+        functools.partial(prompt_kernel, blocks=blocks, count=len(pairs), last=last),
+        in_specs=[SMEM] + [VMEM] * (len(pairs) + 7),
+        out_specs=[VMEM] * (1 + len(pairs)),
+        out_shape=[out] + [pair_out] * len(pairs),
         compiler_params=PARAMS,
         cost_estimate=cost(row_count, len(pairs) * size, width),
         name="prompt_part",
-    )(info, *pairs, *rows, query_acc, *earlier)
+    )(info, *pairs, *rows, query_acc)
+
+
+def group_kernel(*refs):
+    share_refs, total_ref = refs[:-1], refs[-1]
+    stacks, prompt_count, _, owned, width = total_ref.shape
+    size = stacks * owned
+    for which in range(2):
+        rows = slice(which * size, (which + 1) * size)
+        totals = [jnp.zeros((size, width), F32)] * prompt_count
+        for ref in share_refs:
+            share = ref[rows].astype(F32)
+            mark = ref[2 * size :].astype(F32)[:1]
+            for i in range(prompt_count):
+                totals[i] += jnp.where(mark == float(i), share, 0.0)
+        for i in range(prompt_count):
+            total_ref[:, i, which] = totals[i].astype(BF16).reshape(stacks, owned, width)
+
+
+def group_sum(shares, shape):
+    return pl.pallas_call(
+        group_kernel,
+        in_specs=[VMEM] * len(shares),
+        out_specs=VMEM,
+        out_shape=jax.ShapeDtypeStruct(shape, BF16),
+        compiler_params=PARAMS,
+        name="group_sum",
+    )(*shares)
 
 
 def exchange(blocks, axes):
@@ -205,9 +218,7 @@
     prompt_count, owned = key_prompt.shape[:2]
     heads, stacks, lines = lax.axis_size("head"), lax.axis_size("z"), lax.axis_size("y")
     place = lax.axis_index("head")
-    info = jnp.stack(
-        [prompt_id[0], lax.axis_index("c"), lax.axis_index("y"), place, lengths[0]]
-    ).astype(jnp.int32)
+    info = jnp.stack([prompt_id[0], place, lengths[0]]).astype(jnp.int32)
 
     own_pair = jnp.stack([key_prompt, value_prompt], 1).reshape(-1, width)
     stacked = exchange(copies(own_pair, stacks).reshape(-1, width), "z")
@@ -228,25 +239,33 @@
     )
     near, key_grad = lax.optimization_barrier(([stacked, moved[1], moved[lines - 1]], key_grad))
     near_other = [trade(block, "c", lambda j: j ^ 1) for block in near]
-    query_acc, first = prompt_part(info, near, rows, query_acc, seq_len)
+
+    shares = []
+
+    def send(parts, places):
+        for part, (steps, other) in zip(parts, places, strict=True):
+            if not steps and not other:
+                shares.append(part)
+                continue
+            target = lambda j, s=steps, o=other: 2 * ((j // 2 - s) % lines) + (j % 2 ^ o)
+            shares.append(trade(part, GROUP, target))
+
+    query_acc, *parts = prompt_part(info, near, rows, query_acc, seq_len)
     far, query_acc = lax.optimization_barrier((moved[2], query_acc))
     far_other = trade(far, "c", lambda j: j ^ 1)
-    query_acc, second = prompt_part(info, near_other, rows, query_acc, seq_len)
-    order = [(steps, other) for other in (False, True) for steps in (0, 1, lines - 1)]
-    order += [(2, False), (2, True)]
-    query_grad, pair_grad = prompt_part(
-        info, [far, far_other], rows, query_acc, seq_len, (first, second), order
-    )
-
-    shares = exchange(pair_grad, GROUP)
-    ids = shares[:, -MARK : 1 - MARK, :1]
-    shares = shares[:, :-MARK].astype(F32)
-    totals = jnp.stack(
-        [jnp.sum(jnp.where(ids == i, shares, 0.0), 0) for i in range(prompt_count)], 0
-    )
-    totals = totals.reshape(prompt_count, 2, stacks, owned, width).transpose(2, 0, 1, 3, 4)
-    totals = totals.astype(BF16).reshape(stacks, -1, width)
-    final = jnp.sum(exchange(totals, "z").astype(F32), 0).astype(BF16)
+    send(parts, [(0, 0), (1, 0), (lines - 1, 0)])
+    query_acc, *parts = prompt_part(info, [far, far_other], rows, query_acc, seq_len)
+    send(parts, [(2, 0), (2, 1)])
+    query_acc, near_other, shares[:3] = lax.optimization_barrier(
+        (query_acc, near_other, shares[:3])
+    )
+    query_grad, *parts = prompt_part(info, near_other, rows, query_acc, seq_len, True)
+    parts, shares[3:] = lax.optimization_barrier((parts, shares[3:]))
+    send(parts, [(0, 1), (1, 1), (lines - 1, 1)])
+
+    totals = group_sum(shares, (stacks, prompt_count, 2, owned, width))
+    final = exchange(totals.reshape(-1, prompt_count * 2 * owned, width), "z")
+    final = jnp.sum(final.astype(F32), 0).astype(BF16)
     final = final.reshape(prompt_count, 2, owned, width)
     return (query_grad[None], key_grad[None], value_grad[None], final[:, 0], final[:, 1])
 

time: 99.5 us -> 95.8 us (0.963)
  the two profiles are of different devices: /device:TPU:6 before, /device:TPU:1 now
where the time goes in v4:
time: 95.8 us; the launch traced here: 95.5 us
  starting transfers between devices  33.6 us (35%)
  Pallas kernels  23.4 us (24%)
  blocking collectives  18.4 us (19%)
  waiting for transfers between devices  15.6 us (16%)
  between operations  2.06 us (2%)
  local copies, waits for them, and re-layouts  1.44 us (2%)
  other arithmetic  1.01 us (1%)
    ppermute x17, starting transfers between devices, trade(): lax.ppermute(block, axis, [(i, target(i)) for i in range(lax.axis_size(ax...  24.6 us
    all_to_all x1, blocking collectives, exchange(): return lax.all_to_all(blocks, axes, split_axis=0, concat_axis=0, tiled=True)  18.4 us
    pallas_call x3, Pallas kernels, prompt_part(): pl.pallas_call(functools.partial(prompt_kernel, blocks=blocks, count=len(...  18 us
    ppermute x17, waiting for transfers between devices, trade(): lax.ppermute(block, axis, [(i, target(i)) for i in range(lax.axis_size(ax...  15.6 us
    all_to_all x1, starting transfers between devices, exchange(): return lax.all_to_all(blocks, axes, split_axis=0, concat_axis=0, tiled=True)  9.01 us
    pallas_call x1, Pallas kernels, suffix_part(): pl.pallas_call(suffix_kernel, in_specs=[SMEM] + [VMEM] * (5 + len(grads))...  4.93 us
  transfers between devices with their start and end apart: 18, of which 5 were waited for; matrix products, arithmetic and copies ran while one was open for 0% of the time, Pallas kernels for 24%

profile of v4, /device:TPU:1, one launch (start us, length us, event | category | flops | bytes accessed | tf_op | source)
XLA Modules:
  0.0 95.5 jit_solution(8836826711911144081)
XLA Ops:
  0.6 0.0 copy-start.4
  0.6 0.0 copy-start.5
  0.7 0.0 copy-start
  0.7 0.0 copy-start.1
  0.7 0.0 copy-start.2
  0.7 0.0 copy-start.3
  0.7 0.9 pad_maximum_fusion
  1.6 0.7 broadcast_in_dim.17
  2.3 9.0 %all-to-all-start = ((bf16[8,128,128]{2,1,0:T(8,128)(2,1)}), bf16[8,128,128]{2,1,0:T(8,128)(2,1)S(1)}, u32[]{:S(2)}, u32[]{:S(2)}) async-start(bf16[8,128,128]{2,1,0:T(8,128)(2,1)} %broadcast_in_dim.17), calls=%async_computation | async-start | bytes 524288 | tf_op jit(solution)/shard_map/all_to_all | solution.py:201
  11.3 0.0 copy-done.4
  11.3 0.1 dynamic-slice_bitcast_fusion
  11.4 1.3 %collective-permute-start = (bf16[96,896]{1,0:T(8,128)(2,1)S(1)}, bf16[96,896]{1,0:T(8,128)(2,1)S(1)}, u32[]{:S(2)}, u32[]{:S(2)}) collective-permute-start(bf16[96,896]{1,0:T(8,128)(2,1)S(1)} %get-tuple-element.94), channel_id=1, source_target_pairs={{0,1},{1,0},{2,3},{3,2},{4,5},{5,4},{6,7},{7,6},{8,9},{9,8},{10,11... | collective-permute-start | bytes 516104 | tf_op jit(solution)/shard_map/ppermute | solution.py:205
  12.7 2.5 %collective-permute-start.1 = (bf16[96,896]{1,0:T(8,128)(2,1)S(1)}, bf16[96,896]{1,0:T(8,128)(2,1)S(1)}, u32[]{:S(2)}, u32[]{:S(2)}) collective-permute-start(bf16[96,896]{1,0:T(8,128)(2,1)S(1)} %get-tuple-element.96), channel_id=1, source_target_pairs={{0,2},{1,3},{2,0},{3,1},{4,6},{5,7},{6,4},{7,5},{8,10},{9,11},{10,... | collective-permute-start | bytes 516104 | tf_op jit(solution)/shard_map/ppermute | solution.py:205
  15.2 0.2 collective-permute-start.2
  16.7 0.1 pad_add_fusion.info_ref
  16.7 0.0 collective-permute-done.refs_1_
  16.7 5.6 %collective-permute-done.1.refs_2_ = bf16[96,896]{1,0:T(8,128)(2,1)S(1)} collective-permute-done((bf16[96,896]{1,0:T(8,128)(2,1)S(1)}, bf16[96,896]{1,0:T(8,128)(2,1)S(1)}, u32[]{:S(2)}, u32[]{:S(2)}) %collective-permute-start.1) | collective-permute-done | bytes 172064 | tf_op jit(solution)/shard_map/ppermute | solution.py:205
  22.3 2.9 %collective-permute-done.2.refs_3_ = bf16[96,896]{1,0:T(8,128)(2,1)S(1)} collective-permute-done((bf16[96,896]{1,0:T(8,128)(2,1)S(1)}, bf16[96,896]{1,0:T(8,128)(2,1)S(1)}, u32[]{:S(2)}, u32[]{:S(2)}) %collective-permute-start.2) | collective-permute-done | bytes 172064 | tf_op jit(solution)/shard_map/ppermute | solution.py:205
  25.2 0.0 all-to-all-done
  25.2 1.3 %collective-permute-start.4 = (bf16[8,2,2,32,128]{4,3,2,1,0:T(8,128)(2,1)S(1)}, bf16[8,2,2,32,128]{4,3,2,1,0:T(8,128)(2,1)S(1)}, u32[]{:S(2)}, u32[]{:S(2)}) collective-permute-start(bf16[8,2,2,32,128]{4,3,2,1,0:T(8,128)(2,1)S(1)} %bitcast.31), channel_id=1, source_target_pairs={{0,8},{8,16},{16,24},{24,0},{1,9},{9,17},{17,25},{25,1},{2,10},{10... | collective-permute-start | bytes 786440 | tf_op jit(solution)/shard_map/ppermute | solution.py:205
  26.5 1.4 %collective-permute-start.5 = (bf16[8,2,2,32,128]{4,3,2,1,0:T(8,128)(2,1)S(1)}, bf16[8,2,2,32,128]{4,3,2,1,0:T(8,128)(2,1)S(1)}, u32[]{:S(2)}, u32[]{:S(2)}) collective-permute-start(bf16[8,2,2,32,128]{4,3,2,1,0:T(8,128)(2,1)S(1)} %bitcast.32), channel_id=1, source_target_pairs={{0,24},{8,0},{16,8},{24,16},{1,25},{9,1},{17,9},{25,17},{2,26},{10... | collective-permute-start | bytes 786440 | tf_op jit(solution)/shard_map/ppermute | solution.py:205
  27.9 0.0 copy-done.5
  27.9 1.6 %collective-permute-start.3 = (bf16[8,2,2,32,128]{4,3,2,1,0:T(8,128)(2,1)S(1)}, bf16[8,2,2,32,128]{4,3,2,1,0:T(8,128)(2,1)S(1)}, u32[]{:S(2)}, u32[]{:S(2)}) collective-permute-start(bf16[8,2,2,32,128]{4,3,2,1,0:T(8,128)(2,1)S(1)} %bitcast.33), channel_id=1, source_target_pairs={{0,16},{8,24},{16,0},{24,8},{1,17},{9,25},{17,1},{25,9},{2,18},{10... | collective-permute-start | bytes 786440 | tf_op jit(solution)/shard_map/ppermute | solution.py:205
  29.6 0.0 copy-done
  29.6 0.0 copy-done.1
  29.6 0.0 copy-done.2
  29.6 0.0 copy-done.3
  29.6 4.9 %suffix_part.1 = (bf16[2688,128]{1,0:T(8,128)(2,1)S(1)}, bf16[2688,128]{1,0:T(8,128)(2,1)S(1)}, bf16[128,2688]{1,0:T(8,128)(2,1)S(1)}, bf16[128,2688]{1,0:T(8,12...) custom-call(s32[3]{0:T(128)S(1)} %pad_add_fusion.info_ref, ...), custom_call_target="tpu_custom_call" | custom-call | flops 1321205760 | bytes 5505024 | tf_op jit(solution)/shard_map/suffix_part/pallas_call | solution.py:91
  34.5 0.0 collective-permute-done.4.refs_1_
  34.5 0.0 collective-permute-done.5.refs_2_
  34.5 6.3 %prompt_part.3 = (f32[128,2688]{1,0:T(8,128)S(1)}, bf16[528,128]{1,0:T(8,128)(2,1)S(1)}, bf16[528,128]{1,0:T(8,128)(2,1)S(1)}, bf16[528,128]{1,0:T(8,128)(2,1)S(1)}) custom-call(s32[3]{0:T(128)S(1)} %pad_add_fusion.info_ref, bf16[8,2,2,32,128]{4,3,2,1,0:T(8,128)(2,1)S(1)} %bitcast.34, bf16[8,2,2,32,128]{4,3,2,1,0:T(8,128)(2,1)S(1)} %collective-permute-done.4.refs_1_, ...), custom_call_target="tpu_custom_call" | custom-call | flops 2642411520 | bytes 5505024 | tf_op jit(solution)/shard_map/prompt_part/pallas_call | solution.py:162
  40.8 0.0 collective-permute-done.3.refs_0_
  40.8 3.0 %collective-permute-start.6 = (bf16[8,2,2,32,128]{4,3,2,1,0:T(8,128)(2,1)S(1)}, bf16[8,2,2,32,128]{4,3,2,1,0:T(8,128)(2,1)S(1)}, u32[]{:S(2)}, u32[]{:S(2)}) collective-permute-start(bf16[8,2,2,32,128]{4,3,2,1,0:T(8,128)(2,1)S(1)} %collective-permute-done.3.refs_0_), channel_id=1, source_target_pairs={{0,4},{4,0},{1,5},{5,1},{2,6},{6,2},{3,7},{7,3},{8,12},{12,8},{9,1... | collective-permute-start | bytes 786440 | tf_op jit(solution)/shard_map/ppermute | solution.py:205
  43.8 0.1 collective-permute-start.7
  43.9 0.4 collective-permute-start.8
  44.3 0.1 collective-permute-start.9
  44.4 6.0 %collective-permute-start.10 = (bf16[528,128]{1,0:T(8,128)(2,1)S(1)}, bf16[528,128]{1,0:T(8,128)(2,1)S(1)}, u32[]{:S(2)}, u32[]{:S(2)}) collective-permute-start(bf16[528,128]{1,0:T(8,128)(2,1)S(1)} %get-tuple-element.71), channel_id=1, source_target_pairs={{0,24},{4,28},{8,0},{12,4},{16,8},{20,12},{24,16},{28,20},{1,25},{... | collective-permute-start | bytes 405512 | tf_op jit(solution)/shard_map/ppermute | solution.py:205
  50.4 0.0 collective-permute-done.6.refs_1_
  50.4 0.0 collective-permute-start.11
  50.4 4.7 %prompt_part.4 = (f32[128,2688]{1,0:T(8,128)S(1)}, bf16[528,128]{1,0:T(8,128)(2,1)S(1)}, bf16[528,128]{1,0:T(8,128)(2,1)S(1)}) custom-call(s32[3]{0:T(128)S(1)} %pad_add_fusion.info_ref, bf16[8,2,2,32,128]{4,3,2,1,0:T(8,128)(2,1)S(1)} %collective-permute-done.3.refs_0_, bf16[8,2,2,32,128]{4,3,2,1,0:T(8,128)(2,1)S(1)} %collective-permute-done.6.refs_1_, ...), custom_call_target="tpu_custom_call" | custom-call | flops 1761607680 | bytes 5505024 | tf_op jit(solution)/shard_map/prompt_part/pallas_call | solution.py:162
  55.1 0.0 collective-permute-done.10.refs_1_
  55.2 0.9 collective-permute-done.11.refs_2_
  56.1 0.0 collective-permute-done.7.refs_0_
  56.1 0.0 collective-permute-done.8.refs_1_
  56.1 0.0 collective-permute-done.9.refs_2_
  56.1 0.9 collective-permute-start.12
  57.0 3.9 %collective-permute-start.13 = (bf16[528,128]{1,0:T(8,128)(2,1)S(1)}, bf16[528,128]{1,0:T(8,128)(2,1)S(1)}, u32[]{:S(2)}, u32[]{:S(2)}) collective-permute-start(bf16[528,128]{1,0:T(8,128)(2,1)S(1)} %get-tuple-element.87), channel_id=1, source_target_pairs={{0,20},{4,16},{8,28},{12,24},{16,4},{20,0},{24,12},{28,8},{1,21},{... | collective-permute-start | bytes 405512 | tf_op jit(solution)/shard_map/ppermute | solution.py:205
  60.9 7.1 %prompt_part.5 = (bf16[384,896]{1,0:T(8,128)(2,1)}, bf16[528,128]{1,0:T(8,128)(2,1)S(1)}, bf16[528,128]{1,0:T(8,128)(2,1)S(1)}, bf16[528,128]{1,0:T(8,128)(2,1)S(1)}) custom-call(s32[3]{0:T(128)S(1)} %pad_add_fusion.info_ref, bf16[8,2,2,32,128]{4,3,2,1,0:T(8,128)(2,1)S(1)} %collective-permute-done.7.refs_0_, ...), custom_call_target="tpu_custom_call" | custom-call | flops 2642411520 | bytes 5505024 | tf_op jit(solution)/shard_map/prompt_part/pallas_call | solution.py:162
  67.9 0.0 collective-permute-done.12.refs_3_
  67.9 0.0 collective-permute-done.13.refs_4_
  67.9 0.0 collective-permute-start.14
  68.0 1.6 %collective-permute-start.15 = (bf16[528,128]{1,0:T(8,128)(2,1)S(1)}, bf16[528,128]{1,0:T(8,128)(2,1)S(1)}, u32[]{:S(2)}, u32[]{:S(2)}) collective-permute-start(bf16[528,128]{1,0:T(8,128)(2,1)S(1)} %get-tuple-element.91), channel_id=1, source_target_pairs={{0,28},{4,24},{8,4},{12,0},{16,12},{20,8},{24,20},{28,16},{1,29},{... | collective-permute-start | bytes 405512 | tf_op jit(solution)/shard_map/ppermute | solution.py:205
  69.5 0.3 collective-permute-start.16
  69.8 0.0 collective-permute-done.14.refs_5_
  69.8 4.2 %collective-permute-done.15.refs_6_ = bf16[528,128]{1,0:T(8,128)(2,1)S(1)} collective-permute-done((bf16[528,128]{1,0:T(8,128)(2,1)S(1)}, bf16[528,128]{1,0:T(8,128)(2,1)S(1)}, u32[]{:S(2)}, u32[]{:S(2)}) %collective-permute-start.15) | collective-permute-done | bytes 135200 | tf_op jit(solution)/shard_map/ppermute | solution.py:205
  73.9 2.1 %collective-permute-done.16.refs_7_ = bf16[528,128]{1,0:T(8,128)(2,1)S(1)} collective-permute-done((bf16[528,128]{1,0:T(8,128)(2,1)S(1)}, bf16[528,128]{1,0:T(8,128)(2,1)S(1)}, u32[]{:S(2)}, u32[]{:S(2)}) %collective-permute-start.16) | collective-permute-done | bytes 135200 | tf_op jit(solution)/shard_map/ppermute | solution.py:205
  76.0 0.4 group_sum.1
  76.4 18.4 %all_to_all.14 = bf16[8,128,128]{2,1,0:T(8,128)(2,1)S(1)} all-to-all(bf16[8,128,128]{2,1,0:T(8,128)(2,1)S(1)} %bitcast.30), channel_id=1, replica_groups=mesh['z'=8,'y'=4,'c'=2,'head'=4] {'z'}, dimensions={0} | all-to-all | bytes 524288 | tf_op jit(solution)/shard_map/all_to_all | solution.py:201
  94.9 0.6 slice_bitcast_fusion
  (2 shorter events, 0.0 us)
Async XLA Ops:
  0.6 10.7 %copy-start.4 = (bf16[1,96,3584]{2,1,0:T(8,128)(2,1)S(1)}, bf16[1,96,3584]{2,1,0:T(8,128)(2,1)}, u32[]{:S(2)}) copy-start(bf16[1,96,3584]{2,1,0:T(8,128)(2,1)} %param.16) | copy-start | bytes 2064388
  0.6 27.3 %copy-start.5 = (f32[1,7,384]{2,0,1:T(1,128)S(1)}, f32[1,7,384]{2,0,1:T(1,128)}, u32[]{:S(2)}) copy-start(f32[1,7,384]{2,0,1:T(1,128)} %param.17) | copy-start | bytes 32260
  0.7 28.9 %copy-start = (bf16[1,384,896]{2,1,0:T(8,128)(2,1)S(1)}, bf16[1,384,896]{2,1,0:T(8,128)(2,1)}, u32[]{:S(2)}) copy-start(bf16[1,384,896]{2,1,0:T(8,128)(2,1)} %param.10) | copy-start | bytes 2064388
  0.7 28.9 %copy-start.1 = (bf16[1,384,896]{2,1,0:T(8,128)(2,1)S(1)}, bf16[1,384,896]{2,1,0:T(8,128)(2,1)}, u32[]{:S(2)}) copy-start(bf16[1,384,896]{2,1,0:T(8,128)(2,1)} %param.15) | copy-start | bytes 2064388
  0.7 28.9 %copy-start.2 = (bf16[1,384,128]{2,1,0:T(8,128)(2,1)S(1)}, bf16[1,384,128]{2,1,0:T(8,128)(2,1)}, u32[]{:S(2)}) copy-start(bf16[1,384,128]{2,1,0:T(8,128)(2,1)} %param.11) | copy-start | bytes 294916
  0.7 28.9 %copy-start.3 = (bf16[1,384,128]{2,1,0:T(8,128)(2,1)S(1)}, bf16[1,384,128]{2,1,0:T(8,128)(2,1)}, u32[]{:S(2)}) copy-start(bf16[1,384,128]{2,1,0:T(8,128)(2,1)} %param.12) | copy-start | bytes 294916
  2.3 22.9 %all-to-all-start = ((bf16[8,128,128]{2,1,0:T(8,128)(2,1)}), bf16[8,128,128]{2,1,0:T(8,128)(2,1)S(1)}, u32[]{:S(2)}, u32[]{:S(2)}) async-start(bf16[8,128,128]{2,1,0:T(8,128)(2,1)} %broadcast_in_dim.17), calls=%async_computation | async-start | bytes 524288 | tf_op jit(solution)/shard_map/all_to_all | solution.py:201
  11.4 5.3 %collective-permute-start = (bf16[96,896]{1,0:T(8,128)(2,1)S(1)}, bf16[96,896]{1,0:T(8,128)(2,1)S(1)}, u32[]{:S(2)}, u32[]{:S(2)}) collective-permute-start(bf16[96,896]{1,0:T(8,128)(2,1)S(1)} %get-tuple-element.94), channel_id=1, source_target_pairs={{0,1},{1,0},{2,3},{3,2},{4,5},{5,4},{6,7},{7,6},{8,9},{9,8},{10,11... | collective-permute-start | bytes 516104 | tf_op jit(solution)/shard_map/ppermute | solution.py:205
  12.7 9.6 %collective-permute-start.1 = (bf16[96,896]{1,0:T(8,128)(2,1)S(1)}, bf16[96,896]{1,0:T(8,128)(2,1)S(1)}, u32[]{:S(2)}, u32[]{:S(2)}) collective-permute-start(bf16[96,896]{1,0:T(8,128)(2,1)S(1)} %get-tuple-element.96), channel_id=1, source_target_pairs={{0,2},{1,3},{2,0},{3,1},{4,6},{5,7},{6,4},{7,5},{8,10},{9,11},{10,... | collective-permute-start | bytes 516104 | tf_op jit(solution)/shard_map/ppermute | solution.py:205
  15.2 10.0 %collective-permute-start.2 = (bf16[96,896]{1,0:T(8,128)(2,1)S(1)}, bf16[96,896]{1,0:T(8,128)(2,1)S(1)}, u32[]{:S(2)}, u32[]{:S(2)}) collective-permute-start(bf16[96,896]{1,0:T(8,128)(2,1)S(1)} %get-tuple-element.93), channel_id=1, source_target_pairs={{0,3},{1,2},{2,1},{3,0},{4,7},{5,6},{6,5},{7,4},{8,11},{9,10},{10,... | collective-permute-start | bytes 516104 | tf_op jit(solution)/shard_map/ppermute | solution.py:205
  25.2 9.3 %collective-permute-start.4 = (bf16[8,2,2,32,128]{4,3,2,1,0:T(8,128)(2,1)S(1)}, bf16[8,2,2,32,128]{4,3,2,1,0:T(8,128)(2,1)S(1)}, u32[]{:S(2)}, u32[]{:S(2)}) collective-permute-start(bf16[8,2,2,32,128]{4,3,2,1,0:T(8,128)(2,1)S(1)} %bitcast.31), channel_id=1, source_target_pairs={{0,8},{8,16},{16,24},{24,0},{1,9},{9,17},{17,25},{25,1},{2,10},{10... | collective-permute-start | bytes 786440 | tf_op jit(solution)/shard_map/ppermute | solution.py:205
  26.5 8.0 %collective-permute-start.5 = (bf16[8,2,2,32,128]{4,3,2,1,0:T(8,128)(2,1)S(1)}, bf16[8,2,2,32,128]{4,3,2,1,0:T(8,128)(2,1)S(1)}, u32[]{:S(2)}, u32[]{:S(2)}) collective-permute-start(bf16[8,2,2,32,128]{4,3,2,1,0:T(8,128)(2,1)S(1)} %bitcast.32), channel_id=1, source_target_pairs={{0,24},{8,0},{16,8},{24,16},{1,25},{9,1},{17,9},{25,17},{2,26},{10... | collective-permute-start | bytes 786440 | tf_op jit(solution)/shard_map/ppermute | solution.py:205
  27.9 12.9 %collective-permute-start.3 = (bf16[8,2,2,32,128]{4,3,2,1,0:T(8,128)(2,1)S(1)}, bf16[8,2,2,32,128]{4,3,2,1,0:T(8,128)(2,1)S(1)}, u32[]{:S(2)}, u32[]{:S(2)}) collective-permute-start(bf16[8,2,2,32,128]{4,3,2,1,0:T(8,128)(2,1)S(1)} %bitcast.33), channel_id=1, source_target_pairs={{0,16},{8,24},{16,0},{24,8},{1,17},{9,25},{17,1},{25,9},{2,18},{10... | collective-permute-start | bytes 786440 | tf_op jit(solution)/shard_map/ppermute | solution.py:205
  40.8 9.7 %collective-permute-start.6 = (bf16[8,2,2,32,128]{4,3,2,1,0:T(8,128)(2,1)S(1)}, bf16[8,2,2,32,128]{4,3,2,1,0:T(8,128)(2,1)S(1)}, u32[]{:S(2)}, u32[]{:S(2)}) collective-permute-start(bf16[8,2,2,32,128]{4,3,2,1,0:T(8,128)(2,1)S(1)} %collective-permute-done.3.refs_0_), channel_id=1, source_target_pairs={{0,4},{4,0},{1,5},{5,1},{2,6},{6,2},{3,7},{7,3},{8,12},{12,8},{9,1... | collective-permute-start | bytes 786440 | tf_op jit(solution)/shard_map/ppermute | solution.py:205
  43.8 12.3 %collective-permute-start.7 = (bf16[8,2,2,32,128]{4,3,2,1,0:T(8,128)(2,1)S(1)}, bf16[8,2,2,32,128]{4,3,2,1,0:T(8,128)(2,1)S(1)}, u32[]{:S(2)}, u32[]{:S(2)}) collective-permute-start(bf16[8,2,2,32,128]{4,3,2,1,0:T(8,128)(2,1)S(1)} %bitcast.35), channel_id=1, source_target_pairs={{0,4},{4,0},{1,5},{5,1},{2,6},{6,2},{3,7},{7,3},{8,12},{12,8},{9,1... | collective-permute-start | bytes 786440 | tf_op jit(solution)/shard_map/ppermute | solution.py:205
  43.9 12.2 %collective-permute-start.8 = (bf16[8,2,2,32,128]{4,3,2,1,0:T(8,128)(2,1)S(1)}, bf16[8,2,2,32,128]{4,3,2,1,0:T(8,128)(2,1)S(1)}, u32[]{:S(2)}, u32[]{:S(2)}) collective-permute-start(bf16[8,2,2,32,128]{4,3,2,1,0:T(8,128)(2,1)S(1)} %collective-permute-done.4.refs_1_), channel_id=1, source_target_pairs={{0,4},{4,0},{1,5},{5,1},{2,6},{6,2},{3,7},{7,3},{8,12},{12,8},{9,1... | collective-permute-start | bytes 786440 | tf_op jit(solution)/shard_map/ppermute | solution.py:205
  44.3 11.8 %collective-permute-start.9 = (bf16[8,2,2,32,128]{4,3,2,1,0:T(8,128)(2,1)S(1)}, bf16[8,2,2,32,128]{4,3,2,1,0:T(8,128)(2,1)S(1)}, u32[]{:S(2)}, u32[]{:S(2)}) collective-permute-start(bf16[8,2,2,32,128]{4,3,2,1,0:T(8,128)(2,1)S(1)} %collective-permute-done.5.refs_2_), channel_id=1, source_target_pairs={{0,4},{4,0},{1,5},{5,1},{2,6},{6,2},{3,7},{7,3},{8,12},{12,8},{9,1... | collective-permute-start | bytes 786440 | tf_op jit(solution)/shard_map/ppermute | solution.py:205
  44.4 10.7 %collective-permute-start.10 = (bf16[528,128]{1,0:T(8,128)(2,1)S(1)}, bf16[528,128]{1,0:T(8,128)(2,1)S(1)}, u32[]{:S(2)}, u32[]{:S(2)}) collective-permute-start(bf16[528,128]{1,0:T(8,128)(2,1)S(1)} %get-tuple-element.71), channel_id=1, source_target_pairs={{0,24},{4,28},{8,0},{12,4},{16,8},{20,12},{24,16},{28,20},{1,25},{... | collective-permute-start | bytes 405512 | tf_op jit(solution)/shard_map/ppermute | solution.py:205
  50.4 5.6 %collective-permute-start.11 = (bf16[528,128]{1,0:T(8,128)(2,1)S(1)}, bf16[528,128]{1,0:T(8,128)(2,1)S(1)}, u32[]{:S(2)}, u32[]{:S(2)}) collective-permute-start(bf16[528,128]{1,0:T(8,128)(2,1)S(1)} %get-tuple-element.72), channel_id=1, source_target_pairs={{0,8},{4,12},{8,16},{12,20},{16,24},{20,28},{24,0},{28,4},{1,9},{5... | collective-permute-start | bytes 405512 | tf_op jit(solution)/shard_map/ppermute | solution.py:205
  56.1 11.8 %collective-permute-start.12 = (bf16[528,128]{1,0:T(8,128)(2,1)S(1)}, bf16[528,128]{1,0:T(8,128)(2,1)S(1)}, u32[]{:S(2)}, u32[]{:S(2)}) collective-permute-start(bf16[528,128]{1,0:T(8,128)(2,1)S(1)} %get-tuple-element.86), channel_id=1, source_target_pairs={{0,16},{4,20},{8,24},{12,28},{16,0},{20,4},{24,8},{28,12},{1,17},{... | collective-permute-start | bytes 405512 | tf_op jit(solution)/shard_map/ppermute | solution.py:205
  57.0 10.9 %collective-permute-start.13 = (bf16[528,128]{1,0:T(8,128)(2,1)S(1)}, bf16[528,128]{1,0:T(8,128)(2,1)S(1)}, u32[]{:S(2)}, u32[]{:S(2)}) collective-permute-start(bf16[528,128]{1,0:T(8,128)(2,1)S(1)} %get-tuple-element.87), channel_id=1, source_target_pairs={{0,20},{4,16},{8,28},{12,24},{16,4},{20,0},{24,12},{28,8},{1,21},{... | collective-permute-start | bytes 405512 | tf_op jit(solution)/shard_map/ppermute | solution.py:205
  67.9 1.8 %collective-permute-start.14 = (bf16[528,128]{1,0:T(8,128)(2,1)S(1)}, bf16[528,128]{1,0:T(8,128)(2,1)S(1)}, u32[]{:S(2)}, u32[]{:S(2)}) collective-permute-start(bf16[528,128]{1,0:T(8,128)(2,1)S(1)} %get-tuple-element.90), channel_id=1, source_target_pairs={{0,4},{4,0},{8,12},{12,8},{16,20},{20,16},{24,28},{28,24},{1,5},{5... | collective-permute-start | bytes 405512 | tf_op jit(solution)/shard_map/ppermute | solution.py:205
  68.0 6.0 %collective-permute-start.15 = (bf16[528,128]{1,0:T(8,128)(2,1)S(1)}, bf16[528,128]{1,0:T(8,128)(2,1)S(1)}, u32[]{:S(2)}, u32[]{:S(2)}) collective-permute-start(bf16[528,128]{1,0:T(8,128)(2,1)S(1)} %get-tuple-element.91), channel_id=1, source_target_pairs={{0,28},{4,24},{8,4},{12,0},{16,12},{20,8},{24,20},{28,16},{1,29},{... | collective-permute-start | bytes 405512 | tf_op jit(solution)/shard_map/ppermute | solution.py:205
  69.5 6.5 %collective-permute-start.16 = (bf16[528,128]{1,0:T(8,128)(2,1)S(1)}, bf16[528,128]{1,0:T(8,128)(2,1)S(1)}, u32[]{:S(2)}, u32[]{:S(2)}) collective-permute-start(bf16[528,128]{1,0:T(8,128)(2,1)S(1)} %get-tuple-element.92), channel_id=1, source_target_pairs={{0,12},{4,8},{8,20},{12,16},{16,28},{20,24},{24,4},{28,0},{1,13},{... | collective-permute-start | bytes 405512 | tf_op jit(solution)/shard_map/ppermute | solution.py:205

commit v5 on v4

--- a/solution.py
+++ b/solution.py
@@ -227,7 +227,7 @@
         at = (place ^ i) * columns
         piece = lax.dynamic_slice_in_dim(grad_out[0], at, columns, axis=1)
         grads.append(trade(piece, "head", lambda j, i=i: j ^ i) if i else piece)
-    stacked, info, *grads = lax.optimization_barrier((stacked, info, *grads))
+    stacked, info = lax.optimization_barrier((stacked, info))
     stacked = stacked.reshape(stacks, prompt_count, 2, owned, width)
 
     moved = {

time: 95.8 us -> 88.7 us (0.926)
  the two profiles are of different devices: /device:TPU:1 before, /device:TPU:6 now
where the time goes in v5:
time: 88.7 us; the launch traced here: 87.5 us
  starting transfers between devices  28.9 us (33%)
  Pallas kernels  23.4 us (26%)
  blocking collectives  15.3 us (17%)
  waiting for transfers between devices  14.7 us (17%)
  local copies, waits for them, and re-layouts  2.2 us (2%)
  between operations  2.08 us (2%)
  other arithmetic  1.01 us (1%)
    ppermute x17, starting transfers between devices, trade(): lax.ppermute(block, axis, [(i, target(i)) for i in range(lax.axis_size(ax...  20.4 us
    pallas_call x3, Pallas kernels, prompt_part(): pl.pallas_call(functools.partial(prompt_kernel, blocks=blocks, count=len(...  18 us
    all_to_all x1, blocking collectives, exchange(): return lax.all_to_all(blocks, axes, split_axis=0, concat_axis=0, tiled=True)  15.3 us
    ppermute x17, waiting for transfers between devices, trade(): lax.ppermute(block, axis, [(i, target(i)) for i in range(lax.axis_size(ax...  9.71 us
    all_to_all x1, starting transfers between devices, exchange(): return lax.all_to_all(blocks, axes, split_axis=0, concat_axis=0, tiled=True)  8.47 us
    all_to_all x1, waiting for transfers between devices, exchange(): return lax.all_to_all(blocks, axes, split_axis=0, concat_axis=0, tiled=True)  4.98 us
    pallas_call x1, Pallas kernels, suffix_part(): pl.pallas_call(suffix_kernel, in_specs=[SMEM] + [VMEM] * (5 + len(grads))...  4.94 us
  transfers between devices with their start and end apart: 18, of which 5 were waited for; matrix products, arithmetic and copies ran while one was open for 1% of the time, Pallas kernels for 26%

profile of v5, /device:TPU:6, one launch (start us, length us, event | category | flops | bytes accessed | tf_op | source)
XLA Modules:
  0.0 87.5 jit_solution(1701584178709316570)
XLA Ops:
  0.6 0.0 copy-start.4
  0.6 0.0 copy-start.5
  0.7 0.0 copy-start
  0.7 0.0 copy-start.1
  0.7 0.0 copy-start.2
  0.7 0.0 copy-start.3
  0.7 0.9 %pad_maximum_fusion = bf16[2,2,32,128]{3,2,1,0:T(8,128)(2,1)S(1)} fusion(bf16[2,1,32,128]{3,2,1,0:T(8,128)(2,1)} %bitcast.43, bf16[2,1,32,128]{3,2,1,0:T(8,128)(2,1)} %bitcast.44), kind=kLoop, calls=%fused_computation.4 | loop fusion | flops 16384 | bytes 65536 | tf_op jit(solution)/shard_map/stack | solution.py:223
  1.6 0.7 broadcast_in_dim.17
  2.3 8.5 %all-to-all-start = ((bf16[8,128,128]{2,1,0:T(8,128)(2,1)}), bf16[8,128,128]{2,1,0:T(8,128)(2,1)S(1)}, u32[]{:S(2)}, u32[]{:S(2)}) async-start(bf16[8,128,128]{2,1,0:T(8,128)(2,1)} %broadcast_in_dim.17), calls=%async_computation | async-start | bytes 524288 | tf_op jit(solution)/shard_map/all_to_all | solution.py:201
  10.8 0.0 copy-done.4
  10.8 0.8 dynamic-slice_bitcast_fusion
  11.6 0.8 collective-permute-start.3
  12.4 1.1 %collective-permute-start.4 = (bf16[96,896]{1,0:T(8,128)(2,1)}, bf16[96,896]{1,0:T(8,128)(2,1)S(1)}, u32[]{:S(2)}, u32[]{:S(2)}) collective-permute-start(bf16[96,896]{1,0:T(8,128)(2,1)} %get-tuple-element.88), channel_id=1, source_target_pairs={{0,2},{1,3},{2,0},{3,1},{4,6},{5,7},{6,4},{7,5},{8,10},{9,11},{10,... | collective-permute-start | bytes 516104 | tf_op jit(solution)/shard_map/ppermute | solution.py:205
  13.6 2.8 %collective-permute-start.5 = (bf16[96,896]{1,0:T(8,128)(2,1)S(1)}, bf16[96,896]{1,0:T(8,128)(2,1)S(1)}, u32[]{:S(2)}, u32[]{:S(2)}) collective-permute-start(bf16[96,896]{1,0:T(8,128)(2,1)S(1)} %get-tuple-element.85), channel_id=1, source_target_pairs={{0,3},{1,2},{2,1},{3,0},{4,7},{5,6},{6,5},{7,4},{8,11},{9,10},{10,... | collective-permute-start | bytes 516104 | tf_op jit(solution)/shard_map/ppermute | solution.py:205
  17.6 0.1 pad_add_fusion.info_ref
  17.7 5.0 %all-to-all-done = bf16[8,128,128]{2,1,0:T(8,128)(2,1)S(1)} async-done(((bf16[8,128,128]{2,1,0:T(8,128)(2,1)}), bf16[8,128,128]{2,1,0:T(8,128)(2,1)S(1)}, u32[]{:S(2)}, u32[]{:S(2)}) %all-to-all-start) | async-done | bytes 262176 | tf_op jit(solution)/shard_map/all_to_all | solution.py:201
  22.7 1.6 %collective-permute-start.1 = (bf16[8,2,2,32,128]{4,3,2,1,0:T(8,128)(2,1)S(1)}, bf16[8,2,2,32,128]{4,3,2,1,0:T(8,128)(2,1)S(1)}, u32[]{:S(2)}, u32[]{:S(2)}) collective-permute-start(bf16[8,2,2,32,128]{4,3,2,1,0:T(8,128)(2,1)S(1)} %bitcast.31), channel_id=1, source_target_pairs={{0,8},{8,16},{16,24},{24,0},{1,9},{9,17},{17,25},{25,1},{2,10},{10... | collective-permute-start | bytes 786440 | tf_op jit(solution)/shard_map/ppermute | solution.py:205
  24.2 1.7 %collective-permute-start.2 = (bf16[8,2,2,32,128]{4,3,2,1,0:T(8,128)(2,1)S(1)}, bf16[8,2,2,32,128]{4,3,2,1,0:T(8,128)(2,1)S(1)}, u32[]{:S(2)}, u32[]{:S(2)}) collective-permute-start(bf16[8,2,2,32,128]{4,3,2,1,0:T(8,128)(2,1)S(1)} %bitcast.32), channel_id=1, source_target_pairs={{0,24},{8,0},{16,8},{24,16},{1,25},{9,1},{17,9},{25,17},{2,26},{10... | collective-permute-start | bytes 786440 | tf_op jit(solution)/shard_map/ppermute | solution.py:205
  25.9 0.0 copy-done.5
  25.9 0.0 collective-permute-done.3.refs_1_
  25.9 2.3 %collective-permute-start = (bf16[8,2,2,32,128]{4,3,2,1,0:T(8,128)(2,1)S(1)}, bf16[8,2,2,32,128]{4,3,2,1,0:T(8,128)(2,1)S(1)}, u32[]{:S(2)}, u32[]{:S(2)}) collective-permute-start(bf16[8,2,2,32,128]{4,3,2,1,0:T(8,128)(2,1)S(1)} %bitcast.33), channel_id=1, source_target_pairs={{0,16},{8,24},{16,0},{24,8},{1,17},{9,25},{17,1},{25,9},{2,18},{10... | collective-permute-start | bytes 786440 | tf_op jit(solution)/shard_map/ppermute | solution.py:205
  28.2 0.0 collective-permute-done.4.refs_2_
  28.2 0.0 collective-permute-done.5.refs_3_
  28.2 0.0 copy-done
  28.2 0.0 copy-done.1
  28.2 0.0 copy-done.2
  28.2 0.0 copy-done.3
  28.2 4.9 %suffix_part.1 = (bf16[2688,128]{1,0:T(8,128)(2,1)S(1)}, bf16[2688,128]{1,0:T(8,128)(2,1)S(1)}, bf16[128,2688]{1,0:T(8,128)(2,1)S(1)}, bf16[128,2688]{1,0:T(8,12...) custom-call(s32[3]{0:T(128)S(1)} %pad_add_fusion.info_ref, ...), custom_call_target="tpu_custom_call" | custom-call | flops 1321205760 | bytes 5505024 | tf_op jit(solution)/shard_map/suffix_part/pallas_call | solution.py:91
  33.1 0.0 collective-permute-done.1.refs_1_
  33.1 2.0 %collective-permute-done.2.refs_2_ = bf16[8,2,2,32,128]{4,3,2,1,0:T(8,128)(2,1)S(1)} collective-permute-done((bf16[8,2,2,32,128]{4,3,2,1,0:T(8,128)(2,1)S(1)}, bf16[8,2,2,32,128]{4,3,2,1,0:T(8,128)(2,1)S(1)}, u32[]{:S(2)}, u32[]{:S(2)}) %collective-permute-start.2) | collective-permute-done | bytes 262176 | tf_op jit(solution)/shard_map/ppermute | solution.py:205
  35.1 6.3 %prompt_part.3 = (f32[128,2688]{1,0:T(8,128)S(1)}, bf16[528,128]{1,0:T(8,128)(2,1)S(1)}, bf16[528,128]{1,0:T(8,128)(2,1)S(1)}, bf16[528,128]{1,0:T(8,128)(2,1)S(1)}) custom-call(s32[3]{0:T(128)S(1)} %pad_add_fusion.info_ref, bf16[8,2,2,32,128]{4,3,2,1,0:T(8,128)(2,1)S(1)} %bitcast.34, bf16[8,2,2,32,128]{4,3,2,1,0:T(8,128)(2,1)S(1)} %collective-permute-done.1.refs_1_, ...), custom_call_target="tpu_custom_call" | custom-call | flops 2642411520 | bytes 5505024 | tf_op jit(solution)/shard_map/prompt_part/pallas_call | solution.py:162
  41.4 0.0 collective-permute-done.refs_0_
  41.4 0.1 collective-permute-start.6
  41.5 0.5 collective-permute-start.7
  42.0 0.1 collective-permute-start.8
  42.1 0.4 collective-permute-start.9
  42.5 3.7 %collective-permute-start.10 = (bf16[528,128]{1,0:T(8,128)(2,1)S(1)}, bf16[528,128]{1,0:T(8,128)(2,1)S(1)}, u32[]{:S(2)}, u32[]{:S(2)}) collective-permute-start(bf16[528,128]{1,0:T(8,128)(2,1)S(1)} %get-tuple-element.63), channel_id=1, source_target_pairs={{0,24},{4,28},{8,0},{12,4},{16,8},{20,12},{24,16},{28,20},{1,25},{... | collective-permute-start | bytes 405512 | tf_op jit(solution)/shard_map/ppermute | solution.py:205
  46.2 0.0 collective-permute-done.6.refs_1_
  46.2 0.0 collective-permute-start.11
  46.2 4.7 %prompt_part.4 = (f32[128,2688]{1,0:T(8,128)S(1)}, bf16[528,128]{1,0:T(8,128)(2,1)S(1)}, bf16[528,128]{1,0:T(8,128)(2,1)S(1)}) custom-call(s32[3]{0:T(128)S(1)} %pad_add_fusion.info_ref, bf16[8,2,2,32,128]{4,3,2,1,0:T(8,128)(2,1)S(1)} %collective-permute-done.refs_0_, bf16[8,2,2,32,128]{4,3,2,1,0:T(8,128)(2,1)S(1)} %collective-permute-done.6.refs_1_, ...), custom_call_target="tpu_custom_call" | custom-call | flops 1761607680 | bytes 5505024 | tf_op jit(solution)/shard_map/prompt_part/pallas_call | solution.py:162
  50.9 0.0 collective-permute-done.10.refs_1_
  50.9 1.8 %collective-permute-done.11.refs_2_ = bf16[528,128]{1,0:T(8,128)(2,1)S(1)} collective-permute-done((bf16[528,128]{1,0:T(8,128)(2,1)S(1)}, bf16[528,128]{1,0:T(8,128)(2,1)S(1)}, u32[]{:S(2)}, u32[]{:S(2)}) %collective-permute-start.11) | collective-permute-done | bytes 135200 | tf_op jit(solution)/shard_map/ppermute | solution.py:205
  52.7 0.0 collective-permute-done.7.refs_0_
  52.7 0.0 collective-permute-done.8.refs_1_
  52.7 0.0 collective-permute-done.9.refs_2_
  52.7 0.3 collective-permute-start.12
  53.0 1.6 %collective-permute-start.13 = (bf16[528,128]{1,0:T(8,128)(2,1)S(1)}, bf16[528,128]{1,0:T(8,128)(2,1)S(1)}, u32[]{:S(2)}, u32[]{:S(2)}) collective-permute-start(bf16[528,128]{1,0:T(8,128)(2,1)S(1)} %get-tuple-element.79), channel_id=1, source_target_pairs={{0,20},{4,16},{8,28},{12,24},{16,4},{20,0},{24,12},{28,8},{1,21},{... | collective-permute-start | bytes 405512 | tf_op jit(solution)/shard_map/ppermute | solution.py:205
  54.6 7.1 %prompt_part.5 = (bf16[384,896]{1,0:T(8,128)(2,1)}, bf16[528,128]{1,0:T(8,128)(2,1)S(1)}, bf16[528,128]{1,0:T(8,128)(2,1)S(1)}, bf16[528,128]{1,0:T(8,128)(2,1)S(1)}) custom-call(s32[3]{0:T(128)S(1)} %pad_add_fusion.info_ref, bf16[8,2,2,32,128]{4,3,2,1,0:T(8,128)(2,1)S(1)} %collective-permute-done.7.refs_0_, ...), custom_call_target="tpu_custom_call" | custom-call | flops 2642411520 | bytes 5505024 | tf_op jit(solution)/shard_map/prompt_part/pallas_call | solution.py:162
  61.6 0.0 collective-permute-done.12.refs_3_
  61.6 0.0 collective-permute-done.13.refs_4_
  61.6 1.8 %collective-permute-start.14 = (bf16[528,128]{1,0:T(8,128)(2,1)S(1)}, bf16[528,128]{1,0:T(8,128)(2,1)S(1)}, u32[]{:S(2)}, u32[]{:S(2)}) collective-permute-start(bf16[528,128]{1,0:T(8,128)(2,1)S(1)} %get-tuple-element.82), channel_id=1, source_target_pairs={{0,4},{4,0},{8,12},{12,8},{16,20},{20,16},{24,28},{28,24},{1,5},{5... | collective-permute-start | bytes 405512 | tf_op jit(solution)/shard_map/ppermute | solution.py:205
  63.5 1.1 %collective-permute-start.15 = (bf16[528,128]{1,0:T(8,128)(2,1)S(1)}, bf16[528,128]{1,0:T(8,128)(2,1)S(1)}, u32[]{:S(2)}, u32[]{:S(2)}) collective-permute-start(bf16[528,128]{1,0:T(8,128)(2,1)S(1)} %get-tuple-element.83), channel_id=1, source_target_pairs={{0,28},{4,24},{8,4},{12,0},{16,12},{20,8},{24,20},{28,16},{1,29},{... | collective-permute-start | bytes 405512 | tf_op jit(solution)/shard_map/ppermute | solution.py:205
  64.6 0.6 collective-permute-start.16
  65.2 0.0 collective-permute-done.14.refs_5_
  65.2 3.9 %collective-permute-done.15.refs_6_ = bf16[528,128]{1,0:T(8,128)(2,1)S(1)} collective-permute-done((bf16[528,128]{1,0:T(8,128)(2,1)S(1)}, bf16[528,128]{1,0:T(8,128)(2,1)S(1)}, u32[]{:S(2)}, u32[]{:S(2)}) %collective-permute-start.15) | collective-permute-done | bytes 135200 | tf_op jit(solution)/shard_map/ppermute | solution.py:205
  69.1 2.1 %collective-permute-done.16.refs_7_ = bf16[528,128]{1,0:T(8,128)(2,1)S(1)} collective-permute-done((bf16[528,128]{1,0:T(8,128)(2,1)S(1)}, bf16[528,128]{1,0:T(8,128)(2,1)S(1)}, u32[]{:S(2)}, u32[]{:S(2)}) %collective-permute-start.16) | collective-permute-done | bytes 135200 | tf_op jit(solution)/shard_map/ppermute | solution.py:205
  71.2 0.4 group_sum.1
  71.6 15.3 %all_to_all.14 = bf16[8,128,128]{2,1,0:T(8,128)(2,1)S(1)} all-to-all(bf16[8,128,128]{2,1,0:T(8,128)(2,1)S(1)} %bitcast.30), channel_id=1, replica_groups=mesh['z'=8,'y'=4,'c'=2,'head'=4] {'z'}, dimensions={0} | all-to-all | bytes 524288 | tf_op jit(solution)/shard_map/all_to_all | solution.py:201
  86.9 0.6 slice_bitcast_fusion
  (2 shorter events, 0.0 us)
Async XLA Ops:
  0.6 10.2 %copy-start.4 = (bf16[1,96,3584]{2,1,0:T(8,128)(2,1)S(1)}, bf16[1,96,3584]{2,1,0:T(8,128)(2,1)}, u32[]{:S(2)}) copy-start(bf16[1,96,3584]{2,1,0:T(8,128)(2,1)} %param.16) | copy-start | bytes 2064388
  0.6 25.3 %copy-start.5 = (f32[1,7,384]{2,0,1:T(1,128)S(1)}, f32[1,7,384]{2,0,1:T(1,128)}, u32[]{:S(2)}) copy-start(f32[1,7,384]{2,0,1:T(1,128)} %param.17) | copy-start | bytes 32260
  0.7 27.5 %copy-start = (bf16[1,384,896]{2,1,0:T(8,128)(2,1)S(1)}, bf16[1,384,896]{2,1,0:T(8,128)(2,1)}, u32[]{:S(2)}) copy-start(bf16[1,384,896]{2,1,0:T(8,128)(2,1)} %param.10) | copy-start | bytes 2064388
  0.7 27.5 %copy-start.1 = (bf16[1,384,896]{2,1,0:T(8,128)(2,1)S(1)}, bf16[1,384,896]{2,1,0:T(8,128)(2,1)}, u32[]{:S(2)}) copy-start(bf16[1,384,896]{2,1,0:T(8,128)(2,1)} %param.15) | copy-start | bytes 2064388
  0.7 27.5 %copy-start.2 = (bf16[1,384,128]{2,1,0:T(8,128)(2,1)S(1)}, bf16[1,384,128]{2,1,0:T(8,128)(2,1)}, u32[]{:S(2)}) copy-start(bf16[1,384,128]{2,1,0:T(8,128)(2,1)} %param.11) | copy-start | bytes 294916
  0.7 27.5 %copy-start.3 = (bf16[1,384,128]{2,1,0:T(8,128)(2,1)S(1)}, bf16[1,384,128]{2,1,0:T(8,128)(2,1)}, u32[]{:S(2)}) copy-start(bf16[1,384,128]{2,1,0:T(8,128)(2,1)} %param.12) | copy-start | bytes 294916
  2.3 20.3 %all-to-all-start = ((bf16[8,128,128]{2,1,0:T(8,128)(2,1)}), bf16[8,128,128]{2,1,0:T(8,128)(2,1)S(1)}, u32[]{:S(2)}, u32[]{:S(2)}) async-start(bf16[8,128,128]{2,1,0:T(8,128)(2,1)} %broadcast_in_dim.17), calls=%async_computation | async-start | bytes 524288 | tf_op jit(solution)/shard_map/all_to_all | solution.py:201
  11.6 14.3 %collective-permute-start.3 = (bf16[96,896]{1,0:T(8,128)(2,1)}, bf16[96,896]{1,0:T(8,128)(2,1)S(1)}, u32[]{:S(2)}, u32[]{:S(2)}) collective-permute-start(bf16[96,896]{1,0:T(8,128)(2,1)} %get-tuple-element.86), channel_id=1, source_target_pairs={{0,1},{1,0},{2,3},{3,2},{4,5},{5,4},{6,7},{7,6},{8,9},{9,8},{10,11... | collective-permute-start | bytes 516104 | tf_op jit(solution)/shard_map/ppermute | solution.py:205
  12.4 15.7 %collective-permute-start.4 = (bf16[96,896]{1,0:T(8,128)(2,1)}, bf16[96,896]{1,0:T(8,128)(2,1)S(1)}, u32[]{:S(2)}, u32[]{:S(2)}) collective-permute-start(bf16[96,896]{1,0:T(8,128)(2,1)} %get-tuple-element.88), channel_id=1, source_target_pairs={{0,2},{1,3},{2,0},{3,1},{4,6},{5,7},{6,4},{7,5},{8,10},{9,11},{10,... | collective-permute-start | bytes 516104 | tf_op jit(solution)/shard_map/ppermute | solution.py:205
  13.6 14.6 %collective-permute-start.5 = (bf16[96,896]{1,0:T(8,128)(2,1)S(1)}, bf16[96,896]{1,0:T(8,128)(2,1)S(1)}, u32[]{:S(2)}, u32[]{:S(2)}) collective-permute-start(bf16[96,896]{1,0:T(8,128)(2,1)S(1)} %get-tuple-element.85), channel_id=1, source_target_pairs={{0,3},{1,2},{2,1},{3,0},{4,7},{5,6},{6,5},{7,4},{8,11},{9,10},{10,... | collective-permute-start | bytes 516104 | tf_op jit(solution)/shard_map/ppermute | solution.py:205
  22.7 10.5 %collective-permute-start.1 = (bf16[8,2,2,32,128]{4,3,2,1,0:T(8,128)(2,1)S(1)}, bf16[8,2,2,32,128]{4,3,2,1,0:T(8,128)(2,1)S(1)}, u32[]{:S(2)}, u32[]{:S(2)}) collective-permute-start(bf16[8,2,2,32,128]{4,3,2,1,0:T(8,128)(2,1)S(1)} %bitcast.31), channel_id=1, source_target_pairs={{0,8},{8,16},{16,24},{24,0},{1,9},{9,17},{17,25},{25,1},{2,10},{10... | collective-permute-start | bytes 786440 | tf_op jit(solution)/shard_map/ppermute | solution.py:205
  24.2 10.9 %collective-permute-start.2 = (bf16[8,2,2,32,128]{4,3,2,1,0:T(8,128)(2,1)S(1)}, bf16[8,2,2,32,128]{4,3,2,1,0:T(8,128)(2,1)S(1)}, u32[]{:S(2)}, u32[]{:S(2)}) collective-permute-start(bf16[8,2,2,32,128]{4,3,2,1,0:T(8,128)(2,1)S(1)} %bitcast.32), channel_id=1, source_target_pairs={{0,24},{8,0},{16,8},{24,16},{1,25},{9,1},{17,9},{25,17},{2,26},{10... | collective-permute-start | bytes 786440 | tf_op jit(solution)/shard_map/ppermute | solution.py:205
  25.9 15.5 %collective-permute-start = (bf16[8,2,2,32,128]{4,3,2,1,0:T(8,128)(2,1)S(1)}, bf16[8,2,2,32,128]{4,3,2,1,0:T(8,128)(2,1)S(1)}, u32[]{:S(2)}, u32[]{:S(2)}) collective-permute-start(bf16[8,2,2,32,128]{4,3,2,1,0:T(8,128)(2,1)S(1)} %bitcast.33), channel_id=1, source_target_pairs={{0,16},{8,24},{16,0},{24,8},{1,17},{9,25},{17,1},{25,9},{2,18},{10... | collective-permute-start | bytes 786440 | tf_op jit(solution)/shard_map/ppermute | solution.py:205
  41.4 4.8 %collective-permute-start.6 = (bf16[8,2,2,32,128]{4,3,2,1,0:T(8,128)(2,1)S(1)}, bf16[8,2,2,32,128]{4,3,2,1,0:T(8,128)(2,1)S(1)}, u32[]{:S(2)}, u32[]{:S(2)}) collective-permute-start(bf16[8,2,2,32,128]{4,3,2,1,0:T(8,128)(2,1)S(1)} %collective-permute-done.refs_0_), channel_id=1, source_target_pairs={{0,4},{4,0},{1,5},{5,1},{2,6},{6,2},{3,7},{7,3},{8,12},{12,8},{9,1... | collective-permute-start | bytes 786440 | tf_op jit(solution)/shard_map/ppermute | solution.py:205
  41.5 11.2 %collective-permute-start.7 = (bf16[8,2,2,32,128]{4,3,2,1,0:T(8,128)(2,1)S(1)}, bf16[8,2,2,32,128]{4,3,2,1,0:T(8,128)(2,1)S(1)}, u32[]{:S(2)}, u32[]{:S(2)}) collective-permute-start(bf16[8,2,2,32,128]{4,3,2,1,0:T(8,128)(2,1)S(1)} %bitcast.35), channel_id=1, source_target_pairs={{0,4},{4,0},{1,5},{5,1},{2,6},{6,2},{3,7},{7,3},{8,12},{12,8},{9,1... | collective-permute-start | bytes 786440 | tf_op jit(solution)/shard_map/ppermute | solution.py:205
  42.0 10.7 %collective-permute-start.8 = (bf16[8,2,2,32,128]{4,3,2,1,0:T(8,128)(2,1)S(1)}, bf16[8,2,2,32,128]{4,3,2,1,0:T(8,128)(2,1)S(1)}, u32[]{:S(2)}, u32[]{:S(2)}) collective-permute-start(bf16[8,2,2,32,128]{4,3,2,1,0:T(8,128)(2,1)S(1)} %collective-permute-done.1.refs_1_), channel_id=1, source_target_pairs={{0,4},{4,0},{1,5},{5,1},{2,6},{6,2},{3,7},{7,3},{8,12},{12,8},{9,1... | collective-permute-start | bytes 786440 | tf_op jit(solution)/shard_map/ppermute | solution.py:205
  42.1 10.6 %collective-permute-start.9 = (bf16[8,2,2,32,128]{4,3,2,1,0:T(8,128)(2,1)S(1)}, bf16[8,2,2,32,128]{4,3,2,1,0:T(8,128)(2,1)S(1)}, u32[]{:S(2)}, u32[]{:S(2)}) collective-permute-start(bf16[8,2,2,32,128]{4,3,2,1,0:T(8,128)(2,1)S(1)} %collective-permute-done.2.refs_2_), channel_id=1, source_target_pairs={{0,4},{4,0},{1,5},{5,1},{2,6},{6,2},{3,7},{7,3},{8,12},{12,8},{9,1... | collective-permute-start | bytes 786440 | tf_op jit(solution)/shard_map/ppermute | solution.py:205
  42.5 8.4 %collective-permute-start.10 = (bf16[528,128]{1,0:T(8,128)(2,1)S(1)}, bf16[528,128]{1,0:T(8,128)(2,1)S(1)}, u32[]{:S(2)}, u32[]{:S(2)}) collective-permute-start(bf16[528,128]{1,0:T(8,128)(2,1)S(1)} %get-tuple-element.63), channel_id=1, source_target_pairs={{0,24},{4,28},{8,0},{12,4},{16,8},{20,12},{24,16},{28,20},{1,25},{... | collective-permute-start | bytes 405512 | tf_op jit(solution)/shard_map/ppermute | solution.py:205
  46.2 6.5 %collective-permute-start.11 = (bf16[528,128]{1,0:T(8,128)(2,1)S(1)}, bf16[528,128]{1,0:T(8,128)(2,1)S(1)}, u32[]{:S(2)}, u32[]{:S(2)}) collective-permute-start(bf16[528,128]{1,0:T(8,128)(2,1)S(1)} %get-tuple-element.64), channel_id=1, source_target_pairs={{0,8},{4,12},{8,16},{12,20},{16,24},{20,28},{24,0},{28,4},{1,9},{5... | collective-permute-start | bytes 405512 | tf_op jit(solution)/shard_map/ppermute | solution.py:205
  52.7 8.9 %collective-permute-start.12 = (bf16[528,128]{1,0:T(8,128)(2,1)S(1)}, bf16[528,128]{1,0:T(8,128)(2,1)S(1)}, u32[]{:S(2)}, u32[]{:S(2)}) collective-permute-start(bf16[528,128]{1,0:T(8,128)(2,1)S(1)} %get-tuple-element.78), channel_id=1, source_target_pairs={{0,16},{4,20},{8,24},{12,28},{16,0},{20,4},{24,8},{28,12},{1,17},{... | collective-permute-start | bytes 405512 | tf_op jit(solution)/shard_map/ppermute | solution.py:205
  53.0 8.7 %collective-permute-start.13 = (bf16[528,128]{1,0:T(8,128)(2,1)S(1)}, bf16[528,128]{1,0:T(8,128)(2,1)S(1)}, u32[]{:S(2)}, u32[]{:S(2)}) collective-permute-start(bf16[528,128]{1,0:T(8,128)(2,1)S(1)} %get-tuple-element.79), channel_id=1, source_target_pairs={{0,20},{4,16},{8,28},{12,24},{16,4},{20,0},{24,12},{28,8},{1,21},{... | collective-permute-start | bytes 405512 | tf_op jit(solution)/shard_map/ppermute | solution.py:205
  61.6 3.6 %collective-permute-start.14 = (bf16[528,128]{1,0:T(8,128)(2,1)S(1)}, bf16[528,128]{1,0:T(8,128)(2,1)S(1)}, u32[]{:S(2)}, u32[]{:S(2)}) collective-permute-start(bf16[528,128]{1,0:T(8,128)(2,1)S(1)} %get-tuple-element.82), channel_id=1, source_target_pairs={{0,4},{4,0},{8,12},{12,8},{16,20},{20,16},{24,28},{28,24},{1,5},{5... | collective-permute-start | bytes 405512 | tf_op jit(solution)/shard_map/ppermute | solution.py:205
  63.5 5.6 %collective-permute-start.15 = (bf16[528,128]{1,0:T(8,128)(2,1)S(1)}, bf16[528,128]{1,0:T(8,128)(2,1)S(1)}, u32[]{:S(2)}, u32[]{:S(2)}) collective-permute-start(bf16[528,128]{1,0:T(8,128)(2,1)S(1)} %get-tuple-element.83), channel_id=1, source_target_pairs={{0,28},{4,24},{8,4},{12,0},{16,12},{20,8},{24,20},{28,16},{1,29},{... | collective-permute-start | bytes 405512 | tf_op jit(solution)/shard_map/ppermute | solution.py:205
  64.6 6.5 %collective-permute-start.16 = (bf16[528,128]{1,0:T(8,128)(2,1)S(1)}, bf16[528,128]{1,0:T(8,128)(2,1)S(1)}, u32[]{:S(2)}, u32[]{:S(2)}) collective-permute-start(bf16[528,128]{1,0:T(8,128)(2,1)S(1)} %get-tuple-element.84), channel_id=1, source_target_pairs={{0,12},{4,8},{8,20},{12,16},{16,28},{20,24},{24,4},{28,0},{1,13},{... | collective-permute-start | bytes 405512 | tf_op jit(solution)/shard_map/ppermute | solution.py:205

commit v6 on v5

v6 whole, which is shorter than its diff:
```python
import functools

import jax
import jax.numpy as jnp
from jax import lax
from jax.experimental import pallas as pl
from jax.experimental.pallas import tpu as pltpu
from jax.sharding import Mesh
from jax.sharding import PartitionSpec as P

BF16 = jnp.bfloat16
F32 = jnp.float32
GROUP = ("y", "c")
LOG2E = 1.4426950408889634
VMEM = pl.BlockSpec(memory_space=pltpu.VMEM)
SMEM = pl.BlockSpec(memory_space=pltpu.SMEM)
PARAMS = pltpu.CompilerParams(vmem_limit_bytes=28 * 1024 * 1024)
MARK = 16


def cost(row_count, key_count, width):
    pairs = row_count * key_count
    return pl.CostEstimate(
        flops=10 * pairs * width, bytes_accessed=16 * row_count * width, transcendentals=pairs
    )


def score_blocks(key_rows, value_rows, query_t, grad_t, norm_row, delta_row, visible=None):
    scale = key_rows.shape[1] ** (-0.5)
    scores_t = jnp.dot(key_rows, query_t, preferred_element_type=F32)
    weights_t = jnp.exp2(scores_t * (scale * LOG2E) - norm_row)
    if visible is not None:
        weights_t = jnp.where(visible, weights_t, jnp.zeros_like(weights_t))
    weight_grad_t = jnp.dot(value_rows, grad_t, preferred_element_type=F32)
    score_grad_t = (weights_t * (weight_grad_t - delta_row) * scale).astype(BF16)
    return weights_t.astype(BF16), score_grad_t


def prepare_kernel(info_ref, query_ref, out_ref, norm_ref, *refs):
    grad_refs, refs = refs[:-5], refs[-5:]
    grad_rows_ref, query_t_ref, grad_t_ref, norm_row_ref, delta_row_ref = refs
    group_size, seq_len = norm_ref.shape
    width = query_ref.shape[1] // group_size
    part = grad_refs[0].shape[0]
    at = lax.broadcasted_iota(jnp.int32, grad_refs[0].shape, 0)
    for i, piece in enumerate(grad_refs):
        start = pl.multiple_of((info_ref[1] ^ i) * part, part)
        rows = piece[...]
        rows = jnp.where(at + start < info_ref[2], rows, jnp.zeros_like(rows))
        grad_rows_ref[pl.ds(start, part), :] = rows
    for head in range(group_size):
        cols = slice(head * width, (head + 1) * width)
        rows = slice(head * seq_len, (head + 1) * seq_len)
        grad_t = grad_rows_ref[:, cols].T
        out_t = out_ref[:, cols].T
        query_t_ref[:, rows] = query_ref[:, cols].T
        grad_t_ref[:, rows] = grad_t
        norm_row_ref[:, rows] = norm_ref[head : head + 1, :] * LOG2E
        delta_row_ref[:, rows] = jnp.sum(
            grad_t.astype(F32) * out_t.astype(F32), axis=0, keepdims=True
        )


def prepare(info, query, attn_out, log_norm, grads):
    group_size, seq_len = log_norm.shape
    width = query.shape[1] // group_size
    row_count = group_size * seq_len
    shape = jax.ShapeDtypeStruct
    return pl.pallas_call(
        prepare_kernel,
        in_specs=[SMEM] + [VMEM] * (3 + len(grads)),
        out_specs=[VMEM] * 5,
        out_shape=[
            shape(query.shape, BF16),
            shape((width, row_count), BF16),
            shape((width, row_count), BF16),
            shape((1, row_count), F32),
            shape((1, row_count), F32),
        ],
        compiler_params=PARAMS,
        cost_estimate=pl.CostEstimate(
            flops=2 * row_count * width, bytes_accessed=12 * row_count * width, transcendentals=0
        ),
        name="prepare",
    )(info, query, attn_out, log_norm, *grads)


def attend_head(head, row_refs, key_rows, value_rows, key_t, visible=None):
    query_ref, grad_rows_ref, query_t_ref, grad_t_ref, norm_row_ref, delta_row_ref = row_refs
    width = key_rows.shape[1]
    seq_len = query_ref.shape[0]
    cols = slice(head * width, (head + 1) * width)
    rows = slice(head * seq_len, (head + 1) * seq_len)
    weights_t, score_grad_t = score_blocks(
        key_rows, value_rows, query_t_ref[:, rows], grad_t_ref[:, rows],
        norm_row_ref[:, rows], delta_row_ref[:, rows], visible,
    )
    query_part = jnp.dot(key_t, score_grad_t, preferred_element_type=F32)
    key_part = jnp.dot(score_grad_t, query_ref[:, cols], preferred_element_type=F32)
    value_part = jnp.dot(weights_t, grad_rows_ref[:, cols], preferred_element_type=F32)
    return rows, cols, query_part, key_part, value_part


def suffix_kernel(*refs):
    row_refs, refs = refs[:6], refs[6:]
    query_acc_ref, key_ref, value_ref, query_grad_ref, key_grad_ref, value_grad_ref = refs
    seq_len, width = key_ref.shape
    key_at = lax.broadcasted_iota(jnp.int32, (seq_len, seq_len), 0)
    query_at = lax.broadcasted_iota(jnp.int32, (seq_len, seq_len), 1)
    causal = key_at <= query_at
    key_rows, value_rows = key_ref[...], value_ref[...]
    key_t = key_rows.T
    key_acc = jnp.zeros((seq_len, width), F32)
    value_acc = jnp.zeros((seq_len, width), F32)
    for head in range(query_grad_ref.shape[1] // width):
        rows, cols, query_part, key_part, value_part = attend_head(
            head, row_refs, key_rows, value_rows, key_t, causal
        )
        query_grad_ref[:, cols] = (query_part + query_acc_ref[:, rows]).T.astype(BF16)
        key_acc += key_part
        value_acc += value_part
    key_grad_ref[...] = key_acc.astype(BF16)
    value_grad_ref[...] = value_acc.astype(BF16)


def suffix_part(rows, query_acc, key_suffix, value_suffix):
    seq_len, width = key_suffix.shape
    suffix = jax.ShapeDtypeStruct(key_suffix.shape, BF16)
    return pl.pallas_call(
        suffix_kernel,
        in_specs=[VMEM] * (len(rows) + 3),
        out_specs=[VMEM] * 3,
        out_shape=[jax.ShapeDtypeStruct(rows[0].shape, BF16), suffix, suffix],
        compiler_params=PARAMS,
        cost_estimate=cost(query_acc.shape[1], seq_len, width),
        name="suffix_part",
    )(*rows, query_acc, key_suffix, value_suffix)


def prompt_kernel(info_ref, *refs, count, first):
    pair_refs, row_refs, refs = refs[:count], refs[count : count + 6], refs[count + 6 :]
    query_acc_ref = None if first else refs[0]
    query_out_ref, *pair_grad_refs = refs if first else refs[1:]
    chosen = info_ref[0]
    width = query_out_ref.shape[0]

    def rows_of(which):
        parts = [ref[:, chosen, which] for ref in pair_refs]
        return jnp.concatenate([part.reshape(-1, width) for part in parts], 0)

    key_rows, value_rows = rows_of(0), rows_of(1)
    key_t = key_rows.T
    key_acc = jnp.zeros(key_rows.shape, F32)
    value_acc = jnp.zeros(key_rows.shape, F32)
    for head in range(row_refs[0].shape[1] // width):
        rows, _, query_part, key_part, value_part = attend_head(
            head, row_refs, key_rows, value_rows, key_t
        )
        query_out_ref[:, rows] = query_part if first else query_part + query_acc_ref[:, rows]
        key_acc += key_part
        value_acc += value_part
    size = key_rows.shape[0] // count
    key_grad, value_grad = key_acc.astype(BF16), value_acc.astype(BF16)
    mark = jnp.full((MARK, width), chosen.astype(F32), F32).astype(BF16)
    for i, ref in enumerate(pair_grad_refs):
        ref[:size] = key_grad[i * size : (i + 1) * size]
        ref[size : 2 * size] = value_grad[i * size : (i + 1) * size]
        ref[2 * size :] = mark


def prompt_part(info, pairs, rows, query_acc=None):
    width, row_count = rows[2].shape
    stacks, _, _, owned, _ = pairs[0].shape
    size = stacks * owned
    out = jax.ShapeDtypeStruct((width, row_count), F32)
    pair_out = jax.ShapeDtypeStruct((2 * size + MARK, width), BF16)
    more = [] if query_acc is None else [query_acc]
    return pl.pallas_call(
        functools.partial(prompt_kernel, count=len(pairs), first=query_acc is None),
        in_specs=[SMEM] + [VMEM] * (len(pairs) + len(rows) + len(more)),
        out_specs=[VMEM] * (1 + len(pairs)),
        out_shape=[out] + [pair_out] * len(pairs),
        compiler_params=PARAMS,
        cost_estimate=cost(row_count, len(pairs) * size, width),
        name="prompt_part",
    )(info, *pairs, *rows, *more)


def group_kernel(*refs):
    share_refs, total_ref = refs[:-1], refs[-1]
    stacks, prompt_count, _, owned, width = total_ref.shape
    size = stacks * owned
    for which in range(2):
        rows = slice(which * size, (which + 1) * size)
        totals = [jnp.zeros((size, width), F32)] * prompt_count
        for ref in share_refs:
            share = ref[rows].astype(F32)
            mark = ref[2 * size :].astype(F32)[:1]
            for i in range(prompt_count):
                totals[i] += jnp.where(mark == float(i), share, 0.0)
        for i in range(prompt_count):
            total_ref[:, i, which] = totals[i].astype(BF16).reshape(stacks, owned, width)


def group_sum(shares, shape):
    return pl.pallas_call(
        group_kernel,
        in_specs=[VMEM] * len(shares),
        out_specs=VMEM,
        out_shape=jax.ShapeDtypeStruct(shape, BF16),
        compiler_params=PARAMS,
        name="group_sum",
    )(*shares)


def exchange(blocks, axes):
    return lax.all_to_all(blocks, axes, split_axis=0, concat_axis=0, tiled=True)


def trade(block, axis, target):
    return lax.ppermute(block, axis, [(i, target(i)) for i in range(lax.axis_size(axis))])


def copies(block, count):
    return jnp.broadcast_to(block[None], (count,) + block.shape)


def per_device(
    query, key_suffix, value_suffix, key_prompt, value_prompt, attn_out, grad_out, log_norm,
    prompt_id, lengths,
):
    columns = query.shape[2]
    width = key_suffix.shape[2]
    prompt_count, owned = key_prompt.shape[:2]
    heads, stacks, lines = lax.axis_size("head"), lax.axis_size("z"), lax.axis_size("y")
    place = lax.axis_index("head")
    info = jnp.stack([prompt_id[0], place, lengths[0]]).astype(jnp.int32)

    own_pair = jnp.stack([key_prompt, value_prompt], 1).reshape(-1, width)
    stacked = exchange(copies(own_pair, stacks).reshape(-1, width), "z")
    grads = []
    for i in range(heads):
        at = (place ^ i) * columns
        piece = lax.dynamic_slice_in_dim(grad_out[0], at, columns, axis=1)
        grads.append(trade(piece, "head", lambda j, i=i: j ^ i) if i else piece)
    stacked, info = lax.optimization_barrier((stacked, info))
    stacked = stacked.reshape(stacks, prompt_count, 2, owned, width)

    moved = {
        steps: trade(stacked, "y", lambda j, steps=steps: (j + steps) % lines)
        for steps in (1, lines - 1, 2)
    }
    stacked, grads = lax.optimization_barrier((stacked, grads))
    other = trade(stacked, "c", lambda j: j ^ 1)
    rows = [query[0], *prepare(info, query[0], attn_out[0], log_norm[0], grads)]
    beside, rows[-1] = lax.optimization_barrier(([moved[1], moved[lines - 1]], rows[-1]))
    beside_other = [trade(block, "c", lambda j: j ^ 1) for block in beside]

    shares = []

    def send(parts, places):
        for part, (steps, across) in zip(parts, places, strict=True):
            if not steps and not across:
                shares.append(part)
                continue
            target = lambda j, s=steps, o=across: 2 * ((j // 2 - s) % lines) + (j % 2 ^ o)
            shares.append(trade(part, GROUP, target))

    query_acc, *parts = prompt_part(info, [stacked, *beside, other], rows)
    far, query_acc = lax.optimization_barrier((moved[2], query_acc))
    far_other = trade(far, "c", lambda j: j ^ 1)
    send(parts, [(0, 0), (1, 0), (lines - 1, 0), (0, 1)])
    query_acc, *parts = prompt_part(info, [*beside_other, far, far_other], rows, query_acc)
    parts, shares = lax.optimization_barrier((parts, shares))
    send(parts, [(1, 1), (lines - 1, 1), (2, 0), (2, 1)])

    query_grad, key_grad, value_grad = suffix_part(rows, query_acc, key_suffix[0], value_suffix[0])
    key_grad, shares = lax.optimization_barrier((key_grad, shares))

    totals = group_sum(shares, (stacks, prompt_count, 2, owned, width))
    final = exchange(totals.reshape(-1, prompt_count * 2 * owned, width), "z")
    final = jnp.sum(final.astype(F32), 0).astype(BF16)
    final = final.reshape(prompt_count, 2, owned, width)
    return (query_grad[None], key_grad[None], value_grad[None], final[:, 0], final[:, 1])


def solution(mesh):
    roll, head = mesh.devices.shape
    fine = Mesh(mesh.devices.reshape(roll // 8, 4, 2, head), ("z", "y", "c", "head"))
    rolls = ("z", "y", "c")
    by_rollout = P(rolls, None, "head")
    by_key = P(None, rolls, "head")
    by_row = P(rolls, "head", None)
    in_specs = (
        by_rollout, by_rollout, by_rollout, by_key, by_key, by_rollout, by_row, by_row,
        P(rolls), P(rolls),
    )
    out_specs = (by_rollout, by_rollout, by_rollout, by_key, by_key)
    return jax.shard_map(
        per_device, mesh=fine, in_specs=in_specs, out_specs=out_specs, check_vma=False
    )
```

time: 88.7 us -> 87.7 us (0.989)
  waiting for transfers between devices: 14.7 us -> 19.9 us
  starting transfers between devices: 28.9 us -> 26.5 us
  Pallas kernels: 23.4 us -> 21.1 us
    ppermute x17, waiting for transfers between devices: 9.71 us -> 14.3 us  [trade(): lax.ppermute(block, axis, [(i, target(i)) for i in range(lax.axis_size(ax...]
    ppermute x17, starting transfers between devices: 20.4 us -> 18.1 us  [trade(): lax.ppermute(block, axis, [(i, target(i)) for i in range(lax.axis_size(ax...]
    pallas_call x4, Pallas kernels: 22.9 us -> 20.7 us  [the longest x2 15.3 us: prompt_part(): pl.pallas_call(functools.partial(prompt_kernel, count=len(pairs), first=q...]
  transfers between devices with their start and end apart: 18 -> 18, of which waited for: 5 -> 4; matrix products, arithmetic and copies ran while one was open for 1% -> 0% of each run, Pallas kernels for 26% -> 24%
where the time goes in v6:
time: 87.7 us; the launch traced here: 87 us
  starting transfers between devices  26.5 us (30%)
  Pallas kernels  21.1 us (24%)
  waiting for transfers between devices  19.9 us (23%)
  blocking collectives  14.8 us (17%)
  between operations  2.12 us (2%)
  local copies, waits for them, and re-layouts  1.45 us (2%)
  other arithmetic  1 us (1%)
    ppermute x17, starting transfers between devices, trade(): lax.ppermute(block, axis, [(i, target(i)) for i in range(lax.axis_size(ax...  18.1 us
    pallas_call x2, Pallas kernels, prompt_part(): pl.pallas_call(functools.partial(prompt_kernel, count=len(pairs), first=q...  15.3 us
    all_to_all x1, blocking collectives, exchange(): return lax.all_to_all(blocks, axes, split_axis=0, concat_axis=0, tiled=True)  14.8 us
    ppermute x17, waiting for transfers between devices, trade(): lax.ppermute(block, axis, [(i, target(i)) for i in range(lax.axis_size(ax...  14.3 us
    all_to_all x1, starting transfers between devices, exchange(): return lax.all_to_all(blocks, axes, split_axis=0, concat_axis=0, tiled=True)  8.47 us
    all_to_all x1, waiting for transfers between devices, exchange(): return lax.all_to_all(blocks, axes, split_axis=0, concat_axis=0, tiled=True)  5.64 us
    pallas_call x1, Pallas kernels, suffix_part(): pl.pallas_call(suffix_kernel, in_specs=[VMEM] * (len(rows) + 3), out_spec...  4.19 us
  transfers between devices with their start and end apart: 18, of which 4 were waited for; matrix products, arithmetic and copies ran while one was open for 0% of the time, Pallas kernels for 24%

profile of v6, /device:TPU:6, one launch (start us, length us, event | category | flops | bytes accessed | tf_op | source)
XLA Modules:
  0.0 87.0 jit_solution(2872329444807286257)
XLA Ops:
  0.6 0.0 copy-start.4
  0.6 0.0 copy-start.5
  0.7 0.0 copy-start
  0.7 0.0 copy-start.1
  0.7 0.9 %pad_maximum_fusion = bf16[2,2,32,128]{3,2,1,0:T(8,128)(2,1)S(1)} fusion(bf16[2,1,32,128]{3,2,1,0:T(8,128)(2,1)} %bitcast.46, bf16[2,1,32,128]{3,2,1,0:T(8,128)(2,1)} %bitcast.47), kind=kLoop, calls=%fused_computation.4 | loop fusion | flops 16384 | bytes 65536 | tf_op jit(solution)/shard_map/stack | solution.py:239
  1.6 0.7 broadcast_in_dim.17
  2.3 8.5 %all-to-all-start = ((bf16[8,128,128]{2,1,0:T(8,128)(2,1)}), bf16[8,128,128]{2,1,0:T(8,128)(2,1)S(1)}, u32[]{:S(2)}, u32[]{:S(2)}) async-start(bf16[8,128,128]{2,1,0:T(8,128)(2,1)} %broadcast_in_dim.17), calls=%async_computation | async-start | bytes 524288 | tf_op jit(solution)/shard_map/all_to_all | solution.py:217
  10.8 0.0 copy-done.4
  10.8 0.1 dynamic-slice_bitcast_fusion
  10.8 0.6 collective-permute-start.2
  11.4 0.9 %collective-permute-start = (bf16[96,896]{1,0:T(8,128)(2,1)S(1)}, bf16[96,896]{1,0:T(8,128)(2,1)S(1)}, u32[]{:S(2)}, u32[]{:S(2)}) collective-permute-start(bf16[96,896]{1,0:T(8,128)(2,1)S(1)} %get-tuple-element.100), channel_id=1, source_target_pairs={{0,1},{1,0},{2,3},{3,2},{4,5},{5,4},{6,7},{7,6},{8,9},{9,8},{10,11... | collective-permute-start | bytes 516104 | tf_op jit(solution)/shard_map/ppermute | solution.py:221
  12.3 3.3 %collective-permute-start.1 = (bf16[96,896]{1,0:T(8,128)(2,1)S(1)}, bf16[96,896]{1,0:T(8,128)(2,1)S(1)}, u32[]{:S(2)}, u32[]{:S(2)}) collective-permute-start(bf16[96,896]{1,0:T(8,128)(2,1)S(1)} %get-tuple-element.102), channel_id=1, source_target_pairs={{0,2},{1,3},{2,0},{3,1},{4,6},{5,7},{6,4},{7,5},{8,10},{9,11},{10,... | collective-permute-start | bytes 516104 | tf_op jit(solution)/shard_map/ppermute | solution.py:221
  16.9 0.1 pad_add_fusion.info_ref
  17.0 5.6 %all-to-all-done = bf16[8,128,128]{2,1,0:T(8,128)(2,1)S(1)} async-done(((bf16[8,128,128]{2,1,0:T(8,128)(2,1)}), bf16[8,128,128]{2,1,0:T(8,128)(2,1)S(1)}, u32[]{:S(2)}, u32[]{:S(2)}) %all-to-all-start) | async-done | bytes 262176 | tf_op jit(solution)/shard_map/all_to_all | solution.py:217
  22.6 3.0 %collective-permute-start.4 = (bf16[8,2,2,32,128]{4,3,2,1,0:T(8,128)(2,1)S(1)}, bf16[8,2,2,32,128]{4,3,2,1,0:T(8,128)(2,1)S(1)}, u32[]{:S(2)}, u32[]{:S(2)}) collective-permute-start(bf16[8,2,2,32,128]{4,3,2,1,0:T(8,128)(2,1)S(1)} %bitcast.36), channel_id=1, source_target_pairs={{0,24},{8,0},{16,8},{24,16},{1,25},{9,1},{17,9},{25,17},{2,26},{10... | collective-permute-start | bytes 786440 | tf_op jit(solution)/shard_map/ppermute | solution.py:221
  25.6 0.0 collective-permute-start.3
  25.7 0.0 collective-permute-done.2.refs_3_
  25.7 0.0 collective-permute-done.refs_1_
  25.7 0.0 collective-permute-done.1.refs_2_
  25.7 0.1 collective-permute-start.8
  25.8 0.0 copy-done.5
  25.8 2.3 %collective-permute-start.7 = (bf16[8,2,2,32,128]{4,3,2,1,0:T(8,128)(2,1)S(1)}, bf16[8,2,2,32,128]{4,3,2,1,0:T(8,128)(2,1)S(1)}, u32[]{:S(2)}, u32[]{:S(2)}) collective-permute-start(bf16[8,2,2,32,128]{4,3,2,1,0:T(8,128)(2,1)S(1)} %bitcast.39), channel_id=1, source_target_pairs={{0,16},{8,24},{16,0},{24,8},{1,17},{9,25},{17,1},{25,9},{2,18},{10... | collective-permute-start | bytes 786440 | tf_op jit(solution)/shard_map/ppermute | solution.py:221
  28.1 0.0 copy-done
  28.1 0.0 copy-done.1
  28.1 1.2 %prepare.1 = (bf16[384,896]{1,0:T(8,128)(2,1)S(1)}, bf16[128,2688]{1,0:T(8,128)(2,1)S(1)}, bf16[128,2688]{1,0:T(8,128)(2,1)S(1)}, f32[1,2688]{1,0:T(1,128)S(1)}, f32[1,2688]{1,0:T(1,128)S(1)}) custom-call(s32[3]{0:T(128)S(1)} %pad_add_fusion.info_ref, bf16[384,896]{1,0:T(8,128)(2,1)S(1)} %bitcast.32, bf16[384,896]{1,0:T(8,128)(2,1)S(1)} %bitcast.31, ...), custom_call_target="tpu_custom_call" | custom-call | flops 688128 | bytes 4128768 | tf_op jit(solution)/shard_map/prepare/pallas_call | solution.py:69
  29.3 0.2 collective-permute-done.4.refs_2_
  29.5 9.3 %collective-permute-done.3.refs_1_ = bf16[8,2,2,32,128]{4,3,2,1,0:T(8,128)(2,1)S(1)} collective-permute-done((bf16[8,2,2,32,128]{4,3,2,1,0:T(8,128)(2,1)S(1)}, bf16[8,2,2,32,128]{4,3,2,1,0:T(8,128)(2,1)S(1)}, u32[]{:S(2)}, u32[]{:S(2)}) %collective-permute-start.3) | collective-permute-done | bytes 262176 | tf_op jit(solution)/shard_map/ppermute | solution.py:221
  38.8 0.0 collective-permute-start.5
  38.8 0.5 collective-permute-start.6
  39.3 0.0 collective-permute-done.8.refs_3_
  39.3 7.7 %prompt_part.2 = (f32[128,2688]{1,0:T(8,128)S(1)}, bf16[528,128]{1,0:T(8,128)(2,1)S(1)}, bf16[528,128]{1,0:T(8,128)(2,1)S(1)}, bf16[528,128]{1,0:T(8,128)(2,1)S(1)}, bf16[528,128]{1,0:T(8,128)(2,1)S(1)}) custom-call(s32[3]{0:T(128)S(1)} %pad_add_fusion.info_ref, bf16[8,2,2,32,128]{4,3,2,1,0:T(8,128)(2,1)S(1)} %bitcast.40, ...), custom_call_target="tpu_custom_call" | custom-call | flops 3523215360 | bytes 5505024 | tf_op jit(solution)/shard_map/prompt_part/pallas_call | solution.py:178
  47.1 0.0 collective-permute-done.7.refs_2_
  47.1 0.1 collective-permute-start.9
  47.2 0.1 collective-permute-start.10
  47.3 2.0 %collective-permute-start.11 = (bf16[528,128]{1,0:T(8,128)(2,1)S(1)}, bf16[528,128]{1,0:T(8,128)(2,1)S(1)}, u32[]{:S(2)}, u32[]{:S(2)}) collective-permute-start(bf16[528,128]{1,0:T(8,128)(2,1)S(1)} %get-tuple-element.79), channel_id=1, source_target_pairs={{0,8},{4,12},{8,16},{12,20},{16,24},{20,28},{24,0},{28,4},{1,9},{5... | collective-permute-start | bytes 405512 | tf_op jit(solution)/shard_map/ppermute | solution.py:221
  49.3 0.0 collective-permute-done.5.refs_0_
  49.3 0.0 copy-start.2
  49.3 0.0 copy-start.3
  49.3 0.0 collective-permute-start.12
  49.3 0.0 collective-permute-done.6.refs_1_
  49.3 0.0 collective-permute-done.9.refs_3_
  49.3 7.6 %prompt_part.3 = (f32[128,2688]{1,0:T(8,128)S(1)}, bf16[528,128]{1,0:T(8,128)(2,1)S(1)}, bf16[528,128]{1,0:T(8,128)(2,1)S(1)}, bf16[528,128]{1,0:T(8,128)(2,1)S(1)}, bf16[528,128]{1,0:T(8,128)(2,1)S(1)}) custom-call(s32[3]{0:T(128)S(1)} %pad_add_fusion.info_ref, bf16[8,2,2,32,128]{4,3,2,1,0:T(8,128)(2,1)S(1)} %collective-permute-done.5.refs_0_, ...), custom_call_target="tpu_custom_call" | custom-call | flops 3523215360 | bytes 5505024 | tf_op jit(solution)/shard_map/prompt_part/pallas_call | solution.py:178
  56.9 0.0 collective-permute-done.10.refs_1_
  56.9 0.0 collective-permute-done.11.refs_2_
  56.9 0.0 collective-permute-done.12.refs_3_
  57.0 1.5 %collective-permute-start.13 = (bf16[528,128]{1,0:T(8,128)(2,1)S(1)}, bf16[528,128]{1,0:T(8,128)(2,1)S(1)}, u32[]{:S(2)}, u32[]{:S(2)}) collective-permute-start(bf16[528,128]{1,0:T(8,128)(2,1)S(1)} %get-tuple-element.85), channel_id=1, source_target_pairs={{0,28},{4,24},{8,4},{12,0},{16,12},{20,8},{24,20},{28,16},{1,29},{... | collective-permute-start | bytes 405512 | tf_op jit(solution)/shard_map/ppermute | solution.py:221
  58.4 0.4 collective-permute-start.14
  58.8 1.2 %collective-permute-start.15 = (bf16[528,128]{1,0:T(8,128)(2,1)S(1)}, bf16[528,128]{1,0:T(8,128)(2,1)S(1)}, u32[]{:S(2)}, u32[]{:S(2)}) collective-permute-start(bf16[528,128]{1,0:T(8,128)(2,1)S(1)} %get-tuple-element.87), channel_id=1, source_target_pairs={{0,16},{4,20},{8,24},{12,28},{16,0},{20,4},{24,8},{28,12},{1,17},{... | collective-permute-start | bytes 405512 | tf_op jit(solution)/shard_map/ppermute | solution.py:221
  60.0 2.1 %collective-permute-start.16 = (bf16[528,128]{1,0:T(8,128)(2,1)S(1)}, bf16[528,128]{1,0:T(8,128)(2,1)S(1)}, u32[]{:S(2)}, u32[]{:S(2)}) collective-permute-start(bf16[528,128]{1,0:T(8,128)(2,1)S(1)} %get-tuple-element.88), channel_id=1, source_target_pairs={{0,20},{4,16},{8,28},{12,24},{16,4},{20,0},{24,12},{28,8},{1,21},{... | collective-permute-start | bytes 405512 | tf_op jit(solution)/shard_map/ppermute | solution.py:221
  62.1 0.0 copy-done.2
  62.1 0.0 copy-done.3
  62.1 4.2 %suffix_part.1 = (bf16[384,896]{1,0:T(8,128)(2,1)}, bf16[384,128]{1,0:T(8,128)(2,1)}, bf16[384,128]{1,0:T(8,128)(2,1)}) custom-call(bf16[384,896]{1,0:T(8,128)(2,1)S(1)} %bitcast.35, bf16[384,896]{1,0:T(8,128)(2,1)S(1)} %get-tuple-element.58.refs_5_.refs_1_, bf16[128,2688]{1,0:T(8,128)(2,1)S(1)} %get-tuple-element.59.refs_6_.refs_2_, ...), custom_call_target="tpu_custom_call" | custom-call | flops 1321205760 | bytes 5505024 | tf_op jit(solution)/shard_map/suffix_part/pallas_call | solution.py:129
  66.3 0.0 collective-permute-done.13.refs_4_
  66.3 4.8 %collective-permute-done.14.refs_5_ = bf16[528,128]{1,0:T(8,128)(2,1)S(1)} collective-permute-done((bf16[528,128]{1,0:T(8,128)(2,1)S(1)}, bf16[528,128]{1,0:T(8,128)(2,1)S(1)}, u32[]{:S(2)}, u32[]{:S(2)}) %collective-permute-start.14) | collective-permute-done | bytes 135200 | tf_op jit(solution)/shard_map/ppermute | solution.py:221
  71.1 0.0 collective-permute-done.15.refs_6_
  71.1 0.0 collective-permute-done.16.refs_7_
  71.1 0.4 group_sum.1
  71.5 14.8 %all_to_all.14 = bf16[8,128,128]{2,1,0:T(8,128)(2,1)S(1)} all-to-all(bf16[8,128,128]{2,1,0:T(8,128)(2,1)S(1)} %bitcast.30), channel_id=1, replica_groups=mesh['z'=8,'y'=4,'c'=2,'head'=4] {'z'}, dimensions={0} | all-to-all | bytes 524288 | tf_op jit(solution)/shard_map/all_to_all | solution.py:217
  86.4 0.6 slice_bitcast_fusion
  (2 shorter events, 0.0 us)
Async XLA Ops:
  0.6 10.1 %copy-start.4 = (bf16[1,96,3584]{2,1,0:T(8,128)(2,1)S(1)}, bf16[1,96,3584]{2,1,0:T(8,128)(2,1)}, u32[]{:S(2)}) copy-start(bf16[1,96,3584]{2,1,0:T(8,128)(2,1)} %param.16) | copy-start | bytes 2064388
  0.6 25.1 %copy-start.5 = (f32[1,7,384]{2,0,1:T(1,128)S(1)}, f32[1,7,384]{2,0,1:T(1,128)}, u32[]{:S(2)}) copy-start(f32[1,7,384]{2,0,1:T(1,128)} %param.17) | copy-start | bytes 32260
  0.7 27.5 %copy-start = (bf16[1,384,896]{2,1,0:T(8,128)(2,1)S(1)}, bf16[1,384,896]{2,1,0:T(8,128)(2,1)}, u32[]{:S(2)}) copy-start(bf16[1,384,896]{2,1,0:T(8,128)(2,1)} %param.15) | copy-start | bytes 2064388
  0.7 27.5 %copy-start.1 = (bf16[1,384,896]{2,1,0:T(8,128)(2,1)S(1)}, bf16[1,384,896]{2,1,0:T(8,128)(2,1)}, u32[]{:S(2)}) copy-start(bf16[1,384,896]{2,1,0:T(8,128)(2,1)} %param.10) | copy-start | bytes 2064388
  2.3 20.3 %all-to-all-start = ((bf16[8,128,128]{2,1,0:T(8,128)(2,1)}), bf16[8,128,128]{2,1,0:T(8,128)(2,1)S(1)}, u32[]{:S(2)}, u32[]{:S(2)}) async-start(bf16[8,128,128]{2,1,0:T(8,128)(2,1)} %broadcast_in_dim.17), calls=%async_computation | async-start | bytes 524288 | tf_op jit(solution)/shard_map/all_to_all | solution.py:217
  10.8 14.8 %collective-permute-start.2 = (bf16[96,896]{1,0:T(8,128)(2,1)S(1)}, bf16[96,896]{1,0:T(8,128)(2,1)S(1)}, u32[]{:S(2)}, u32[]{:S(2)}) collective-permute-start(bf16[96,896]{1,0:T(8,128)(2,1)S(1)} %get-tuple-element.99), channel_id=1, source_target_pairs={{0,3},{1,2},{2,1},{3,0},{4,7},{5,6},{6,5},{7,4},{8,11},{9,10},{10,... | collective-permute-start | bytes 516104 | tf_op jit(solution)/shard_map/ppermute | solution.py:221
  11.4 14.3 %collective-permute-start = (bf16[96,896]{1,0:T(8,128)(2,1)S(1)}, bf16[96,896]{1,0:T(8,128)(2,1)S(1)}, u32[]{:S(2)}, u32[]{:S(2)}) collective-permute-start(bf16[96,896]{1,0:T(8,128)(2,1)S(1)} %get-tuple-element.100), channel_id=1, source_target_pairs={{0,1},{1,0},{2,3},{3,2},{4,5},{5,4},{6,7},{7,6},{8,9},{9,8},{10,11... | collective-permute-start | bytes 516104 | tf_op jit(solution)/shard_map/ppermute | solution.py:221
  12.3 13.4 %collective-permute-start.1 = (bf16[96,896]{1,0:T(8,128)(2,1)S(1)}, bf16[96,896]{1,0:T(8,128)(2,1)S(1)}, u32[]{:S(2)}, u32[]{:S(2)}) collective-permute-start(bf16[96,896]{1,0:T(8,128)(2,1)S(1)} %get-tuple-element.102), channel_id=1, source_target_pairs={{0,2},{1,3},{2,0},{3,1},{4,6},{5,7},{6,4},{7,5},{8,10},{9,11},{10,... | collective-permute-start | bytes 516104 | tf_op jit(solution)/shard_map/ppermute | solution.py:221
  22.6 6.9 %collective-permute-start.4 = (bf16[8,2,2,32,128]{4,3,2,1,0:T(8,128)(2,1)S(1)}, bf16[8,2,2,32,128]{4,3,2,1,0:T(8,128)(2,1)S(1)}, u32[]{:S(2)}, u32[]{:S(2)}) collective-permute-start(bf16[8,2,2,32,128]{4,3,2,1,0:T(8,128)(2,1)S(1)} %bitcast.36), channel_id=1, source_target_pairs={{0,24},{8,0},{16,8},{24,16},{1,25},{9,1},{17,9},{25,17},{2,26},{10... | collective-permute-start | bytes 786440 | tf_op jit(solution)/shard_map/ppermute | solution.py:221
  25.6 13.2 %collective-permute-start.3 = (bf16[8,2,2,32,128]{4,3,2,1,0:T(8,128)(2,1)S(1)}, bf16[8,2,2,32,128]{4,3,2,1,0:T(8,128)(2,1)S(1)}, u32[]{:S(2)}, u32[]{:S(2)}) collective-permute-start(bf16[8,2,2,32,128]{4,3,2,1,0:T(8,128)(2,1)S(1)} %bitcast.37), channel_id=1, source_target_pairs={{0,8},{8,16},{16,24},{24,0},{1,9},{9,17},{17,25},{25,1},{2,10},{10... | collective-permute-start | bytes 786440 | tf_op jit(solution)/shard_map/ppermute | solution.py:221
  25.7 13.7 %collective-permute-start.8 = (bf16[8,2,2,32,128]{4,3,2,1,0:T(8,128)(2,1)S(1)}, bf16[8,2,2,32,128]{4,3,2,1,0:T(8,128)(2,1)S(1)}, u32[]{:S(2)}, u32[]{:S(2)}) collective-permute-start(bf16[8,2,2,32,128]{4,3,2,1,0:T(8,128)(2,1)S(1)} %bitcast.38), channel_id=1, source_target_pairs={{0,4},{4,0},{1,5},{5,1},{2,6},{6,2},{3,7},{7,3},{8,12},{12,8},{9,1... | collective-permute-start | bytes 786440 | tf_op jit(solution)/shard_map/ppermute | solution.py:221
  25.8 21.3 %collective-permute-start.7 = (bf16[8,2,2,32,128]{4,3,2,1,0:T(8,128)(2,1)S(1)}, bf16[8,2,2,32,128]{4,3,2,1,0:T(8,128)(2,1)S(1)}, u32[]{:S(2)}, u32[]{:S(2)}) collective-permute-start(bf16[8,2,2,32,128]{4,3,2,1,0:T(8,128)(2,1)S(1)} %bitcast.39), channel_id=1, source_target_pairs={{0,16},{8,24},{16,0},{24,8},{1,17},{9,25},{17,1},{25,9},{2,18},{10... | collective-permute-start | bytes 786440 | tf_op jit(solution)/shard_map/ppermute | solution.py:221
  38.8 10.5 %collective-permute-start.5 = (bf16[8,2,2,32,128]{4,3,2,1,0:T(8,128)(2,1)S(1)}, bf16[8,2,2,32,128]{4,3,2,1,0:T(8,128)(2,1)S(1)}, u32[]{:S(2)}, u32[]{:S(2)}) collective-permute-start(bf16[8,2,2,32,128]{4,3,2,1,0:T(8,128)(2,1)S(1)} %collective-permute-done.3.refs_1_), channel_id=1, source_target_pairs={{0,4},{4,0},{1,5},{5,1},{2,6},{6,2},{3,7},{7,3},{8,12},{12,8},{9,1... | collective-permute-start | bytes 786440 | tf_op jit(solution)/shard_map/ppermute | solution.py:221
  38.8 10.5 %collective-permute-start.6 = (bf16[8,2,2,32,128]{4,3,2,1,0:T(8,128)(2,1)S(1)}, bf16[8,2,2,32,128]{4,3,2,1,0:T(8,128)(2,1)S(1)}, u32[]{:S(2)}, u32[]{:S(2)}) collective-permute-start(bf16[8,2,2,32,128]{4,3,2,1,0:T(8,128)(2,1)S(1)} %collective-permute-done.4.refs_2_), channel_id=1, source_target_pairs={{0,4},{4,0},{1,5},{5,1},{2,6},{6,2},{3,7},{7,3},{8,12},{12,8},{9,1... | collective-permute-start | bytes 786440 | tf_op jit(solution)/shard_map/ppermute | solution.py:221
  47.1 2.2 %collective-permute-start.9 = (bf16[8,2,2,32,128]{4,3,2,1,0:T(8,128)(2,1)S(1)}, bf16[8,2,2,32,128]{4,3,2,1,0:T(8,128)(2,1)S(1)}, u32[]{:S(2)}, u32[]{:S(2)}) collective-permute-start(bf16[8,2,2,32,128]{4,3,2,1,0:T(8,128)(2,1)S(1)} %collective-permute-done.7.refs_2_), channel_id=1, source_target_pairs={{0,4},{4,0},{1,5},{5,1},{2,6},{6,2},{3,7},{7,3},{8,12},{12,8},{9,1... | collective-permute-start | bytes 786440 | tf_op jit(solution)/shard_map/ppermute | solution.py:221
  47.2 9.8 %collective-permute-start.10 = (bf16[528,128]{1,0:T(8,128)(2,1)S(1)}, bf16[528,128]{1,0:T(8,128)(2,1)S(1)}, u32[]{:S(2)}, u32[]{:S(2)}) collective-permute-start(bf16[528,128]{1,0:T(8,128)(2,1)S(1)} %get-tuple-element.78), channel_id=1, source_target_pairs={{0,24},{4,28},{8,0},{12,4},{16,8},{20,12},{24,16},{28,20},{1,25},{... | collective-permute-start | bytes 405512 | tf_op jit(solution)/shard_map/ppermute | solution.py:221
  47.3 9.7 %collective-permute-start.11 = (bf16[528,128]{1,0:T(8,128)(2,1)S(1)}, bf16[528,128]{1,0:T(8,128)(2,1)S(1)}, u32[]{:S(2)}, u32[]{:S(2)}) collective-permute-start(bf16[528,128]{1,0:T(8,128)(2,1)S(1)} %get-tuple-element.79), channel_id=1, source_target_pairs={{0,8},{4,12},{8,16},{12,20},{16,24},{20,28},{24,0},{28,4},{1,9},{5... | collective-permute-start | bytes 405512 | tf_op jit(solution)/shard_map/ppermute | solution.py:221
  49.3 12.8 %copy-start.2 = (bf16[1,384,128]{2,1,0:T(8,128)(2,1)S(1)}, bf16[1,384,128]{2,1,0:T(8,128)(2,1)}, u32[]{:S(2)}) copy-start(bf16[1,384,128]{2,1,0:T(8,128)(2,1)} %param.11) | copy-start | bytes 294916
  49.3 12.8 %copy-start.3 = (bf16[1,384,128]{2,1,0:T(8,128)(2,1)S(1)}, bf16[1,384,128]{2,1,0:T(8,128)(2,1)}, u32[]{:S(2)}) copy-start(bf16[1,384,128]{2,1,0:T(8,128)(2,1)} %param.12) | copy-start | bytes 294916
  49.3 7.7 %collective-permute-start.12 = (bf16[528,128]{1,0:T(8,128)(2,1)S(1)}, bf16[528,128]{1,0:T(8,128)(2,1)S(1)}, u32[]{:S(2)}, u32[]{:S(2)}) collective-permute-start(bf16[528,128]{1,0:T(8,128)(2,1)S(1)} %get-tuple-element.80), channel_id=1, source_target_pairs={{0,4},{4,0},{8,12},{12,8},{16,20},{20,16},{24,28},{28,24},{1,5},{5... | collective-permute-start | bytes 405512 | tf_op jit(solution)/shard_map/ppermute | solution.py:221
  57.0 9.4 %collective-permute-start.13 = (bf16[528,128]{1,0:T(8,128)(2,1)S(1)}, bf16[528,128]{1,0:T(8,128)(2,1)S(1)}, u32[]{:S(2)}, u32[]{:S(2)}) collective-permute-start(bf16[528,128]{1,0:T(8,128)(2,1)S(1)} %get-tuple-element.85), channel_id=1, source_target_pairs={{0,28},{4,24},{8,4},{12,0},{16,12},{20,8},{24,20},{28,16},{1,29},{... | collective-permute-start | bytes 405512 | tf_op jit(solution)/shard_map/ppermute | solution.py:221
  58.4 12.7 %collective-permute-start.14 = (bf16[528,128]{1,0:T(8,128)(2,1)S(1)}, bf16[528,128]{1,0:T(8,128)(2,1)S(1)}, u32[]{:S(2)}, u32[]{:S(2)}) collective-permute-start(bf16[528,128]{1,0:T(8,128)(2,1)S(1)} %get-tuple-element.86), channel_id=1, source_target_pairs={{0,12},{4,8},{8,20},{12,16},{16,28},{20,24},{24,4},{28,0},{1,13},{... | collective-permute-start | bytes 405512 | tf_op jit(solution)/shard_map/ppermute | solution.py:221
  58.8 12.3 %collective-permute-start.15 = (bf16[528,128]{1,0:T(8,128)(2,1)S(1)}, bf16[528,128]{1,0:T(8,128)(2,1)S(1)}, u32[]{:S(2)}, u32[]{:S(2)}) collective-permute-start(bf16[528,128]{1,0:T(8,128)(2,1)S(1)} %get-tuple-element.87), channel_id=1, source_target_pairs={{0,16},{4,20},{8,24},{12,28},{16,0},{20,4},{24,8},{28,12},{1,17},{... | collective-permute-start | bytes 405512 | tf_op jit(solution)/shard_map/ppermute | solution.py:221
  60.0 11.1 %collective-permute-start.16 = (bf16[528,128]{1,0:T(8,128)(2,1)S(1)}, bf16[528,128]{1,0:T(8,128)(2,1)S(1)}, u32[]{:S(2)}, u32[]{:S(2)}) collective-permute-start(bf16[528,128]{1,0:T(8,128)(2,1)S(1)} %get-tuple-element.88), channel_id=1, source_target_pairs={{0,20},{4,16},{8,28},{12,24},{16,4},{20,0},{24,12},{28,8},{1,21},{... | collective-permute-start | bytes 405512 | tf_op jit(solution)/shard_map/ppermute | solution.py:221

commit v7 on v6

--- a/solution.py
+++ b/solution.py
@@ -34,6 +34,23 @@
     weight_grad_t = jnp.dot(value_rows, grad_t, preferred_element_type=F32)
     score_grad_t = (weights_t * (weight_grad_t - delta_row) * scale).astype(BF16)
     return weights_t.astype(BF16), score_grad_t
+
+
+def spread_kernel(key_ref, value_ref, out_ref):
+    for i in range(out_ref.shape[0]):
+        out_ref[i, :, 0] = key_ref[...]
+        out_ref[i, :, 1] = value_ref[...]
+
+
+def spread(keys, values, count):
+    prompt_count, owned, width = keys.shape
+    return pl.pallas_call(
+        spread_kernel,
+        in_specs=[VMEM] * 2,
+        out_specs=VMEM,
+        out_shape=jax.ShapeDtypeStruct((count, prompt_count, 2, owned, width), BF16),
+        name="spread",
+    )(keys, values)
 
 
 def prepare_kernel(info_ref, query_ref, out_ref, norm_ref, *refs):
@@ -221,10 +238,6 @@
     return lax.ppermute(block, axis, [(i, target(i)) for i in range(lax.axis_size(axis))])
 
 
-def copies(block, count):
-    return jnp.broadcast_to(block[None], (count,) + block.shape)
-
-
 def per_device(
     query, key_suffix, value_suffix, key_prompt, value_prompt, attn_out, grad_out, log_norm,
     prompt_id, lengths,
@@ -236,8 +249,7 @@
     place = lax.axis_index("head")
     info = jnp.stack([prompt_id[0], place, lengths[0]]).astype(jnp.int32)
 
-    own_pair = jnp.stack([key_prompt, value_prompt], 1).reshape(-1, width)
-    stacked = exchange(copies(own_pair, stacks).reshape(-1, width), "z")
+    stacked = exchange(spread(key_prompt, value_prompt, stacks).reshape(stacks, -1, width), "z")
     grads = []
     for i in range(heads):
         at = (place ^ i) * columns
@@ -248,12 +260,15 @@
 
     moved = {
         steps: trade(stacked, "y", lambda j, steps=steps: (j + steps) % lines)
-        for steps in (1, lines - 1, 2)
+        for steps in (1, lines - 1)
     }
     stacked, grads = lax.optimization_barrier((stacked, grads))
     other = trade(stacked, "c", lambda j: j ^ 1)
     rows = [query[0], *prepare(info, query[0], attn_out[0], log_norm[0], grads)]
-    beside, rows[-1] = lax.optimization_barrier(([moved[1], moved[lines - 1]], rows[-1]))
+    beside, rows[-1], source = lax.optimization_barrier(
+        ([moved[1], moved[lines - 1]], rows[-1], stacked)
+    )
+    far = trade(source, "y", lambda j: (j + 2) % lines)
     beside_other = [trade(block, "c", lambda j: j ^ 1) for block in beside]
 
     shares = []
@@ -267,12 +282,12 @@
             shares.append(trade(part, GROUP, target))
 
     query_acc, *parts = prompt_part(info, [stacked, *beside, other], rows)
-    far, query_acc = lax.optimization_barrier((moved[2], query_acc))
+    far, query_acc = lax.optimization_barrier((far, query_acc))
     far_other = trade(far, "c", lambda j: j ^ 1)
     send(parts, [(0, 0), (1, 0), (lines - 1, 0), (0, 1)])
-    query_acc, *parts = prompt_part(info, [*beside_other, far, far_other], rows, query_acc)
+    query_acc, *parts = prompt_part(info, [far, far_other, *beside_other], rows, query_acc)
     parts, shares = lax.optimization_barrier((parts, shares))
-    send(parts, [(1, 1), (lines - 1, 1), (2, 0), (2, 1)])
+    send(parts, [(2, 0), (2, 1), (1, 1), (lines - 1, 1)])
 
     query_grad, key_grad, value_grad = suffix_part(rows, query_acc, key_suffix[0], value_suffix[0])
     key_grad, shares = lax.optimization_barrier((key_grad, shares))

time: 87.7 us -> 82.2 us (0.937)
  waiting for transfers between devices: 19.9 us -> 14.2 us
  Pallas kernels: 21.1 us -> 22.5 us
  starting transfers between devices: 26.5 us -> 25.2 us
  other arithmetic: 1 us -> 0.12 us
    ppermute x17, waiting for transfers between devices: 14.3 us -> 9.75 us  [trade(): lax.ppermute(block, axis, [(i, target(i)) for i in range(lax.axis_size(ax...]
    pallas_call x0 -> x1, Pallas kernels: none -> 1.58 us  [spread(): pl.pallas_call(spread_kernel, in_specs=[VMEM] * 2, out_specs=VMEM, out_sh...]
    ppermute x17, starting transfers between devices: 18.1 us -> 16.8 us  [trade(): lax.ppermute(block, axis, [(i, target(i)) for i in range(lax.axis_size(ax...]
    dynamic_slice x1, local copies, waits for them, and re-layouts: 0.07 us -> 1.22 us  [per_device(): piece = lax.dynamic_slice_in_dim(grad_out[0], at, columns, axis=1)]
    all_to_all x1, waiting for transfers between devices: 5.64 us -> 4.49 us  [exchange(): return lax.all_to_all(blocks, axes, split_axis=0, concat_axis=0, tiled=True)]
    another operation x1 -> x0, other arithmetic: 0.88 us -> none  [per_device(): own_pair = jnp.stack([key_prompt, value_prompt], 1).reshape(-1, width)]
  transfers between devices with their start and end apart: 18 -> 18, of which waited for: 4 -> 6; matrix products, arithmetic and copies ran while one was open for 0% -> 2% of each run, Pallas kernels for 24% -> 25%
where the time goes in v7:
time: 82.2 us; the launch traced here: 80.9 us
  starting transfers between devices  25.2 us (31%)
  Pallas kernels  22.5 us (27%)
  blocking collectives  14.8 us (18%)
  waiting for transfers between devices  14.2 us (17%)
  between operations  2.11 us (3%)
  local copies, waits for them, and re-layouts  1.86 us (2%)
    ppermute x17, starting transfers between devices, trade(): lax.ppermute(block, axis, [(i, target(i)) for i in range(lax.axis_size(ax...  16.8 us
    pallas_call x2, Pallas kernels, prompt_part(): pl.pallas_call(functools.partial(prompt_kernel, count=len(pairs), first=q...  15.1 us
    all_to_all x1, blocking collectives, exchange(): return lax.all_to_all(blocks, axes, split_axis=0, concat_axis=0, tiled=True)  14.8 us
    ppermute x17, waiting for transfers between devices, trade(): lax.ppermute(block, axis, [(i, target(i)) for i in range(lax.axis_size(ax...  9.75 us
    all_to_all x1, starting transfers between devices, exchange(): return lax.all_to_all(blocks, axes, split_axis=0, concat_axis=0, tiled=True)  8.47 us
    all_to_all x1, waiting for transfers between devices, exchange(): return lax.all_to_all(blocks, axes, split_axis=0, concat_axis=0, tiled=True)  4.49 us
    pallas_call x1, Pallas kernels, suffix_part(): pl.pallas_call(suffix_kernel, in_specs=[VMEM] * (len(rows) + 3), out_spec...  4.18 us
  transfers between devices with their start and end apart: 18, of which 6 were waited for; matrix products, arithmetic and copies ran while one was open for 2% of the time, Pallas kernels for 25%

profile of v7, /device:TPU:6, one launch (start us, length us, event | category | flops | bytes accessed | tf_op | source)
XLA Modules:
  0.0 80.9 jit_solution(13999294224372914464)
XLA Ops:
  0.6 0.0 copy-start.4
  0.6 0.0 copy-start
  0.7 0.0 copy-start.1
  0.7 1.6 %spread.1 = bf16[8,2,2,32,128]{4,3,2,1,0:T(8,128)(2,1)} custom-call(bf16[2,32,128]{2,1,0:T(8,128)(2,1)} %key_ref.1, bf16[2,32,128]{2,1,0:T(8,128)(2,1)} %value_ref.1), custom_call_target="tpu_custom_call" | custom-call | tf_op jit(solution)/shard_map/spread/pallas_call | solution.py:47
  2.2 8.5 %all-to-all-start = ((bf16[8,128,128]{2,1,0:T(8,128)(2,1)}), bf16[8,128,128]{2,1,0:T(8,128)(2,1)S(1)}, u32[]{:S(2)}, u32[]{:S(2)}) async-start(bf16[8,128,128]{2,1,0:T(8,128)(2,1)} %bitcast.41), calls=%async_computation | async-start | bytes 524288 | tf_op jit(solution)/shard_map/all_to_all | solution.py:234
  10.7 1.2 %dynamic-slice_bitcast_fusion = (bf16[96,896]{1,0:T(8,128)(2,1)S(1)}, bf16[96,896]{1,0:T(8,128)(2,1)S(1)}, bf16[96,896]{1,0:T(8,128)(2,1)S(1)}, bf16[96,896]{1,0:T(8,128)(2,1)S(1)}) fusion(bf16[1,96,3584]{2,1,0:T(8,128)(2,1)} %param.16, s32[]{:T(128)S(6)} %select_n.15, s32[]{:T(128)S(6)} %select_n.13, s32[]{:T(128)S(6)} %select_n.12, s32[]{:T(128)S(6)} %select_n.14), kind=kLoop, calls=%fused_computation | loop fusion | bytes 1376272 | tf_op jit(solution)/shard_map/dynamic_slice | solution.py:256
  11.9 0.6 collective-permute-start.2
  12.5 0.9 %collective-permute-start = (bf16[96,896]{1,0:T(8,128)(2,1)S(1)}, bf16[96,896]{1,0:T(8,128)(2,1)S(1)}, u32[]{:S(2)}, u32[]{:S(2)}) collective-permute-start(bf16[96,896]{1,0:T(8,128)(2,1)S(1)} %get-tuple-element.102), channel_id=1, source_target_pairs={{0,1},{1,0},{2,3},{3,2},{4,5},{5,4},{6,7},{7,6},{8,9},{9,8},{10,11... | collective-permute-start | bytes 516104 | tf_op jit(solution)/shard_map/ppermute | solution.py:238
  13.4 3.3 %collective-permute-start.1 = (bf16[96,896]{1,0:T(8,128)(2,1)S(1)}, bf16[96,896]{1,0:T(8,128)(2,1)S(1)}, u32[]{:S(2)}, u32[]{:S(2)}) collective-permute-start(bf16[96,896]{1,0:T(8,128)(2,1)S(1)} %get-tuple-element.104), channel_id=1, source_target_pairs={{0,2},{1,3},{2,0},{3,1},{4,6},{5,7},{6,4},{7,5},{8,10},{9,11},{10,... | collective-permute-start | bytes 516104 | tf_op jit(solution)/shard_map/ppermute | solution.py:238
  18.0 0.1 pad_add_fusion.info_ref
  18.1 4.5 %all-to-all-done = bf16[8,128,128]{2,1,0:T(8,128)(2,1)S(1)} async-done(((bf16[8,128,128]{2,1,0:T(8,128)(2,1)}), bf16[8,128,128]{2,1,0:T(8,128)(2,1)S(1)}, u32[]{:S(2)}, u32[]{:S(2)}) %all-to-all-start) | async-done | bytes 262176 | tf_op jit(solution)/shard_map/all_to_all | solution.py:234
  22.6 3.0 %collective-permute-start.4 = (bf16[8,2,2,32,128]{4,3,2,1,0:T(8,128)(2,1)S(1)}, bf16[8,2,2,32,128]{4,3,2,1,0:T(8,128)(2,1)S(1)}, u32[]{:S(2)}, u32[]{:S(2)}) collective-permute-start(bf16[8,2,2,32,128]{4,3,2,1,0:T(8,128)(2,1)S(1)} %bitcast.33), channel_id=1, source_target_pairs={{0,24},{8,0},{16,8},{24,16},{1,25},{9,1},{17,9},{25,17},{2,26},{10... | collective-permute-start | bytes 786440 | tf_op jit(solution)/shard_map/ppermute | solution.py:238
  25.6 0.0 collective-permute-start.3
  25.6 0.0 collective-permute-done.2.refs_3_
  25.6 0.0 collective-permute-done.refs_1_
  25.6 0.0 collective-permute-done.1.refs_2_
  25.6 0.1 collective-permute-start.6
  25.7 0.0 copy-done.4
  25.7 0.0 copy-done
  25.8 0.0 copy-done.1
  25.8 1.2 %prepare.1 = (bf16[384,896]{1,0:T(8,128)(2,1)S(1)}, bf16[128,2688]{1,0:T(8,128)(2,1)S(1)}, bf16[128,2688]{1,0:T(8,128)(2,1)S(1)}, f32[1,2688]{1,0:T(1,128)S(1)}, f32[1,2688]{1,0:T(1,128)S(1)}) custom-call(s32[3]{0:T(128)S(1)} %pad_add_fusion.info_ref, bf16[384,896]{1,0:T(8,128)(2,1)S(1)} %bitcast.29, bf16[384,896]{1,0:T(8,128)(2,1)S(1)} %bitcast.28, ...), custom_call_target="tpu_custom_call" | custom-call | flops 688128 | bytes 4128768 | tf_op jit(solution)/shard_map/prepare/pallas_call | solution.py:86
  27.0 2.5 %collective-permute-done.4.refs_2_ = bf16[8,2,2,32,128]{4,3,2,1,0:T(8,128)(2,1)S(1)} collective-permute-done((bf16[8,2,2,32,128]{4,3,2,1,0:T(8,128)(2,1)S(1)}, bf16[8,2,2,32,128]{4,3,2,1,0:T(8,128)(2,1)S(1)}, u32[]{:S(2)}, u32[]{:S(2)}) %collective-permute-start.4) | collective-permute-done | bytes 262176 | tf_op jit(solution)/shard_map/ppermute | solution.py:238
  29.5 3.7 %collective-permute-done.3.refs_1_ = bf16[8,2,2,32,128]{4,3,2,1,0:T(8,128)(2,1)S(1)} collective-permute-done((bf16[8,2,2,32,128]{4,3,2,1,0:T(8,128)(2,1)S(1)}, bf16[8,2,2,32,128]{4,3,2,1,0:T(8,128)(2,1)S(1)}, u32[]{:S(2)}, u32[]{:S(2)}) %collective-permute-start.3) | collective-permute-done | bytes 262176 | tf_op jit(solution)/shard_map/ppermute | solution.py:238
  33.2 0.0 collective-permute-start.5
  33.2 0.0 collective-permute-start.8
  33.2 0.5 collective-permute-start.9
  33.7 0.0 collective-permute-done.6.refs_3_
  33.7 7.6 %prompt_part.2 = (f32[128,2688]{1,0:T(8,128)S(1)}, bf16[528,128]{1,0:T(8,128)(2,1)S(1)}, bf16[528,128]{1,0:T(8,128)(2,1)S(1)}, bf16[528,128]{1,0:T(8,128)(2,1)S(1)}, bf16[528,128]{1,0:T(8,128)(2,1)S(1)}) custom-call(s32[3]{0:T(128)S(1)} %pad_add_fusion.info_ref, bf16[8,2,2,32,128]{4,3,2,1,0:T(8,128)(2,1)S(1)} %bitcast.37, ...), custom_call_target="tpu_custom_call" | custom-call | flops 3523215360 | bytes 5505024 | tf_op jit(solution)/shard_map/prompt_part/pallas_call | solution.py:195
  41.3 0.0 collective-permute-done.5.refs_0_
  41.4 0.1 collective-permute-start.7
  41.5 1.5 %collective-permute-start.10 = (bf16[528,128]{1,0:T(8,128)(2,1)S(1)}, bf16[528,128]{1,0:T(8,128)(2,1)S(1)}, u32[]{:S(2)}, u32[]{:S(2)}) collective-permute-start(bf16[528,128]{1,0:T(8,128)(2,1)S(1)} %get-tuple-element.80), channel_id=1, source_target_pairs={{0,24},{4,28},{8,0},{12,4},{16,8},{20,12},{24,16},{28,20},{1,25},{... | collective-permute-start | bytes 405512 | tf_op jit(solution)/shard_map/ppermute | solution.py:238
  43.0 0.6 collective-permute-start.11
  43.6 0.0 collective-permute-done.8.refs_2_
  43.6 0.0 copy-start.2
  43.6 0.0 copy-start.3
  43.6 0.2 collective-permute-start.12
  43.7 0.0 collective-permute-done.9.refs_3_
  43.7 0.0 collective-permute-done.7.refs_1_
  43.8 7.5 %prompt_part.3 = (f32[128,2688]{1,0:T(8,128)S(1)}, bf16[528,128]{1,0:T(8,128)(2,1)S(1)}, bf16[528,128]{1,0:T(8,128)(2,1)S(1)}, bf16[528,128]{1,0:T(8,128)(2,1)S(1)}, bf16[528,128]{1,0:T(8,128)(2,1)S(1)}) custom-call(s32[3]{0:T(128)S(1)} %pad_add_fusion.info_ref, bf16[8,2,2,32,128]{4,3,2,1,0:T(8,128)(2,1)S(1)} %collective-permute-done.5.refs_0_, ...), custom_call_target="tpu_custom_call" | custom-call | flops 3523215360 | bytes 5505024 | tf_op jit(solution)/shard_map/prompt_part/pallas_call | solution.py:195
  51.3 0.0 collective-permute-done.10.refs_1_
  51.3 0.0 collective-permute-done.11.refs_2_
  51.3 0.0 collective-permute-done.12.refs_3_
  51.3 3.5 %collective-permute-start.13 = (bf16[528,128]{1,0:T(8,128)(2,1)S(1)}, bf16[528,128]{1,0:T(8,128)(2,1)S(1)}, u32[]{:S(2)}, u32[]{:S(2)}) collective-permute-start(bf16[528,128]{1,0:T(8,128)(2,1)S(1)} %get-tuple-element.87), channel_id=1, source_target_pairs={{0,16},{4,20},{8,24},{12,28},{16,0},{20,4},{24,8},{28,12},{1,17},{... | collective-permute-start | bytes 405512 | tf_op jit(solution)/shard_map/ppermute | solution.py:238
  54.8 0.2 collective-permute-start.14
  55.0 2.3 %collective-permute-start.15 = (bf16[528,128]{1,0:T(8,128)(2,1)S(1)}, bf16[528,128]{1,0:T(8,128)(2,1)S(1)}, u32[]{:S(2)}, u32[]{:S(2)}) collective-permute-start(bf16[528,128]{1,0:T(8,128)(2,1)S(1)} %get-tuple-element.89), channel_id=1, source_target_pairs={{0,28},{4,24},{8,4},{12,0},{16,12},{20,8},{24,20},{28,16},{1,29},{... | collective-permute-start | bytes 405512 | tf_op jit(solution)/shard_map/ppermute | solution.py:238
  57.3 0.0 collective-permute-start.16
  57.3 0.0 copy-done.2
  57.3 0.0 copy-done.3
  57.3 4.2 %suffix_part.1 = (bf16[384,896]{1,0:T(8,128)(2,1)}, bf16[384,128]{1,0:T(8,128)(2,1)}, bf16[384,128]{1,0:T(8,128)(2,1)}) custom-call(bf16[384,896]{1,0:T(8,128)(2,1)S(1)} %bitcast.32, bf16[384,896]{1,0:T(8,128)(2,1)S(1)} %get-tuple-element.59.refs_5_.refs_1_, bf16[128,2688]{1,0:T(8,128)(2,1)S(1)} %get-tuple-element.60.refs_6_.refs_2_, ...), custom_call_target="tpu_custom_call" | custom-call | flops 1321205760 | bytes 5505024 | tf_op jit(solution)/shard_map/suffix_part/pallas_call | solution.py:146
  61.5 0.0 collective-permute-done.13.refs_4_
  61.5 0.4 collective-permute-done.14.refs_5_
  61.9 2.3 %collective-permute-done.15.refs_6_ = bf16[528,128]{1,0:T(8,128)(2,1)S(1)} collective-permute-done((bf16[528,128]{1,0:T(8,128)(2,1)S(1)}, bf16[528,128]{1,0:T(8,128)(2,1)S(1)}, u32[]{:S(2)}, u32[]{:S(2)}) %collective-permute-start.15) | collective-permute-done | bytes 135200 | tf_op jit(solution)/shard_map/ppermute | solution.py:238
  64.2 0.8 collective-permute-done.16.refs_7_
  65.0 0.4 group_sum.1
  65.4 14.8 %all_to_all.10 = bf16[8,128,128]{2,1,0:T(8,128)(2,1)S(1)} all-to-all(bf16[8,128,128]{2,1,0:T(8,128)(2,1)S(1)} %bitcast.27), channel_id=1, replica_groups=mesh['z'=8,'y'=4,'c'=2,'head'=4] {'z'}, dimensions={0} | all-to-all | bytes 524288 | tf_op jit(solution)/shard_map/all_to_all | solution.py:234
  80.3 0.6 slice_bitcast_fusion
  (2 shorter events, 0.0 us)
Async XLA Ops:
  0.6 25.1 %copy-start.4 = (f32[1,7,384]{2,0,1:T(1,128)S(1)}, f32[1,7,384]{2,0,1:T(1,128)}, u32[]{:S(2)}) copy-start(f32[1,7,384]{2,0,1:T(1,128)} %param.17) | copy-start | bytes 32260
  0.6 25.1 %copy-start = (bf16[1,384,896]{2,1,0:T(8,128)(2,1)S(1)}, bf16[1,384,896]{2,1,0:T(8,128)(2,1)}, u32[]{:S(2)}) copy-start(bf16[1,384,896]{2,1,0:T(8,128)(2,1)} %param.15) | copy-start | bytes 2064388
  0.7 25.1 %copy-start.1 = (bf16[1,384,896]{2,1,0:T(8,128)(2,1)S(1)}, bf16[1,384,896]{2,1,0:T(8,128)(2,1)}, u32[]{:S(2)}) copy-start(bf16[1,384,896]{2,1,0:T(8,128)(2,1)} %param.10) | copy-start | bytes 2064388
  2.2 20.3 %all-to-all-start = ((bf16[8,128,128]{2,1,0:T(8,128)(2,1)}), bf16[8,128,128]{2,1,0:T(8,128)(2,1)S(1)}, u32[]{:S(2)}, u32[]{:S(2)}) async-start(bf16[8,128,128]{2,1,0:T(8,128)(2,1)} %bitcast.41), calls=%async_computation | async-start | bytes 524288 | tf_op jit(solution)/shard_map/all_to_all | solution.py:234
  11.9 13.7 %collective-permute-start.2 = (bf16[96,896]{1,0:T(8,128)(2,1)S(1)}, bf16[96,896]{1,0:T(8,128)(2,1)S(1)}, u32[]{:S(2)}, u32[]{:S(2)}) collective-permute-start(bf16[96,896]{1,0:T(8,128)(2,1)S(1)} %get-tuple-element.101), channel_id=1, source_target_pairs={{0,3},{1,2},{2,1},{3,0},{4,7},{5,6},{6,5},{7,4},{8,11},{9,10},{10,... | collective-permute-start | bytes 516104 | tf_op jit(solution)/shard_map/ppermute | solution.py:238
  12.5 13.1 %collective-permute-start = (bf16[96,896]{1,0:T(8,128)(2,1)S(1)}, bf16[96,896]{1,0:T(8,128)(2,1)S(1)}, u32[]{:S(2)}, u32[]{:S(2)}) collective-permute-start(bf16[96,896]{1,0:T(8,128)(2,1)S(1)} %get-tuple-element.102), channel_id=1, source_target_pairs={{0,1},{1,0},{2,3},{3,2},{4,5},{5,4},{6,7},{7,6},{8,9},{9,8},{10,11... | collective-permute-start | bytes 516104 | tf_op jit(solution)/shard_map/ppermute | solution.py:238
  13.4 12.2 %collective-permute-start.1 = (bf16[96,896]{1,0:T(8,128)(2,1)S(1)}, bf16[96,896]{1,0:T(8,128)(2,1)S(1)}, u32[]{:S(2)}, u32[]{:S(2)}) collective-permute-start(bf16[96,896]{1,0:T(8,128)(2,1)S(1)} %get-tuple-element.104), channel_id=1, source_target_pairs={{0,2},{1,3},{2,0},{3,1},{4,6},{5,7},{6,4},{7,5},{8,10},{9,11},{10,... | collective-permute-start | bytes 516104 | tf_op jit(solution)/shard_map/ppermute | solution.py:238
  22.6 6.9 %collective-permute-start.4 = (bf16[8,2,2,32,128]{4,3,2,1,0:T(8,128)(2,1)S(1)}, bf16[8,2,2,32,128]{4,3,2,1,0:T(8,128)(2,1)S(1)}, u32[]{:S(2)}, u32[]{:S(2)}) collective-permute-start(bf16[8,2,2,32,128]{4,3,2,1,0:T(8,128)(2,1)S(1)} %bitcast.33), channel_id=1, source_target_pairs={{0,24},{8,0},{16,8},{24,16},{1,25},{9,1},{17,9},{25,17},{2,26},{10... | collective-permute-start | bytes 786440 | tf_op jit(solution)/shard_map/ppermute | solution.py:238
  25.6 7.6 %collective-permute-start.3 = (bf16[8,2,2,32,128]{4,3,2,1,0:T(8,128)(2,1)S(1)}, bf16[8,2,2,32,128]{4,3,2,1,0:T(8,128)(2,1)S(1)}, u32[]{:S(2)}, u32[]{:S(2)}) collective-permute-start(bf16[8,2,2,32,128]{4,3,2,1,0:T(8,128)(2,1)S(1)} %bitcast.34), channel_id=1, source_target_pairs={{0,8},{8,16},{16,24},{24,0},{1,9},{9,17},{17,25},{25,1},{2,10},{10... | collective-permute-start | bytes 786440 | tf_op jit(solution)/shard_map/ppermute | solution.py:238
  25.6 8.1 %collective-permute-start.6 = (bf16[8,2,2,32,128]{4,3,2,1,0:T(8,128)(2,1)S(1)}, bf16[8,2,2,32,128]{4,3,2,1,0:T(8,128)(2,1)S(1)}, u32[]{:S(2)}, u32[]{:S(2)}) collective-permute-start(bf16[8,2,2,32,128]{4,3,2,1,0:T(8,128)(2,1)S(1)} %bitcast.35), channel_id=1, source_target_pairs={{0,4},{4,0},{1,5},{5,1},{2,6},{6,2},{3,7},{7,3},{8,12},{12,8},{9,1... | collective-permute-start | bytes 786440 | tf_op jit(solution)/shard_map/ppermute | solution.py:238
  33.2 8.2 %collective-permute-start.5 = (bf16[8,2,2,32,128]{4,3,2,1,0:T(8,128)(2,1)S(1)}, bf16[8,2,2,32,128]{4,3,2,1,0:T(8,128)(2,1)S(1)}, u32[]{:S(2)}, u32[]{:S(2)}) collective-permute-start(bf16[8,2,2,32,128]{4,3,2,1,0:T(8,128)(2,1)S(1)} %bitcast.36), channel_id=1, source_target_pairs={{0,16},{8,24},{16,0},{24,8},{1,17},{9,25},{17,1},{25,9},{2,18},{10... | collective-permute-start | bytes 786440 | tf_op jit(solution)/shard_map/ppermute | solution.py:238
  33.2 10.4 %collective-permute-start.8 = (bf16[8,2,2,32,128]{4,3,2,1,0:T(8,128)(2,1)S(1)}, bf16[8,2,2,32,128]{4,3,2,1,0:T(8,128)(2,1)S(1)}, u32[]{:S(2)}, u32[]{:S(2)}) collective-permute-start(bf16[8,2,2,32,128]{4,3,2,1,0:T(8,128)(2,1)S(1)} %collective-permute-done.3.refs_1_), channel_id=1, source_target_pairs={{0,4},{4,0},{1,5},{5,1},{2,6},{6,2},{3,7},{7,3},{8,12},{12,8},{9,1... | collective-permute-start | bytes 786440 | tf_op jit(solution)/shard_map/ppermute | solution.py:238
  33.2 10.5 %collective-permute-start.9 = (bf16[8,2,2,32,128]{4,3,2,1,0:T(8,128)(2,1)S(1)}, bf16[8,2,2,32,128]{4,3,2,1,0:T(8,128)(2,1)S(1)}, u32[]{:S(2)}, u32[]{:S(2)}) collective-permute-start(bf16[8,2,2,32,128]{4,3,2,1,0:T(8,128)(2,1)S(1)} %collective-permute-done.4.refs_2_), channel_id=1, source_target_pairs={{0,4},{4,0},{1,5},{5,1},{2,6},{6,2},{3,7},{7,3},{8,12},{12,8},{9,1... | collective-permute-start | bytes 786440 | tf_op jit(solution)/shard_map/ppermute | solution.py:238
  41.4 2.4 %collective-permute-start.7 = (bf16[8,2,2,32,128]{4,3,2,1,0:T(8,128)(2,1)S(1)}, bf16[8,2,2,32,128]{4,3,2,1,0:T(8,128)(2,1)S(1)}, u32[]{:S(2)}, u32[]{:S(2)}) collective-permute-start(bf16[8,2,2,32,128]{4,3,2,1,0:T(8,128)(2,1)S(1)} %collective-permute-done.5.refs_0_), channel_id=1, source_target_pairs={{0,4},{4,0},{1,5},{5,1},{2,6},{6,2},{3,7},{7,3},{8,12},{12,8},{9,1... | collective-permute-start | bytes 786440 | tf_op jit(solution)/shard_map/ppermute | solution.py:238
  41.5 9.8 %collective-permute-start.10 = (bf16[528,128]{1,0:T(8,128)(2,1)S(1)}, bf16[528,128]{1,0:T(8,128)(2,1)S(1)}, u32[]{:S(2)}, u32[]{:S(2)}) collective-permute-start(bf16[528,128]{1,0:T(8,128)(2,1)S(1)} %get-tuple-element.80), channel_id=1, source_target_pairs={{0,24},{4,28},{8,0},{12,4},{16,8},{20,12},{24,16},{28,20},{1,25},{... | collective-permute-start | bytes 405512 | tf_op jit(solution)/shard_map/ppermute | solution.py:238
  43.0 8.3 %collective-permute-start.11 = (bf16[528,128]{1,0:T(8,128)(2,1)S(1)}, bf16[528,128]{1,0:T(8,128)(2,1)S(1)}, u32[]{:S(2)}, u32[]{:S(2)}) collective-permute-start(bf16[528,128]{1,0:T(8,128)(2,1)S(1)} %get-tuple-element.81), channel_id=1, source_target_pairs={{0,8},{4,12},{8,16},{12,20},{16,24},{20,28},{24,0},{28,4},{1,9},{5... | collective-permute-start | bytes 405512 | tf_op jit(solution)/shard_map/ppermute | solution.py:238
  43.6 13.7 %copy-start.2 = (bf16[1,384,128]{2,1,0:T(8,128)(2,1)S(1)}, bf16[1,384,128]{2,1,0:T(8,128)(2,1)}, u32[]{:S(2)}) copy-start(bf16[1,384,128]{2,1,0:T(8,128)(2,1)} %param.11) | copy-start | bytes 294916
  43.6 13.7 %copy-start.3 = (bf16[1,384,128]{2,1,0:T(8,128)(2,1)S(1)}, bf16[1,384,128]{2,1,0:T(8,128)(2,1)}, u32[]{:S(2)}) copy-start(bf16[1,384,128]{2,1,0:T(8,128)(2,1)} %param.12) | copy-start | bytes 294916
  43.6 7.7 %collective-permute-start.12 = (bf16[528,128]{1,0:T(8,128)(2,1)S(1)}, bf16[528,128]{1,0:T(8,128)(2,1)S(1)}, u32[]{:S(2)}, u32[]{:S(2)}) collective-permute-start(bf16[528,128]{1,0:T(8,128)(2,1)S(1)} %get-tuple-element.82), channel_id=1, source_target_pairs={{0,4},{4,0},{8,12},{12,8},{16,20},{20,16},{24,28},{28,24},{1,5},{5... | collective-permute-start | bytes 405512 | tf_op jit(solution)/shard_map/ppermute | solution.py:238
  51.3 10.2 %collective-permute-start.13 = (bf16[528,128]{1,0:T(8,128)(2,1)S(1)}, bf16[528,128]{1,0:T(8,128)(2,1)S(1)}, u32[]{:S(2)}, u32[]{:S(2)}) collective-permute-start(bf16[528,128]{1,0:T(8,128)(2,1)S(1)} %get-tuple-element.87), channel_id=1, source_target_pairs={{0,16},{4,20},{8,24},{12,28},{16,0},{20,4},{24,8},{28,12},{1,17},{... | collective-permute-start | bytes 405512 | tf_op jit(solution)/shard_map/ppermute | solution.py:238
  54.8 7.1 %collective-permute-start.14 = (bf16[528,128]{1,0:T(8,128)(2,1)S(1)}, bf16[528,128]{1,0:T(8,128)(2,1)S(1)}, u32[]{:S(2)}, u32[]{:S(2)}) collective-permute-start(bf16[528,128]{1,0:T(8,128)(2,1)S(1)} %get-tuple-element.88), channel_id=1, source_target_pairs={{0,20},{4,16},{8,28},{12,24},{16,4},{20,0},{24,12},{28,8},{1,21},{... | collective-permute-start | bytes 405512 | tf_op jit(solution)/shard_map/ppermute | solution.py:238
  55.0 9.3 %collective-permute-start.15 = (bf16[528,128]{1,0:T(8,128)(2,1)S(1)}, bf16[528,128]{1,0:T(8,128)(2,1)S(1)}, u32[]{:S(2)}, u32[]{:S(2)}) collective-permute-start(bf16[528,128]{1,0:T(8,128)(2,1)S(1)} %get-tuple-element.89), channel_id=1, source_target_pairs={{0,28},{4,24},{8,4},{12,0},{16,12},{20,8},{24,20},{28,16},{1,29},{... | collective-permute-start | bytes 405512 | tf_op jit(solution)/shard_map/ppermute | solution.py:238
  57.3 7.7 %collective-permute-start.16 = (bf16[528,128]{1,0:T(8,128)(2,1)S(1)}, bf16[528,128]{1,0:T(8,128)(2,1)S(1)}, u32[]{:S(2)}, u32[]{:S(2)}) collective-permute-start(bf16[528,128]{1,0:T(8,128)(2,1)S(1)} %get-tuple-element.90), channel_id=1, source_target_pairs={{0,12},{4,8},{8,20},{12,16},{16,28},{20,24},{24,4},{28,0},{1,13},{... | collective-permute-start | bytes 405512 | tf_op jit(solution)/shard_map/ppermute | solution.py:238

commit v8 on v7

--- a/solution.py
+++ b/solution.py
@@ -102,20 +102,33 @@
     )(info, query, attn_out, log_norm, *grads)
 
 
-def attend_head(head, row_refs, key_rows, value_rows, key_t, visible=None):
+def attend_heads(row_refs, key_rows, value_rows, emit, visible=None):
     query_ref, grad_rows_ref, query_t_ref, grad_t_ref, norm_row_ref, delta_row_ref = row_refs
     width = key_rows.shape[1]
     seq_len = query_ref.shape[0]
-    cols = slice(head * width, (head + 1) * width)
-    rows = slice(head * seq_len, (head + 1) * seq_len)
-    weights_t, score_grad_t = score_blocks(
-        key_rows, value_rows, query_t_ref[:, rows], grad_t_ref[:, rows],
-        norm_row_ref[:, rows], delta_row_ref[:, rows], visible,
-    )
-    query_part = jnp.dot(key_t, score_grad_t, preferred_element_type=F32)
-    key_part = jnp.dot(score_grad_t, query_ref[:, cols], preferred_element_type=F32)
-    value_part = jnp.dot(weights_t, grad_rows_ref[:, cols], preferred_element_type=F32)
-    return rows, cols, query_part, key_part, value_part
+    head_count = query_ref.shape[1] // width
+    key_t = key_rows.T
+    key_acc = jnp.zeros(key_rows.shape, F32)
+    value_acc = jnp.zeros(key_rows.shape, F32)
+
+    def scores_of(head):
+        rows = slice(head * seq_len, (head + 1) * seq_len)
+        return score_blocks(
+            key_rows, value_rows, query_t_ref[:, rows], grad_t_ref[:, rows],
+            norm_row_ref[:, rows], delta_row_ref[:, rows], visible,
+        )
+
+    ahead = scores_of(0)
+    for head in range(head_count):
+        weights_t, score_grad_t = ahead
+        if head + 1 < head_count:
+            ahead = scores_of(head + 1)
+        cols = slice(head * width, (head + 1) * width)
+        rows = slice(head * seq_len, (head + 1) * seq_len)
+        emit(rows, cols, jnp.dot(key_t, score_grad_t, preferred_element_type=F32))
+        key_acc += jnp.dot(score_grad_t, query_ref[:, cols], preferred_element_type=F32)
+        value_acc += jnp.dot(weights_t, grad_rows_ref[:, cols], preferred_element_type=F32)
+    return key_acc.astype(BF16), value_acc.astype(BF16)
 
 
 def suffix_kernel(*refs):
@@ -125,19 +138,13 @@
     key_at = lax.broadcasted_iota(jnp.int32, (seq_len, seq_len), 0)
     query_at = lax.broadcasted_iota(jnp.int32, (seq_len, seq_len), 1)
     causal = key_at <= query_at
-    key_rows, value_rows = key_ref[...], value_ref[...]
-    key_t = key_rows.T
-    key_acc = jnp.zeros((seq_len, width), F32)
-    value_acc = jnp.zeros((seq_len, width), F32)
-    for head in range(query_grad_ref.shape[1] // width):
-        rows, cols, query_part, key_part, value_part = attend_head(
-            head, row_refs, key_rows, value_rows, key_t, causal
-        )
+
+    def emit(rows, cols, query_part):
         query_grad_ref[:, cols] = (query_part + query_acc_ref[:, rows]).T.astype(BF16)
-        key_acc += key_part
-        value_acc += value_part
-    key_grad_ref[...] = key_acc.astype(BF16)
-    value_grad_ref[...] = value_acc.astype(BF16)
+
+    key_grad_ref[...], value_grad_ref[...] = attend_heads(
+        row_refs, key_ref[...], value_ref[...], emit, causal
+    )
 
 
 def suffix_part(rows, query_acc, key_suffix, value_suffix):
@@ -165,19 +172,11 @@
         parts = [ref[:, chosen, which] for ref in pair_refs]
         return jnp.concatenate([part.reshape(-1, width) for part in parts], 0)
 
-    key_rows, value_rows = rows_of(0), rows_of(1)
-    key_t = key_rows.T
-    key_acc = jnp.zeros(key_rows.shape, F32)
-    value_acc = jnp.zeros(key_rows.shape, F32)
-    for head in range(row_refs[0].shape[1] // width):
-        rows, _, query_part, key_part, value_part = attend_head(
-            head, row_refs, key_rows, value_rows, key_t
-        )
+    def emit(rows, cols, query_part):
         query_out_ref[:, rows] = query_part if first else query_part + query_acc_ref[:, rows]
-        key_acc += key_part
-        value_acc += value_part
-    size = key_rows.shape[0] // count
-    key_grad, value_grad = key_acc.astype(BF16), value_acc.astype(BF16)
+
+    key_grad, value_grad = attend_heads(row_refs, rows_of(0), rows_of(1), emit)
+    size = key_grad.shape[0] // count
     mark = jnp.full((MARK, width), chosen.astype(F32), F32).astype(BF16)
     for i, ref in enumerate(pair_grad_refs):
         ref[:size] = key_grad[i * size : (i + 1) * size]
@@ -285,9 +284,12 @@
     far, query_acc = lax.optimization_barrier((far, query_acc))
     far_other = trade(far, "c", lambda j: j ^ 1)
     send(parts, [(0, 0), (1, 0), (lines - 1, 0), (0, 1)])
-    query_acc, *parts = prompt_part(info, [far, far_other, *beside_other], rows, query_acc)
+    query_acc, *parts = prompt_part(info, [far, far_other], rows, query_acc)
+    query_acc, beside_other, shares = lax.optimization_barrier((query_acc, beside_other, shares))
+    send(parts, [(2, 0), (2, 1)])
+    query_acc, *parts = prompt_part(info, beside_other, rows, query_acc)
     parts, shares = lax.optimization_barrier((parts, shares))
-    send(parts, [(2, 0), (2, 1), (1, 1), (lines - 1, 1)])
+    send(parts, [(1, 1), (lines - 1, 1)])
 
     query_grad, key_grad, value_grad = suffix_part(rows, query_acc, key_suffix[0], value_suffix[0])
     key_grad, shares = lax.optimization_barrier((key_grad, shares))

time: 82.2 us -> 83.9 us (1.021); the launches traced: 80.9 us -> 83.6 us
  waiting for transfers between devices: 14.2 us -> 18.3 us
  starting transfers between devices: 25.2 us -> 22.9 us
    ppermute x17, waiting for transfers between devices: 9.75 us -> 13.8 us  [trade(): lax.ppermute(block, axis, [(i, target(i)) for i in range(lax.axis_size(ax...]
    ppermute x17, starting transfers between devices: 16.8 us -> 14.4 us  [trade(): lax.ppermute(block, axis, [(i, target(i)) for i in range(lax.axis_size(ax...]
    pallas_call x2 -> x3, Pallas kernels: 15.1 us -> 15.8 us  [prompt_part(): pl.pallas_call(functools.partial(prompt_kernel, count=len(pairs), first=q...]
  transfers between devices with their start and end apart: 18 -> 18, of which waited for: 6 -> 8; matrix products, arithmetic and copies ran while one was open for 2% -> 2% of each run, Pallas kernels for 25% -> 25%
where the time goes in v8:
time: 83.9 us; the launch traced here: 83.6 us
  starting transfers between devices  22.9 us (27%)
  Pallas kernels  22.7 us (27%)
  waiting for transfers between devices  18.3 us (22%)
  blocking collectives  15.6 us (19%)
  between operations  2.07 us (2%)
  local copies, waits for them, and re-layouts  1.86 us (2%)
    pallas_call x3, Pallas kernels, prompt_part(): pl.pallas_call(functools.partial(prompt_kernel, count=len(pairs), first=q...  15.8 us
    all_to_all x1, blocking collectives, exchange(): return lax.all_to_all(blocks, axes, split_axis=0, concat_axis=0, tiled=True)  15.6 us
    ppermute x17, starting transfers between devices, trade(): lax.ppermute(block, axis, [(i, target(i)) for i in range(lax.axis_size(ax...  14.4 us
    ppermute x17, waiting for transfers between devices, trade(): lax.ppermute(block, axis, [(i, target(i)) for i in range(lax.axis_size(ax...  13.8 us
    all_to_all x1, starting transfers between devices, exchange(): return lax.all_to_all(blocks, axes, split_axis=0, concat_axis=0, tiled=True)  8.47 us
    all_to_all x1, waiting for transfers between devices, exchange(): return lax.all_to_all(blocks, axes, split_axis=0, concat_axis=0, tiled=True)  4.49 us
    pallas_call x1, Pallas kernels, suffix_part(): pl.pallas_call(suffix_kernel, in_specs=[VMEM] * (len(rows) + 3), out_spec...  3.67 us
  transfers between devices with their start and end apart: 18, of which 8 were waited for; matrix products, arithmetic and copies ran while one was open for 2% of the time, Pallas kernels for 25%

profile of v8, /device:TPU:6, one launch (start us, length us, event | category | flops | bytes accessed | tf_op | source)
XLA Modules:
  0.0 83.6 jit_solution(3484942845515686344)
XLA Ops:
  0.6 0.0 copy-start.4
  0.6 0.0 copy-start
  0.7 0.0 copy-start.1
  0.7 1.6 %spread.1 = bf16[8,2,2,32,128]{4,3,2,1,0:T(8,128)(2,1)} custom-call(bf16[2,32,128]{2,1,0:T(8,128)(2,1)} %key_ref.1, bf16[2,32,128]{2,1,0:T(8,128)(2,1)} %value_ref.1), custom_call_target="tpu_custom_call" | custom-call | tf_op jit(solution)/shard_map/spread/pallas_call | solution.py:47
  2.2 8.5 %all-to-all-start = ((bf16[8,128,128]{2,1,0:T(8,128)(2,1)}), bf16[8,128,128]{2,1,0:T(8,128)(2,1)S(1)}, u32[]{:S(2)}, u32[]{:S(2)}) async-start(bf16[8,128,128]{2,1,0:T(8,128)(2,1)} %bitcast.42), calls=%async_computation | async-start | bytes 524288 | tf_op jit(solution)/shard_map/all_to_all | solution.py:233
  10.7 1.2 %dynamic-slice_bitcast_fusion = (bf16[96,896]{1,0:T(8,128)(2,1)S(1)}, bf16[96,896]{1,0:T(8,128)(2,1)S(1)}, bf16[96,896]{1,0:T(8,128)(2,1)S(1)}, bf16[96,896]{1,0:T(8,128)(2,1)S(1)}) fusion(bf16[1,96,3584]{2,1,0:T(8,128)(2,1)} %param.16, s32[]{:T(128)S(6)} %select_n.15, s32[]{:T(128)S(6)} %select_n.13, s32[]{:T(128)S(6)} %select_n.12, s32[]{:T(128)S(6)} %select_n.14), kind=kLoop, calls=%fused_computation | loop fusion | bytes 1376272 | tf_op jit(solution)/shard_map/dynamic_slice | solution.py:255
  11.9 0.6 collective-permute-start.2
  12.5 0.9 %collective-permute-start = (bf16[96,896]{1,0:T(8,128)(2,1)S(1)}, bf16[96,896]{1,0:T(8,128)(2,1)S(1)}, u32[]{:S(2)}, u32[]{:S(2)}) collective-permute-start(bf16[96,896]{1,0:T(8,128)(2,1)S(1)} %get-tuple-element.118), channel_id=1, source_target_pairs={{0,1},{1,0},{2,3},{3,2},{4,5},{5,4},{6,7},{7,6},{8,9},{9,8},{10,11... | collective-permute-start | bytes 516104 | tf_op jit(solution)/shard_map/ppermute | solution.py:237
  13.4 3.3 %collective-permute-start.1 = (bf16[96,896]{1,0:T(8,128)(2,1)S(1)}, bf16[96,896]{1,0:T(8,128)(2,1)S(1)}, u32[]{:S(2)}, u32[]{:S(2)}) collective-permute-start(bf16[96,896]{1,0:T(8,128)(2,1)S(1)} %get-tuple-element.120), channel_id=1, source_target_pairs={{0,2},{1,3},{2,0},{3,1},{4,6},{5,7},{6,4},{7,5},{8,10},{9,11},{10,... | collective-permute-start | bytes 516104 | tf_op jit(solution)/shard_map/ppermute | solution.py:237
  18.0 0.1 pad_add_fusion.info_ref
  18.1 4.5 %all-to-all-done = bf16[8,128,128]{2,1,0:T(8,128)(2,1)S(1)} async-done(((bf16[8,128,128]{2,1,0:T(8,128)(2,1)}), bf16[8,128,128]{2,1,0:T(8,128)(2,1)S(1)}, u32[]{:S(2)}, u32[]{:S(2)}) %all-to-all-start) | async-done | bytes 262176 | tf_op jit(solution)/shard_map/all_to_all | solution.py:233
  22.6 3.0 %collective-permute-start.4 = (bf16[8,2,2,32,128]{4,3,2,1,0:T(8,128)(2,1)S(1)}, bf16[8,2,2,32,128]{4,3,2,1,0:T(8,128)(2,1)S(1)}, u32[]{:S(2)}, u32[]{:S(2)}) collective-permute-start(bf16[8,2,2,32,128]{4,3,2,1,0:T(8,128)(2,1)S(1)} %bitcast.34), channel_id=1, source_target_pairs={{0,24},{8,0},{16,8},{24,16},{1,25},{9,1},{17,9},{25,17},{2,26},{10... | collective-permute-start | bytes 786440 | tf_op jit(solution)/shard_map/ppermute | solution.py:237
  25.6 0.0 collective-permute-start.3
  25.6 0.0 collective-permute-done.2.refs_3_
  25.6 0.0 collective-permute-done.refs_1_
  25.6 0.0 collective-permute-done.1.refs_2_
  25.6 0.1 collective-permute-start.6
  25.7 0.0 copy-done.4
  25.7 0.0 copy-done
  25.8 0.0 copy-done.1
  25.8 1.2 %prepare.1 = (bf16[384,896]{1,0:T(8,128)(2,1)S(1)}, bf16[128,2688]{1,0:T(8,128)(2,1)S(1)}, bf16[128,2688]{1,0:T(8,128)(2,1)S(1)}, f32[1,2688]{1,0:T(1,128)S(1)}, f32[1,2688]{1,0:T(1,128)S(1)}) custom-call(s32[3]{0:T(128)S(1)} %pad_add_fusion.info_ref, bf16[384,896]{1,0:T(8,128)(2,1)S(1)} %bitcast.29, bf16[384,896]{1,0:T(8,128)(2,1)S(1)} %bitcast.28, ...), custom_call_target="tpu_custom_call" | custom-call | flops 688128 | bytes 4128768 | tf_op jit(solution)/shard_map/prepare/pallas_call | solution.py:86
  27.0 2.5 %collective-permute-done.4.refs_2_ = bf16[8,2,2,32,128]{4,3,2,1,0:T(8,128)(2,1)S(1)} collective-permute-done((bf16[8,2,2,32,128]{4,3,2,1,0:T(8,128)(2,1)S(1)}, bf16[8,2,2,32,128]{4,3,2,1,0:T(8,128)(2,1)S(1)}, u32[]{:S(2)}, u32[]{:S(2)}) %collective-permute-start.4) | collective-permute-done | bytes 262176 | tf_op jit(solution)/shard_map/ppermute | solution.py:237
  29.5 3.7 %collective-permute-done.3.refs_1_ = bf16[8,2,2,32,128]{4,3,2,1,0:T(8,128)(2,1)S(1)} collective-permute-done((bf16[8,2,2,32,128]{4,3,2,1,0:T(8,128)(2,1)S(1)}, bf16[8,2,2,32,128]{4,3,2,1,0:T(8,128)(2,1)S(1)}, u32[]{:S(2)}, u32[]{:S(2)}) %collective-permute-start.3) | collective-permute-done | bytes 262176 | tf_op jit(solution)/shard_map/ppermute | solution.py:237
  33.2 0.0 collective-permute-start.5
  33.2 0.0 collective-permute-done.6.refs_3_
  33.2 7.6 %prompt_part.3 = (f32[128,2688]{1,0:T(8,128)S(1)}, bf16[528,128]{1,0:T(8,128)(2,1)S(1)}, bf16[528,128]{1,0:T(8,128)(2,1)S(1)}, bf16[528,128]{1,0:T(8,128)(2,1)S(1)}, bf16[528,128]{1,0:T(8,128)(2,1)S(1)}) custom-call(s32[3]{0:T(128)S(1)} %pad_add_fusion.info_ref, bf16[8,2,2,32,128]{4,3,2,1,0:T(8,128)(2,1)S(1)} %bitcast.38, ...), custom_call_target="tpu_custom_call" | custom-call | flops 3523215360 | bytes 5505024 | tf_op jit(solution)/shard_map/prompt_part/pallas_call | solution.py:194
  40.8 0.3 collective-permute-done.5.refs_0_
  41.1 0.0 collective-permute-start.7
  41.1 0.5 collective-permute-start.8
  41.6 0.0 collective-permute-start.9
  41.6 1.4 %collective-permute-start.10 = (bf16[528,128]{1,0:T(8,128)(2,1)S(1)}, bf16[528,128]{1,0:T(8,128)(2,1)S(1)}, u32[]{:S(2)}, u32[]{:S(2)}) collective-permute-start(bf16[528,128]{1,0:T(8,128)(2,1)S(1)} %get-tuple-element.82), channel_id=1, source_target_pairs={{0,24},{4,28},{8,0},{12,4},{16,8},{20,12},{24,16},{28,20},{1,25},{... | collective-permute-start | bytes 405512 | tf_op jit(solution)/shard_map/ppermute | solution.py:237
  42.9 0.7 collective-permute-start.11
  43.6 0.0 collective-permute-done.7.refs_1_
  43.6 0.0 collective-permute-start.12
  43.6 4.1 %prompt_part.4 = (f32[128,2688]{1,0:T(8,128)S(1)}, bf16[528,128]{1,0:T(8,128)(2,1)S(1)}, bf16[528,128]{1,0:T(8,128)(2,1)S(1)}) custom-call(s32[3]{0:T(128)S(1)} %pad_add_fusion.info_ref, bf16[8,2,2,32,128]{4,3,2,1,0:T(8,128)(2,1)S(1)} %collective-permute-done.5.refs_0_, bf16[8,2,2,32,128]{4,3,2,1,0:T(8,128)(2,1)S(1)} %collective-permute-done.7.refs_1_, ...), custom_call_target="tpu_custom_call" | custom-call | flops 1761607680 | bytes 5505024 | tf_op jit(solution)/shard_map/prompt_part/pallas_call | solution.py:194
  47.7 0.0 collective-permute-done.10.refs_1_
  47.7 2.0 %collective-permute-done.11.refs_2_ = bf16[528,128]{1,0:T(8,128)(2,1)S(1)} collective-permute-done((bf16[528,128]{1,0:T(8,128)(2,1)S(1)}, bf16[528,128]{1,0:T(8,128)(2,1)S(1)}, u32[]{:S(2)}, u32[]{:S(2)}) %collective-permute-start.11) | collective-permute-done | bytes 135200 | tf_op jit(solution)/shard_map/ppermute | solution.py:237
  49.8 0.0 collective-permute-done.12.refs_3_
  49.8 0.0 collective-permute-done.8.refs_0_
  49.8 0.0 collective-permute-done.9.refs_1_
  49.8 1.5 %collective-permute-start.13 = (bf16[528,128]{1,0:T(8,128)(2,1)S(1)}, bf16[528,128]{1,0:T(8,128)(2,1)S(1)}, u32[]{:S(2)}, u32[]{:S(2)}) collective-permute-start(bf16[528,128]{1,0:T(8,128)(2,1)S(1)} %get-tuple-element.97), channel_id=1, source_target_pairs={{0,16},{4,20},{8,24},{12,28},{16,0},{20,4},{24,8},{28,12},{1,17},{... | collective-permute-start | bytes 405512 | tf_op jit(solution)/shard_map/ppermute | solution.py:237
  51.3 0.0 copy-start.2
  51.3 0.0 copy-start.3
  51.3 0.8 collective-permute-start.14
  52.1 4.1 %prompt_part.5 = (f32[128,2688]{1,0:T(8,128)S(1)}, bf16[528,128]{1,0:T(8,128)(2,1)S(1)}, bf16[528,128]{1,0:T(8,128)(2,1)S(1)}) custom-call(s32[3]{0:T(128)S(1)} %pad_add_fusion.info_ref, bf16[8,2,2,32,128]{4,3,2,1,0:T(8,128)(2,1)S(1)} %collective-permute-done.8.refs_0_, bf16[8,2,2,32,128]{4,3,2,1,0:T(8,128)(2,1)S(1)} %collective-permute-done.9.refs_1_, ...), custom_call_target="tpu_custom_call" | custom-call | flops 1761607680 | bytes 5505024 | tf_op jit(solution)/shard_map/prompt_part/pallas_call | solution.py:194
  56.2 0.8 collective-permute-done.13.refs_4_
  57.0 1.7 %collective-permute-done.14.refs_5_ = bf16[528,128]{1,0:T(8,128)(2,1)S(1)} collective-permute-done((bf16[528,128]{1,0:T(8,128)(2,1)S(1)}, bf16[528,128]{1,0:T(8,128)(2,1)S(1)}, u32[]{:S(2)}, u32[]{:S(2)}) %collective-permute-start.14) | collective-permute-done | bytes 135200 | tf_op jit(solution)/shard_map/ppermute | solution.py:237
  58.7 1.6 %collective-permute-start.15 = (bf16[528,128]{1,0:T(8,128)(2,1)S(1)}, bf16[528,128]{1,0:T(8,128)(2,1)S(1)}, u32[]{:S(2)}, u32[]{:S(2)}) collective-permute-start(bf16[528,128]{1,0:T(8,128)(2,1)S(1)} %get-tuple-element.105), channel_id=1, source_target_pairs={{0,28},{4,24},{8,4},{12,0},{16,12},{20,8},{24,20},{28,16},{1,29},{... | collective-permute-start | bytes 405512 | tf_op jit(solution)/shard_map/ppermute | solution.py:237
  60.3 0.1 collective-permute-start.16
  60.4 0.0 copy-done.2
  60.4 0.0 copy-done.3
  60.4 3.7 %suffix_part.1 = (bf16[384,896]{1,0:T(8,128)(2,1)}, bf16[384,128]{1,0:T(8,128)(2,1)}, bf16[384,128]{1,0:T(8,128)(2,1)}) custom-call(bf16[384,896]{1,0:T(8,128)(2,1)S(1)} %bitcast.33, bf16[384,896]{1,0:T(8,128)(2,1)S(1)} %get-tuple-element.67.refs_5_.refs_3_.refs_1_, bf16[128,2688]{1,0:T(8,128)(2,1)S(1)} %get-tuple-element.68.refs_6_.refs_4_.refs_2_, ...), custom_call_target="tpu_custom_call" | custom-call | flops 1321205760 | bytes 5505024 | tf_op jit(solution)/shard_map/suffix_part/pallas_call | solution.py:153
  64.1 0.0 collective-permute-done.15.refs_6_
  64.1 2.8 %collective-permute-done.16.refs_7_ = bf16[528,128]{1,0:T(8,128)(2,1)S(1)} collective-permute-done((bf16[528,128]{1,0:T(8,128)(2,1)S(1)}, bf16[528,128]{1,0:T(8,128)(2,1)S(1)}, u32[]{:S(2)}, u32[]{:S(2)}) %collective-permute-start.16) | collective-permute-done | bytes 135200 | tf_op jit(solution)/shard_map/ppermute | solution.py:237
  66.9 0.4 group_sum.1
  67.3 15.6 %all_to_all.10 = bf16[8,128,128]{2,1,0:T(8,128)(2,1)S(1)} all-to-all(bf16[8,128,128]{2,1,0:T(8,128)(2,1)S(1)} %bitcast.27), channel_id=1, replica_groups=mesh['z'=8,'y'=4,'c'=2,'head'=4] {'z'}, dimensions={0} | all-to-all | bytes 524288 | tf_op jit(solution)/shard_map/all_to_all | solution.py:233
  83.0 0.6 slice_bitcast_fusion
  (2 shorter events, 0.0 us)
Async XLA Ops:
  0.6 25.1 %copy-start.4 = (f32[1,7,384]{2,0,1:T(1,128)S(1)}, f32[1,7,384]{2,0,1:T(1,128)}, u32[]{:S(2)}) copy-start(f32[1,7,384]{2,0,1:T(1,128)} %param.17) | copy-start | bytes 32260
  0.6 25.1 %copy-start = (bf16[1,384,896]{2,1,0:T(8,128)(2,1)S(1)}, bf16[1,384,896]{2,1,0:T(8,128)(2,1)}, u32[]{:S(2)}) copy-start(bf16[1,384,896]{2,1,0:T(8,128)(2,1)} %param.15) | copy-start | bytes 2064388
  0.7 25.1 %copy-start.1 = (bf16[1,384,896]{2,1,0:T(8,128)(2,1)S(1)}, bf16[1,384,896]{2,1,0:T(8,128)(2,1)}, u32[]{:S(2)}) copy-start(bf16[1,384,896]{2,1,0:T(8,128)(2,1)} %param.10) | copy-start | bytes 2064388
  2.2 20.3 %all-to-all-start = ((bf16[8,128,128]{2,1,0:T(8,128)(2,1)}), bf16[8,128,128]{2,1,0:T(8,128)(2,1)S(1)}, u32[]{:S(2)}, u32[]{:S(2)}) async-start(bf16[8,128,128]{2,1,0:T(8,128)(2,1)} %bitcast.42), calls=%async_computation | async-start | bytes 524288 | tf_op jit(solution)/shard_map/all_to_all | solution.py:233
  11.9 13.7 %collective-permute-start.2 = (bf16[96,896]{1,0:T(8,128)(2,1)S(1)}, bf16[96,896]{1,0:T(8,128)(2,1)S(1)}, u32[]{:S(2)}, u32[]{:S(2)}) collective-permute-start(bf16[96,896]{1,0:T(8,128)(2,1)S(1)} %get-tuple-element.117), channel_id=1, source_target_pairs={{0,3},{1,2},{2,1},{3,0},{4,7},{5,6},{6,5},{7,4},{8,11},{9,10},{10,... | collective-permute-start | bytes 516104 | tf_op jit(solution)/shard_map/ppermute | solution.py:237
  12.5 13.1 %collective-permute-start = (bf16[96,896]{1,0:T(8,128)(2,1)S(1)}, bf16[96,896]{1,0:T(8,128)(2,1)S(1)}, u32[]{:S(2)}, u32[]{:S(2)}) collective-permute-start(bf16[96,896]{1,0:T(8,128)(2,1)S(1)} %get-tuple-element.118), channel_id=1, source_target_pairs={{0,1},{1,0},{2,3},{3,2},{4,5},{5,4},{6,7},{7,6},{8,9},{9,8},{10,11... | collective-permute-start | bytes 516104 | tf_op jit(solution)/shard_map/ppermute | solution.py:237
  13.4 12.2 %collective-permute-start.1 = (bf16[96,896]{1,0:T(8,128)(2,1)S(1)}, bf16[96,896]{1,0:T(8,128)(2,1)S(1)}, u32[]{:S(2)}, u32[]{:S(2)}) collective-permute-start(bf16[96,896]{1,0:T(8,128)(2,1)S(1)} %get-tuple-element.120), channel_id=1, source_target_pairs={{0,2},{1,3},{2,0},{3,1},{4,6},{5,7},{6,4},{7,5},{8,10},{9,11},{10,... | collective-permute-start | bytes 516104 | tf_op jit(solution)/shard_map/ppermute | solution.py:237
  22.6 6.9 %collective-permute-start.4 = (bf16[8,2,2,32,128]{4,3,2,1,0:T(8,128)(2,1)S(1)}, bf16[8,2,2,32,128]{4,3,2,1,0:T(8,128)(2,1)S(1)}, u32[]{:S(2)}, u32[]{:S(2)}) collective-permute-start(bf16[8,2,2,32,128]{4,3,2,1,0:T(8,128)(2,1)S(1)} %bitcast.34), channel_id=1, source_target_pairs={{0,24},{8,0},{16,8},{24,16},{1,25},{9,1},{17,9},{25,17},{2,26},{10... | collective-permute-start | bytes 786440 | tf_op jit(solution)/shard_map/ppermute | solution.py:237
  25.6 7.6 %collective-permute-start.3 = (bf16[8,2,2,32,128]{4,3,2,1,0:T(8,128)(2,1)S(1)}, bf16[8,2,2,32,128]{4,3,2,1,0:T(8,128)(2,1)S(1)}, u32[]{:S(2)}, u32[]{:S(2)}) collective-permute-start(bf16[8,2,2,32,128]{4,3,2,1,0:T(8,128)(2,1)S(1)} %bitcast.35), channel_id=1, source_target_pairs={{0,8},{8,16},{16,24},{24,0},{1,9},{9,17},{17,25},{25,1},{2,10},{10... | collective-permute-start | bytes 786440 | tf_op jit(solution)/shard_map/ppermute | solution.py:237
  25.6 7.6 %collective-permute-start.6 = (bf16[8,2,2,32,128]{4,3,2,1,0:T(8,128)(2,1)S(1)}, bf16[8,2,2,32,128]{4,3,2,1,0:T(8,128)(2,1)S(1)}, u32[]{:S(2)}, u32[]{:S(2)}) collective-permute-start(bf16[8,2,2,32,128]{4,3,2,1,0:T(8,128)(2,1)S(1)} %bitcast.36), channel_id=1, source_target_pairs={{0,4},{4,0},{1,5},{5,1},{2,6},{6,2},{3,7},{7,3},{8,12},{12,8},{9,1... | collective-permute-start | bytes 786440 | tf_op jit(solution)/shard_map/ppermute | solution.py:237
  33.2 7.9 %collective-permute-start.5 = (bf16[8,2,2,32,128]{4,3,2,1,0:T(8,128)(2,1)S(1)}, bf16[8,2,2,32,128]{4,3,2,1,0:T(8,128)(2,1)S(1)}, u32[]{:S(2)}, u32[]{:S(2)}) collective-permute-start(bf16[8,2,2,32,128]{4,3,2,1,0:T(8,128)(2,1)S(1)} %bitcast.37), channel_id=1, source_target_pairs={{0,16},{8,24},{16,0},{24,8},{1,17},{9,25},{17,1},{25,9},{2,18},{10... | collective-permute-start | bytes 786440 | tf_op jit(solution)/shard_map/ppermute | solution.py:237
  41.1 2.5 %collective-permute-start.7 = (bf16[8,2,2,32,128]{4,3,2,1,0:T(8,128)(2,1)S(1)}, bf16[8,2,2,32,128]{4,3,2,1,0:T(8,128)(2,1)S(1)}, u32[]{:S(2)}, u32[]{:S(2)}) collective-permute-start(bf16[8,2,2,32,128]{4,3,2,1,0:T(8,128)(2,1)S(1)} %collective-permute-done.5.refs_0_), channel_id=1, source_target_pairs={{0,4},{4,0},{1,5},{5,1},{2,6},{6,2},{3,7},{7,3},{8,12},{12,8},{9,1... | collective-permute-start | bytes 786440 | tf_op jit(solution)/shard_map/ppermute | solution.py:237
  41.1 8.7 %collective-permute-start.8 = (bf16[8,2,2,32,128]{4,3,2,1,0:T(8,128)(2,1)S(1)}, bf16[8,2,2,32,128]{4,3,2,1,0:T(8,128)(2,1)S(1)}, u32[]{:S(2)}, u32[]{:S(2)}) collective-permute-start(bf16[8,2,2,32,128]{4,3,2,1,0:T(8,128)(2,1)S(1)} %collective-permute-done.3.refs_1_), channel_id=1, source_target_pairs={{0,4},{4,0},{1,5},{5,1},{2,6},{6,2},{3,7},{7,3},{8,12},{12,8},{9,1... | collective-permute-start | bytes 786440 | tf_op jit(solution)/shard_map/ppermute | solution.py:237
  41.6 8.2 %collective-permute-start.9 = (bf16[8,2,2,32,128]{4,3,2,1,0:T(8,128)(2,1)S(1)}, bf16[8,2,2,32,128]{4,3,2,1,0:T(8,128)(2,1)S(1)}, u32[]{:S(2)}, u32[]{:S(2)}) collective-permute-start(bf16[8,2,2,32,128]{4,3,2,1,0:T(8,128)(2,1)S(1)} %collective-permute-done.4.refs_2_), channel_id=1, source_target_pairs={{0,4},{4,0},{1,5},{5,1},{2,6},{6,2},{3,7},{7,3},{8,12},{12,8},{9,1... | collective-permute-start | bytes 786440 | tf_op jit(solution)/shard_map/ppermute | solution.py:237
  41.6 6.2 %collective-permute-start.10 = (bf16[528,128]{1,0:T(8,128)(2,1)S(1)}, bf16[528,128]{1,0:T(8,128)(2,1)S(1)}, u32[]{:S(2)}, u32[]{:S(2)}) collective-permute-start(bf16[528,128]{1,0:T(8,128)(2,1)S(1)} %get-tuple-element.82), channel_id=1, source_target_pairs={{0,24},{4,28},{8,0},{12,4},{16,8},{20,12},{24,16},{28,20},{1,25},{... | collective-permute-start | bytes 405512 | tf_op jit(solution)/shard_map/ppermute | solution.py:237
  42.9 6.8 %collective-permute-start.11 = (bf16[528,128]{1,0:T(8,128)(2,1)S(1)}, bf16[528,128]{1,0:T(8,128)(2,1)S(1)}, u32[]{:S(2)}, u32[]{:S(2)}) collective-permute-start(bf16[528,128]{1,0:T(8,128)(2,1)S(1)} %get-tuple-element.83), channel_id=1, source_target_pairs={{0,8},{4,12},{8,16},{12,20},{16,24},{20,28},{24,0},{28,4},{1,9},{5... | collective-permute-start | bytes 405512 | tf_op jit(solution)/shard_map/ppermute | solution.py:237
  43.6 6.2 %collective-permute-start.12 = (bf16[528,128]{1,0:T(8,128)(2,1)S(1)}, bf16[528,128]{1,0:T(8,128)(2,1)S(1)}, u32[]{:S(2)}, u32[]{:S(2)}) collective-permute-start(bf16[528,128]{1,0:T(8,128)(2,1)S(1)} %get-tuple-element.84), channel_id=1, source_target_pairs={{0,4},{4,0},{8,12},{12,8},{16,20},{20,16},{24,28},{28,24},{1,5},{5... | collective-permute-start | bytes 405512 | tf_op jit(solution)/shard_map/ppermute | solution.py:237
  49.8 7.2 %collective-permute-start.13 = (bf16[528,128]{1,0:T(8,128)(2,1)S(1)}, bf16[528,128]{1,0:T(8,128)(2,1)S(1)}, u32[]{:S(2)}, u32[]{:S(2)}) collective-permute-start(bf16[528,128]{1,0:T(8,128)(2,1)S(1)} %get-tuple-element.97), channel_id=1, source_target_pairs={{0,16},{4,20},{8,24},{12,28},{16,0},{20,4},{24,8},{28,12},{1,17},{... | collective-permute-start | bytes 405512 | tf_op jit(solution)/shard_map/ppermute | solution.py:237
  51.3 9.1 %copy-start.2 = (bf16[1,384,128]{2,1,0:T(8,128)(2,1)S(1)}, bf16[1,384,128]{2,1,0:T(8,128)(2,1)}, u32[]{:S(2)}) copy-start(bf16[1,384,128]{2,1,0:T(8,128)(2,1)} %param.11) | copy-start | bytes 294916
  51.3 9.1 %copy-start.3 = (bf16[1,384,128]{2,1,0:T(8,128)(2,1)S(1)}, bf16[1,384,128]{2,1,0:T(8,128)(2,1)}, u32[]{:S(2)}) copy-start(bf16[1,384,128]{2,1,0:T(8,128)(2,1)} %param.12) | copy-start | bytes 294916
  51.3 7.4 %collective-permute-start.14 = (bf16[528,128]{1,0:T(8,128)(2,1)S(1)}, bf16[528,128]{1,0:T(8,128)(2,1)S(1)}, u32[]{:S(2)}, u32[]{:S(2)}) collective-permute-start(bf16[528,128]{1,0:T(8,128)(2,1)S(1)} %get-tuple-element.98), channel_id=1, source_target_pairs={{0,20},{4,16},{8,28},{12,24},{16,4},{20,0},{24,12},{28,8},{1,21},{... | collective-permute-start | bytes 405512 | tf_op jit(solution)/shard_map/ppermute | solution.py:237
  58.7 5.4 %collective-permute-start.15 = (bf16[528,128]{1,0:T(8,128)(2,1)S(1)}, bf16[528,128]{1,0:T(8,128)(2,1)S(1)}, u32[]{:S(2)}, u32[]{:S(2)}) collective-permute-start(bf16[528,128]{1,0:T(8,128)(2,1)S(1)} %get-tuple-element.105), channel_id=1, source_target_pairs={{0,28},{4,24},{8,4},{12,0},{16,12},{20,8},{24,20},{28,16},{1,29},{... | collective-permute-start | bytes 405512 | tf_op jit(solution)/shard_map/ppermute | solution.py:237
  60.3 6.6 %collective-permute-start.16 = (bf16[528,128]{1,0:T(8,128)(2,1)S(1)}, bf16[528,128]{1,0:T(8,128)(2,1)S(1)}, u32[]{:S(2)}, u32[]{:S(2)}) collective-permute-start(bf16[528,128]{1,0:T(8,128)(2,1)S(1)} %get-tuple-element.106), channel_id=1, source_target_pairs={{0,12},{4,8},{8,20},{12,16},{16,28},{20,24},{24,4},{28,0},{1,13},{... | collective-permute-start | bytes 405512 | tf_op jit(solution)/shard_map/ppermute | solution.py:237

commit v9 on v8

--- a/solution.py
+++ b/solution.py
@@ -273,6 +273,7 @@
     shares = []
 
     def send(parts, places):
+        parts, shares[:] = lax.optimization_barrier((parts, shares))
         for part, (steps, across) in zip(parts, places, strict=True):
             if not steps and not across:
                 shares.append(part)
@@ -284,12 +285,11 @@
     far, query_acc = lax.optimization_barrier((far, query_acc))
     far_other = trade(far, "c", lambda j: j ^ 1)
     send(parts, [(0, 0), (1, 0), (lines - 1, 0), (0, 1)])
+    query_acc, *parts = prompt_part(info, beside_other, rows, query_acc)
+    query_acc, far_other = lax.optimization_barrier((query_acc, far_other))
+    send(parts, [(1, 1), (lines - 1, 1)])
     query_acc, *parts = prompt_part(info, [far, far_other], rows, query_acc)
-    query_acc, beside_other, shares = lax.optimization_barrier((query_acc, beside_other, shares))
     send(parts, [(2, 0), (2, 1)])
-    query_acc, *parts = prompt_part(info, beside_other, rows, query_acc)
-    parts, shares = lax.optimization_barrier((parts, shares))
-    send(parts, [(1, 1), (lines - 1, 1)])
 
     query_grad, key_grad, value_grad = suffix_part(rows, query_acc, key_suffix[0], value_suffix[0])
     key_grad, shares = lax.optimization_barrier((key_grad, shares))

time: 83.9 us -> 83.9 us (level)
  starting transfers between devices: 22.9 us -> 24.5 us
  waiting for transfers between devices: 18.3 us -> 16.9 us
    ppermute x17, starting transfers between devices: 14.4 us -> 16 us  [trade(): lax.ppermute(block, axis, [(i, target(i)) for i in range(lax.axis_size(ax...]
    ppermute x17, waiting for transfers between devices: 13.8 us -> 12.5 us  [trade(): lax.ppermute(block, axis, [(i, target(i)) for i in range(lax.axis_size(ax...]
  transfers between devices with their start and end apart: 18 -> 18, of which waited for: 8 -> 7; matrix products, arithmetic and copies ran while one was open for 2% -> 2% of each run, Pallas kernels for 25% -> 25%
where the time goes in v9:
time: 83.9 us; the launch traced here: 83.1 us
  starting transfers between devices  24.5 us (29%)
  Pallas kernels  22.8 us (27%)
  waiting for transfers between devices  16.9 us (20%)
  blocking collectives  14.9 us (18%)
  between operations  2.09 us (2%)
  local copies, waits for them, and re-layouts  1.86 us (2%)
    ppermute x17, starting transfers between devices, trade(): lax.ppermute(block, axis, [(i, target(i)) for i in range(lax.axis_size(ax...  16 us
    pallas_call x3, Pallas kernels, prompt_part(): pl.pallas_call(functools.partial(prompt_kernel, count=len(pairs), first=q...  15.8 us
    all_to_all x1, blocking collectives, exchange(): return lax.all_to_all(blocks, axes, split_axis=0, concat_axis=0, tiled=True)  14.9 us
    ppermute x17, waiting for transfers between devices, trade(): lax.ppermute(block, axis, [(i, target(i)) for i in range(lax.axis_size(ax...  12.5 us
    all_to_all x1, starting transfers between devices, exchange(): return lax.all_to_all(blocks, axes, split_axis=0, concat_axis=0, tiled=True)  8.47 us
    all_to_all x1, waiting for transfers between devices, exchange(): return lax.all_to_all(blocks, axes, split_axis=0, concat_axis=0, tiled=True)  4.49 us
    pallas_call x1, Pallas kernels, suffix_part(): pl.pallas_call(suffix_kernel, in_specs=[VMEM] * (len(rows) + 3), out_spec...  3.71 us
  transfers between devices with their start and end apart: 18, of which 7 were waited for; matrix products, arithmetic and copies ran while one was open for 2% of the time, Pallas kernels for 25%

profile of v9, /device:TPU:6, one launch (start us, length us, event | category | flops | bytes accessed | tf_op | source)
XLA Modules:
  0.0 83.1 jit_solution(7763334253527493635)
XLA Ops:
  0.6 0.0 copy-start.4
  0.6 0.0 copy-start
  0.7 0.0 copy-start.1
  0.7 1.6 %spread.1 = bf16[8,2,2,32,128]{4,3,2,1,0:T(8,128)(2,1)} custom-call(bf16[2,32,128]{2,1,0:T(8,128)(2,1)} %key_ref.1, bf16[2,32,128]{2,1,0:T(8,128)(2,1)} %value_ref.1), custom_call_target="tpu_custom_call" | custom-call | tf_op jit(solution)/shard_map/spread/pallas_call | solution.py:47
  2.2 8.5 %all-to-all-start = ((bf16[8,128,128]{2,1,0:T(8,128)(2,1)}), bf16[8,128,128]{2,1,0:T(8,128)(2,1)S(1)}, u32[]{:S(2)}, u32[]{:S(2)}) async-start(bf16[8,128,128]{2,1,0:T(8,128)(2,1)} %bitcast.42), calls=%async_computation | async-start | bytes 524288 | tf_op jit(solution)/shard_map/all_to_all | solution.py:233
  10.7 1.2 %dynamic-slice_bitcast_fusion = (bf16[96,896]{1,0:T(8,128)(2,1)S(1)}, bf16[96,896]{1,0:T(8,128)(2,1)S(1)}, bf16[96,896]{1,0:T(8,128)(2,1)S(1)}, bf16[96,896]{1,0:T(8,128)(2,1)S(1)}) fusion(bf16[1,96,3584]{2,1,0:T(8,128)(2,1)} %param.16, s32[]{:T(128)S(6)} %select_n.15, s32[]{:T(128)S(6)} %select_n.13, s32[]{:T(128)S(6)} %select_n.12, s32[]{:T(128)S(6)} %select_n.14), kind=kLoop, calls=%fused_computation | loop fusion | bytes 1376272 | tf_op jit(solution)/shard_map/dynamic_slice | solution.py:255
  11.9 0.6 collective-permute-start.2
  12.5 0.9 %collective-permute-start = (bf16[96,896]{1,0:T(8,128)(2,1)S(1)}, bf16[96,896]{1,0:T(8,128)(2,1)S(1)}, u32[]{:S(2)}, u32[]{:S(2)}) collective-permute-start(bf16[96,896]{1,0:T(8,128)(2,1)S(1)} %get-tuple-element.128), channel_id=1, source_target_pairs={{0,1},{1,0},{2,3},{3,2},{4,5},{5,4},{6,7},{7,6},{8,9},{9,8},{10,11... | collective-permute-start | bytes 516104 | tf_op jit(solution)/shard_map/ppermute | solution.py:237
  13.4 3.3 %collective-permute-start.1 = (bf16[96,896]{1,0:T(8,128)(2,1)S(1)}, bf16[96,896]{1,0:T(8,128)(2,1)S(1)}, u32[]{:S(2)}, u32[]{:S(2)}) collective-permute-start(bf16[96,896]{1,0:T(8,128)(2,1)S(1)} %get-tuple-element.130), channel_id=1, source_target_pairs={{0,2},{1,3},{2,0},{3,1},{4,6},{5,7},{6,4},{7,5},{8,10},{9,11},{10,... | collective-permute-start | bytes 516104 | tf_op jit(solution)/shard_map/ppermute | solution.py:237
  18.0 0.1 pad_add_fusion.info_ref
  18.1 4.5 %all-to-all-done = bf16[8,128,128]{2,1,0:T(8,128)(2,1)S(1)} async-done(((bf16[8,128,128]{2,1,0:T(8,128)(2,1)}), bf16[8,128,128]{2,1,0:T(8,128)(2,1)S(1)}, u32[]{:S(2)}, u32[]{:S(2)}) %all-to-all-start) | async-done | bytes 262176 | tf_op jit(solution)/shard_map/all_to_all | solution.py:233
  22.6 3.0 %collective-permute-start.4 = (bf16[8,2,2,32,128]{4,3,2,1,0:T(8,128)(2,1)S(1)}, bf16[8,2,2,32,128]{4,3,2,1,0:T(8,128)(2,1)S(1)}, u32[]{:S(2)}, u32[]{:S(2)}) collective-permute-start(bf16[8,2,2,32,128]{4,3,2,1,0:T(8,128)(2,1)S(1)} %bitcast.34), channel_id=1, source_target_pairs={{0,24},{8,0},{16,8},{24,16},{1,25},{9,1},{17,9},{25,17},{2,26},{10... | collective-permute-start | bytes 786440 | tf_op jit(solution)/shard_map/ppermute | solution.py:237
  25.6 0.0 collective-permute-start.3
  25.6 0.0 collective-permute-done.2.refs_3_
  25.6 0.0 collective-permute-done.refs_1_
  25.6 0.0 collective-permute-done.1.refs_2_
  25.6 0.1 collective-permute-start.6
  25.7 0.0 copy-done.4
  25.7 0.0 copy-done
  25.8 0.0 copy-done.1
  25.8 1.2 %prepare.1 = (bf16[384,896]{1,0:T(8,128)(2,1)S(1)}, bf16[128,2688]{1,0:T(8,128)(2,1)S(1)}, bf16[128,2688]{1,0:T(8,128)(2,1)S(1)}, f32[1,2688]{1,0:T(1,128)S(1)}, f32[1,2688]{1,0:T(1,128)S(1)}) custom-call(s32[3]{0:T(128)S(1)} %pad_add_fusion.info_ref, bf16[384,896]{1,0:T(8,128)(2,1)S(1)} %bitcast.29, bf16[384,896]{1,0:T(8,128)(2,1)S(1)} %bitcast.28, ...), custom_call_target="tpu_custom_call" | custom-call | flops 688128 | bytes 4128768 | tf_op jit(solution)/shard_map/prepare/pallas_call | solution.py:86
  27.0 2.5 %collective-permute-done.4.refs_2_ = bf16[8,2,2,32,128]{4,3,2,1,0:T(8,128)(2,1)S(1)} collective-permute-done((bf16[8,2,2,32,128]{4,3,2,1,0:T(8,128)(2,1)S(1)}, bf16[8,2,2,32,128]{4,3,2,1,0:T(8,128)(2,1)S(1)}, u32[]{:S(2)}, u32[]{:S(2)}) %collective-permute-start.4) | collective-permute-done | bytes 262176 | tf_op jit(solution)/shard_map/ppermute | solution.py:237
  29.5 3.7 %collective-permute-done.3.refs_1_ = bf16[8,2,2,32,128]{4,3,2,1,0:T(8,128)(2,1)S(1)} collective-permute-done((bf16[8,2,2,32,128]{4,3,2,1,0:T(8,128)(2,1)S(1)}, bf16[8,2,2,32,128]{4,3,2,1,0:T(8,128)(2,1)S(1)}, u32[]{:S(2)}, u32[]{:S(2)}) %collective-permute-start.3) | collective-permute-done | bytes 262176 | tf_op jit(solution)/shard_map/ppermute | solution.py:237
  33.2 0.0 collective-permute-start.5
  33.2 0.0 collective-permute-start.7
  33.2 0.5 collective-permute-start.8
  33.7 0.0 collective-permute-done.6.refs_3_
  33.7 7.6 %prompt_part.3 = (f32[128,2688]{1,0:T(8,128)S(1)}, bf16[528,128]{1,0:T(8,128)(2,1)S(1)}, bf16[528,128]{1,0:T(8,128)(2,1)S(1)}, bf16[528,128]{1,0:T(8,128)(2,1)S(1)}, bf16[528,128]{1,0:T(8,128)(2,1)S(1)}) custom-call(s32[3]{0:T(128)S(1)} %pad_add_fusion.info_ref, bf16[8,2,2,32,128]{4,3,2,1,0:T(8,128)(2,1)S(1)} %bitcast.38, ...), custom_call_target="tpu_custom_call" | custom-call | flops 3523215360 | bytes 5505024 | tf_op jit(solution)/shard_map/prompt_part/pallas_call | solution.py:194
  41.3 0.0 collective-permute-done.5.refs_0_
  41.3 0.1 collective-permute-start.9
  41.4 1.5 %collective-permute-start.10 = (bf16[528,128]{1,0:T(8,128)(2,1)S(1)}, bf16[528,128]{1,0:T(8,128)(2,1)S(1)}, u32[]{:S(2)}, u32[]{:S(2)}) collective-permute-start(bf16[528,128]{1,0:T(8,128)(2,1)S(1)} %get-tuple-element.100), channel_id=1, source_target_pairs={{0,24},{4,28},{8,0},{12,4},{16,8},{20,12},{24,16},{28,20},{1,25},{... | collective-permute-start | bytes 405512 | tf_op jit(solution)/shard_map/ppermute | solution.py:237
  42.9 0.6 collective-permute-start.11
  43.5 0.0 collective-permute-done.7.refs_0_
  43.5 0.0 collective-permute-start.12
  43.5 0.0 collective-permute-done.8.refs_1_
  43.5 4.1 %prompt_part.4 = (f32[128,2688]{1,0:T(8,128)S(1)}, bf16[528,128]{1,0:T(8,128)(2,1)S(1)}, bf16[528,128]{1,0:T(8,128)(2,1)S(1)}) custom-call(s32[3]{0:T(128)S(1)} %pad_add_fusion.info_ref, bf16[8,2,2,32,128]{4,3,2,1,0:T(8,128)(2,1)S(1)} %collective-permute-done.7.refs_0_, bf16[8,2,2,32,128]{4,3,2,1,0:T(8,128)(2,1)S(1)} %collective-permute-done.8.refs_1_, ...), custom_call_target="tpu_custom_call" | custom-call | flops 1761607680 | bytes 5505024 | tf_op jit(solution)/shard_map/prompt_part/pallas_call | solution.py:194
  47.6 0.0 collective-permute-done.10.refs_1_
  47.6 2.1 %collective-permute-done.11.refs_2_ = bf16[528,128]{1,0:T(8,128)(2,1)S(1)} collective-permute-done((bf16[528,128]{1,0:T(8,128)(2,1)S(1)}, bf16[528,128]{1,0:T(8,128)(2,1)S(1)}, u32[]{:S(2)}, u32[]{:S(2)}) %collective-permute-start.11) | collective-permute-done | bytes 135200 | tf_op jit(solution)/shard_map/ppermute | solution.py:237
  49.8 0.0 collective-permute-done.12.refs_3_
  49.8 0.7 collective-permute-start.13
  50.5 1.0 %collective-permute-start.14 = (bf16[528,128]{1,0:T(8,128)(2,1)S(1)}, bf16[528,128]{1,0:T(8,128)(2,1)S(1)}, u32[]{:S(2)}, u32[]{:S(2)}) collective-permute-start(bf16[528,128]{1,0:T(8,128)(2,1)S(1)} %get-tuple-element.108), channel_id=1, source_target_pairs={{0,12},{4,8},{8,20},{12,16},{16,28},{20,24},{24,4},{28,0},{1,13},{... | collective-permute-start | bytes 405512 | tf_op jit(solution)/shard_map/ppermute | solution.py:237
  51.5 0.0 collective-permute-done.9.refs_1_
  51.5 0.0 copy-start.2
  51.5 0.0 copy-start.3
  51.5 4.1 %prompt_part.5 = (f32[128,2688]{1,0:T(8,128)S(1)}, bf16[528,128]{1,0:T(8,128)(2,1)S(1)}, bf16[528,128]{1,0:T(8,128)(2,1)S(1)}) custom-call(s32[3]{0:T(128)S(1)} %pad_add_fusion.info_ref, bf16[8,2,2,32,128]{4,3,2,1,0:T(8,128)(2,1)S(1)} %collective-permute-done.5.refs_0_, bf16[8,2,2,32,128]{4,3,2,1,0:T(8,128)(2,1)S(1)} %collective-permute-done.9.refs_1_, ...), custom_call_target="tpu_custom_call" | custom-call | flops 1761607680 | bytes 5505024 | tf_op jit(solution)/shard_map/prompt_part/pallas_call | solution.py:194
  55.7 0.0 collective-permute-done.13.refs_4_
  55.7 1.0 %collective-permute-done.14.refs_5_ = bf16[528,128]{1,0:T(8,128)(2,1)S(1)} collective-permute-done((bf16[528,128]{1,0:T(8,128)(2,1)S(1)}, bf16[528,128]{1,0:T(8,128)(2,1)S(1)}, u32[]{:S(2)}, u32[]{:S(2)}) %collective-permute-start.14) | collective-permute-done | bytes 135200 | tf_op jit(solution)/shard_map/ppermute | solution.py:237
  56.6 0.9 %collective-permute-start.15 = (bf16[528,128]{1,0:T(8,128)(2,1)S(1)}, bf16[528,128]{1,0:T(8,128)(2,1)S(1)}, u32[]{:S(2)}, u32[]{:S(2)}) collective-permute-start(bf16[528,128]{1,0:T(8,128)(2,1)S(1)} %get-tuple-element.115), channel_id=1, source_target_pairs={{0,16},{4,20},{8,24},{12,28},{16,0},{20,4},{24,8},{28,12},{1,17},{... | collective-permute-start | bytes 405512 | tf_op jit(solution)/shard_map/ppermute | solution.py:237
  57.5 2.7 %collective-permute-start.16 = (bf16[528,128]{1,0:T(8,128)(2,1)S(1)}, bf16[528,128]{1,0:T(8,128)(2,1)S(1)}, u32[]{:S(2)}, u32[]{:S(2)}) collective-permute-start(bf16[528,128]{1,0:T(8,128)(2,1)S(1)} %get-tuple-element.116), channel_id=1, source_target_pairs={{0,20},{4,16},{8,28},{12,24},{16,4},{20,0},{24,12},{28,8},{1,21},{... | collective-permute-start | bytes 405512 | tf_op jit(solution)/shard_map/ppermute | solution.py:237
  60.3 0.0 copy-done.2
  60.3 0.0 copy-done.3
  60.3 3.7 %suffix_part.1 = (bf16[384,896]{1,0:T(8,128)(2,1)}, bf16[384,128]{1,0:T(8,128)(2,1)}, bf16[384,128]{1,0:T(8,128)(2,1)}) custom-call(bf16[384,896]{1,0:T(8,128)(2,1)S(1)} %bitcast.33, bf16[384,896]{1,0:T(8,128)(2,1)S(1)} %get-tuple-element.72.refs_5_.refs_3_.refs_1_, bf16[128,2688]{1,0:T(8,128)(2,1)S(1)} %get-tuple-element.73.refs_6_.refs_4_.refs_2_, ...), custom_call_target="tpu_custom_call" | custom-call | flops 1321205760 | bytes 5505024 | tf_op jit(solution)/shard_map/suffix_part/pallas_call | solution.py:153
  64.0 0.6 collective-permute-done.15.refs_6_
  64.6 2.5 %collective-permute-done.16.refs_7_ = bf16[528,128]{1,0:T(8,128)(2,1)S(1)} collective-permute-done((bf16[528,128]{1,0:T(8,128)(2,1)S(1)}, bf16[528,128]{1,0:T(8,128)(2,1)S(1)}, u32[]{:S(2)}, u32[]{:S(2)}) %collective-permute-start.16) | collective-permute-done | bytes 135200 | tf_op jit(solution)/shard_map/ppermute | solution.py:237
  67.1 0.4 group_sum.1
  67.6 14.9 %all_to_all.10 = bf16[8,128,128]{2,1,0:T(8,128)(2,1)S(1)} all-to-all(bf16[8,128,128]{2,1,0:T(8,128)(2,1)S(1)} %bitcast.27), channel_id=1, replica_groups=mesh['z'=8,'y'=4,'c'=2,'head'=4] {'z'}, dimensions={0} | all-to-all | bytes 524288 | tf_op jit(solution)/shard_map/all_to_all | solution.py:233
  82.5 0.6 slice_bitcast_fusion
  (2 shorter events, 0.0 us)
Async XLA Ops:
  0.6 25.1 %copy-start.4 = (f32[1,7,384]{2,0,1:T(1,128)S(1)}, f32[1,7,384]{2,0,1:T(1,128)}, u32[]{:S(2)}) copy-start(f32[1,7,384]{2,0,1:T(1,128)} %param.17) | copy-start | bytes 32260
  0.6 25.1 %copy-start = (bf16[1,384,896]{2,1,0:T(8,128)(2,1)S(1)}, bf16[1,384,896]{2,1,0:T(8,128)(2,1)}, u32[]{:S(2)}) copy-start(bf16[1,384,896]{2,1,0:T(8,128)(2,1)} %param.15) | copy-start | bytes 2064388
  0.7 25.1 %copy-start.1 = (bf16[1,384,896]{2,1,0:T(8,128)(2,1)S(1)}, bf16[1,384,896]{2,1,0:T(8,128)(2,1)}, u32[]{:S(2)}) copy-start(bf16[1,384,896]{2,1,0:T(8,128)(2,1)} %param.10) | copy-start | bytes 2064388
  2.2 20.3 %all-to-all-start = ((bf16[8,128,128]{2,1,0:T(8,128)(2,1)}), bf16[8,128,128]{2,1,0:T(8,128)(2,1)S(1)}, u32[]{:S(2)}, u32[]{:S(2)}) async-start(bf16[8,128,128]{2,1,0:T(8,128)(2,1)} %bitcast.42), calls=%async_computation | async-start | bytes 524288 | tf_op jit(solution)/shard_map/all_to_all | solution.py:233
  11.9 13.7 %collective-permute-start.2 = (bf16[96,896]{1,0:T(8,128)(2,1)S(1)}, bf16[96,896]{1,0:T(8,128)(2,1)S(1)}, u32[]{:S(2)}, u32[]{:S(2)}) collective-permute-start(bf16[96,896]{1,0:T(8,128)(2,1)S(1)} %get-tuple-element.127), channel_id=1, source_target_pairs={{0,3},{1,2},{2,1},{3,0},{4,7},{5,6},{6,5},{7,4},{8,11},{9,10},{10,... | collective-permute-start | bytes 516104 | tf_op jit(solution)/shard_map/ppermute | solution.py:237
  12.5 13.1 %collective-permute-start = (bf16[96,896]{1,0:T(8,128)(2,1)S(1)}, bf16[96,896]{1,0:T(8,128)(2,1)S(1)}, u32[]{:S(2)}, u32[]{:S(2)}) collective-permute-start(bf16[96,896]{1,0:T(8,128)(2,1)S(1)} %get-tuple-element.128), channel_id=1, source_target_pairs={{0,1},{1,0},{2,3},{3,2},{4,5},{5,4},{6,7},{7,6},{8,9},{9,8},{10,11... | collective-permute-start | bytes 516104 | tf_op jit(solution)/shard_map/ppermute | solution.py:237
  13.4 12.2 %collective-permute-start.1 = (bf16[96,896]{1,0:T(8,128)(2,1)S(1)}, bf16[96,896]{1,0:T(8,128)(2,1)S(1)}, u32[]{:S(2)}, u32[]{:S(2)}) collective-permute-start(bf16[96,896]{1,0:T(8,128)(2,1)S(1)} %get-tuple-element.130), channel_id=1, source_target_pairs={{0,2},{1,3},{2,0},{3,1},{4,6},{5,7},{6,4},{7,5},{8,10},{9,11},{10,... | collective-permute-start | bytes 516104 | tf_op jit(solution)/shard_map/ppermute | solution.py:237
  22.6 6.9 %collective-permute-start.4 = (bf16[8,2,2,32,128]{4,3,2,1,0:T(8,128)(2,1)S(1)}, bf16[8,2,2,32,128]{4,3,2,1,0:T(8,128)(2,1)S(1)}, u32[]{:S(2)}, u32[]{:S(2)}) collective-permute-start(bf16[8,2,2,32,128]{4,3,2,1,0:T(8,128)(2,1)S(1)} %bitcast.34), channel_id=1, source_target_pairs={{0,24},{8,0},{16,8},{24,16},{1,25},{9,1},{17,9},{25,17},{2,26},{10... | collective-permute-start | bytes 786440 | tf_op jit(solution)/shard_map/ppermute | solution.py:237
  25.6 7.6 %collective-permute-start.3 = (bf16[8,2,2,32,128]{4,3,2,1,0:T(8,128)(2,1)S(1)}, bf16[8,2,2,32,128]{4,3,2,1,0:T(8,128)(2,1)S(1)}, u32[]{:S(2)}, u32[]{:S(2)}) collective-permute-start(bf16[8,2,2,32,128]{4,3,2,1,0:T(8,128)(2,1)S(1)} %bitcast.35), channel_id=1, source_target_pairs={{0,8},{8,16},{16,24},{24,0},{1,9},{9,17},{17,25},{25,1},{2,10},{10... | collective-permute-start | bytes 786440 | tf_op jit(solution)/shard_map/ppermute | solution.py:237
  25.6 8.1 %collective-permute-start.6 = (bf16[8,2,2,32,128]{4,3,2,1,0:T(8,128)(2,1)S(1)}, bf16[8,2,2,32,128]{4,3,2,1,0:T(8,128)(2,1)S(1)}, u32[]{:S(2)}, u32[]{:S(2)}) collective-permute-start(bf16[8,2,2,32,128]{4,3,2,1,0:T(8,128)(2,1)S(1)} %bitcast.36), channel_id=1, source_target_pairs={{0,4},{4,0},{1,5},{5,1},{2,6},{6,2},{3,7},{7,3},{8,12},{12,8},{9,1... | collective-permute-start | bytes 786440 | tf_op jit(solution)/shard_map/ppermute | solution.py:237
  33.2 8.1 %collective-permute-start.5 = (bf16[8,2,2,32,128]{4,3,2,1,0:T(8,128)(2,1)S(1)}, bf16[8,2,2,32,128]{4,3,2,1,0:T(8,128)(2,1)S(1)}, u32[]{:S(2)}, u32[]{:S(2)}) collective-permute-start(bf16[8,2,2,32,128]{4,3,2,1,0:T(8,128)(2,1)S(1)} %bitcast.37), channel_id=1, source_target_pairs={{0,16},{8,24},{16,0},{24,8},{1,17},{9,25},{17,1},{25,9},{2,18},{10... | collective-permute-start | bytes 786440 | tf_op jit(solution)/shard_map/ppermute | solution.py:237
  33.2 10.3 %collective-permute-start.7 = (bf16[8,2,2,32,128]{4,3,2,1,0:T(8,128)(2,1)S(1)}, bf16[8,2,2,32,128]{4,3,2,1,0:T(8,128)(2,1)S(1)}, u32[]{:S(2)}, u32[]{:S(2)}) collective-permute-start(bf16[8,2,2,32,128]{4,3,2,1,0:T(8,128)(2,1)S(1)} %collective-permute-done.3.refs_1_), channel_id=1, source_target_pairs={{0,4},{4,0},{1,5},{5,1},{2,6},{6,2},{3,7},{7,3},{8,12},{12,8},{9,1... | collective-permute-start | bytes 786440 | tf_op jit(solution)/shard_map/ppermute | solution.py:237
  33.2 10.3 %collective-permute-start.8 = (bf16[8,2,2,32,128]{4,3,2,1,0:T(8,128)(2,1)S(1)}, bf16[8,2,2,32,128]{4,3,2,1,0:T(8,128)(2,1)S(1)}, u32[]{:S(2)}, u32[]{:S(2)}) collective-permute-start(bf16[8,2,2,32,128]{4,3,2,1,0:T(8,128)(2,1)S(1)} %collective-permute-done.4.refs_2_), channel_id=1, source_target_pairs={{0,4},{4,0},{1,5},{5,1},{2,6},{6,2},{3,7},{7,3},{8,12},{12,8},{9,1... | collective-permute-start | bytes 786440 | tf_op jit(solution)/shard_map/ppermute | solution.py:237
  41.3 10.2 %collective-permute-start.9 = (bf16[8,2,2,32,128]{4,3,2,1,0:T(8,128)(2,1)S(1)}, bf16[8,2,2,32,128]{4,3,2,1,0:T(8,128)(2,1)S(1)}, u32[]{:S(2)}, u32[]{:S(2)}) collective-permute-start(bf16[8,2,2,32,128]{4,3,2,1,0:T(8,128)(2,1)S(1)} %collective-permute-done.5.refs_0_), channel_id=1, source_target_pairs={{0,4},{4,0},{1,5},{5,1},{2,6},{6,2},{3,7},{7,3},{8,12},{12,8},{9,1... | collective-permute-start | bytes 786440 | tf_op jit(solution)/shard_map/ppermute | solution.py:237
  41.4 6.3 %collective-permute-start.10 = (bf16[528,128]{1,0:T(8,128)(2,1)S(1)}, bf16[528,128]{1,0:T(8,128)(2,1)S(1)}, u32[]{:S(2)}, u32[]{:S(2)}) collective-permute-start(bf16[528,128]{1,0:T(8,128)(2,1)S(1)} %get-tuple-element.100), channel_id=1, source_target_pairs={{0,24},{4,28},{8,0},{12,4},{16,8},{20,12},{24,16},{28,20},{1,25},{... | collective-permute-start | bytes 405512 | tf_op jit(solution)/shard_map/ppermute | solution.py:237
  42.9 6.9 %collective-permute-start.11 = (bf16[528,128]{1,0:T(8,128)(2,1)S(1)}, bf16[528,128]{1,0:T(8,128)(2,1)S(1)}, u32[]{:S(2)}, u32[]{:S(2)}) collective-permute-start(bf16[528,128]{1,0:T(8,128)(2,1)S(1)} %get-tuple-element.101), channel_id=1, source_target_pairs={{0,8},{4,12},{8,16},{12,20},{16,24},{20,28},{24,0},{28,4},{1,9},{5... | collective-permute-start | bytes 405512 | tf_op jit(solution)/shard_map/ppermute | solution.py:237
  43.5 6.3 %collective-permute-start.12 = (bf16[528,128]{1,0:T(8,128)(2,1)S(1)}, bf16[528,128]{1,0:T(8,128)(2,1)S(1)}, u32[]{:S(2)}, u32[]{:S(2)}) collective-permute-start(bf16[528,128]{1,0:T(8,128)(2,1)S(1)} %get-tuple-element.102), channel_id=1, source_target_pairs={{0,4},{4,0},{8,12},{12,8},{16,20},{20,16},{24,28},{28,24},{1,5},{5... | collective-permute-start | bytes 405512 | tf_op jit(solution)/shard_map/ppermute | solution.py:237
  49.8 5.9 %collective-permute-start.13 = (bf16[528,128]{1,0:T(8,128)(2,1)S(1)}, bf16[528,128]{1,0:T(8,128)(2,1)S(1)}, u32[]{:S(2)}, u32[]{:S(2)}) collective-permute-start(bf16[528,128]{1,0:T(8,128)(2,1)S(1)} %get-tuple-element.107), channel_id=1, source_target_pairs={{0,28},{4,24},{8,4},{12,0},{16,12},{20,8},{24,20},{28,16},{1,29},{... | collective-permute-start | bytes 405512 | tf_op jit(solution)/shard_map/ppermute | solution.py:237
  50.5 6.1 %collective-permute-start.14 = (bf16[528,128]{1,0:T(8,128)(2,1)S(1)}, bf16[528,128]{1,0:T(8,128)(2,1)S(1)}, u32[]{:S(2)}, u32[]{:S(2)}) collective-permute-start(bf16[528,128]{1,0:T(8,128)(2,1)S(1)} %get-tuple-element.108), channel_id=1, source_target_pairs={{0,12},{4,8},{8,20},{12,16},{16,28},{20,24},{24,4},{28,0},{1,13},{... | collective-permute-start | bytes 405512 | tf_op jit(solution)/shard_map/ppermute | solution.py:237
  51.5 8.8 %copy-start.2 = (bf16[1,384,128]{2,1,0:T(8,128)(2,1)S(1)}, bf16[1,384,128]{2,1,0:T(8,128)(2,1)}, u32[]{:S(2)}) copy-start(bf16[1,384,128]{2,1,0:T(8,128)(2,1)} %param.11) | copy-start | bytes 294916
  51.5 8.8 %copy-start.3 = (bf16[1,384,128]{2,1,0:T(8,128)(2,1)S(1)}, bf16[1,384,128]{2,1,0:T(8,128)(2,1)}, u32[]{:S(2)}) copy-start(bf16[1,384,128]{2,1,0:T(8,128)(2,1)} %param.12) | copy-start | bytes 294916
  56.6 8.0 %collective-permute-start.15 = (bf16[528,128]{1,0:T(8,128)(2,1)S(1)}, bf16[528,128]{1,0:T(8,128)(2,1)S(1)}, u32[]{:S(2)}, u32[]{:S(2)}) collective-permute-start(bf16[528,128]{1,0:T(8,128)(2,1)S(1)} %get-tuple-element.115), channel_id=1, source_target_pairs={{0,16},{4,20},{8,24},{12,28},{16,0},{20,4},{24,8},{28,12},{1,17},{... | collective-permute-start | bytes 405512 | tf_op jit(solution)/shard_map/ppermute | solution.py:237
  57.5 9.6 %collective-permute-start.16 = (bf16[528,128]{1,0:T(8,128)(2,1)S(1)}, bf16[528,128]{1,0:T(8,128)(2,1)S(1)}, u32[]{:S(2)}, u32[]{:S(2)}) collective-permute-start(bf16[528,128]{1,0:T(8,128)(2,1)S(1)} %get-tuple-element.116), channel_id=1, source_target_pairs={{0,20},{4,16},{8,28},{12,24},{16,4},{20,0},{24,12},{28,8},{1,21},{... | collective-permute-start | bytes 405512 | tf_op jit(solution)/shard_map/ppermute | solution.py:237

commit v10 on v8

--- a/solution.py
+++ b/solution.py
@@ -107,7 +107,6 @@
     width = key_rows.shape[1]
     seq_len = query_ref.shape[0]
     head_count = query_ref.shape[1] // width
-    key_t = key_rows.T
     key_acc = jnp.zeros(key_rows.shape, F32)
     value_acc = jnp.zeros(key_rows.shape, F32)
 
@@ -125,57 +124,68 @@
             ahead = scores_of(head + 1)
         cols = slice(head * width, (head + 1) * width)
         rows = slice(head * seq_len, (head + 1) * seq_len)
-        emit(rows, cols, jnp.dot(key_t, score_grad_t, preferred_element_type=F32))
+        emit(rows, cols, score_grad_t)
         key_acc += jnp.dot(score_grad_t, query_ref[:, cols], preferred_element_type=F32)
         value_acc += jnp.dot(weights_t, grad_rows_ref[:, cols], preferred_element_type=F32)
     return key_acc.astype(BF16), value_acc.astype(BF16)
 
 
-def suffix_kernel(*refs):
+def rows_of(pair_refs, chosen, which):
+    parts = [ref[:, chosen, which] for ref in pair_refs]
+    return jnp.concatenate([part.reshape(-1, part.shape[-1]) for part in parts], 0)
+
+
+def suffix_kernel(info_ref, *refs, counts):
     row_refs, refs = refs[:6], refs[6:]
-    query_acc_ref, key_ref, value_ref, query_grad_ref, key_grad_ref, value_grad_ref = refs
-    seq_len, width = key_ref.shape
+    chosen = info_ref[0]
+    earlier = []
+    for count in counts:
+        earlier.append((rows_of(refs[:count], chosen, 0).T, refs[count]))
+        refs = refs[count + 1 :]
+    key_ref, value_ref, query_grad_ref, key_grad_ref, value_grad_ref = refs
+    seq_len = key_ref.shape[0]
     key_at = lax.broadcasted_iota(jnp.int32, (seq_len, seq_len), 0)
     query_at = lax.broadcasted_iota(jnp.int32, (seq_len, seq_len), 1)
     causal = key_at <= query_at
-
-    def emit(rows, cols, query_part):
-        query_grad_ref[:, cols] = (query_part + query_acc_ref[:, rows]).T.astype(BF16)
+    key_t = key_ref[...].T
+
+    def emit(rows, cols, score_grad_t):
+        total = jnp.dot(key_t, score_grad_t, preferred_element_type=F32)
+        for prompt_key_t, score_ref in earlier:
+            total += jnp.dot(prompt_key_t, score_ref[:, rows], preferred_element_type=F32)
+        query_grad_ref[:, cols] = total.T.astype(BF16)
 
     key_grad_ref[...], value_grad_ref[...] = attend_heads(
         row_refs, key_ref[...], value_ref[...], emit, causal
     )
 
 
-def suffix_part(rows, query_acc, key_suffix, value_suffix):
+def suffix_part(info, rows, earlier, key_suffix, value_suffix):
     seq_len, width = key_suffix.shape
     suffix = jax.ShapeDtypeStruct(key_suffix.shape, BF16)
-    return pl.pallas_call(
-        suffix_kernel,
-        in_specs=[VMEM] * (len(rows) + 3),
+    flat = [item for pairs, scores in earlier for item in (*pairs, scores)]
+    return pl.pallas_call(
+        functools.partial(suffix_kernel, counts=[len(pairs) for pairs, _ in earlier]),
+        in_specs=[SMEM] + [VMEM] * (len(rows) + len(flat) + 2),
         out_specs=[VMEM] * 3,
         out_shape=[jax.ShapeDtypeStruct(rows[0].shape, BF16), suffix, suffix],
         compiler_params=PARAMS,
-        cost_estimate=cost(query_acc.shape[1], seq_len, width),
+        cost_estimate=cost(rows[2].shape[1], seq_len, width),
         name="suffix_part",
-    )(*rows, query_acc, key_suffix, value_suffix)
-
-
-def prompt_kernel(info_ref, *refs, count, first):
-    pair_refs, row_refs, refs = refs[:count], refs[count : count + 6], refs[count + 6 :]
-    query_acc_ref = None if first else refs[0]
-    query_out_ref, *pair_grad_refs = refs if first else refs[1:]
+    )(info, *rows, *flat, key_suffix, value_suffix)
+
+
+def prompt_kernel(info_ref, *refs, count):
+    pair_refs, row_refs = refs[:count], refs[count : count + 6]
+    score_out_ref, *pair_grad_refs = refs[count + 6 :]
     chosen = info_ref[0]
-    width = query_out_ref.shape[0]
-
-    def rows_of(which):
-        parts = [ref[:, chosen, which] for ref in pair_refs]
-        return jnp.concatenate([part.reshape(-1, width) for part in parts], 0)
-
-    def emit(rows, cols, query_part):
-        query_out_ref[:, rows] = query_part if first else query_part + query_acc_ref[:, rows]
-
-    key_grad, value_grad = attend_heads(row_refs, rows_of(0), rows_of(1), emit)
+    width = pair_grad_refs[0].shape[1]
+
+    def emit(rows, cols, score_grad_t):
+        score_out_ref[:, rows] = score_grad_t
+
+    keys, values = rows_of(pair_refs, chosen, 0), rows_of(pair_refs, chosen, 1)
+    key_grad, value_grad = attend_heads(row_refs, keys, values, emit)
     size = key_grad.shape[0] // count
     mark = jnp.full((MARK, width), chosen.astype(F32), F32).astype(BF16)
     for i, ref in enumerate(pair_grad_refs):
@@ -184,22 +194,21 @@
         ref[2 * size :] = mark
 
 
-def prompt_part(info, pairs, rows, query_acc=None):
+def prompt_part(info, pairs, rows):
     width, row_count = rows[2].shape
     stacks, _, _, owned, _ = pairs[0].shape
     size = stacks * owned
-    out = jax.ShapeDtypeStruct((width, row_count), F32)
     pair_out = jax.ShapeDtypeStruct((2 * size + MARK, width), BF16)
-    more = [] if query_acc is None else [query_acc]
-    return pl.pallas_call(
-        functools.partial(prompt_kernel, count=len(pairs), first=query_acc is None),
-        in_specs=[SMEM] + [VMEM] * (len(pairs) + len(rows) + len(more)),
+    return pl.pallas_call(
+        functools.partial(prompt_kernel, count=len(pairs)),
+        in_specs=[SMEM] + [VMEM] * (len(pairs) + len(rows)),
         out_specs=[VMEM] * (1 + len(pairs)),
-        out_shape=[out] + [pair_out] * len(pairs),
+        out_shape=[jax.ShapeDtypeStruct((len(pairs) * size, row_count), BF16)]
+        + [pair_out] * len(pairs),
         compiler_params=PARAMS,
         cost_estimate=cost(row_count, len(pairs) * size, width),
         name="prompt_part",
-    )(info, *pairs, *rows, *more)
+    )(info, *pairs, *rows)
 
 
 def group_kernel(*refs):
@@ -229,8 +238,11 @@
     )(*shares)
 
 
-def exchange(blocks, axes):
-    return lax.all_to_all(blocks, axes, split_axis=0, concat_axis=0, tiled=True)
+def exchange(blocks, axis):
+    groups = [list(range(lax.axis_size(axis)))[::-1]]
+    return lax.all_to_all(
+        blocks, axis, split_axis=0, concat_axis=0, axis_index_groups=groups, tiled=True
+    )
 
 
 def trade(block, axis, target):
@@ -280,18 +292,18 @@
             target = lambda j, s=steps, o=across: 2 * ((j // 2 - s) % lines) + (j % 2 ^ o)
             shares.append(trade(part, GROUP, target))
 
-    query_acc, *parts = prompt_part(info, [stacked, *beside, other], rows)
-    far, query_acc = lax.optimization_barrier((far, query_acc))
-    far_other = trade(far, "c", lambda j: j ^ 1)
+    near = [stacked, *beside, other]
+    near_scores, *parts = prompt_part(info, near, rows)
+    far, parts = lax.optimization_barrier((far, parts))
+    late = [far, trade(far, "c", lambda j: j ^ 1), *beside_other]
     send(parts, [(0, 0), (1, 0), (lines - 1, 0), (0, 1)])
-    query_acc, *parts = prompt_part(info, [far, far_other], rows, query_acc)
-    query_acc, beside_other, shares = lax.optimization_barrier((query_acc, beside_other, shares))
-    send(parts, [(2, 0), (2, 1)])
-    query_acc, *parts = prompt_part(info, beside_other, rows, query_acc)
+    late_scores, *parts = prompt_part(info, late, rows)
     parts, shares = lax.optimization_barrier((parts, shares))
-    send(parts, [(1, 1), (lines - 1, 1)])
-
-    query_grad, key_grad, value_grad = suffix_part(rows, query_acc, key_suffix[0], value_suffix[0])
+    send(parts, [(2, 0), (2, 1), (1, 1), (lines - 1, 1)])
+
+    query_grad, key_grad, value_grad = suffix_part(
+        info, rows, [(near, near_scores), (late, late_scores)], key_suffix[0], value_suffix[0]
+    )
     key_grad, shares = lax.optimization_barrier((key_grad, shares))
 
     totals = group_sum(shares, (stacks, prompt_count, 2, owned, width))

time: 83.9 us -> 79 us (0.942)
  waiting for transfers between devices: 18.3 us -> 4.38 us
  starting transfers between devices: 22.9 us -> 29.4 us
  local copies, waits for them, and re-layouts: 1.86 us -> 4.75 us
  blocking collectives: 15.6 us -> 14.3 us
    ppermute x17, waiting for transfers between devices: 13.8 us -> 4.38 us  [trade(): lax.ppermute(block, axis, [(i, target(i)) for i in range(lax.axis_size(ax...]
    ppermute x17, starting transfers between devices: 14.4 us -> 20.2 us  [trade(): lax.ppermute(block, axis, [(i, target(i)) for i in range(lax.axis_size(ax...]
    all_to_all x1, waiting for transfers between devices: 4.49 us -> 0.01 us  [exchange(): lax.all_to_all(blocks, axis, split_axis=0, concat_axis=0, axis_index_grou...]
    unnamed x11 -> x9, local copies, waits for them, and re-layouts: 0.02 us -> 2.91 us
    all_to_all x1, blocking collectives: 15.6 us -> 14.3 us  [exchange(): lax.all_to_all(blocks, axis, split_axis=0, concat_axis=0, axis_index_grou...]
    pallas_call x4 -> x3, Pallas kernels: 19.5 us -> 19.7 us  [the longest x2 13.3 us: prompt_part(): pl.pallas_call(functools.partial(prompt_kernel, count=len(pairs)), in_spe...]
  transfers between devices with their start and end apart: 18 -> 18, of which waited for: 8 -> 3; matrix products, arithmetic and copies ran while one was open for 2% -> 3% of each run, Pallas kernels for 25% -> 27%
where the time goes in v10:
time: 79 us; the launch traced here: 77.9 us
  starting transfers between devices  29.4 us (37%)
  Pallas kernels  22.8 us (29%)
  blocking collectives  14.3 us (18%)
  local copies, waits for them, and re-layouts  4.75 us (6%)
  waiting for transfers between devices  4.38 us (6%)
  between operations  2.04 us (3%)
    ppermute x17, starting transfers between devices, trade(): lax.ppermute(block, axis, [(i, target(i)) for i in range(lax.axis_size(ax...  20.2 us
    all_to_all x1, blocking collectives, exchange(): lax.all_to_all(blocks, axis, split_axis=0, concat_axis=0, axis_index_grou...  14.3 us
    pallas_call x2, Pallas kernels, prompt_part(): pl.pallas_call(functools.partial(prompt_kernel, count=len(pairs)), in_spe...  13.3 us
    all_to_all x1, starting transfers between devices, exchange(): lax.all_to_all(blocks, axis, split_axis=0, concat_axis=0, axis_index_grou...  9.21 us
    pallas_call x1, Pallas kernels, suffix_part(): pl.pallas_call(functools.partial(suffix_kernel, counts=[len(pairs) for pa...  6.35 us
    ppermute x17, waiting for transfers between devices, trade(): lax.ppermute(block, axis, [(i, target(i)) for i in range(lax.axis_size(ax...  4.38 us
    unnamed x9, local copies, waits for them, and re-layouts  2.91 us
  transfers between devices with their start and end apart: 18, of which 3 were waited for; matrix products, arithmetic and copies ran while one was open for 3% of the time, Pallas kernels for 27%

profile of v10, /device:TPU:6, one launch (start us, length us, event | category | flops | bytes accessed | tf_op | source)
XLA Modules:
  0.0 77.9 jit_solution(15050155028211904434)
XLA Ops:
  0.6 1.5 %spread.1 = bf16[8,2,2,32,128]{4,3,2,1,0:T(8,128)(2,1)} custom-call(bf16[2,32,128]{2,1,0:T(8,128)(2,1)} %key_ref.1, bf16[2,32,128]{2,1,0:T(8,128)(2,1)} %value_ref.1), custom_call_target="tpu_custom_call" | custom-call | tf_op jit(solution)/shard_map/spread/pallas_call | solution.py:47
  2.1 9.2 %all-to-all-start = ((bf16[8,128,128]{2,1,0:T(8,128)(2,1)}), bf16[8,128,128]{2,1,0:T(8,128)(2,1)S(1)}, u32[]{:S(2)}, u32[]{:S(2)}) async-start(bf16[8,128,128]{2,1,0:T(8,128)(2,1)} %bitcast.42), calls=%async_computation | async-start | bytes 524288 | tf_op jit(solution)/shard_map/all_to_all | solution.py:243
  11.3 1.2 %dynamic-slice_bitcast_fusion = (bf16[96,896]{1,0:T(8,128)(2,1)S(1)}, bf16[96,896]{1,0:T(8,128)(2,1)S(1)}, bf16[96,896]{1,0:T(8,128)(2,1)S(1)}, bf16[96,896]{1,0:T(8,128)(2,1)S(1)}) fusion(bf16[1,96,3584]{2,1,0:T(8,128)(2,1)} %param.16, s32[]{:T(128)S(6)} %select_n.15, s32[]{:T(128)S(6)} %select_n.13, s32[]{:T(128)S(6)} %select_n.12, s32[]{:T(128)S(6)} %select_n.14), kind=kLoop, calls=%fused_computation | loop fusion | bytes 1376272 | tf_op jit(solution)/shard_map/dynamic_slice | solution.py:267
  12.5 0.6 collective-permute-start.2
  13.1 0.9 %collective-permute-start = (bf16[96,896]{1,0:T(8,128)(2,1)S(1)}, bf16[96,896]{1,0:T(8,128)(2,1)S(1)}, u32[]{:S(2)}, u32[]{:S(2)}) collective-permute-start(bf16[96,896]{1,0:T(8,128)(2,1)S(1)} %get-tuple-element.108), channel_id=1, source_target_pairs={{0,1},{1,0},{2,3},{3,2},{4,5},{5,4},{6,7},{7,6},{8,9},{9,8},{10,11... | collective-permute-start | bytes 516104 | tf_op jit(solution)/shard_map/ppermute | solution.py:249
  14.0 3.3 %collective-permute-start.1 = (bf16[96,896]{1,0:T(8,128)(2,1)S(1)}, bf16[96,896]{1,0:T(8,128)(2,1)S(1)}, u32[]{:S(2)}, u32[]{:S(2)}) collective-permute-start(bf16[96,896]{1,0:T(8,128)(2,1)S(1)} %get-tuple-element.110), channel_id=1, source_target_pairs={{0,2},{1,3},{2,0},{3,1},{4,6},{5,7},{6,4},{7,5},{8,10},{9,11},{10,... | collective-permute-start | bytes 516104 | tf_op jit(solution)/shard_map/ppermute | solution.py:249
  18.6 0.1 pad_add_fusion.info_ref
  18.7 0.0 all-to-all-done
  18.7 3.0 %collective-permute-start.4 = (bf16[8,2,2,32,128]{4,3,2,1,0:T(8,128)(2,1)S(1)}, bf16[8,2,2,32,128]{4,3,2,1,0:T(8,128)(2,1)S(1)}, u32[]{:S(2)}, u32[]{:S(2)}) collective-permute-start(bf16[8,2,2,32,128]{4,3,2,1,0:T(8,128)(2,1)S(1)} %bitcast.31), channel_id=1, source_target_pairs={{0,24},{8,0},{16,8},{24,16},{1,25},{9,1},{17,9},{25,17},{2,26},{10... | collective-permute-start | bytes 786440 | tf_op jit(solution)/shard_map/ppermute | solution.py:249
  21.7 0.0 collective-permute-start.3
  21.8 0.0 collective-permute-done.2.refs_3_
  21.8 0.0 collective-permute-done.refs_1_
  21.8 2.8 %collective-permute-done.1.refs_2_ = bf16[96,896]{1,0:T(8,128)(2,1)S(1)} collective-permute-done((bf16[96,896]{1,0:T(8,128)(2,1)S(1)}, bf16[96,896]{1,0:T(8,128)(2,1)S(1)}, u32[]{:S(2)}, u32[]{:S(2)}) %collective-permute-start.1) | collective-permute-done | bytes 172064 | tf_op jit(solution)/shard_map/ppermute | solution.py:249
  24.5 0.0 collective-permute-start.5
  24.6 0.7 copy.17
  25.3 0.0 copy-start
  25.3 1.1 %copy-done = bf16[1,384,896]{2,1,0:T(8,128)(2,1)S(1)} copy-done((bf16[1,384,896]{2,1,0:T(8,128)(2,1)S(1)}, bf16[1,384,896]{2,1,0:T(8,128)(2,1)}, u32[]{:S(2)}) %copy-start) | copy-done | bytes 688152
  26.4 0.0 copy-start.1
  26.4 1.1 %copy-done.1 = bf16[1,384,896]{2,1,0:T(8,128)(2,1)S(1)} copy-done((bf16[1,384,896]{2,1,0:T(8,128)(2,1)S(1)}, bf16[1,384,896]{2,1,0:T(8,128)(2,1)}, u32[]{:S(2)}) %copy-start.1) | copy-done | bytes 688152
  27.5 1.2 %prepare.1 = (bf16[384,896]{1,0:T(8,128)(2,1)S(1)}, bf16[128,2688]{1,0:T(8,128)(2,1)S(1)}, bf16[128,2688]{1,0:T(8,128)(2,1)S(1)}, f32[1,2688]{1,0:T(1,128)S(1)}, f32[1,2688]{1,0:T(1,128)S(1)}) custom-call(s32[3]{0:T(128)S(1)} %pad_add_fusion.info_ref, bf16[384,896]{1,0:T(8,128)(2,1)S(1)} %bitcast.27, bf16[384,896]{1,0:T(8,128)(2,1)S(1)} %bitcast.38, ...), custom_call_target="tpu_custom_call" | custom-call | flops 688128 | bytes 4128768 | tf_op jit(solution)/shard_map/prepare/pallas_call | solution.py:86
  28.7 0.0 collective-permute-done.4.refs_2_.refs_8_
  28.7 0.9 %collective-permute-done.3.refs_1_.refs_7_ = bf16[8,2,2,32,128]{4,3,2,1,0:T(8,128)(2,1)S(1)} collective-permute-done((bf16[8,2,2,32,128]{4,3,2,1,0:T(8,128)(2,1)S(1)}, bf16[8,2,2,32,128]{4,3,2,1,0:T(8,128)(2,1)S(1)}, u32[]{:S(2)}, u32[]{:S(2)}) %collective-permute-start.3) | collective-permute-done | bytes 262176 | tf_op jit(solution)/shard_map/ppermute | solution.py:249
  29.6 2.4 %collective-permute-start.6 = (bf16[8,2,2,32,128]{4,3,2,1,0:T(8,128)(2,1)S(1)}, bf16[8,2,2,32,128]{4,3,2,1,0:T(8,128)(2,1)S(1)}, u32[]{:S(2)}, u32[]{:S(2)}) collective-permute-start(bf16[8,2,2,32,128]{4,3,2,1,0:T(8,128)(2,1)S(1)} %bitcast.34), channel_id=1, source_target_pairs={{0,16},{8,24},{16,0},{24,8},{1,17},{9,25},{17,1},{25,9},{2,18},{10... | collective-permute-start | bytes 786440 | tf_op jit(solution)/shard_map/ppermute | solution.py:249
  32.0 0.2 collective-permute-start.8
  32.2 0.3 collective-permute-start.9
  32.5 0.0 collective-permute-done.5.refs_3_.refs_9_
  32.5 6.6 %prompt_part.2 = (bf16[1024,2688]{1,0:T(8,128)(2,1)S(1)}, bf16[528,128]{1,0:T(8,128)(2,1)S(1)}, bf16[528,128]{1,0:T(8,128)(2,1)S(1)}, bf16[528,128]{1,0:T(8,128)(2,1)S(1)}, bf16[528,128]{1,0:T(8,128)(2,1)S(1)}) custom-call(s32[3]{0:T(128)S(1)} %pad_add_fusion.info_ref, bf16[8,2,2,32,128]{4,3,2,1,0:T(8,128)(2,1)S(1)} %bitcast.35, ...), custom_call_target="tpu_custom_call" | custom-call | flops 3523215360 | bytes 5505024 | tf_op jit(solution)/shard_map/prompt_part/pallas_call | solution.py:202
  39.1 0.0 collective-permute-done.6.refs_0_.refs_11_
  39.1 0.0 copy-start.2
  39.1 0.0 copy-start.3
  39.2 0.3 collective-permute-start.7
  39.5 2.6 %collective-permute-start.10 = (bf16[528,128]{1,0:T(8,128)(2,1)S(1)}, bf16[528,128]{1,0:T(8,128)(2,1)S(1)}, u32[]{:S(2)}, u32[]{:S(2)}) collective-permute-start(bf16[528,128]{1,0:T(8,128)(2,1)S(1)} %get-tuple-element.86), channel_id=1, source_target_pairs={{0,24},{4,28},{8,0},{12,4},{16,8},{20,12},{24,16},{28,20},{1,25},{... | collective-permute-start | bytes 405512 | tf_op jit(solution)/shard_map/ppermute | solution.py:249
  42.1 0.0 collective-permute-start.11
  42.1 0.0 collective-permute-done.8.refs_2_.refs_13_
  42.1 0.2 collective-permute-start.12
  42.3 0.0 collective-permute-done.9.refs_3_.refs_14_
  42.3 0.0 collective-permute-done.7.refs_1_.refs_12_
  42.3 6.7 %prompt_part.3 = (bf16[1024,2688]{1,0:T(8,128)(2,1)S(1)}, bf16[528,128]{1,0:T(8,128)(2,1)S(1)}, bf16[528,128]{1,0:T(8,128)(2,1)S(1)}, bf16[528,128]{1,0:T(8,128)(2,1)S(1)}, bf16[528,128]{1,0:T(8,128)(2,1)S(1)}) custom-call(s32[3]{0:T(128)S(1)} %pad_add_fusion.info_ref, bf16[8,2,2,32,128]{4,3,2,1,0:T(8,128)(2,1)S(1)} %collective-permute-done.6.refs_0_.refs_11_, ...), custom_call_target="tpu_custom_call" | custom-call | flops 3523215360 | bytes 5505024 | tf_op jit(solution)/shard_map/prompt_part/pallas_call | solution.py:202
  49.0 0.0 collective-permute-done.10.refs_1_
  49.0 0.0 collective-permute-done.11.refs_2_
  49.0 0.0 collective-permute-done.12.refs_3_
  49.0 2.1 %collective-permute-start.13 = (bf16[528,128]{1,0:T(8,128)(2,1)S(1)}, bf16[528,128]{1,0:T(8,128)(2,1)S(1)}, u32[]{:S(2)}, u32[]{:S(2)}) collective-permute-start(bf16[528,128]{1,0:T(8,128)(2,1)S(1)} %get-tuple-element.93), channel_id=1, source_target_pairs={{0,16},{4,20},{8,24},{12,28},{16,0},{20,4},{24,8},{28,12},{1,17},{... | collective-permute-start | bytes 405512 | tf_op jit(solution)/shard_map/ppermute | solution.py:249
  51.2 1.2 %collective-permute-start.14 = (bf16[528,128]{1,0:T(8,128)(2,1)S(1)}, bf16[528,128]{1,0:T(8,128)(2,1)S(1)}, u32[]{:S(2)}, u32[]{:S(2)}) collective-permute-start(bf16[528,128]{1,0:T(8,128)(2,1)S(1)} %get-tuple-element.94), channel_id=1, source_target_pairs={{0,20},{4,16},{8,28},{12,24},{16,4},{20,0},{24,12},{28,8},{1,21},{... | collective-permute-start | bytes 405512 | tf_op jit(solution)/shard_map/ppermute | solution.py:249
  52.3 3.1 %collective-permute-start.15 = (bf16[528,128]{1,0:T(8,128)(2,1)S(1)}, bf16[528,128]{1,0:T(8,128)(2,1)S(1)}, u32[]{:S(2)}, u32[]{:S(2)}) collective-permute-start(bf16[528,128]{1,0:T(8,128)(2,1)S(1)} %get-tuple-element.95), channel_id=1, source_target_pairs={{0,28},{4,24},{8,4},{12,0},{16,12},{20,8},{24,20},{28,16},{1,29},{... | collective-permute-start | bytes 405512 | tf_op jit(solution)/shard_map/ppermute | solution.py:249
  55.5 0.0 collective-permute-start.16
  55.5 0.0 copy-done.2
  55.5 0.0 copy-done.3
  55.5 6.4 %suffix_part.1 = (bf16[384,896]{1,0:T(8,128)(2,1)}, bf16[384,128]{1,0:T(8,128)(2,1)}, bf16[384,128]{1,0:T(8,128)(2,1)}) custom-call(s32[3]{0:T(128)S(1)} %pad_add_fusion.info_ref, bf16[384,896]{1,0:T(8,128)(2,1)S(1)} %bitcast.30, bf16[384,896]{1,0:T(8,128)(2,1)S(1)} %get-tuple-element.62.refs_5_.refs_1_, ...), custom_call_target="tpu_custom_call" | custom-call | flops 1321205760 | bytes 5505024 | tf_op jit(solution)/shard_map/suffix_part/pallas_call | solution.py:167
  61.8 0.0 collective-permute-done.13.refs_4_
  61.8 0.0 collective-permute-done.14.refs_5_
  61.8 0.6 collective-permute-done.15.refs_6_
  62.5 0.0 collective-permute-done.16.refs_7_
  62.5 0.4 group_sum.1
  62.9 14.3 %all_to_all.10 = bf16[8,128,128]{2,1,0:T(8,128)(2,1)S(1)} all-to-all(bf16[8,128,128]{2,1,0:T(8,128)(2,1)S(1)} %bitcast.37), channel_id=1, replica_groups={{224,192,160,128,96,64,32,0},{225,193,161,129,97,65,33,1},{226,194,162,..., dimensions={0} | all-to-all | bytes 524288 | tf_op jit(solution)/shard_map/all_to_all | solution.py:243
  77.2 0.6 slice_bitcast_fusion
  (1 shorter events, 0.0 us)
Async XLA Ops:
  2.1 16.6 %all-to-all-start = ((bf16[8,128,128]{2,1,0:T(8,128)(2,1)}), bf16[8,128,128]{2,1,0:T(8,128)(2,1)S(1)}, u32[]{:S(2)}, u32[]{:S(2)}) async-start(bf16[8,128,128]{2,1,0:T(8,128)(2,1)} %bitcast.42), calls=%async_computation | async-start | bytes 524288 | tf_op jit(solution)/shard_map/all_to_all | solution.py:243
  12.5 9.2 %collective-permute-start.2 = (bf16[96,896]{1,0:T(8,128)(2,1)S(1)}, bf16[96,896]{1,0:T(8,128)(2,1)S(1)}, u32[]{:S(2)}, u32[]{:S(2)}) collective-permute-start(bf16[96,896]{1,0:T(8,128)(2,1)S(1)} %get-tuple-element.107), channel_id=1, source_target_pairs={{0,3},{1,2},{2,1},{3,0},{4,7},{5,6},{6,5},{7,4},{8,11},{9,10},{10,... | collective-permute-start | bytes 516104 | tf_op jit(solution)/shard_map/ppermute | solution.py:249
  13.1 8.6 %collective-permute-start = (bf16[96,896]{1,0:T(8,128)(2,1)S(1)}, bf16[96,896]{1,0:T(8,128)(2,1)S(1)}, u32[]{:S(2)}, u32[]{:S(2)}) collective-permute-start(bf16[96,896]{1,0:T(8,128)(2,1)S(1)} %get-tuple-element.108), channel_id=1, source_target_pairs={{0,1},{1,0},{2,3},{3,2},{4,5},{5,4},{6,7},{7,6},{8,9},{9,8},{10,11... | collective-permute-start | bytes 516104 | tf_op jit(solution)/shard_map/ppermute | solution.py:249
  14.0 10.6 %collective-permute-start.1 = (bf16[96,896]{1,0:T(8,128)(2,1)S(1)}, bf16[96,896]{1,0:T(8,128)(2,1)S(1)}, u32[]{:S(2)}, u32[]{:S(2)}) collective-permute-start(bf16[96,896]{1,0:T(8,128)(2,1)S(1)} %get-tuple-element.110), channel_id=1, source_target_pairs={{0,2},{1,3},{2,0},{3,1},{4,6},{5,7},{6,4},{7,5},{8,10},{9,11},{10,... | collective-permute-start | bytes 516104 | tf_op jit(solution)/shard_map/ppermute | solution.py:249
  18.7 10.0 %collective-permute-start.4 = (bf16[8,2,2,32,128]{4,3,2,1,0:T(8,128)(2,1)S(1)}, bf16[8,2,2,32,128]{4,3,2,1,0:T(8,128)(2,1)S(1)}, u32[]{:S(2)}, u32[]{:S(2)}) collective-permute-start(bf16[8,2,2,32,128]{4,3,2,1,0:T(8,128)(2,1)S(1)} %bitcast.31), channel_id=1, source_target_pairs={{0,24},{8,0},{16,8},{24,16},{1,25},{9,1},{17,9},{25,17},{2,26},{10... | collective-permute-start | bytes 786440 | tf_op jit(solution)/shard_map/ppermute | solution.py:249
  21.7 7.9 %collective-permute-start.3 = (bf16[8,2,2,32,128]{4,3,2,1,0:T(8,128)(2,1)S(1)}, bf16[8,2,2,32,128]{4,3,2,1,0:T(8,128)(2,1)S(1)}, u32[]{:S(2)}, u32[]{:S(2)}) collective-permute-start(bf16[8,2,2,32,128]{4,3,2,1,0:T(8,128)(2,1)S(1)} %bitcast.32), channel_id=1, source_target_pairs={{0,8},{8,16},{16,24},{24,0},{1,9},{9,17},{17,25},{25,1},{2,10},{10... | collective-permute-start | bytes 786440 | tf_op jit(solution)/shard_map/ppermute | solution.py:249
  24.5 7.9 %collective-permute-start.5 = (bf16[8,2,2,32,128]{4,3,2,1,0:T(8,128)(2,1)S(1)}, bf16[8,2,2,32,128]{4,3,2,1,0:T(8,128)(2,1)S(1)}, u32[]{:S(2)}, u32[]{:S(2)}) collective-permute-start(bf16[8,2,2,32,128]{4,3,2,1,0:T(8,128)(2,1)S(1)} %bitcast.33), channel_id=1, source_target_pairs={{0,4},{4,0},{1,5},{5,1},{2,6},{6,2},{3,7},{7,3},{8,12},{12,8},{9,1... | collective-permute-start | bytes 786440 | tf_op jit(solution)/shard_map/ppermute | solution.py:249
  25.3 1.1 %copy-start = (bf16[1,384,896]{2,1,0:T(8,128)(2,1)S(1)}, bf16[1,384,896]{2,1,0:T(8,128)(2,1)}, u32[]{:S(2)}) copy-start(bf16[1,384,896]{2,1,0:T(8,128)(2,1)} %param.10) | copy-start | bytes 2064388
  26.4 1.1 %copy-start.1 = (bf16[1,384,896]{2,1,0:T(8,128)(2,1)S(1)}, bf16[1,384,896]{2,1,0:T(8,128)(2,1)}, u32[]{:S(2)}) copy-start(bf16[1,384,896]{2,1,0:T(8,128)(2,1)} %param.15) | copy-start | bytes 2064388
  29.6 9.5 %collective-permute-start.6 = (bf16[8,2,2,32,128]{4,3,2,1,0:T(8,128)(2,1)S(1)}, bf16[8,2,2,32,128]{4,3,2,1,0:T(8,128)(2,1)S(1)}, u32[]{:S(2)}, u32[]{:S(2)}) collective-permute-start(bf16[8,2,2,32,128]{4,3,2,1,0:T(8,128)(2,1)S(1)} %bitcast.34), channel_id=1, source_target_pairs={{0,16},{8,24},{16,0},{24,8},{1,17},{9,25},{17,1},{25,9},{2,18},{10... | collective-permute-start | bytes 786440 | tf_op jit(solution)/shard_map/ppermute | solution.py:249
  32.0 10.1 %collective-permute-start.8 = (bf16[8,2,2,32,128]{4,3,2,1,0:T(8,128)(2,1)S(1)}, bf16[8,2,2,32,128]{4,3,2,1,0:T(8,128)(2,1)S(1)}, u32[]{:S(2)}, u32[]{:S(2)}) collective-permute-start(bf16[8,2,2,32,128]{4,3,2,1,0:T(8,128)(2,1)S(1)} %collective-permute-done.3.refs_1_.refs_7_), channel_id=1, source_target_pairs={{0,4},{4,0},{1,5},{5,1},{2,6},{6,2},{3,7},{7,3},{8,12},{12,8},{9,1... | collective-permute-start | bytes 786440 | tf_op jit(solution)/shard_map/ppermute | solution.py:249
  32.2 10.1 %collective-permute-start.9 = (bf16[8,2,2,32,128]{4,3,2,1,0:T(8,128)(2,1)S(1)}, bf16[8,2,2,32,128]{4,3,2,1,0:T(8,128)(2,1)S(1)}, u32[]{:S(2)}, u32[]{:S(2)}) collective-permute-start(bf16[8,2,2,32,128]{4,3,2,1,0:T(8,128)(2,1)S(1)} %collective-permute-done.4.refs_2_.refs_8_), channel_id=1, source_target_pairs={{0,4},{4,0},{1,5},{5,1},{2,6},{6,2},{3,7},{7,3},{8,12},{12,8},{9,1... | collective-permute-start | bytes 786440 | tf_op jit(solution)/shard_map/ppermute | solution.py:249
  39.1 16.3 %copy-start.2 = (bf16[1,384,128]{2,1,0:T(8,128)(2,1)S(1)}, bf16[1,384,128]{2,1,0:T(8,128)(2,1)}, u32[]{:S(2)}) copy-start(bf16[1,384,128]{2,1,0:T(8,128)(2,1)} %param.11) | copy-start | bytes 294916
  39.1 16.3 %copy-start.3 = (bf16[1,384,128]{2,1,0:T(8,128)(2,1)S(1)}, bf16[1,384,128]{2,1,0:T(8,128)(2,1)}, u32[]{:S(2)}) copy-start(bf16[1,384,128]{2,1,0:T(8,128)(2,1)} %param.12) | copy-start | bytes 294916
  39.2 3.1 %collective-permute-start.7 = (bf16[8,2,2,32,128]{4,3,2,1,0:T(8,128)(2,1)S(1)}, bf16[8,2,2,32,128]{4,3,2,1,0:T(8,128)(2,1)S(1)}, u32[]{:S(2)}, u32[]{:S(2)}) collective-permute-start(bf16[8,2,2,32,128]{4,3,2,1,0:T(8,128)(2,1)S(1)} %collective-permute-done.6.refs_0_.refs_11_), channel_id=1, source_target_pairs={{0,4},{4,0},{1,5},{5,1},{2,6},{6,2},{3,7},{7,3},{8,12},{12,8},{9,1... | collective-permute-start | bytes 786440 | tf_op jit(solution)/shard_map/ppermute | solution.py:249
  39.5 9.5 %collective-permute-start.10 = (bf16[528,128]{1,0:T(8,128)(2,1)S(1)}, bf16[528,128]{1,0:T(8,128)(2,1)S(1)}, u32[]{:S(2)}, u32[]{:S(2)}) collective-permute-start(bf16[528,128]{1,0:T(8,128)(2,1)S(1)} %get-tuple-element.86), channel_id=1, source_target_pairs={{0,24},{4,28},{8,0},{12,4},{16,8},{20,12},{24,16},{28,20},{1,25},{... | collective-permute-start | bytes 405512 | tf_op jit(solution)/shard_map/ppermute | solution.py:249
  42.1 6.9 %collective-permute-start.11 = (bf16[528,128]{1,0:T(8,128)(2,1)S(1)}, bf16[528,128]{1,0:T(8,128)(2,1)S(1)}, u32[]{:S(2)}, u32[]{:S(2)}) collective-permute-start(bf16[528,128]{1,0:T(8,128)(2,1)S(1)} %get-tuple-element.87), channel_id=1, source_target_pairs={{0,8},{4,12},{8,16},{12,20},{16,24},{20,28},{24,0},{28,4},{1,9},{5... | collective-permute-start | bytes 405512 | tf_op jit(solution)/shard_map/ppermute | solution.py:249
  42.1 6.9 %collective-permute-start.12 = (bf16[528,128]{1,0:T(8,128)(2,1)S(1)}, bf16[528,128]{1,0:T(8,128)(2,1)S(1)}, u32[]{:S(2)}, u32[]{:S(2)}) collective-permute-start(bf16[528,128]{1,0:T(8,128)(2,1)S(1)} %get-tuple-element.88), channel_id=1, source_target_pairs={{0,4},{4,0},{8,12},{12,8},{16,20},{20,16},{24,28},{28,24},{1,5},{5... | collective-permute-start | bytes 405512 | tf_op jit(solution)/shard_map/ppermute | solution.py:249
  49.0 12.8 %collective-permute-start.13 = (bf16[528,128]{1,0:T(8,128)(2,1)S(1)}, bf16[528,128]{1,0:T(8,128)(2,1)S(1)}, u32[]{:S(2)}, u32[]{:S(2)}) collective-permute-start(bf16[528,128]{1,0:T(8,128)(2,1)S(1)} %get-tuple-element.93), channel_id=1, source_target_pairs={{0,16},{4,20},{8,24},{12,28},{16,0},{20,4},{24,8},{28,12},{1,17},{... | collective-permute-start | bytes 405512 | tf_op jit(solution)/shard_map/ppermute | solution.py:249
  51.2 10.7 %collective-permute-start.14 = (bf16[528,128]{1,0:T(8,128)(2,1)S(1)}, bf16[528,128]{1,0:T(8,128)(2,1)S(1)}, u32[]{:S(2)}, u32[]{:S(2)}) collective-permute-start(bf16[528,128]{1,0:T(8,128)(2,1)S(1)} %get-tuple-element.94), channel_id=1, source_target_pairs={{0,20},{4,16},{8,28},{12,24},{16,4},{20,0},{24,12},{28,8},{1,21},{... | collective-permute-start | bytes 405512 | tf_op jit(solution)/shard_map/ppermute | solution.py:249
  52.3 10.1 %collective-permute-start.15 = (bf16[528,128]{1,0:T(8,128)(2,1)S(1)}, bf16[528,128]{1,0:T(8,128)(2,1)S(1)}, u32[]{:S(2)}, u32[]{:S(2)}) collective-permute-start(bf16[528,128]{1,0:T(8,128)(2,1)S(1)} %get-tuple-element.95), channel_id=1, source_target_pairs={{0,28},{4,24},{8,4},{12,0},{16,12},{20,8},{24,20},{28,16},{1,29},{... | collective-permute-start | bytes 405512 | tf_op jit(solution)/shard_map/ppermute | solution.py:249
  55.5 7.0 %collective-permute-start.16 = (bf16[528,128]{1,0:T(8,128)(2,1)S(1)}, bf16[528,128]{1,0:T(8,128)(2,1)S(1)}, u32[]{:S(2)}, u32[]{:S(2)}) collective-permute-start(bf16[528,128]{1,0:T(8,128)(2,1)S(1)} %get-tuple-element.96), channel_id=1, source_target_pairs={{0,12},{4,8},{8,20},{12,16},{16,28},{20,24},{24,4},{28,0},{1,13},{... | collective-permute-start | bytes 405512 | tf_op jit(solution)/shard_map/ppermute | solution.py:249

commit v11 on v10

--- a/solution.py
+++ b/solution.py
@@ -239,9 +239,10 @@
 
 
 def exchange(blocks, axis):
-    groups = [list(range(lax.axis_size(axis)))[::-1]]
+    order = list(range(lax.axis_size(axis)))[::-1]
+    order.insert(len(order) - 2, order.pop(2))
     return lax.all_to_all(
-        blocks, axis, split_axis=0, concat_axis=0, axis_index_groups=groups, tiled=True
+        blocks, axis, split_axis=0, concat_axis=0, axis_index_groups=[order], tiled=True
     )
 
 

time: 79 us -> 81 us (1.025)
  waiting for transfers between devices: 4.38 us -> 7.85 us
  starting transfers between devices: 29.4 us -> 26 us
  blocking collectives: 14.3 us -> 16.6 us
    ppermute x17, starting transfers between devices: 20.2 us -> 16.8 us  [trade(): lax.ppermute(block, axis, [(i, target(i)) for i in range(lax.axis_size(ax...]
    all_to_all x1, blocking collectives: 14.3 us -> 16.6 us  [exchange(): lax.all_to_all(blocks, axis, split_axis=0, concat_axis=0, axis_index_grou...]
    all_to_all x1, waiting for transfers between devices: 0.01 us -> 2.07 us  [exchange(): lax.all_to_all(blocks, axis, split_axis=0, concat_axis=0, axis_index_grou...]
    ppermute x17, waiting for transfers between devices: 4.38 us -> 5.78 us  [trade(): lax.ppermute(block, axis, [(i, target(i)) for i in range(lax.axis_size(ax...]
  transfers between devices with their start and end apart: 18 -> 18, of which waited for: 3 -> 6; matrix products, arithmetic and copies ran while one was open for 3% -> 3% of each run, Pallas kernels for 27% -> 26%
where the time goes in v11:
time: 81 us; the launch traced here: 80.1 us
  starting transfers between devices  26 us (32%)
  Pallas kernels  22.8 us (28%)
  blocking collectives  16.6 us (20%)
  waiting for transfers between devices  7.85 us (10%)
  local copies, waits for them, and re-layouts  4.75 us (6%)
  between operations  2.02 us (2%)
    ppermute x17, starting transfers between devices, trade(): lax.ppermute(block, axis, [(i, target(i)) for i in range(lax.axis_size(ax...  16.8 us
    all_to_all x1, blocking collectives, exchange(): lax.all_to_all(blocks, axis, split_axis=0, concat_axis=0, axis_index_grou...  16.6 us
    pallas_call x2, Pallas kernels, prompt_part(): pl.pallas_call(functools.partial(prompt_kernel, count=len(pairs)), in_spe...  13.3 us
    all_to_all x1, starting transfers between devices, exchange(): lax.all_to_all(blocks, axis, split_axis=0, concat_axis=0, axis_index_grou...  9.21 us
    pallas_call x1, Pallas kernels, suffix_part(): pl.pallas_call(functools.partial(suffix_kernel, counts=[len(pairs) for pa...  6.35 us
    ppermute x17, waiting for transfers between devices, trade(): lax.ppermute(block, axis, [(i, target(i)) for i in range(lax.axis_size(ax...  5.78 us
    unnamed x9, local copies, waits for them, and re-layouts  2.91 us
    all_to_all x1, waiting for transfers between devices, exchange(): lax.all_to_all(blocks, axis, split_axis=0, concat_axis=0, axis_index_grou...  2.07 us
  transfers between devices with their start and end apart: 18, of which 6 were waited for; matrix products, arithmetic and copies ran while one was open for 3% of the time, Pallas kernels for 26%

profile of v11, /device:TPU:6, one launch (start us, length us, event | category | flops | bytes accessed | tf_op | source)
XLA Modules:
  0.0 80.1 jit_solution(1928525810617734365)
XLA Ops:
  0.6 1.5 %spread.1 = bf16[8,2,2,32,128]{4,3,2,1,0:T(8,128)(2,1)} custom-call(bf16[2,32,128]{2,1,0:T(8,128)(2,1)} %key_ref.1, bf16[2,32,128]{2,1,0:T(8,128)(2,1)} %value_ref.1), custom_call_target="tpu_custom_call" | custom-call | tf_op jit(solution)/shard_map/spread/pallas_call | solution.py:47
  2.1 9.2 %all-to-all-start = ((bf16[8,128,128]{2,1,0:T(8,128)(2,1)}), bf16[8,128,128]{2,1,0:T(8,128)(2,1)S(1)}, u32[]{:S(2)}, u32[]{:S(2)}) async-start(bf16[8,128,128]{2,1,0:T(8,128)(2,1)} %bitcast.42), calls=%async_computation | async-start | bytes 524288 | tf_op jit(solution)/shard_map/all_to_all | solution.py:244
  11.3 1.2 %dynamic-slice_bitcast_fusion = (bf16[96,896]{1,0:T(8,128)(2,1)S(1)}, bf16[96,896]{1,0:T(8,128)(2,1)S(1)}, bf16[96,896]{1,0:T(8,128)(2,1)S(1)}, bf16[96,896]{1,0:T(8,128)(2,1)S(1)}) fusion(bf16[1,96,3584]{2,1,0:T(8,128)(2,1)} %param.16, s32[]{:T(128)S(6)} %select_n.15, s32[]{:T(128)S(6)} %select_n.13, s32[]{:T(128)S(6)} %select_n.12, s32[]{:T(128)S(6)} %select_n.14), kind=kLoop, calls=%fused_computation | loop fusion | bytes 1376272 | tf_op jit(solution)/shard_map/dynamic_slice | solution.py:268
  12.5 0.6 collective-permute-start.2
  13.1 0.9 %collective-permute-start = (bf16[96,896]{1,0:T(8,128)(2,1)S(1)}, bf16[96,896]{1,0:T(8,128)(2,1)S(1)}, u32[]{:S(2)}, u32[]{:S(2)}) collective-permute-start(bf16[96,896]{1,0:T(8,128)(2,1)S(1)} %get-tuple-element.108), channel_id=1, source_target_pairs={{0,1},{1,0},{2,3},{3,2},{4,5},{5,4},{6,7},{7,6},{8,9},{9,8},{10,11... | collective-permute-start | bytes 516104 | tf_op jit(solution)/shard_map/ppermute | solution.py:250
  14.0 3.3 %collective-permute-start.1 = (bf16[96,896]{1,0:T(8,128)(2,1)S(1)}, bf16[96,896]{1,0:T(8,128)(2,1)S(1)}, u32[]{:S(2)}, u32[]{:S(2)}) collective-permute-start(bf16[96,896]{1,0:T(8,128)(2,1)S(1)} %get-tuple-element.110), channel_id=1, source_target_pairs={{0,2},{1,3},{2,0},{3,1},{4,6},{5,7},{6,4},{7,5},{8,10},{9,11},{10,... | collective-permute-start | bytes 516104 | tf_op jit(solution)/shard_map/ppermute | solution.py:250
  18.6 0.1 pad_add_fusion.info_ref
  18.7 2.1 %all-to-all-done = bf16[8,128,128]{2,1,0:T(8,128)(2,1)S(1)} async-done(((bf16[8,128,128]{2,1,0:T(8,128)(2,1)}), bf16[8,128,128]{2,1,0:T(8,128)(2,1)S(1)}, u32[]{:S(2)}, u32[]{:S(2)}) %all-to-all-start) | async-done | bytes 262176 | tf_op jit(solution)/shard_map/all_to_all | solution.py:244
  20.8 3.0 %collective-permute-start.4 = (bf16[8,2,2,32,128]{4,3,2,1,0:T(8,128)(2,1)S(1)}, bf16[8,2,2,32,128]{4,3,2,1,0:T(8,128)(2,1)S(1)}, u32[]{:S(2)}, u32[]{:S(2)}) collective-permute-start(bf16[8,2,2,32,128]{4,3,2,1,0:T(8,128)(2,1)S(1)} %bitcast.31), channel_id=1, source_target_pairs={{0,24},{8,0},{16,8},{24,16},{1,25},{9,1},{17,9},{25,17},{2,26},{10... | collective-permute-start | bytes 786440 | tf_op jit(solution)/shard_map/ppermute | solution.py:250
  23.8 0.0 collective-permute-start.3
  23.8 0.0 collective-permute-done.2.refs_3_
  23.8 0.0 collective-permute-done.refs_1_
  23.8 0.7 collective-permute-done.1.refs_2_
  24.5 0.0 collective-permute-start.5
  24.6 0.7 copy.17
  25.3 0.0 copy-start
  25.3 1.1 %copy-done = bf16[1,384,896]{2,1,0:T(8,128)(2,1)S(1)} copy-done((bf16[1,384,896]{2,1,0:T(8,128)(2,1)S(1)}, bf16[1,384,896]{2,1,0:T(8,128)(2,1)}, u32[]{:S(2)}) %copy-start) | copy-done | bytes 688152
  26.4 0.0 copy-start.1
  26.4 1.1 %copy-done.1 = bf16[1,384,896]{2,1,0:T(8,128)(2,1)S(1)} copy-done((bf16[1,384,896]{2,1,0:T(8,128)(2,1)S(1)}, bf16[1,384,896]{2,1,0:T(8,128)(2,1)}, u32[]{:S(2)}) %copy-start.1) | copy-done | bytes 688152
  27.5 1.2 %prepare.1 = (bf16[384,896]{1,0:T(8,128)(2,1)S(1)}, bf16[128,2688]{1,0:T(8,128)(2,1)S(1)}, bf16[128,2688]{1,0:T(8,128)(2,1)S(1)}, f32[1,2688]{1,0:T(1,128)S(1)}, f32[1,2688]{1,0:T(1,128)S(1)}) custom-call(s32[3]{0:T(128)S(1)} %pad_add_fusion.info_ref, bf16[384,896]{1,0:T(8,128)(2,1)S(1)} %bitcast.27, bf16[384,896]{1,0:T(8,128)(2,1)S(1)} %bitcast.38, ...), custom_call_target="tpu_custom_call" | custom-call | flops 688128 | bytes 4128768 | tf_op jit(solution)/shard_map/prepare/pallas_call | solution.py:86
  28.7 0.2 collective-permute-done.4.refs_2_.refs_8_
  28.9 3.4 %collective-permute-done.3.refs_1_.refs_7_ = bf16[8,2,2,32,128]{4,3,2,1,0:T(8,128)(2,1)S(1)} collective-permute-done((bf16[8,2,2,32,128]{4,3,2,1,0:T(8,128)(2,1)S(1)}, bf16[8,2,2,32,128]{4,3,2,1,0:T(8,128)(2,1)S(1)}, u32[]{:S(2)}, u32[]{:S(2)}) %collective-permute-start.3) | collective-permute-done | bytes 262176 | tf_op jit(solution)/shard_map/ppermute | solution.py:250
  32.3 0.0 collective-permute-start.6
  32.3 0.0 collective-permute-start.8
  32.3 0.5 collective-permute-start.9
  32.8 0.0 collective-permute-done.5.refs_3_.refs_9_
  32.8 6.6 %prompt_part.2 = (bf16[1024,2688]{1,0:T(8,128)(2,1)S(1)}, bf16[528,128]{1,0:T(8,128)(2,1)S(1)}, bf16[528,128]{1,0:T(8,128)(2,1)S(1)}, bf16[528,128]{1,0:T(8,128)(2,1)S(1)}, bf16[528,128]{1,0:T(8,128)(2,1)S(1)}) custom-call(s32[3]{0:T(128)S(1)} %pad_add_fusion.info_ref, bf16[8,2,2,32,128]{4,3,2,1,0:T(8,128)(2,1)S(1)} %bitcast.35, ...), custom_call_target="tpu_custom_call" | custom-call | flops 3523215360 | bytes 5505024 | tf_op jit(solution)/shard_map/prompt_part/pallas_call | solution.py:202
  39.5 0.7 collective-permute-done.6.refs_0_.refs_11_
  40.2 0.0 copy-start.2
  40.2 0.0 copy-start.3
  40.2 0.0 collective-permute-start.7
  40.2 1.9 %collective-permute-start.10 = (bf16[528,128]{1,0:T(8,128)(2,1)S(1)}, bf16[528,128]{1,0:T(8,128)(2,1)S(1)}, u32[]{:S(2)}, u32[]{:S(2)}) collective-permute-start(bf16[528,128]{1,0:T(8,128)(2,1)S(1)} %get-tuple-element.86), channel_id=1, source_target_pairs={{0,24},{4,28},{8,0},{12,4},{16,8},{20,12},{24,16},{28,20},{1,25},{... | collective-permute-start | bytes 405512 | tf_op jit(solution)/shard_map/ppermute | solution.py:250
  42.1 0.2 collective-permute-start.11
  42.3 0.0 collective-permute-done.8.refs_2_.refs_13_
  42.3 0.0 collective-permute-start.12
  42.3 0.0 collective-permute-done.9.refs_3_.refs_14_
  42.3 0.0 collective-permute-done.7.refs_1_.refs_12_
  42.3 6.7 %prompt_part.3 = (bf16[1024,2688]{1,0:T(8,128)(2,1)S(1)}, bf16[528,128]{1,0:T(8,128)(2,1)S(1)}, bf16[528,128]{1,0:T(8,128)(2,1)S(1)}, bf16[528,128]{1,0:T(8,128)(2,1)S(1)}, bf16[528,128]{1,0:T(8,128)(2,1)S(1)}) custom-call(s32[3]{0:T(128)S(1)} %pad_add_fusion.info_ref, bf16[8,2,2,32,128]{4,3,2,1,0:T(8,128)(2,1)S(1)} %collective-permute-done.6.refs_0_.refs_11_, ...), custom_call_target="tpu_custom_call" | custom-call | flops 3523215360 | bytes 5505024 | tf_op jit(solution)/shard_map/prompt_part/pallas_call | solution.py:202
  49.1 0.0 collective-permute-done.10.refs_1_
  49.1 0.0 collective-permute-done.11.refs_2_
  49.1 0.0 collective-permute-done.12.refs_3_
  49.1 3.0 %collective-permute-start.13 = (bf16[528,128]{1,0:T(8,128)(2,1)S(1)}, bf16[528,128]{1,0:T(8,128)(2,1)S(1)}, u32[]{:S(2)}, u32[]{:S(2)}) collective-permute-start(bf16[528,128]{1,0:T(8,128)(2,1)S(1)} %get-tuple-element.93), channel_id=1, source_target_pairs={{0,16},{4,20},{8,24},{12,28},{16,0},{20,4},{24,8},{28,12},{1,17},{... | collective-permute-start | bytes 405512 | tf_op jit(solution)/shard_map/ppermute | solution.py:250
  52.1 0.4 collective-permute-start.14
  52.5 2.9 %collective-permute-start.15 = (bf16[528,128]{1,0:T(8,128)(2,1)S(1)}, bf16[528,128]{1,0:T(8,128)(2,1)S(1)}, u32[]{:S(2)}, u32[]{:S(2)}) collective-permute-start(bf16[528,128]{1,0:T(8,128)(2,1)S(1)} %get-tuple-element.95), channel_id=1, source_target_pairs={{0,28},{4,24},{8,4},{12,0},{16,12},{20,8},{24,20},{28,16},{1,29},{... | collective-permute-start | bytes 405512 | tf_op jit(solution)/shard_map/ppermute | solution.py:250
  55.5 0.0 collective-permute-start.16
  55.5 0.0 copy-done.2
  55.5 0.0 copy-done.3
  55.5 6.4 %suffix_part.1 = (bf16[384,896]{1,0:T(8,128)(2,1)}, bf16[384,128]{1,0:T(8,128)(2,1)}, bf16[384,128]{1,0:T(8,128)(2,1)}) custom-call(s32[3]{0:T(128)S(1)} %pad_add_fusion.info_ref, bf16[384,896]{1,0:T(8,128)(2,1)S(1)} %bitcast.30, bf16[384,896]{1,0:T(8,128)(2,1)S(1)} %get-tuple-element.62.refs_5_.refs_1_, ...), custom_call_target="tpu_custom_call" | custom-call | flops 1321205760 | bytes 5505024 | tf_op jit(solution)/shard_map/suffix_part/pallas_call | solution.py:167
  61.8 0.0 collective-permute-done.13.refs_4_
  61.8 0.0 collective-permute-done.14.refs_5_
  61.8 0.6 collective-permute-done.15.refs_6_
  62.5 0.0 collective-permute-done.16.refs_7_
  62.5 0.4 group_sum.1
  62.9 16.6 %all_to_all.10 = bf16[8,128,128]{2,1,0:T(8,128)(2,1)S(1)} all-to-all(bf16[8,128,128]{2,1,0:T(8,128)(2,1)S(1)} %bitcast.37), channel_id=1, replica_groups={{224,192,128,96,64,32,160,0},{225,193,129,97,65,33,161,1},{226,194,130,..., dimensions={0} | all-to-all | bytes 524288 | tf_op jit(solution)/shard_map/all_to_all | solution.py:244
  79.5 0.6 slice_bitcast_fusion
  (1 shorter events, 0.0 us)
Async XLA Ops:
  2.1 18.7 %all-to-all-start = ((bf16[8,128,128]{2,1,0:T(8,128)(2,1)}), bf16[8,128,128]{2,1,0:T(8,128)(2,1)S(1)}, u32[]{:S(2)}, u32[]{:S(2)}) async-start(bf16[8,128,128]{2,1,0:T(8,128)(2,1)} %bitcast.42), calls=%async_computation | async-start | bytes 524288 | tf_op jit(solution)/shard_map/all_to_all | solution.py:244
  12.5 11.3 %collective-permute-start.2 = (bf16[96,896]{1,0:T(8,128)(2,1)S(1)}, bf16[96,896]{1,0:T(8,128)(2,1)S(1)}, u32[]{:S(2)}, u32[]{:S(2)}) collective-permute-start(bf16[96,896]{1,0:T(8,128)(2,1)S(1)} %get-tuple-element.107), channel_id=1, source_target_pairs={{0,3},{1,2},{2,1},{3,0},{4,7},{5,6},{6,5},{7,4},{8,11},{9,10},{10,... | collective-permute-start | bytes 516104 | tf_op jit(solution)/shard_map/ppermute | solution.py:250
  13.1 10.7 %collective-permute-start = (bf16[96,896]{1,0:T(8,128)(2,1)S(1)}, bf16[96,896]{1,0:T(8,128)(2,1)S(1)}, u32[]{:S(2)}, u32[]{:S(2)}) collective-permute-start(bf16[96,896]{1,0:T(8,128)(2,1)S(1)} %get-tuple-element.108), channel_id=1, source_target_pairs={{0,1},{1,0},{2,3},{3,2},{4,5},{5,4},{6,7},{7,6},{8,9},{9,8},{10,11... | collective-permute-start | bytes 516104 | tf_op jit(solution)/shard_map/ppermute | solution.py:250
  14.0 10.6 %collective-permute-start.1 = (bf16[96,896]{1,0:T(8,128)(2,1)S(1)}, bf16[96,896]{1,0:T(8,128)(2,1)S(1)}, u32[]{:S(2)}, u32[]{:S(2)}) collective-permute-start(bf16[96,896]{1,0:T(8,128)(2,1)S(1)} %get-tuple-element.110), channel_id=1, source_target_pairs={{0,2},{1,3},{2,0},{3,1},{4,6},{5,7},{6,4},{7,5},{8,10},{9,11},{10,... | collective-permute-start | bytes 516104 | tf_op jit(solution)/shard_map/ppermute | solution.py:250
  20.8 8.1 %collective-permute-start.4 = (bf16[8,2,2,32,128]{4,3,2,1,0:T(8,128)(2,1)S(1)}, bf16[8,2,2,32,128]{4,3,2,1,0:T(8,128)(2,1)S(1)}, u32[]{:S(2)}, u32[]{:S(2)}) collective-permute-start(bf16[8,2,2,32,128]{4,3,2,1,0:T(8,128)(2,1)S(1)} %bitcast.31), channel_id=1, source_target_pairs={{0,24},{8,0},{16,8},{24,16},{1,25},{9,1},{17,9},{25,17},{2,26},{10... | collective-permute-start | bytes 786440 | tf_op jit(solution)/shard_map/ppermute | solution.py:250
  23.8 8.5 %collective-permute-start.3 = (bf16[8,2,2,32,128]{4,3,2,1,0:T(8,128)(2,1)S(1)}, bf16[8,2,2,32,128]{4,3,2,1,0:T(8,128)(2,1)S(1)}, u32[]{:S(2)}, u32[]{:S(2)}) collective-permute-start(bf16[8,2,2,32,128]{4,3,2,1,0:T(8,128)(2,1)S(1)} %bitcast.32), channel_id=1, source_target_pairs={{0,8},{8,16},{16,24},{24,0},{1,9},{9,17},{17,25},{25,1},{2,10},{10... | collective-permute-start | bytes 786440 | tf_op jit(solution)/shard_map/ppermute | solution.py:250
  24.5 8.3 %collective-permute-start.5 = (bf16[8,2,2,32,128]{4,3,2,1,0:T(8,128)(2,1)S(1)}, bf16[8,2,2,32,128]{4,3,2,1,0:T(8,128)(2,1)S(1)}, u32[]{:S(2)}, u32[]{:S(2)}) collective-permute-start(bf16[8,2,2,32,128]{4,3,2,1,0:T(8,128)(2,1)S(1)} %bitcast.33), channel_id=1, source_target_pairs={{0,4},{4,0},{1,5},{5,1},{2,6},{6,2},{3,7},{7,3},{8,12},{12,8},{9,1... | collective-permute-start | bytes 786440 | tf_op jit(solution)/shard_map/ppermute | solution.py:250
  25.3 1.1 %copy-start = (bf16[1,384,896]{2,1,0:T(8,128)(2,1)S(1)}, bf16[1,384,896]{2,1,0:T(8,128)(2,1)}, u32[]{:S(2)}) copy-start(bf16[1,384,896]{2,1,0:T(8,128)(2,1)} %param.10) | copy-start | bytes 2064388
  26.4 1.1 %copy-start.1 = (bf16[1,384,896]{2,1,0:T(8,128)(2,1)S(1)}, bf16[1,384,896]{2,1,0:T(8,128)(2,1)}, u32[]{:S(2)}) copy-start(bf16[1,384,896]{2,1,0:T(8,128)(2,1)} %param.15) | copy-start | bytes 2064388
  32.3 7.9 %collective-permute-start.6 = (bf16[8,2,2,32,128]{4,3,2,1,0:T(8,128)(2,1)S(1)}, bf16[8,2,2,32,128]{4,3,2,1,0:T(8,128)(2,1)S(1)}, u32[]{:S(2)}, u32[]{:S(2)}) collective-permute-start(bf16[8,2,2,32,128]{4,3,2,1,0:T(8,128)(2,1)S(1)} %bitcast.34), channel_id=1, source_target_pairs={{0,16},{8,24},{16,0},{24,8},{1,17},{9,25},{17,1},{25,9},{2,18},{10... | collective-permute-start | bytes 786440 | tf_op jit(solution)/shard_map/ppermute | solution.py:250
  32.3 10.0 %collective-permute-start.8 = (bf16[8,2,2,32,128]{4,3,2,1,0:T(8,128)(2,1)S(1)}, bf16[8,2,2,32,128]{4,3,2,1,0:T(8,128)(2,1)S(1)}, u32[]{:S(2)}, u32[]{:S(2)}) collective-permute-start(bf16[8,2,2,32,128]{4,3,2,1,0:T(8,128)(2,1)S(1)} %collective-permute-done.3.refs_1_.refs_7_), channel_id=1, source_target_pairs={{0,4},{4,0},{1,5},{5,1},{2,6},{6,2},{3,7},{7,3},{8,12},{12,8},{9,1... | collective-permute-start | bytes 786440 | tf_op jit(solution)/shard_map/ppermute | solution.py:250
  32.3 10.0 %collective-permute-start.9 = (bf16[8,2,2,32,128]{4,3,2,1,0:T(8,128)(2,1)S(1)}, bf16[8,2,2,32,128]{4,3,2,1,0:T(8,128)(2,1)S(1)}, u32[]{:S(2)}, u32[]{:S(2)}) collective-permute-start(bf16[8,2,2,32,128]{4,3,2,1,0:T(8,128)(2,1)S(1)} %collective-permute-done.4.refs_2_.refs_8_), channel_id=1, source_target_pairs={{0,4},{4,0},{1,5},{5,1},{2,6},{6,2},{3,7},{7,3},{8,12},{12,8},{9,1... | collective-permute-start | bytes 786440 | tf_op jit(solution)/shard_map/ppermute | solution.py:250
  40.2 15.3 %copy-start.2 = (bf16[1,384,128]{2,1,0:T(8,128)(2,1)S(1)}, bf16[1,384,128]{2,1,0:T(8,128)(2,1)}, u32[]{:S(2)}) copy-start(bf16[1,384,128]{2,1,0:T(8,128)(2,1)} %param.11) | copy-start | bytes 294916
  40.2 15.3 %copy-start.3 = (bf16[1,384,128]{2,1,0:T(8,128)(2,1)S(1)}, bf16[1,384,128]{2,1,0:T(8,128)(2,1)}, u32[]{:S(2)}) copy-start(bf16[1,384,128]{2,1,0:T(8,128)(2,1)} %param.12) | copy-start | bytes 294916
  40.2 2.1 %collective-permute-start.7 = (bf16[8,2,2,32,128]{4,3,2,1,0:T(8,128)(2,1)S(1)}, bf16[8,2,2,32,128]{4,3,2,1,0:T(8,128)(2,1)S(1)}, u32[]{:S(2)}, u32[]{:S(2)}) collective-permute-start(bf16[8,2,2,32,128]{4,3,2,1,0:T(8,128)(2,1)S(1)} %collective-permute-done.6.refs_0_.refs_11_), channel_id=1, source_target_pairs={{0,4},{4,0},{1,5},{5,1},{2,6},{6,2},{3,7},{7,3},{8,12},{12,8},{9,1... | collective-permute-start | bytes 786440 | tf_op jit(solution)/shard_map/ppermute | solution.py:250
  40.2 8.9 %collective-permute-start.10 = (bf16[528,128]{1,0:T(8,128)(2,1)S(1)}, bf16[528,128]{1,0:T(8,128)(2,1)S(1)}, u32[]{:S(2)}, u32[]{:S(2)}) collective-permute-start(bf16[528,128]{1,0:T(8,128)(2,1)S(1)} %get-tuple-element.86), channel_id=1, source_target_pairs={{0,24},{4,28},{8,0},{12,4},{16,8},{20,12},{24,16},{28,20},{1,25},{... | collective-permute-start | bytes 405512 | tf_op jit(solution)/shard_map/ppermute | solution.py:250
  42.1 7.0 %collective-permute-start.11 = (bf16[528,128]{1,0:T(8,128)(2,1)S(1)}, bf16[528,128]{1,0:T(8,128)(2,1)S(1)}, u32[]{:S(2)}, u32[]{:S(2)}) collective-permute-start(bf16[528,128]{1,0:T(8,128)(2,1)S(1)} %get-tuple-element.87), channel_id=1, source_target_pairs={{0,8},{4,12},{8,16},{12,20},{16,24},{20,28},{24,0},{28,4},{1,9},{5... | collective-permute-start | bytes 405512 | tf_op jit(solution)/shard_map/ppermute | solution.py:250
  42.3 6.8 %collective-permute-start.12 = (bf16[528,128]{1,0:T(8,128)(2,1)S(1)}, bf16[528,128]{1,0:T(8,128)(2,1)S(1)}, u32[]{:S(2)}, u32[]{:S(2)}) collective-permute-start(bf16[528,128]{1,0:T(8,128)(2,1)S(1)} %get-tuple-element.88), channel_id=1, source_target_pairs={{0,4},{4,0},{8,12},{12,8},{16,20},{20,16},{24,28},{28,24},{1,5},{5... | collective-permute-start | bytes 405512 | tf_op jit(solution)/shard_map/ppermute | solution.py:250
  49.1 12.7 %collective-permute-start.13 = (bf16[528,128]{1,0:T(8,128)(2,1)S(1)}, bf16[528,128]{1,0:T(8,128)(2,1)S(1)}, u32[]{:S(2)}, u32[]{:S(2)}) collective-permute-start(bf16[528,128]{1,0:T(8,128)(2,1)S(1)} %get-tuple-element.93), channel_id=1, source_target_pairs={{0,16},{4,20},{8,24},{12,28},{16,0},{20,4},{24,8},{28,12},{1,17},{... | collective-permute-start | bytes 405512 | tf_op jit(solution)/shard_map/ppermute | solution.py:250
  52.1 9.7 %collective-permute-start.14 = (bf16[528,128]{1,0:T(8,128)(2,1)S(1)}, bf16[528,128]{1,0:T(8,128)(2,1)S(1)}, u32[]{:S(2)}, u32[]{:S(2)}) collective-permute-start(bf16[528,128]{1,0:T(8,128)(2,1)S(1)} %get-tuple-element.94), channel_id=1, source_target_pairs={{0,20},{4,16},{8,28},{12,24},{16,4},{20,0},{24,12},{28,8},{1,21},{... | collective-permute-start | bytes 405512 | tf_op jit(solution)/shard_map/ppermute | solution.py:250
  52.5 9.9 %collective-permute-start.15 = (bf16[528,128]{1,0:T(8,128)(2,1)S(1)}, bf16[528,128]{1,0:T(8,128)(2,1)S(1)}, u32[]{:S(2)}, u32[]{:S(2)}) collective-permute-start(bf16[528,128]{1,0:T(8,128)(2,1)S(1)} %get-tuple-element.95), channel_id=1, source_target_pairs={{0,28},{4,24},{8,4},{12,0},{16,12},{20,8},{24,20},{28,16},{1,29},{... | collective-permute-start | bytes 405512 | tf_op jit(solution)/shard_map/ppermute | solution.py:250
  55.5 7.0 %collective-permute-start.16 = (bf16[528,128]{1,0:T(8,128)(2,1)S(1)}, bf16[528,128]{1,0:T(8,128)(2,1)S(1)}, u32[]{:S(2)}, u32[]{:S(2)}) collective-permute-start(bf16[528,128]{1,0:T(8,128)(2,1)S(1)} %get-tuple-element.96), channel_id=1, source_target_pairs={{0,12},{4,8},{8,20},{12,16},{16,28},{20,24},{24,4},{28,0},{1,13},{... | collective-permute-start | bytes 405512 | tf_op jit(solution)/shard_map/ppermute | solution.py:250

commit v12 on v11

--- a/solution.py
+++ b/solution.py
@@ -240,7 +240,7 @@
 
 def exchange(blocks, axis):
     order = list(range(lax.axis_size(axis)))[::-1]
-    order.insert(len(order) - 2, order.pop(2))
+    order.insert(len(order) - 2, order.pop(len(order) - 3))
     return lax.all_to_all(
         blocks, axis, split_axis=0, concat_axis=0, axis_index_groups=[order], tiled=True
     )

time: 81 us -> 79 us (0.975)
  waiting for transfers between devices: 7.85 us -> 4.7 us
  starting transfers between devices: 26 us -> 29.1 us
  blocking collectives: 16.6 us -> 15 us
    ppermute x17, starting transfers between devices: 16.8 us -> 19.9 us  [trade(): lax.ppermute(block, axis, [(i, target(i)) for i in range(lax.axis_size(ax...]
    ppermute x17, waiting for transfers between devices: 5.78 us -> 4.11 us  [trade(): lax.ppermute(block, axis, [(i, target(i)) for i in range(lax.axis_size(ax...]
    all_to_all x1, blocking collectives: 16.6 us -> 15 us  [exchange(): lax.all_to_all(blocks, axis, split_axis=0, concat_axis=0, axis_index_grou...]
    all_to_all x1, waiting for transfers between devices: 2.07 us -> 0.59 us  [exchange(): lax.all_to_all(blocks, axis, split_axis=0, concat_axis=0, axis_index_grou...]
  transfers between devices with their start and end apart: 18 -> 18, of which waited for: 6 -> 4; matrix products, arithmetic and copies ran while one was open for 3% -> 3% of each run, Pallas kernels for 26% -> 27%
where the time goes in v12:
time: 79 us; the launch traced here: 78.5 us
  starting transfers between devices  29.1 us (37%)
  Pallas kernels  22.8 us (29%)
  blocking collectives  15 us (19%)
  local copies, waits for them, and re-layouts  4.75 us (6%)
  waiting for transfers between devices  4.7 us (6%)
  between operations  2.04 us (3%)
    ppermute x17, starting transfers between devices, trade(): lax.ppermute(block, axis, [(i, target(i)) for i in range(lax.axis_size(ax...  19.9 us
    all_to_all x1, blocking collectives, exchange(): lax.all_to_all(blocks, axis, split_axis=0, concat_axis=0, axis_index_grou...  15 us
    pallas_call x2, Pallas kernels, prompt_part(): pl.pallas_call(functools.partial(prompt_kernel, count=len(pairs)), in_spe...  13.3 us
    all_to_all x1, starting transfers between devices, exchange(): lax.all_to_all(blocks, axis, split_axis=0, concat_axis=0, axis_index_grou...  9.21 us
    pallas_call x1, Pallas kernels, suffix_part(): pl.pallas_call(functools.partial(suffix_kernel, counts=[len(pairs) for pa...  6.35 us
    ppermute x17, waiting for transfers between devices, trade(): lax.ppermute(block, axis, [(i, target(i)) for i in range(lax.axis_size(ax...  4.11 us
    unnamed x9, local copies, waits for them, and re-layouts  2.91 us
  transfers between devices with their start and end apart: 18, of which 4 were waited for; matrix products, arithmetic and copies ran while one was open for 3% of the time, Pallas kernels for 27%

profile of v12, /device:TPU:6, one launch (start us, length us, event | category | flops | bytes accessed | tf_op | source)
XLA Modules:
  0.0 78.5 jit_solution(2997151137331752150)
XLA Ops:
  0.6 1.5 %spread.1 = bf16[8,2,2,32,128]{4,3,2,1,0:T(8,128)(2,1)} custom-call(bf16[2,32,128]{2,1,0:T(8,128)(2,1)} %key_ref.1, bf16[2,32,128]{2,1,0:T(8,128)(2,1)} %value_ref.1), custom_call_target="tpu_custom_call" | custom-call | tf_op jit(solution)/shard_map/spread/pallas_call | solution.py:47
  2.1 9.2 %all-to-all-start = ((bf16[8,128,128]{2,1,0:T(8,128)(2,1)}), bf16[8,128,128]{2,1,0:T(8,128)(2,1)S(1)}, u32[]{:S(2)}, u32[]{:S(2)}) async-start(bf16[8,128,128]{2,1,0:T(8,128)(2,1)} %bitcast.42), calls=%async_computation | async-start | bytes 524288 | tf_op jit(solution)/shard_map/all_to_all | solution.py:244
  11.3 1.2 %dynamic-slice_bitcast_fusion = (bf16[96,896]{1,0:T(8,128)(2,1)S(1)}, bf16[96,896]{1,0:T(8,128)(2,1)S(1)}, bf16[96,896]{1,0:T(8,128)(2,1)S(1)}, bf16[96,896]{1,0:T(8,128)(2,1)S(1)}) fusion(bf16[1,96,3584]{2,1,0:T(8,128)(2,1)} %param.16, s32[]{:T(128)S(6)} %select_n.15, s32[]{:T(128)S(6)} %select_n.13, s32[]{:T(128)S(6)} %select_n.12, s32[]{:T(128)S(6)} %select_n.14), kind=kLoop, calls=%fused_computation | loop fusion | bytes 1376272 | tf_op jit(solution)/shard_map/dynamic_slice | solution.py:268
  12.5 0.6 collective-permute-start.2
  13.1 0.9 %collective-permute-start = (bf16[96,896]{1,0:T(8,128)(2,1)S(1)}, bf16[96,896]{1,0:T(8,128)(2,1)S(1)}, u32[]{:S(2)}, u32[]{:S(2)}) collective-permute-start(bf16[96,896]{1,0:T(8,128)(2,1)S(1)} %get-tuple-element.108), channel_id=1, source_target_pairs={{0,1},{1,0},{2,3},{3,2},{4,5},{5,4},{6,7},{7,6},{8,9},{9,8},{10,11... | collective-permute-start | bytes 516104 | tf_op jit(solution)/shard_map/ppermute | solution.py:250
  14.0 3.3 %collective-permute-start.1 = (bf16[96,896]{1,0:T(8,128)(2,1)S(1)}, bf16[96,896]{1,0:T(8,128)(2,1)S(1)}, u32[]{:S(2)}, u32[]{:S(2)}) collective-permute-start(bf16[96,896]{1,0:T(8,128)(2,1)S(1)} %get-tuple-element.110), channel_id=1, source_target_pairs={{0,2},{1,3},{2,0},{3,1},{4,6},{5,7},{6,4},{7,5},{8,10},{9,11},{10,... | collective-permute-start | bytes 516104 | tf_op jit(solution)/shard_map/ppermute | solution.py:250
  18.6 0.1 pad_add_fusion.info_ref
  18.7 0.6 all-to-all-done
  19.3 3.0 %collective-permute-start.4 = (bf16[8,2,2,32,128]{4,3,2,1,0:T(8,128)(2,1)S(1)}, bf16[8,2,2,32,128]{4,3,2,1,0:T(8,128)(2,1)S(1)}, u32[]{:S(2)}, u32[]{:S(2)}) collective-permute-start(bf16[8,2,2,32,128]{4,3,2,1,0:T(8,128)(2,1)S(1)} %bitcast.31), channel_id=1, source_target_pairs={{0,24},{8,0},{16,8},{24,16},{1,25},{9,1},{17,9},{25,17},{2,26},{10... | collective-permute-start | bytes 786440 | tf_op jit(solution)/shard_map/ppermute | solution.py:250
  22.3 0.0 collective-permute-start.3
  22.3 0.0 collective-permute-done.2.refs_3_
  22.3 0.0 collective-permute-done.refs_1_
  22.3 2.2 %collective-permute-done.1.refs_2_ = bf16[96,896]{1,0:T(8,128)(2,1)S(1)} collective-permute-done((bf16[96,896]{1,0:T(8,128)(2,1)S(1)}, bf16[96,896]{1,0:T(8,128)(2,1)S(1)}, u32[]{:S(2)}, u32[]{:S(2)}) %collective-permute-start.1) | collective-permute-done | bytes 172064 | tf_op jit(solution)/shard_map/ppermute | solution.py:250
  24.5 0.0 collective-permute-start.5
  24.6 0.7 copy.17
  25.3 0.0 copy-start
  25.3 1.1 %copy-done = bf16[1,384,896]{2,1,0:T(8,128)(2,1)S(1)} copy-done((bf16[1,384,896]{2,1,0:T(8,128)(2,1)S(1)}, bf16[1,384,896]{2,1,0:T(8,128)(2,1)}, u32[]{:S(2)}) %copy-start) | copy-done | bytes 688152
  26.4 0.0 copy-start.1
  26.4 1.1 %copy-done.1 = bf16[1,384,896]{2,1,0:T(8,128)(2,1)S(1)} copy-done((bf16[1,384,896]{2,1,0:T(8,128)(2,1)S(1)}, bf16[1,384,896]{2,1,0:T(8,128)(2,1)}, u32[]{:S(2)}) %copy-start.1) | copy-done | bytes 688152
  27.5 1.2 %prepare.1 = (bf16[384,896]{1,0:T(8,128)(2,1)S(1)}, bf16[128,2688]{1,0:T(8,128)(2,1)S(1)}, bf16[128,2688]{1,0:T(8,128)(2,1)S(1)}, f32[1,2688]{1,0:T(1,128)S(1)}, f32[1,2688]{1,0:T(1,128)S(1)}) custom-call(s32[3]{0:T(128)S(1)} %pad_add_fusion.info_ref, bf16[384,896]{1,0:T(8,128)(2,1)S(1)} %bitcast.27, bf16[384,896]{1,0:T(8,128)(2,1)S(1)} %bitcast.38, ...), custom_call_target="tpu_custom_call" | custom-call | flops 688128 | bytes 4128768 | tf_op jit(solution)/shard_map/prepare/pallas_call | solution.py:86
  28.7 0.0 collective-permute-done.4.refs_2_.refs_8_
  28.7 1.2 %collective-permute-done.3.refs_1_.refs_7_ = bf16[8,2,2,32,128]{4,3,2,1,0:T(8,128)(2,1)S(1)} collective-permute-done((bf16[8,2,2,32,128]{4,3,2,1,0:T(8,128)(2,1)S(1)}, bf16[8,2,2,32,128]{4,3,2,1,0:T(8,128)(2,1)S(1)}, u32[]{:S(2)}, u32[]{:S(2)}) %collective-permute-start.3) | collective-permute-done | bytes 262176 | tf_op jit(solution)/shard_map/ppermute | solution.py:250
  29.9 2.1 %collective-permute-start.6 = (bf16[8,2,2,32,128]{4,3,2,1,0:T(8,128)(2,1)S(1)}, bf16[8,2,2,32,128]{4,3,2,1,0:T(8,128)(2,1)S(1)}, u32[]{:S(2)}, u32[]{:S(2)}) collective-permute-start(bf16[8,2,2,32,128]{4,3,2,1,0:T(8,128)(2,1)S(1)} %bitcast.34), channel_id=1, source_target_pairs={{0,16},{8,24},{16,0},{24,8},{1,17},{9,25},{17,1},{25,9},{2,18},{10... | collective-permute-start | bytes 786440 | tf_op jit(solution)/shard_map/ppermute | solution.py:250
  32.0 0.2 collective-permute-start.8
  32.2 0.3 collective-permute-start.9
  32.5 0.0 collective-permute-done.5.refs_3_.refs_9_
  32.5 6.6 %prompt_part.2 = (bf16[1024,2688]{1,0:T(8,128)(2,1)S(1)}, bf16[528,128]{1,0:T(8,128)(2,1)S(1)}, bf16[528,128]{1,0:T(8,128)(2,1)S(1)}, bf16[528,128]{1,0:T(8,128)(2,1)S(1)}, bf16[528,128]{1,0:T(8,128)(2,1)S(1)}) custom-call(s32[3]{0:T(128)S(1)} %pad_add_fusion.info_ref, bf16[8,2,2,32,128]{4,3,2,1,0:T(8,128)(2,1)S(1)} %bitcast.35, ...), custom_call_target="tpu_custom_call" | custom-call | flops 3523215360 | bytes 5505024 | tf_op jit(solution)/shard_map/prompt_part/pallas_call | solution.py:202
  39.1 0.0 collective-permute-done.6.refs_0_.refs_11_
  39.1 0.0 copy-start.2
  39.1 0.0 copy-start.3
  39.2 0.3 collective-permute-start.7
  39.5 2.6 %collective-permute-start.10 = (bf16[528,128]{1,0:T(8,128)(2,1)S(1)}, bf16[528,128]{1,0:T(8,128)(2,1)S(1)}, u32[]{:S(2)}, u32[]{:S(2)}) collective-permute-start(bf16[528,128]{1,0:T(8,128)(2,1)S(1)} %get-tuple-element.86), channel_id=1, source_target_pairs={{0,24},{4,28},{8,0},{12,4},{16,8},{20,12},{24,16},{28,20},{1,25},{... | collective-permute-start | bytes 405512 | tf_op jit(solution)/shard_map/ppermute | solution.py:250
  42.1 0.0 collective-permute-start.11
  42.1 0.0 collective-permute-done.8.refs_2_.refs_13_
  42.1 0.2 collective-permute-start.12
  42.3 0.0 collective-permute-done.9.refs_3_.refs_14_
  42.3 0.0 collective-permute-done.7.refs_1_.refs_12_
  42.3 6.7 %prompt_part.3 = (bf16[1024,2688]{1,0:T(8,128)(2,1)S(1)}, bf16[528,128]{1,0:T(8,128)(2,1)S(1)}, bf16[528,128]{1,0:T(8,128)(2,1)S(1)}, bf16[528,128]{1,0:T(8,128)(2,1)S(1)}, bf16[528,128]{1,0:T(8,128)(2,1)S(1)}) custom-call(s32[3]{0:T(128)S(1)} %pad_add_fusion.info_ref, bf16[8,2,2,32,128]{4,3,2,1,0:T(8,128)(2,1)S(1)} %collective-permute-done.6.refs_0_.refs_11_, ...), custom_call_target="tpu_custom_call" | custom-call | flops 3523215360 | bytes 5505024 | tf_op jit(solution)/shard_map/prompt_part/pallas_call | solution.py:202
  49.0 0.0 collective-permute-done.10.refs_1_
  49.0 0.0 collective-permute-done.11.refs_2_
  49.0 0.0 collective-permute-done.12.refs_3_
  49.0 2.1 %collective-permute-start.13 = (bf16[528,128]{1,0:T(8,128)(2,1)S(1)}, bf16[528,128]{1,0:T(8,128)(2,1)S(1)}, u32[]{:S(2)}, u32[]{:S(2)}) collective-permute-start(bf16[528,128]{1,0:T(8,128)(2,1)S(1)} %get-tuple-element.93), channel_id=1, source_target_pairs={{0,16},{4,20},{8,24},{12,28},{16,0},{20,4},{24,8},{28,12},{1,17},{... | collective-permute-start | bytes 405512 | tf_op jit(solution)/shard_map/ppermute | solution.py:250
  51.2 1.2 %collective-permute-start.14 = (bf16[528,128]{1,0:T(8,128)(2,1)S(1)}, bf16[528,128]{1,0:T(8,128)(2,1)S(1)}, u32[]{:S(2)}, u32[]{:S(2)}) collective-permute-start(bf16[528,128]{1,0:T(8,128)(2,1)S(1)} %get-tuple-element.94), channel_id=1, source_target_pairs={{0,20},{4,16},{8,28},{12,24},{16,4},{20,0},{24,12},{28,8},{1,21},{... | collective-permute-start | bytes 405512 | tf_op jit(solution)/shard_map/ppermute | solution.py:250
  52.3 3.1 %collective-permute-start.15 = (bf16[528,128]{1,0:T(8,128)(2,1)S(1)}, bf16[528,128]{1,0:T(8,128)(2,1)S(1)}, u32[]{:S(2)}, u32[]{:S(2)}) collective-permute-start(bf16[528,128]{1,0:T(8,128)(2,1)S(1)} %get-tuple-element.95), channel_id=1, source_target_pairs={{0,28},{4,24},{8,4},{12,0},{16,12},{20,8},{24,20},{28,16},{1,29},{... | collective-permute-start | bytes 405512 | tf_op jit(solution)/shard_map/ppermute | solution.py:250
  55.5 0.0 collective-permute-start.16
  55.5 0.0 copy-done.2
  55.5 0.0 copy-done.3
  55.5 6.4 %suffix_part.1 = (bf16[384,896]{1,0:T(8,128)(2,1)}, bf16[384,128]{1,0:T(8,128)(2,1)}, bf16[384,128]{1,0:T(8,128)(2,1)}) custom-call(s32[3]{0:T(128)S(1)} %pad_add_fusion.info_ref, bf16[384,896]{1,0:T(8,128)(2,1)S(1)} %bitcast.30, bf16[384,896]{1,0:T(8,128)(2,1)S(1)} %get-tuple-element.62.refs_5_.refs_1_, ...), custom_call_target="tpu_custom_call" | custom-call | flops 1321205760 | bytes 5505024 | tf_op jit(solution)/shard_map/suffix_part/pallas_call | solution.py:167
  61.8 0.0 collective-permute-done.13.refs_4_
  61.8 0.0 collective-permute-done.14.refs_5_
  61.8 0.6 collective-permute-done.15.refs_6_
  62.5 0.0 collective-permute-done.16.refs_7_
  62.5 0.4 group_sum.1
  62.9 15.0 %all_to_all.10 = bf16[8,128,128]{2,1,0:T(8,128)(2,1)S(1)} all-to-all(bf16[8,128,128]{2,1,0:T(8,128)(2,1)S(1)} %bitcast.37), channel_id=1, replica_groups={{224,192,160,128,96,32,64,0},{225,193,161,129,97,33,65,1},{226,194,162,..., dimensions={0} | all-to-all | bytes 524288 | tf_op jit(solution)/shard_map/all_to_all | solution.py:244
  77.9 0.6 slice_bitcast_fusion
  (1 shorter events, 0.0 us)
Async XLA Ops:
  2.1 17.2 %all-to-all-start = ((bf16[8,128,128]{2,1,0:T(8,128)(2,1)}), bf16[8,128,128]{2,1,0:T(8,128)(2,1)S(1)}, u32[]{:S(2)}, u32[]{:S(2)}) async-start(bf16[8,128,128]{2,1,0:T(8,128)(2,1)} %bitcast.42), calls=%async_computation | async-start | bytes 524288 | tf_op jit(solution)/shard_map/all_to_all | solution.py:244
  12.5 9.8 %collective-permute-start.2 = (bf16[96,896]{1,0:T(8,128)(2,1)S(1)}, bf16[96,896]{1,0:T(8,128)(2,1)S(1)}, u32[]{:S(2)}, u32[]{:S(2)}) collective-permute-start(bf16[96,896]{1,0:T(8,128)(2,1)S(1)} %get-tuple-element.107), channel_id=1, source_target_pairs={{0,3},{1,2},{2,1},{3,0},{4,7},{5,6},{6,5},{7,4},{8,11},{9,10},{10,... | collective-permute-start | bytes 516104 | tf_op jit(solution)/shard_map/ppermute | solution.py:250
  13.1 9.2 %collective-permute-start = (bf16[96,896]{1,0:T(8,128)(2,1)S(1)}, bf16[96,896]{1,0:T(8,128)(2,1)S(1)}, u32[]{:S(2)}, u32[]{:S(2)}) collective-permute-start(bf16[96,896]{1,0:T(8,128)(2,1)S(1)} %get-tuple-element.108), channel_id=1, source_target_pairs={{0,1},{1,0},{2,3},{3,2},{4,5},{5,4},{6,7},{7,6},{8,9},{9,8},{10,11... | collective-permute-start | bytes 516104 | tf_op jit(solution)/shard_map/ppermute | solution.py:250
  14.0 10.6 %collective-permute-start.1 = (bf16[96,896]{1,0:T(8,128)(2,1)S(1)}, bf16[96,896]{1,0:T(8,128)(2,1)S(1)}, u32[]{:S(2)}, u32[]{:S(2)}) collective-permute-start(bf16[96,896]{1,0:T(8,128)(2,1)S(1)} %get-tuple-element.110), channel_id=1, source_target_pairs={{0,2},{1,3},{2,0},{3,1},{4,6},{5,7},{6,4},{7,5},{8,10},{9,11},{10,... | collective-permute-start | bytes 516104 | tf_op jit(solution)/shard_map/ppermute | solution.py:250
  19.3 9.4 %collective-permute-start.4 = (bf16[8,2,2,32,128]{4,3,2,1,0:T(8,128)(2,1)S(1)}, bf16[8,2,2,32,128]{4,3,2,1,0:T(8,128)(2,1)S(1)}, u32[]{:S(2)}, u32[]{:S(2)}) collective-permute-start(bf16[8,2,2,32,128]{4,3,2,1,0:T(8,128)(2,1)S(1)} %bitcast.31), channel_id=1, source_target_pairs={{0,24},{8,0},{16,8},{24,16},{1,25},{9,1},{17,9},{25,17},{2,26},{10... | collective-permute-start | bytes 786440 | tf_op jit(solution)/shard_map/ppermute | solution.py:250
  22.3 7.6 %collective-permute-start.3 = (bf16[8,2,2,32,128]{4,3,2,1,0:T(8,128)(2,1)S(1)}, bf16[8,2,2,32,128]{4,3,2,1,0:T(8,128)(2,1)S(1)}, u32[]{:S(2)}, u32[]{:S(2)}) collective-permute-start(bf16[8,2,2,32,128]{4,3,2,1,0:T(8,128)(2,1)S(1)} %bitcast.32), channel_id=1, source_target_pairs={{0,8},{8,16},{16,24},{24,0},{1,9},{9,17},{17,25},{25,1},{2,10},{10... | collective-permute-start | bytes 786440 | tf_op jit(solution)/shard_map/ppermute | solution.py:250
  24.5 7.9 %collective-permute-start.5 = (bf16[8,2,2,32,128]{4,3,2,1,0:T(8,128)(2,1)S(1)}, bf16[8,2,2,32,128]{4,3,2,1,0:T(8,128)(2,1)S(1)}, u32[]{:S(2)}, u32[]{:S(2)}) collective-permute-start(bf16[8,2,2,32,128]{4,3,2,1,0:T(8,128)(2,1)S(1)} %bitcast.33), channel_id=1, source_target_pairs={{0,4},{4,0},{1,5},{5,1},{2,6},{6,2},{3,7},{7,3},{8,12},{12,8},{9,1... | collective-permute-start | bytes 786440 | tf_op jit(solution)/shard_map/ppermute | solution.py:250
  25.3 1.1 %copy-start = (bf16[1,384,896]{2,1,0:T(8,128)(2,1)S(1)}, bf16[1,384,896]{2,1,0:T(8,128)(2,1)}, u32[]{:S(2)}) copy-start(bf16[1,384,896]{2,1,0:T(8,128)(2,1)} %param.10) | copy-start | bytes 2064388
  26.4 1.1 %copy-start.1 = (bf16[1,384,896]{2,1,0:T(8,128)(2,1)S(1)}, bf16[1,384,896]{2,1,0:T(8,128)(2,1)}, u32[]{:S(2)}) copy-start(bf16[1,384,896]{2,1,0:T(8,128)(2,1)} %param.15) | copy-start | bytes 2064388
  29.9 9.2 %collective-permute-start.6 = (bf16[8,2,2,32,128]{4,3,2,1,0:T(8,128)(2,1)S(1)}, bf16[8,2,2,32,128]{4,3,2,1,0:T(8,128)(2,1)S(1)}, u32[]{:S(2)}, u32[]{:S(2)}) collective-permute-start(bf16[8,2,2,32,128]{4,3,2,1,0:T(8,128)(2,1)S(1)} %bitcast.34), channel_id=1, source_target_pairs={{0,16},{8,24},{16,0},{24,8},{1,17},{9,25},{17,1},{25,9},{2,18},{10... | collective-permute-start | bytes 786440 | tf_op jit(solution)/shard_map/ppermute | solution.py:250
  32.0 10.1 %collective-permute-start.8 = (bf16[8,2,2,32,128]{4,3,2,1,0:T(8,128)(2,1)S(1)}, bf16[8,2,2,32,128]{4,3,2,1,0:T(8,128)(2,1)S(1)}, u32[]{:S(2)}, u32[]{:S(2)}) collective-permute-start(bf16[8,2,2,32,128]{4,3,2,1,0:T(8,128)(2,1)S(1)} %collective-permute-done.3.refs_1_.refs_7_), channel_id=1, source_target_pairs={{0,4},{4,0},{1,5},{5,1},{2,6},{6,2},{3,7},{7,3},{8,12},{12,8},{9,1... | collective-permute-start | bytes 786440 | tf_op jit(solution)/shard_map/ppermute | solution.py:250
  32.2 10.1 %collective-permute-start.9 = (bf16[8,2,2,32,128]{4,3,2,1,0:T(8,128)(2,1)S(1)}, bf16[8,2,2,32,128]{4,3,2,1,0:T(8,128)(2,1)S(1)}, u32[]{:S(2)}, u32[]{:S(2)}) collective-permute-start(bf16[8,2,2,32,128]{4,3,2,1,0:T(8,128)(2,1)S(1)} %collective-permute-done.4.refs_2_.refs_8_), channel_id=1, source_target_pairs={{0,4},{4,0},{1,5},{5,1},{2,6},{6,2},{3,7},{7,3},{8,12},{12,8},{9,1... | collective-permute-start | bytes 786440 | tf_op jit(solution)/shard_map/ppermute | solution.py:250
  39.1 16.3 %copy-start.2 = (bf16[1,384,128]{2,1,0:T(8,128)(2,1)S(1)}, bf16[1,384,128]{2,1,0:T(8,128)(2,1)}, u32[]{:S(2)}) copy-start(bf16[1,384,128]{2,1,0:T(8,128)(2,1)} %param.11) | copy-start | bytes 294916
  39.1 16.3 %copy-start.3 = (bf16[1,384,128]{2,1,0:T(8,128)(2,1)S(1)}, bf16[1,384,128]{2,1,0:T(8,128)(2,1)}, u32[]{:S(2)}) copy-start(bf16[1,384,128]{2,1,0:T(8,128)(2,1)} %param.12) | copy-start | bytes 294916
  39.2 3.1 %collective-permute-start.7 = (bf16[8,2,2,32,128]{4,3,2,1,0:T(8,128)(2,1)S(1)}, bf16[8,2,2,32,128]{4,3,2,1,0:T(8,128)(2,1)S(1)}, u32[]{:S(2)}, u32[]{:S(2)}) collective-permute-start(bf16[8,2,2,32,128]{4,3,2,1,0:T(8,128)(2,1)S(1)} %collective-permute-done.6.refs_0_.refs_11_), channel_id=1, source_target_pairs={{0,4},{4,0},{1,5},{5,1},{2,6},{6,2},{3,7},{7,3},{8,12},{12,8},{9,1... | collective-permute-start | bytes 786440 | tf_op jit(solution)/shard_map/ppermute | solution.py:250
  39.5 9.5 %collective-permute-start.10 = (bf16[528,128]{1,0:T(8,128)(2,1)S(1)}, bf16[528,128]{1,0:T(8,128)(2,1)S(1)}, u32[]{:S(2)}, u32[]{:S(2)}) collective-permute-start(bf16[528,128]{1,0:T(8,128)(2,1)S(1)} %get-tuple-element.86), channel_id=1, source_target_pairs={{0,24},{4,28},{8,0},{12,4},{16,8},{20,12},{24,16},{28,20},{1,25},{... | collective-permute-start | bytes 405512 | tf_op jit(solution)/shard_map/ppermute | solution.py:250
  42.1 6.9 %collective-permute-start.11 = (bf16[528,128]{1,0:T(8,128)(2,1)S(1)}, bf16[528,128]{1,0:T(8,128)(2,1)S(1)}, u32[]{:S(2)}, u32[]{:S(2)}) collective-permute-start(bf16[528,128]{1,0:T(8,128)(2,1)S(1)} %get-tuple-element.87), channel_id=1, source_target_pairs={{0,8},{4,12},{8,16},{12,20},{16,24},{20,28},{24,0},{28,4},{1,9},{5... | collective-permute-start | bytes 405512 | tf_op jit(solution)/shard_map/ppermute | solution.py:250
  42.1 6.9 %collective-permute-start.12 = (bf16[528,128]{1,0:T(8,128)(2,1)S(1)}, bf16[528,128]{1,0:T(8,128)(2,1)S(1)}, u32[]{:S(2)}, u32[]{:S(2)}) collective-permute-start(bf16[528,128]{1,0:T(8,128)(2,1)S(1)} %get-tuple-element.88), channel_id=1, source_target_pairs={{0,4},{4,0},{8,12},{12,8},{16,20},{20,16},{24,28},{28,24},{1,5},{5... | collective-permute-start | bytes 405512 | tf_op jit(solution)/shard_map/ppermute | solution.py:250
  49.0 12.8 %collective-permute-start.13 = (bf16[528,128]{1,0:T(8,128)(2,1)S(1)}, bf16[528,128]{1,0:T(8,128)(2,1)S(1)}, u32[]{:S(2)}, u32[]{:S(2)}) collective-permute-start(bf16[528,128]{1,0:T(8,128)(2,1)S(1)} %get-tuple-element.93), channel_id=1, source_target_pairs={{0,16},{4,20},{8,24},{12,28},{16,0},{20,4},{24,8},{28,12},{1,17},{... | collective-permute-start | bytes 405512 | tf_op jit(solution)/shard_map/ppermute | solution.py:250
  51.2 10.7 %collective-permute-start.14 = (bf16[528,128]{1,0:T(8,128)(2,1)S(1)}, bf16[528,128]{1,0:T(8,128)(2,1)S(1)}, u32[]{:S(2)}, u32[]{:S(2)}) collective-permute-start(bf16[528,128]{1,0:T(8,128)(2,1)S(1)} %get-tuple-element.94), channel_id=1, source_target_pairs={{0,20},{4,16},{8,28},{12,24},{16,4},{20,0},{24,12},{28,8},{1,21},{... | collective-permute-start | bytes 405512 | tf_op jit(solution)/shard_map/ppermute | solution.py:250
  52.3 10.1 %collective-permute-start.15 = (bf16[528,128]{1,0:T(8,128)(2,1)S(1)}, bf16[528,128]{1,0:T(8,128)(2,1)S(1)}, u32[]{:S(2)}, u32[]{:S(2)}) collective-permute-start(bf16[528,128]{1,0:T(8,128)(2,1)S(1)} %get-tuple-element.95), channel_id=1, source_target_pairs={{0,28},{4,24},{8,4},{12,0},{16,12},{20,8},{24,20},{28,16},{1,29},{... | collective-permute-start | bytes 405512 | tf_op jit(solution)/shard_map/ppermute | solution.py:250
  55.5 7.0 %collective-permute-start.16 = (bf16[528,128]{1,0:T(8,128)(2,1)S(1)}, bf16[528,128]{1,0:T(8,128)(2,1)S(1)}, u32[]{:S(2)}, u32[]{:S(2)}) collective-permute-start(bf16[528,128]{1,0:T(8,128)(2,1)S(1)} %get-tuple-element.96), channel_id=1, source_target_pairs={{0,12},{4,8},{8,20},{12,16},{16,28},{20,24},{24,4},{28,0},{1,13},{... | collective-permute-start | bytes 405512 | tf_op jit(solution)/shard_map/ppermute | solution.py:250
